TPU v7x, 32 devices: a whole 2x2x4 slice. The times are simulated.
32 devices in a mesh: dp: 8 (over y, x, core), chan: 4 (over z).
Axes of the slice: x: 2, y: 2, z: 4, core: 2. Of those that a mesh axis runs over, the one named last changes fastest.
Arguments:
- hidden: bfloat16 [16, 14, 14, 3072], P('dp', None, None, 'chan'), may hold values from -6 to 6
- conv_weight: bfloat16 [3, 3, 64, 3072], P(None, None, None, 'chan'), may hold values from -0.25 to 0.25
- se_down: bfloat16 [3072, 1024], P('chan'), may hold values from -0.875 to 0.875
- se_up: bfloat16 [1024, 3072], P(None, 'chan'), may hold values from -0.75 to 0.75
- proj_weight: bfloat16 [3072, 3072], P('chan'), may hold values from -0.109375 to 0.109375
- grad_out: bfloat16 [16, 14, 14, 3072], P('dp', None, None, 'chan'), may hold values from -6 to 6
Outputs:
- projected: bfloat16 [16, 14, 14, 3072], P('dp', None, None, 'chan')
- grad_hidden: bfloat16 [16, 14, 14, 3072], P('dp', None, None, 'chan')
- grad_proj: float32 [3072, 3072], P('chan', 'dp')
All inputs are finite; a program needn't handle non-finite values.
Results may differ from a plain program's by a relative error of at most 0.024.
Values may be sent and summed in bfloat16 or wider, within the bound.
No kernel may reach another device: no remote copies, remote signals or barrier semaphores. Data moves between devices by JAX's collectives and lax.ppermute only.
A program may use at most 64 MiB of HBM per device.

v0:
```python
import jax
import jax.numpy as jnp
from jax import lax
from jax.sharding import PartitionSpec as P


def grouped(inputs, kernel):
    return lax.conv_general_dilated(
        inputs,
        kernel,
        (1, 1),
        "SAME",
        dimension_numbers=("NHWC", "HWIO", "NHWC"),
        feature_group_count=kernel.shape[3] // kernel.shape[2],
        preferred_element_type=jnp.float32,
    )


def turned(kernel):
    size_in = kernel.shape[2]
    group_count = kernel.shape[3] // size_in
    split = kernel.reshape(3, 3, size_in, group_count, size_in)
    return jnp.transpose(split, (0, 1, 4, 3, 2))[::-1, ::-1].reshape(kernel.shape)


def silu_grad(values):
    logistic = jax.nn.sigmoid(values)
    return logistic * (1.0 + values * (1.0 - logistic))


def on_device(hidden, conv_weight, se_down, se_up, proj_weight, grad_out):
    highest = lax.Precision.HIGHEST
    local_ch = hidden.shape[3]
    cells = hidden.shape[1] * hidden.shape[2]
    convolved = grouped(hidden, conv_weight)
    activated = jax.nn.silu(convolved).astype(jnp.bfloat16)
    act_float = activated.astype(jnp.float32)
    squeezed = jnp.mean(act_float, axis=(1, 2))
    excite_pre = lax.psum(jnp.dot(squeezed, se_down.astype(jnp.float32), precision=highest), "chan")
    gating = jax.nn.sigmoid(
        jnp.dot(jax.nn.silu(excite_pre), se_up.astype(jnp.float32), precision=highest)
    )
    scaled = (act_float * gating[:, None, None, :]).astype(jnp.bfloat16)
    act_rows = scaled.reshape(-1, local_ch)
    weight_cols = proj_weight
    summed = lax.psum_scatter(
        lax.dot_general(
            weight_cols, act_rows, (((0,), (1,)), ((), ())), preferred_element_type=jnp.float32
        ).astype(jnp.bfloat16),
        "chan",
        scatter_dimension=0,
        tiled=True,
    ).astype(jnp.float32)
    out_rows = summed.T
    projected = out_rows.astype(jnp.bfloat16).reshape(hidden.shape)
    shard_piece = lax.all_gather(grad_out, "chan", axis=3, tiled=True)
    width_in = shard_piece.shape[3]
    piece_rows = shard_piece.reshape(-1, width_in)
    weight_cols = proj_weight
    dv_next = lax.dot_general(
        piece_rows, weight_cols, (((1,), (1,)), ((), ())), preferred_element_type=jnp.float32
    )
    dw_block = lax.dot_general(
        act_rows, piece_rows, (((0,), (0,)), ((), ())), preferred_element_type=jnp.float32
    )
    grad_proj = lax.psum_scatter(dw_block, "dp", scatter_dimension=1, tiled=True)
    scaled_grad = dv_next.reshape(hidden.shape)
    gate_grad = jnp.sum(scaled_grad * act_float, axis=(1, 2))
    pre_grad = gate_grad * gating * (1.0 - gating)
    excite_sum = lax.psum(jnp.dot(pre_grad, se_up.astype(jnp.float32).T, precision=highest), "chan")
    excite_grad = excite_sum * silu_grad(excite_pre)
    squeeze_grad = jnp.dot(excite_grad, se_down.astype(jnp.float32).T, precision=highest)
    act_grad = scaled_grad * gating[:, None, None, :] + squeeze_grad[:, None, None, :] / cells
    conv_grad = (act_grad * silu_grad(convolved)).astype(jnp.bfloat16)
    grad_hidden = grouped(conv_grad, turned(conv_weight)).astype(jnp.bfloat16)
    return (projected, grad_hidden, grad_proj)


def solution(mesh):
    in_specs = (
        P("dp", None, None, "chan"),
        P(None, None, None, "chan"),
        P("chan", None),
        P(None, "chan"),
        P("chan", None),
        P("dp", None, None, "chan"),
    )
    out_specs = (P("dp", None, None, "chan"), P("dp", None, None, "chan"), P("chan", "dp"))
    return jax.shard_map(
        on_device, mesh=mesh, in_specs=in_specs, out_specs=out_specs, check_vma=False
    )
```

profile of v0, /device:TPU:0, one launch (start us, length us, event | category | flops | bytes accessed | tf_op | source)
XLA Modules:
  0.0 207.9 jit_solution(8277139778202713347)
XLA Ops:
  7.2 2.1 %copy.32 = bf16[2,14,14,768]{3,2,1,0:T(8,128)(2,1)} copy(bf16[2,14,14,768]{3,0,2,1:T(2,128)(2,1)} %param.11) | data formatting | bytes 1204224 | tf_op args[5]
  9.4 0.0 reduce-scatter.3.cloned.1.call-start
  9.5 1.9 shard_map.89
  11.4 2.7 %shard_map.90 = bf16[3,3,64,12,64]{4,3,2,1,0:T(8,128)(2,1)} reshape(bf16[3,3,64,768]{3,2,1,0:T(8,128)(2,1)S(1)} %copy-done.3) | data formatting | bytes 1769472 | tf_op jit(solution)/shard_map/shard_map
  14.1 11.0 %convert_reduce_fusion = (f32[2,12,64]{2,0,1:T(2,128)S(1)}, f32[2,14,14,12,64]{4,0,3,2,1:T(2,128)}) fusion(bf16[3,3,64,12,64]{4,3,2,1,0:T(8,128)(2,1)} %shard_map.90, bf16[2,14,14,12,64]{4,3,0,2,1:T(8,128)(2,1)} %shard_map.89), kind=kOutput, calls=%fused_computation.6 | convolution fusion | flops 316678656 | bytes 2697216 | tf_op jit(solution)/shard_map/conv_general_dilated | solution.py:8
  25.1 0.1 div.37
  25.2 0.7 fusion.32
  25.9 14.4 %psum.14 = f32[2,1024]{1,0:T(2,128)S(1)} all-reduce(f32[2,1024]{1,0:T(2,128)S(1)} %fusion.32), channel_id=1, replica_groups=mesh['dp'=8,'chan'=4] {'chan'}, use_global_device_ids=true, to_apply=%region_1.2 | all-reduce | flops 2048 | bytes 16384 | tf_op jit(solution)/shard_map/psum | solution.py:39
  40.3 0.7 fusion.13
  41.1 1.3 mul.63
  42.3 2.5 %mul.64 = f32[392,768]{1,0:T(8,128)} reshape(f32[2,14,14,768]{3,2,1,0:T(8,128)} %mul.63) | data formatting | bytes 2408448 | tf_op jit(solution)/shard_map/mul | solution.py:43
  44.8 3.8 %copy.30 = f32[2,14,14,12,64]{4,3,2,1,0:T(8,128)} copy(f32[2,14,14,12,64]{4,0,3,2,1:T(2,128)} %get-tuple-element.13) | data formatting | bytes 2408448 | tf_op jit(solution)/shard_map/conv_general_dilated | solution.py:8
  48.6 3.4 %conv_general_dilated.11 = f32[392,768]{1,0:T(8,128)} reshape(f32[2,14,14,12,64]{4,3,2,1,0:T(8,128)} %copy.30) | data formatting | bytes 2408448 | tf_op jit(solution)/shard_map/conv_general_dilated | solution.py:8
  52.0 6.7 %fusion.2 = bf16[3072,392]{0,1:T(8,128)(2,1)} fusion(bf16[768,3072]{1,0:T(8,128)(2,1)} %param.10, f32[392,768]{1,0:T(8,128)} %mul.64, f32[392,768]{1,0:T(8,128)} %conv_general_dilated.11), kind=kOutput, calls=%fused_computation.4 | convolution fusion | flops 1853300736 | bytes 9535488 | tf_op jit(solution)/shard_map/dot_general | solution.py:47
  58.7 0.0 reduce-scatter.5.cloned.1.call-start
  58.8 3.7 %reshape.36 = f32[2,14,14,768]{3,2,1,0:T(8,128)} reshape(f32[2,14,14,12,64]{4,3,2,1,0:T(8,128)} %copy.30) | data formatting | bytes 2408448 | tf_op jit(solution)/shard_map/conv_general_dilated | solution.py:8
  62.4 7.9 %all-gather.2.cloned.1.call-done = bf16[2,14,14,3072]{3,2,1,0:T(8,128)(2,1)} async-done(((bf16[2,14,14,768]{3,2,1,0:T(8,128)(2,1)}), bf16[2,14,14,3072]{3,2,1,0:T(8,128)(2,1)}) %all-gather.2.cloned.1.call-update) | async-done | bytes 2408464 | tf_op jit(solution)/shard_map/all_gather | solution.py:56
  70.4 8.5 %convolution_bitcast_fusion = f32[768,3072]{1,0:T(8,128)} fusion(bf16[2,14,14,3072]{3,2,1,0:T(8,128)(2,1)} %all-gather.2.cloned.1.call-done, f32[2,768]{1,0:T(2,128)S(1)} %fusion.13, f32[2,14,14,768]{3,2,1,0:T(8,128)} %reshape.36), kind=kOutput, calls=%fused_computation | convolution fusion | flops 1852096512 | bytes 13056000 | tf_op jit(solution)/shard_map/dot_general | solution.py:63
  78.9 7.0 %fusion.4 = (f32[2,768]{1,0:T(2,128)S(1)}, f32[2,14,14,768]{3,2,1,0:T(8,128)}) fusion(f32[2,14,14,768]{3,2,1,0:T(8,128)} %reshape.36, bf16[2,14,14,3072]{3,2,1,0:T(8,128)(2,1)} %all-gather.2.cloned.1.call-done, bf16[768,3072]{1,0:T(8,128)(2,1)} %param.10), kind=kOutput, calls=%fused_computation.11 | convolution fusion | flops 1852094976 | bytes 9541632 | tf_op jit(solution)/shard_map/dot_general | solution.py:60
  85.9 1.3 fusion.23
  87.2 10.6 %psum.15 = f32[2,1024]{1,0:T(2,128)S(1)} all-reduce(f32[2,1024]{1,0:T(2,128)S(1)} %fusion.23), channel_id=1, replica_groups=mesh['dp'=8,'chan'=4] {'chan'}, use_global_device_ids=true, to_apply=%region_4.5 | all-reduce | flops 2048 | bytes 16384 | tf_op jit(solution)/shard_map/psum | solution.py:70
  97.8 1.3 convolution_multiply_fusion
  99.2 0.0 copy-done.2
  99.2 1.9 multiply_convert_fusion
  101.1 1.9 reshape.35
  103.0 15.3 %convolution_convert_fusion.1 = bf16[2,14,14,12,64]{4,0,3,2,1:T(2,128)(2,1)S(1)} fusion(bf16[3,3,64,12,64]{4,3,2,1,0:T(8,128)(2,1)} %shard_map.90, bf16[2,14,14,12,64]{4,3,2,1,0:T(8,128)(2,1)} %reshape.35), kind=kOutput, calls=%fused_computation.10 | convolution fusion | flops 314873856 | bytes 2088960 | tf_op jit(solution)/shard_map/conv_general_dilated | solution.py:8
  118.3 0.3 copy.40
  118.6 1.6 convert_element_type.63
  120.2 0.7 reduce-scatter.3.cloned.1.call-done
  120.9 1.3 reshape.32
  122.2 1.4 copy.41
  123.6 77.8 %reduce-scatter.5.cloned.1.call-done = f32[768,384]{1,0:T(8,128)} async-done(((f32[768,3072]{1,0:T(8,128)}), f32[768,384]{1,0:T(8,128)}) %reduce-scatter.5.cloned.1.call-update) | async-done | bytes 1179664 | tf_op jit(solution)/shard_map/reduce_scatter | solution.py:66
  (15 shorter events, 0.1 us)
Async XLA Ops:
  7.2 33.1 %copy-start = (bf16[1024,768]{1,0:T(8,128)(2,1)S(1)}, bf16[1024,768]{1,0:T(8,128)(2,1)}, u32[]{:S(2)}) copy-start(bf16[1024,768]{1,0:T(8,128)(2,1)} %param.9) | copy-start | bytes 4718596
  7.2 2.3 %copy-start.4 = (bf16[2,14,14,768]{3,0,2,1:T(2,128)(2,1)S(1)}, bf16[2,14,14,768]{3,0,2,1:T(2,128)(2,1)}, u32[]{:S(2)}) copy-start(bf16[2,14,14,768]{3,0,2,1:T(2,128)(2,1)} %param.6) | copy-start | bytes 1806340
  7.2 63.2 %all-gather.2.cloned.1.call-start = ((), (), s32[]{:S(2)}) async-start(), calls=%async_computation.3 | async-start | bytes 3440640 | tf_op jit(solution)/shard_map/all_gather | solution.py:56
  9.4 2.0 copy-start.3
  9.4 111.5 %reduce-scatter.3.cloned.1.call-start = ((), (), s32[]{:S(2)}) async-start(), calls=%async_computation.2 | async-start | bytes 3010560 | tf_op jit(solution)/shard_map/reduce_scatter | solution.py:46
  14.1 11.1 %copy-start.1 = (bf16[768,1024]{1,0:T(8,128)(2,1)S(1)}, bf16[768,1024]{1,0:T(8,128)(2,1)}, u32[]{:S(2)}) copy-start(bf16[768,1024]{1,0:T(8,128)(2,1)} %param.8) | copy-start | bytes 4718596
  58.7 142.7 %reduce-scatter.5.cloned.1.call-start = ((), (), s32[]{:S(2)}) async-start(), calls=%async_computation.4 | async-start | bytes 10616832 | tf_op jit(solution)/shard_map/reduce_scatter | solution.py:66
  97.8 1.4 copy-start.2
Sparse Core Ops, SparseCore 0:
  10.2 60.1 all-gather.1
  72.7 48.1 reduce-scatter.2
  125.4 75.9 reduce-scatter.4
where the time goes:
time: 208 us
  waiting for transfers between devices  86.5 us (42%)
  matrix products  52.5 us (25%)
  local copies, waits for them, and re-layouts  28.1 us (14%)
  blocking collectives  25 us (12%)
  between operations  13.9 us (7%)
    reduce_scatter x1, waiting for transfers between devices, on_device(): lax.psum_scatter(dw_block, 'dp', scatter_dimension=1, tiled=True)  77.8 us
    conv_general_dilated x2, matrix products, grouped(): lax.conv_general_dilated(inputs, kernel, (1, 1), 'SAME', dimension_number...  26.3 us
    psum x1, blocking collectives, on_device(): lax.psum(jnp.dot(squeezed, se_down.astype(jnp.float32), precision=highest...  14.4 us
    conv_general_dilated x3, local copies, waits for them, and re-layouts, grouped(): lax.conv_general_dilated(inputs, kernel, (1, 1), 'SAME', dimension_number...  10.9 us
    psum x1, blocking collectives, on_device(): lax.psum(jnp.dot(pre_grad, se_up.astype(jnp.float32).T, precision=highest...  10.6 us
    dot_general x1, matrix products, on_device(): lax.dot_general(act_rows, piece_rows, (((0,), (0,)), ((), ())), preferred...  8.51 us
    all_gather x1, waiting for transfers between devices, on_device(): shard_piece = lax.all_gather(grad_out, 'chan', axis=3, tiled=True)  7.93 us
    dot_general x1, matrix products, on_device(): lax.dot_general(piece_rows, weight_cols, (((1,), (1,)), ((), ())), prefer...  7.01 us
  transfers between devices with their start and end apart: 3, of which 3 were waited for; matrix products, arithmetic and copies ran while one was open for 39% of the time, Pallas kernels for 0%

commit v1 on v0

v1 whole, which is shorter than its diff:
```python
import functools

import jax
import jax.numpy as jnp
from jax import lax
from jax.experimental import pallas as pl
from jax.experimental.pallas import tpu as pltpu
from jax.sharding import PartitionSpec as P

LANES = 256
VMEM = 40 * 1024 * 1024
F32 = jnp.float32
BF16 = jnp.bfloat16
HIGHEST = lax.Precision.HIGHEST


def params(**more):
    return pltpu.CompilerParams(vmem_limit_bytes=VMEM, **more)


def cost(flops, moved):
    return pl.CostEstimate(flops=flops, bytes_accessed=moved, transcendentals=0)


def silu_grad(values):
    logistic = jax.nn.sigmoid(values)
    return logistic * (1.0 + values * (1.0 - logistic))


def to_rows(images):
    return jnp.transpose(images, (1, 2, 0, 3)).reshape(-1, images.shape[3])


def from_rows(rows, shape):
    count, height, width, channels = shape
    return jnp.transpose(rows.reshape(height, width, count, channels), (1 + 1, 0, 1, 3))


def per_row(values, rows):
    tiled = jnp.concatenate([values] * (8 // values.shape[0]), axis=0)
    return jnp.broadcast_to(tiled[None], (rows // 8, 8, values.shape[1])).reshape(rows, -1)


def image_sum(values, images):
    folded = values.reshape(-1, 8, values.shape[1]).sum(axis=0)
    total = folded[:images]
    for start in range(images, 8, images):
        total = total + folded[start : start + images]
    return total


def convolve(rows_ref, pad_ref, weight_ref, height, width, images, turn):
    line, unit = width * images, 16 * images
    group = weight_ref.shape[2]
    pad_ref[...] = jnp.zeros_like(pad_ref)
    for h in range(height):
        pad_ref[pl.ds(8 + (h + 1) * unit + images, line), :] = rows_ref[pl.ds(h * line, line), :]
    row_group = lax.broadcasted_iota(jnp.int32, (LANES, LANES), 0) // group
    col_group = lax.broadcasted_iota(jnp.int32, (LANES, LANES), 1) // group
    mask = (row_group == col_group).astype(F32).astype(BF16)
    total = None
    for dw in range(3):
        shifted = pad_ref[pl.ds(8 + images * (dw - 1), (height + 2) * unit), :].astype(BF16)
        for dh in range(3):
            tap = weight_ref[2 - dh, 2 - dw] if turn else weight_ref[dh, dw]
            dense = jnp.concatenate([tap] * (LANES // group), axis=0) * mask
            part = lax.dot_general(
                shifted[dh * unit : (dh + height) * unit],
                dense,
                (((1,), (1 if turn else 0,)), ((), ())),
                preferred_element_type=F32,
            )
            total = part if total is None else total + part
    pad_ref[pl.ds(0, height * unit), :] = total
    for h in range(height):
        rows_ref[pl.ds(h * line, line), :] = pad_ref[pl.ds(h * unit + images, line), :]


def conv_forward_body(x_ref, w_ref, conv_ref, act_ref, mean_ref, pad_ref, *, height, width, images):
    conv_ref[...] = x_ref[...].astype(F32)
    convolve(conv_ref, pad_ref, w_ref, height, width, images, False)
    conv = conv_ref[...]
    act = (conv * jax.nn.sigmoid(conv)).astype(BF16)
    act_ref[...] = act
    mean_ref[...] = image_sum(act.astype(F32), images) / (height * width)


def conv_forward(rows, weight, shape):
    images, height, width, channels = shape
    count = rows.shape[0]
    block = pl.BlockSpec((count, LANES), lambda i: (0, i))
    return pl.pallas_call(
        functools.partial(conv_forward_body, height=height, width=width, images=images),
        grid=(channels // LANES,),
        in_specs=[block, pl.BlockSpec((3, 3, weight.shape[2], LANES), lambda i: (0, 0, 0, i))],
        out_specs=[block, block, pl.BlockSpec((images, LANES), lambda i: (0, i))],
        out_shape=[
            jax.ShapeDtypeStruct((count, channels), F32),
            jax.ShapeDtypeStruct((count, channels), BF16),
            jax.ShapeDtypeStruct((images, channels), F32),
        ],
        scratch_shapes=[pltpu.VMEM((16 + (height + 2) * 16 * images, LANES), F32)],
        compiler_params=params(),
        cost_estimate=cost(2 * 9 * count * LANES * channels, 8 * count * channels),
        name="conv_forward",
    )(rows, weight)


def conv_backward_body(
    grad_ref, gate_ref, squeeze_ref, conv_ref, w_ref, out_ref, rows_ref, pad_ref, *, height, width, images
):
    count = grad_ref.shape[0]
    gate = per_row(gate_ref[...], count)
    squeeze = per_row(squeeze_ref[...], count)
    act_grad = grad_ref[...] * gate + squeeze / (height * width)
    rows_ref[...] = act_grad * silu_grad(conv_ref[...])
    convolve(rows_ref, pad_ref, w_ref, height, width, images, True)
    out_ref[...] = rows_ref[...].astype(BF16)


def conv_backward(scaled_grad, gating, squeeze_grad, convolved, weight, shape):
    images, height, width, channels = shape
    count = convolved.shape[0]
    block = pl.BlockSpec((count, LANES), lambda i: (0, i))
    small = pl.BlockSpec((images, LANES), lambda i: (0, i))
    return pl.pallas_call(
        functools.partial(conv_backward_body, height=height, width=width, images=images),
        grid=(channels // LANES,),
        in_specs=[
            block,
            small,
            small,
            block,
            pl.BlockSpec((3, 3, weight.shape[2], LANES), lambda i: (0, 0, 0, i)),
        ],
        out_specs=block,
        out_shape=jax.ShapeDtypeStruct((count, channels), BF16),
        scratch_shapes=[
            pltpu.VMEM((count, LANES), F32),
            pltpu.VMEM((16 + (height + 2) * 16 * images, LANES), F32),
        ],
        compiler_params=params(),
        cost_estimate=cost(2 * 9 * count * LANES * channels, 12 * count * channels),
        name="conv_backward",
    )(scaled_grad, gating, squeeze_grad, convolved, weight)


def project_body(order_ref, act_ref, gate_ref, w_ref, scaled_ref, *out_refs):
    step = pl.program_id(0)

    @pl.when(step == 0)
    def _():
        gate = per_row(gate_ref[...], act_ref.shape[0])
        scaled_ref[...] = (act_ref[...].astype(F32) * gate).astype(BF16)

    part = jnp.dot(scaled_ref[...], w_ref[...], preferred_element_type=F32).astype(BF16)
    for k, out_ref in enumerate(out_refs):

        @pl.when(step == k)
        def _():
            out_ref[...] = part


def project(order, act, gating, weight):
    count, channels = act.shape
    parts = weight.shape[1] // channels
    whole = pl.BlockSpec((count, channels), lambda i, order: (0, 0))
    array = jax.ShapeDtypeStruct((count, channels), BF16)
    return pl.pallas_call(
        project_body,
        grid_spec=pltpu.PrefetchScalarGridSpec(
            num_scalar_prefetch=1,
            grid=(parts,),
            in_specs=[
                whole,
                pl.BlockSpec(gating.shape, lambda i, order: (0, 0)),
                pl.BlockSpec((channels, channels), lambda i, order: (0, order[i])),
            ],
            out_specs=[whole] * (parts + 1),
        ),
        out_shape=[array] * (parts + 1),
        compiler_params=params(),
        cost_estimate=cost(2 * count * weight.size, 2 * weight.size + 12 * count * channels),
        name="project",
    )(order, act, gating, weight)


def input_grad_body(order_ref, *refs, pieces, last, images):
    piece_refs, refs = refs[:pieces], refs[pieces:]
    w_ref, refs = refs[0], refs[1:]
    step = pl.program_id(0)
    if last:
        start_ref, act_ref, out_ref, gate_ref = refs
    else:
        (out_ref,) = refs

    for k, piece_ref in enumerate(piece_refs):

        @pl.when(step == k)
        def _():
            part = lax.dot_general(
                piece_ref[...], w_ref[...], (((1,), (1,)), ((), ())), preferred_element_type=F32
            )
            if k > 0:
                part = out_ref[...] + part
            elif last:
                part = start_ref[...] + part
            out_ref[...] = part
            if last and k == pieces - 1:
                gate_ref[...] = image_sum(part * act_ref[...].astype(F32), images)


def input_grad(order, pieces, weight, images, start=None, act=None):
    count, channels = pieces[0].shape
    last = start is not None
    whole = pl.BlockSpec((count, channels), lambda i, order: (0, 0))
    out_shape = [jax.ShapeDtypeStruct((count, channels), F32)]
    out_specs = [whole]
    operands = list(pieces) + [weight]
    in_specs = [whole] * len(pieces) + [
        pl.BlockSpec((channels, channels), lambda i, order: (0, order[i]))
    ]
    if last:
        operands += [start, act]
        in_specs += [whole, whole]
        out_shape.append(jax.ShapeDtypeStruct((images, channels), F32))
        out_specs.append(pl.BlockSpec((images, channels), lambda i, order: (0, 0)))
    return pl.pallas_call(
        functools.partial(input_grad_body, pieces=len(pieces), last=last, images=images),
        grid_spec=pltpu.PrefetchScalarGridSpec(
            num_scalar_prefetch=1, grid=(len(pieces),), in_specs=in_specs, out_specs=out_specs
        ),
        out_shape=out_shape,
        compiler_params=params(),
        cost_estimate=cost(
            2 * len(pieces) * count * channels * channels,
            len(pieces) * 2 * channels * channels + 8 * count * channels,
        ),
        name="input_grad_last" if last else "input_grad",
    )(order, *operands)


def weight_grad_body(place_ref, own_ref, other_ref, *refs, pieces):
    mine, theirs = refs[:pieces], refs[pieces : 2 * pieces]
    x_send, x_keep, y_send, y_keep = refs[2 * pieces :]
    half = own_ref.shape[1] // 2
    lanes = (((0,), (0,)), ((), ()))
    for k in range(pieces):
        total = lax.dot_general(own_ref[...], mine[k][...], lanes, preferred_element_type=F32)
        total += lax.dot_general(other_ref[...], theirs[k][...], lanes, preferred_element_type=F32)
        total = total.astype(BF16)
        block = place_ref[k]
        to_x, to_y = block % 2, block // 2

        @pl.when(to_x != place_ref[pieces])
        def _():
            x_send[to_y] = total[:half]

        @pl.when(to_x == place_ref[pieces])
        def _():
            x_keep[to_y] = total[:half]

        @pl.when(to_y != place_ref[pieces + 1])
        def _():
            y_send[to_x] = total[half:]

        @pl.when(to_y == place_ref[pieces + 1])
        def _():
            y_keep[to_x] = total[half:]


def weight_grad(place, own, other, mine, theirs):
    channels, columns = own.shape[1], mine[0].shape[1]
    array = jax.ShapeDtypeStruct((2, channels // 2, columns), BF16)
    vmem = pl.BlockSpec(memory_space=pltpu.VMEM)
    pieces = len(mine)
    return pl.pallas_call(
        functools.partial(weight_grad_body, pieces=pieces),
        in_specs=[pl.BlockSpec(memory_space=pltpu.SMEM)] + [vmem] * (2 + 2 * pieces),
        out_specs=[vmem] * 4,
        out_shape=[array] * 4,
        compiler_params=params(),
        cost_estimate=cost(
            4 * pieces * own.shape[0] * channels * columns, 4 * pieces * channels * columns
        ),
        name="weight_grad",
    )(place, own, other, *mine, *theirs)


OUTER = [(0, 1), (1, 0), (2, 3), (3, 2)]
INWARD = [(0, 1), (3, 2)]
OUTWARD = [(1, 0), (2, 3)]
MIDDLE = [(1, 2), (2, 1)]
CROSS = [(0, 3), (3, 0), (1, 2), (2, 1)]


def along_chan(array, pairs):
    return lax.ppermute(array, "chan", pairs)


def along_dp(array, bit):
    return lax.ppermute(array, "dp", [(i, i ^ bit) for i in range(8)])


def small_sum(values):
    values = values + along_chan(values, OUTER)
    return values + along_chan(values, CROSS)


def on_line(hidden, conv_weight, se_down, se_up, proj_weight, grad_out):
    shape = hidden.shape
    images = shape[0]
    z, place = lax.axis_index("chan"), lax.axis_index("dp")
    at_end = (z == 0) | (z == 3)
    core, x, y = place % 2, (place // 2) % 2, place // 4
    order = jnp.array([[0, 1, 2, 3], [1, 0, 2, 3], [2, 3, 1, 0], [3, 2, 1, 0]], jnp.int32)[z]

    own = to_rows(grad_out)
    outer = along_chan(own, OUTER)
    middle = along_chan(own, MIDDLE)

    convolved, act, squeezed = conv_forward(to_rows(hidden), conv_weight, shape)
    excite_pre = small_sum(jnp.dot(squeezed, se_down.astype(F32), precision=HIGHEST))
    gating = jax.nn.sigmoid(jnp.dot(jax.nn.silu(excite_pre), se_up.astype(F32), precision=HIGHEST))

    third = along_chan(middle, OUTWARD)
    far = along_chan(outer, MIDDLE)
    fourth = along_chan(far, OUTWARD)
    third = jnp.where(at_end, third, middle)
    fourth = jnp.where(at_end, fourth, far)
    pieces = [own, outer, third, fourth]

    scaled, p_own, p_outer, p_third, p_fourth = project(order, act, gating, proj_weight)

    def add(a, b):
        return (a.astype(F32) + b.astype(F32)).astype(BF16)

    to_far = add(p_fourth, along_chan(p_fourth, INWARD))
    to_mid = add(p_third, along_chan(p_third, INWARD))
    u_outer = add(p_outer, along_chan(to_far, MIDDLE))
    u_own = add(p_own, along_chan(to_mid, MIDDLE))
    came = along_chan(jnp.where(at_end, p_outer, u_outer), OUTER)
    projected = from_rows(add(jnp.where(at_end, p_own, u_own), came), shape)

    half = shape[3] // 2
    other = along_dp(scaled, 1)
    mine = [lax.dynamic_slice_in_dim(piece, core * half, half, 1) for piece in pieces]
    give = [lax.dynamic_slice_in_dim(piece, (1 - core) * half, half, 1) for piece in pieces]
    theirs = [along_dp(piece, 1) for piece in give]
    slots = jnp.concatenate([order, jnp.stack([x, y]).astype(jnp.int32)])
    x_send, x_keep, y_send, y_keep = weight_grad(slots, scaled, other, mine, theirs)
    x_sum = x_keep.astype(F32) + along_dp(x_send, 2).astype(F32)
    y_sum = y_keep.astype(F32) + along_dp(y_send, 4).astype(F32)

    def pick(array, index):
        return lax.dynamic_index_in_dim(array, index, 0, keepdims=False)

    top = pick(x_sum, y) + along_dp(pick(x_sum, 1 - y).astype(BF16), 4).astype(F32)
    bottom = pick(y_sum, x) + along_dp(pick(y_sum, 1 - x).astype(BF16), 2).astype(F32)
    grad_proj = jnp.concatenate([top, bottom], axis=0)

    (begun,) = input_grad(order[:3], pieces[:3], proj_weight, images)
    scaled_grad, gate_grad = input_grad(order[3:], pieces[3:], proj_weight, images, begun, act)
    pre_grad = gate_grad * gating * (1.0 - gating)
    excite_sum = small_sum(jnp.dot(pre_grad, se_up.astype(F32).T, precision=HIGHEST))
    excite_grad = excite_sum * silu_grad(excite_pre)
    squeeze_grad = jnp.dot(excite_grad, se_down.astype(F32).T, precision=HIGHEST)
    grad_hidden = conv_backward(scaled_grad, gating, squeeze_grad, convolved, conv_weight, shape)
    return (projected, from_rows(grad_hidden, shape), grad_proj)


def on_any(hidden, conv_weight, se_down, se_up, proj_weight, grad_out):
    shape = hidden.shape
    images = shape[0]
    convolved, act, squeezed = conv_forward(to_rows(hidden), conv_weight, shape)
    excite_pre = lax.psum(jnp.dot(squeezed, se_down.astype(F32), precision=HIGHEST), "chan")
    gating = jax.nn.sigmoid(jnp.dot(jax.nn.silu(excite_pre), se_up.astype(F32), precision=HIGHEST))
    count = act.shape[0]
    act_float = act.astype(F32)
    scaled = (act_float * per_row(gating, count)).astype(BF16)
    terms = jnp.dot(scaled, proj_weight, preferred_element_type=F32).astype(BF16)
    projected = lax.psum_scatter(terms, "chan", scatter_dimension=1, tiled=True)
    pieces = lax.all_gather(to_rows(grad_out), "chan", axis=1, tiled=True)
    scaled_grad = lax.dot_general(
        pieces, proj_weight, (((1,), (1,)), ((), ())), preferred_element_type=F32
    )
    terms = lax.dot_general(scaled, pieces, (((0,), (0,)), ((), ())), preferred_element_type=F32)
    grad_proj = lax.psum_scatter(terms, "dp", scatter_dimension=1, tiled=True)
    gate_grad = image_sum(scaled_grad * act_float, images)
    pre_grad = gate_grad * gating * (1.0 - gating)
    excite_sum = lax.psum(jnp.dot(pre_grad, se_up.astype(F32).T, precision=HIGHEST), "chan")
    excite_grad = excite_sum * silu_grad(excite_pre)
    squeeze_grad = jnp.dot(excite_grad, se_down.astype(F32).T, precision=HIGHEST)
    grad_hidden = conv_backward(scaled_grad, gating, squeeze_grad, convolved, conv_weight, shape)
    return (from_rows(projected, shape), from_rows(grad_hidden, shape), grad_proj)


def solution(mesh):
    in_specs = (
        P("dp", None, None, "chan"),
        P(None, None, None, "chan"),
        P("chan", None),
        P(None, "chan"),
        P("chan", None),
        P("dp", None, None, "chan"),
    )
    out_specs = (P("dp", None, None, "chan"), P("dp", None, None, "chan"), P("chan", "dp"))
    on_device = on_line if (mesh.shape["dp"], mesh.shape["chan"]) == (8, 4) else on_any
    return jax.shard_map(
        on_device, mesh=mesh, in_specs=in_specs, out_specs=out_specs, check_vma=False
    )
```

time: 208 us -> 141 us (0.68)
  waiting for transfers between devices: 86.5 us -> 27.5 us
  matrix products: 52.5 us -> 4.08 us
  starting transfers between devices: 0.12 us -> 40.7 us
  blocking collectives: 25 us -> 0 us
  Pallas kernels: 0 us -> 22 us
  between operations: 13.9 us -> 0.93 us
  other arithmetic: 1.88 us -> 13.8 us
  local copies, waits for them, and re-layouts: 28.1 us -> 30.6 us
    reduce_scatter x2 -> x0, waiting for transfers between devices: 78.5 us -> none  [the longest x1 77.8 us: on_device(): lax.psum_scatter(dw_block, 'dp', scatter_dimension=1, tiled=True)]
    ppermute x0 -> x23, starting transfers between devices: none -> 40.7 us  [the longest x14 34.2 us: along_chan(): return lax.ppermute(array, 'chan', pairs)]
    ppermute x0 -> x23, waiting for transfers between devices: none -> 27.5 us  [the longest x14 19.9 us: along_chan(): return lax.ppermute(array, 'chan', pairs)]
    conv_general_dilated x2 -> x0, matrix products: 26.3 us -> none  [grouped(): lax.conv_general_dilated(inputs, kernel, (1, 1), 'SAME', dimension_number...]
    psum x2 -> x0, blocking collectives: 25 us -> none  [the longest x1 14.4 us: on_device(): lax.psum(jnp.dot(squeezed, se_down.astype(jnp.float32), precision=highest...]
    dot_general x7 -> x4, matrix products: 26.3 us -> 4.08 us  [the longest x1 1.32 us: on_line(): jnp.dot(excite_grad, se_down.astype(F32).T, precision=HIGHEST)]
    pallas_call x0 -> x6, Pallas kernels: none -> 22 us  [the longest x1 7.14 us: weight_grad(): pl.pallas_call(functools.partial(weight_grad_body, pieces=pieces), in_spe...]
    unnamed x12 -> x72, local copies, waits for them, and re-layouts: 3.64 us -> 18.7 us
  transfers between devices with their start and end apart: 3 -> 23, of which waited for: 3 -> 9; matrix products, arithmetic and copies ran while one was open for 39% -> 18% of each run, Pallas kernels for 0% -> 16%
where the time goes in v1:
time: 141 us; the launch traced here: 140 us
  starting transfers between devices  40.7 us (29%)
  local copies, waits for them, and re-layouts  30.6 us (22%)
  waiting for transfers between devices  27.5 us (20%)
  Pallas kernels  22 us (16%)
  other arithmetic  13.8 us (10%)
  matrix products  4.08 us (3%)
    ppermute x14, starting transfers between devices, along_chan(): return lax.ppermute(array, 'chan', pairs)  34.2 us
    ppermute x14, waiting for transfers between devices, along_chan(): return lax.ppermute(array, 'chan', pairs)  19.9 us
    unnamed x72, local copies, waits for them, and re-layouts  18.7 us
    ppermute x9, waiting for transfers between devices, along_dp(): return lax.ppermute(array, 'dp', [(i, i ^ bit) for i in range(8)])  7.57 us
    pallas_call x1, Pallas kernels, weight_grad(): pl.pallas_call(functools.partial(weight_grad_body, pieces=pieces), in_spe...  7.14 us
    ppermute x9, starting transfers between devices, along_dp(): return lax.ppermute(array, 'dp', [(i, i ^ bit) for i in range(8)])  6.5 us
    convert_element_type x3, other arithmetic, add(): return (a.astype(F32) + b.astype(F32)).astype(BF16)  5.79 us
    pallas_call x1, Pallas kernels, project(): pl.pallas_call(project_body, grid_spec=pltpu.PrefetchScalarGridSpec(num_s...  4.91 us
  transfers between devices with their start and end apart: 23, of which 9 were waited for; matrix products, arithmetic and copies ran while one was open for 18% of the time, Pallas kernels for 16%

profile of v1, /device:TPU:0, one launch (start us, length us, event | category | flops | bytes accessed | tf_op | source)
XLA Modules:
  0.0 139.6 jit_solution(7534853563371631666)
XLA Ops:
  0.7 2.1 %reshape.24.refs_0_ = bf16[392,768]{1,0:T(8,128)(2,1)S(1)} reshape(bf16[14,14,2,768]{3,2,1,0:T(2,128)(2,1)} %bitcast.24) | data formatting | bytes 1204224 | tf_op jit(solution)/shard_map/reshape | solution.py:31
  2.8 3.1 %collective-permute-start.7 = (bf16[392,768]{1,0:T(8,128)(2,1)S(1)}, bf16[392,768]{1,0:T(8,128)(2,1)S(1)}, u32[]{:S(2)}, u32[]{:S(2)}) collective-permute-start(bf16[392,768]{1,0:T(8,128)(2,1)S(1)} %reshape.24.refs_0_), channel_id=1, source_target_pairs={{0,1},{1,0},{2,3},{3,2},{4,5},{5,4},{6,7},{7,6},{8,9},{9,8},{10,11... | collective-permute-start | bytes 1806344 | tf_op jit(solution)/shard_map/ppermute | solution.py:298
  9.2 2.6 %conv_forward.1 = (f32[392,768]{1,0:T(8,128)S(1)}, bf16[392,768]{1,0:T(8,128)(2,1)S(1)}, f32[2,768]{1,0:T(2,128)S(1)}) custom-call(bf16[392,768]{1,0:T(8,128)(2,1)S(1)} %copy-done.6, bf16[3,3,64,768]{3,2,1,0:T(8,128)(2,1)S(1)} %copy-done.21), custom_call_target="tpu_custom_call" | custom-call | flops 1387266048 | bytes 2408448 | tf_op jit(solution)/shard_map/conv_forward/pallas_call | solution.py:92
  12.9 1.5 %collective-permute-start.10 = (bf16[392,768]{1,0:T(8,128)(2,1)S(1)}, bf16[392,768]{1,0:T(8,128)(2,1)}, u32[]{:S(2)}, u32[]{:S(2)}) collective-permute-start(bf16[392,768]{1,0:T(8,128)(2,1)S(1)} %reshape.24.refs_0_), channel_id=1, source_target_pairs={{1,2},{2,1},{5,6},{6,5},{9,10},{10,9},{13,14},{14,13},{17,18},{18,... | collective-permute-start | bytes 1806344 | tf_op jit(solution)/shard_map/ppermute | solution.py:298
  14.4 5.3 %collective-permute-done = f32[2,1024]{1,0:T(2,128)S(1)} collective-permute-done((f32[2,1024]{1,0:T(2,128)S(1)}, f32[2,1024]{1,0:T(2,128)S(1)}, u32[]{:S(2)}, u32[]{:S(2)}) %collective-permute-start) | collective-permute-done | bytes 8224 | tf_op jit(solution)/shard_map/ppermute | solution.py:298
  19.7 3.8 %collective-permute-start.1 = (f32[2,1024]{1,0:T(2,128)S(1)}, f32[2,1024]{1,0:T(2,128)S(1)}, u32[]{:S(2)}, u32[]{:S(2)}) collective-permute-start(f32[2,1024]{1,0:T(2,128)S(1)} %add.90), channel_id=1, source_target_pairs={{0,3},{3,0},{1,2},{2,1},{4,7},{7,4},{5,6},{6,5},{8,11},{11,8},{9,1... | collective-permute-start | bytes 24584 | tf_op jit(solution)/shard_map/ppermute | solution.py:298
  26.0 2.3 %copy-done.1 = bf16[768,3072]{1,0:T(8,128)(2,1)S(1)} copy-done((bf16[768,3072]{1,0:T(8,128)(2,1)S(1)}, bf16[768,3072]{1,0:T(8,128)(2,1)}, u32[]{:S(2)}) %copy-start.1) | copy-done | bytes 4718616
  28.3 4.9 %project.1 = (bf16[392,768]{1,0:T(8,128)(2,1)}, bf16[392,768]{1,0:T(8,128)(2,1)S(1)}, bf16[392,768]{1,0:T(8,128)(2,1)S(1)}, bf16[392,768]{1,0:T(8,128)(2,1)S(1)}, bf16[392,768]{1,0:T(8,128)(2,1)}) custom-call(s32[4]{0:T(128)S(1)} %get-tuple-element.40.order_ref, bf16[392,768]{1,0:T(8,128)(2,1)S(1)} %get-tuple-element.17.act_ref.refs_3_, ...), custom_call_target="tpu_custom_call" | custom-call | flops 1849688064 | bytes 8331264 | tf_op jit(solution)/shard_map/project/pallas_call | solution.py:169
  35.7 9.4 %collective-permute-start.4 = (bf16[392,768]{1,0:T(8,128)(2,1)}, bf16[392,768]{1,0:T(8,128)(2,1)}, u32[]{:S(2)}, u32[]{:S(2)}) collective-permute-start(bf16[392,768]{1,0:T(8,128)(2,1)} %get-tuple-element.22), channel_id=1, source_target_pairs={{0,1},{3,2},{4,5},{7,6},{8,9},{11,10},{12,13},{15,14},{16,17},{19,... | collective-permute-start | bytes 1806344 | tf_op jit(solution)/shard_map/ppermute | solution.py:298
  45.1 1.5 %collective-permute-start.8 = (bf16[392,768]{1,0:T(8,128)(2,1)S(1)}, bf16[392,768]{1,0:T(8,128)(2,1)}, u32[]{:S(2)}, u32[]{:S(2)}) collective-permute-start(bf16[392,768]{1,0:T(8,128)(2,1)S(1)} %collective-permute-done.7.refs_1_), channel_id=1, source_target_pairs={{1,2},{2,1},{5,6},{6,5},{9,10},{10,9},{13,14},{14,13},{17,18},{18,... | collective-permute-start | bytes 1806344 | tf_op jit(solution)/shard_map/ppermute | solution.py:298
  49.4 5.4 %collective-permute-start.2 = (bf16[392,768]{1,0:T(8,128)(2,1)}, bf16[392,768]{1,0:T(8,128)(2,1)}, u32[]{:S(2)}, u32[]{:S(2)}) collective-permute-start(bf16[392,768]{1,0:T(8,128)(2,1)} %copy-done.4), channel_id=1, source_target_pairs={{0,1},{3,2},{4,5},{7,6},{8,9},{11,10},{12,13},{15,14},{16,17},{19,... | collective-permute-start | bytes 1806344 | tf_op jit(solution)/shard_map/ppermute | solution.py:298
  55.7 1.5 %collective-permute-done.4 = bf16[392,768]{1,0:T(8,128)(2,1)} collective-permute-done((bf16[392,768]{1,0:T(8,128)(2,1)}, bf16[392,768]{1,0:T(8,128)(2,1)}, u32[]{:S(2)}, u32[]{:S(2)}) %collective-permute-start.4) | collective-permute-done | bytes 602144 | tf_op jit(solution)/shard_map/ppermute | solution.py:298
  58.6 2.2 %add_convert_fusion.2 = bf16[392,768]{1,0:T(8,128)(2,1)} fusion(bf16[392,768]{1,0:T(8,128)(2,1)} %collective-permute-done.4, bf16[392,768]{1,0:T(8,128)(2,1)} %get-tuple-element.22), kind=kLoop, calls=%fused_computation.2 | loop fusion | flops 1204224 | bytes 1806336 | tf_op jit(solution)/shard_map/convert_element_type | solution.py:336
  60.8 5.8 %collective-permute-done.11 = bf16[392,768]{1,0:T(8,128)(2,1)S(1)} collective-permute-done((bf16[392,768]{1,0:T(8,128)(2,1)}, bf16[392,768]{1,0:T(8,128)(2,1)S(1)}, u32[]{:S(2)}, u32[]{:S(2)}) %collective-permute-start.11) | collective-permute-done | bytes 602144 | tf_op jit(solution)/shard_map/ppermute | solution.py:298
  66.6 1.5 %collective-permute-start.5 = (bf16[392,768]{1,0:T(8,128)(2,1)}, bf16[392,768]{1,0:T(8,128)(2,1)}, u32[]{:S(2)}, u32[]{:S(2)}) collective-permute-start(bf16[392,768]{1,0:T(8,128)(2,1)} %add_convert_fusion.2), channel_id=1, source_target_pairs={{1,2},{2,1},{5,6},{6,5},{9,10},{10,9},{13,14},{14,13},{17,18},{18,... | collective-permute-start | bytes 1806344 | tf_op jit(solution)/shard_map/ppermute | solution.py:298
  69.1 2.3 %copy-done.2 = bf16[768,3072]{1,0:T(8,128)(2,1)S(1)} copy-done((bf16[768,3072]{1,0:T(8,128)(2,1)S(1)}, bf16[768,3072]{1,0:T(8,128)(2,1)}, u32[]{:S(2)}) %copy-start.2) | copy-done | bytes 4718616
  71.4 3.0 %input_grad.1.refs_2_ = f32[392,768]{1,0:T(8,128)S(1)} custom-call(s32[3]{0:T(128)S(1)} %slice_bitcast_fusion.order_ref, bf16[392,768]{1,0:T(8,128)(2,1)S(1)} %reshape.24.refs_0_, bf16[392,768]{1,0:T(8,128)(2,1)S(1)} %collective-permute-done.7.refs_1_, bf16[392,768]{1,0:T(8,128)(2,1)S(1)} %broadcast_select_fusion.refs_2_, bf16[768,3072]{1,0:T(8,128)(2,1)S(1)} %copy-done.2), custom_call_target="tpu_custom_call" | custom-call | flops 1387266048 | bytes 5947392 | tf_op jit(solution)/shard_map/input_grad/pallas_call | solution.py:228
  74.4 4.7 %collective-permute-done.9 = bf16[392,768]{1,0:T(8,128)(2,1)S(1)} collective-permute-done((bf16[392,768]{1,0:T(8,128)(2,1)}, bf16[392,768]{1,0:T(8,128)(2,1)S(1)}, u32[]{:S(2)}, u32[]{:S(2)}) %collective-permute-start.9) | collective-permute-done | bytes 602144 | tf_op jit(solution)/shard_map/ppermute | solution.py:298
  79.2 2.3 %copy-done.3 = bf16[768,3072]{1,0:T(8,128)(2,1)S(1)} copy-done((bf16[768,3072]{1,0:T(8,128)(2,1)S(1)}, bf16[768,3072]{1,0:T(8,128)(2,1)}, u32[]{:S(2)}) %copy-start.3) | copy-done | bytes 4718616
  87.9 2.1 %add_convert_fusion.4 = bf16[392,768]{1,0:T(8,128)(2,1)} fusion(bf16[392,768]{1,0:T(8,128)(2,1)} %collective-permute-done.2, bf16[392,768]{1,0:T(8,128)(2,1)S(1)} %copy-done.5), kind=kLoop, calls=%fused_computation.4 | loop fusion | flops 1204224 | bytes 1806336 | tf_op jit(solution)/shard_map/convert_element_type | solution.py:336
  90.0 1.5 %collective-permute-start.3 = (bf16[392,768]{1,0:T(8,128)(2,1)}, bf16[392,768]{1,0:T(8,128)(2,1)}, u32[]{:S(2)}, u32[]{:S(2)}) collective-permute-start(bf16[392,768]{1,0:T(8,128)(2,1)} %add_convert_fusion.4), channel_id=1, source_target_pairs={{1,2},{2,1},{5,6},{6,5},{9,10},{10,9},{13,14},{14,13},{17,18},{18,... | collective-permute-start | bytes 1806344 | tf_op jit(solution)/shard_map/ppermute | solution.py:298
  92.2 2.5 %collective-permute-start.13 = (f32[2,1024]{1,0:T(2,128)S(1)}, f32[2,1024]{1,0:T(2,128)S(1)}, u32[]{:S(2)}, u32[]{:S(2)}) collective-permute-start(f32[2,1024]{1,0:T(2,128)S(1)} %add.99), channel_id=1, source_target_pairs={{0,3},{3,0},{1,2},{2,1},{4,7},{7,4},{5,6},{6,5},{8,11},{11,8},{9,1... | collective-permute-start | bytes 24584 | tf_op jit(solution)/shard_map/ppermute | solution.py:298
  100.3 7.1 %weight_grad.1 = (bf16[2,384,384]{2,1,0:T(8,128)(2,1)}, bf16[2,384,384]{2,1,0:T(8,128)(2,1)S(1)}, bf16[2,384,384]{2,1,0:T(8,128)(2,1)}, bf16[2,384,384]{2,1,0:T(8,128)(2,1)S(1)}) custom-call(s32[6]{0:T(128)S(1)} %pad_add_fusion.place_ref, bf16[392,768]{1,0:T(8,128)(2,1)} %get-tuple-element.26.own_ref, bf16[392,768]{1,0:T(8,128)(2,1)} %collective-permute-done.14.other_ref, ...), custom_call_target="tpu_custom_call" | custom-call | flops 1849688064 | bytes 4718592 | tf_op jit(solution)/shard_map/weight_grad/pallas_call | solution.py:277
  107.4 1.5 %collective-permute-start.19 = (bf16[2,384,384]{2,1,0:T(8,128)(2,1)}, bf16[2,384,384]{2,1,0:T(8,128)(2,1)}, u32[]{:S(2)}, u32[]{:S(2)}) collective-permute-start(bf16[2,384,384]{2,1,0:T(8,128)(2,1)} %get-tuple-element.28), channel_id=1, source_target_pairs={{0,8},{4,12},{8,0},{12,4},{16,24},{20,28},{24,16},{28,20},{1,9},{5... | collective-permute-start | bytes 1769480 | tf_op jit(solution)/shard_map/ppermute | solution.py:302
  108.9 2.2 %fusion.4 = bf16[392,768]{1,0:T(8,128)(2,1)} fusion(bf16[392,768]{1,0:T(8,128)(2,1)S(1)} %copy-done.10, bf16[392,768]{1,0:T(8,128)(2,1)} %collective-permute-done.5, pred[]{:T(512)S(6)} %or.3), kind=kLoop, calls=%fused_computation.13 | loop fusion | flops 1505280 | bytes 1806337 | tf_op jit(solution)/shard_map/jit(_where)/select_n | solution.py:342
  111.8 1.5 %collective-permute-start.21 = (bf16[2,384,384]{2,1,0:T(8,128)(2,1)}, bf16[2,384,384]{2,1,0:T(8,128)(2,1)}, u32[]{:S(2)}, u32[]{:S(2)}) collective-permute-start(bf16[2,384,384]{2,1,0:T(8,128)(2,1)} %get-tuple-element.30), channel_id=1, source_target_pairs={{0,16},{4,20},{8,24},{12,28},{16,0},{20,4},{24,8},{28,12},{1,17},{... | collective-permute-start | bytes 1769480 | tf_op jit(solution)/shard_map/ppermute | solution.py:302
  114.7 3.1 %conv_backward.1 = bf16[392,768]{1,0:T(8,128)(2,1)S(1)} custom-call(f32[392,768]{1,0:T(8,128)S(1)} %copy-done.20, f32[2,768]{1,0:T(2,128)S(1)} %fusion.2.gate_ref, f32[2,768]{1,0:T(2,128)S(1)} %fusion.7.squeeze_ref, f32[392,768]{1,0:T(8,128)S(1)} %copy-done.28, bf16[3,3,64,768]{3,2,1,0:T(8,128)(2,1)S(1)} %copy-done.22), custom_call_target="tpu_custom_call" | custom-call | flops 1387266048 | bytes 3612672 | tf_op jit(solution)/shard_map/conv_backward/pallas_call | solution.py:126
  118.9 4.3 %collective-permute-done.19 = bf16[2,384,384]{2,1,0:T(8,128)(2,1)} collective-permute-done((bf16[2,384,384]{2,1,0:T(8,128)(2,1)}, bf16[2,384,384]{2,1,0:T(8,128)(2,1)}, u32[]{:S(2)}, u32[]{:S(2)}) %collective-permute-start.19) | collective-permute-done | bytes 589856 | tf_op jit(solution)/shard_map/ppermute | solution.py:302
  125.2 1.5 %collective-permute-start.20 = (bf16[384,384]{1,0:T(8,128)(2,1)}, bf16[384,384]{1,0:T(8,128)(2,1)}, u32[]{:S(2)}, u32[]{:S(2)}) collective-permute-start(bf16[384,384]{1,0:T(8,128)(2,1)} %fusion.5), channel_id=1, source_target_pairs={{0,16},{4,20},{8,24},{12,28},{16,0},{20,4},{24,8},{28,12},{1,17},{... | collective-permute-start | bytes 884744 | tf_op jit(solution)/shard_map/ppermute | solution.py:302
  129.1 1.5 %collective-permute-start.22 = (bf16[384,384]{1,0:T(8,128)(2,1)}, bf16[384,384]{1,0:T(8,128)(2,1)}, u32[]{:S(2)}, u32[]{:S(2)}) collective-permute-start(bf16[384,384]{1,0:T(8,128)(2,1)} %fusion.6), channel_id=1, source_target_pairs={{0,8},{4,12},{8,0},{12,4},{16,24},{20,28},{24,16},{28,20},{1,9},{5... | collective-permute-start | bytes 884744 | tf_op jit(solution)/shard_map/ppermute | solution.py:302
  130.6 1.5 %add_convert_fusion = bf16[392,768]{1,0:T(8,128)(2,1)S(1)} fusion(bf16[392,768]{1,0:T(8,128)(2,1)} %collective-permute-done.6, bf16[392,768]{1,0:T(8,128)(2,1)S(1)} %copy-done.8, bf16[392,768]{1,0:T(8,128)(2,1)} %collective-permute-done.3, pred[]{:T(512)S(6)} %or.3), kind=kLoop, calls=%fused_computation | loop fusion | flops 2709504 | bytes 2408449 | tf_op jit(solution)/shard_map/convert_element_type | solution.py:336
  134.9 2.6 %collective-permute-done.22 = bf16[384,384]{1,0:T(8,128)(2,1)} collective-permute-done((bf16[384,384]{1,0:T(8,128)(2,1)}, bf16[384,384]{1,0:T(8,128)(2,1)}, u32[]{:S(2)}, u32[]{:S(2)}) %collective-permute-start.22) | collective-permute-done | bytes 294944 | tf_op jit(solution)/shard_map/ppermute | solution.py:302
  (123 shorter events, 40.5 us)
Async XLA Ops:
  0.6 24.6 %copy-start = (bf16[1024,768]{1,0:T(8,128)(2,1)S(1)}, bf16[1024,768]{1,0:T(8,128)(2,1)}, u32[]{:S(2)}) copy-start(bf16[1024,768]{1,0:T(8,128)(2,1)} %param.10) | copy-start | bytes 4718596
  2.8 42.3 %collective-permute-start.7 = (bf16[392,768]{1,0:T(8,128)(2,1)S(1)}, bf16[392,768]{1,0:T(8,128)(2,1)S(1)}, u32[]{:S(2)}, u32[]{:S(2)}) collective-permute-start(bf16[392,768]{1,0:T(8,128)(2,1)S(1)} %reshape.24.refs_0_), channel_id=1, source_target_pairs={{0,1},{1,0},{2,3},{3,2},{4,5},{5,4},{6,7},{7,6},{8,9},{9,8},{10,11... | collective-permute-start | bytes 1806344 | tf_op jit(solution)/shard_map/ppermute | solution.py:298
  12.8 6.8 %collective-permute-start = (f32[2,1024]{1,0:T(2,128)S(1)}, f32[2,1024]{1,0:T(2,128)S(1)}, u32[]{:S(2)}, u32[]{:S(2)}) collective-permute-start(f32[2,1024]{1,0:T(2,128)S(1)} %fusion.26), channel_id=1, source_target_pairs={{0,1},{1,0},{2,3},{3,2},{4,5},{5,4},{6,7},{7,6},{8,9},{9,8},{10,11... | collective-permute-start | bytes 24584 | tf_op jit(solution)/shard_map/ppermute | solution.py:298
  12.9 35.2 %collective-permute-start.10 = (bf16[392,768]{1,0:T(8,128)(2,1)S(1)}, bf16[392,768]{1,0:T(8,128)(2,1)}, u32[]{:S(2)}, u32[]{:S(2)}) collective-permute-start(bf16[392,768]{1,0:T(8,128)(2,1)S(1)} %reshape.24.refs_0_), channel_id=1, source_target_pairs={{1,2},{2,1},{5,6},{6,5},{9,10},{10,9},{13,14},{14,13},{17,18},{18,... | collective-permute-start | bytes 1806344 | tf_op jit(solution)/shard_map/ppermute | solution.py:298
  19.7 5.6 %collective-permute-start.1 = (f32[2,1024]{1,0:T(2,128)S(1)}, f32[2,1024]{1,0:T(2,128)S(1)}, u32[]{:S(2)}, u32[]{:S(2)}) collective-permute-start(f32[2,1024]{1,0:T(2,128)S(1)} %add.90), channel_id=1, source_target_pairs={{0,3},{3,0},{1,2},{2,1},{4,7},{7,4},{5,6},{6,5},{8,11},{11,8},{9,1... | collective-permute-start | bytes 24584 | tf_op jit(solution)/shard_map/ppermute | solution.py:298
  35.7 21.6 %collective-permute-start.4 = (bf16[392,768]{1,0:T(8,128)(2,1)}, bf16[392,768]{1,0:T(8,128)(2,1)}, u32[]{:S(2)}, u32[]{:S(2)}) collective-permute-start(bf16[392,768]{1,0:T(8,128)(2,1)} %get-tuple-element.22), channel_id=1, source_target_pairs={{0,1},{3,2},{4,5},{7,6},{8,9},{11,10},{12,13},{15,14},{16,17},{19,... | collective-permute-start | bytes 1806344 | tf_op jit(solution)/shard_map/ppermute | solution.py:298
  45.1 12.2 %collective-permute-start.8 = (bf16[392,768]{1,0:T(8,128)(2,1)S(1)}, bf16[392,768]{1,0:T(8,128)(2,1)}, u32[]{:S(2)}, u32[]{:S(2)}) collective-permute-start(bf16[392,768]{1,0:T(8,128)(2,1)S(1)} %collective-permute-done.7.refs_1_), channel_id=1, source_target_pairs={{1,2},{2,1},{5,6},{6,5},{9,10},{10,9},{13,14},{14,13},{17,18},{18,... | collective-permute-start | bytes 1806344 | tf_op jit(solution)/shard_map/ppermute | solution.py:298
  47.5 38.3 %collective-permute-start.15 = (bf16[392,384]{1,0:T(8,128)(2,1)}, bf16[392,384]{1,0:T(8,128)(2,1)}, u32[]{:S(2)}, u32[]{:S(2)}) collective-permute-start(bf16[392,384]{1,0:T(8,128)(2,1)} %get-tuple-element.37), channel_id=1, source_target_pairs={{0,4},{4,0},{8,12},{12,8},{16,20},{20,16},{24,28},{28,24},{1,5},{5... | collective-permute-start | bytes 903176 | tf_op jit(solution)/shard_map/ppermute | solution.py:302
  48.1 18.5 %collective-permute-start.11 = (bf16[392,768]{1,0:T(8,128)(2,1)}, bf16[392,768]{1,0:T(8,128)(2,1)S(1)}, u32[]{:S(2)}, u32[]{:S(2)}) collective-permute-start(bf16[392,768]{1,0:T(8,128)(2,1)} %collective-permute-done.10), channel_id=1, source_target_pairs={{1,0},{2,3},{5,4},{6,7},{9,8},{10,11},{13,12},{14,15},{17,16},{18,... | collective-permute-start | bytes 1806344 | tf_op jit(solution)/shard_map/ppermute | solution.py:298
  49.4 36.4 %collective-permute-start.2 = (bf16[392,768]{1,0:T(8,128)(2,1)}, bf16[392,768]{1,0:T(8,128)(2,1)}, u32[]{:S(2)}, u32[]{:S(2)}) collective-permute-start(bf16[392,768]{1,0:T(8,128)(2,1)} %copy-done.4), channel_id=1, source_target_pairs={{0,1},{3,2},{4,5},{7,6},{8,9},{11,10},{12,13},{15,14},{16,17},{19,... | collective-permute-start | bytes 1806344 | tf_op jit(solution)/shard_map/ppermute | solution.py:298
  57.3 32.7 %collective-permute-start.14 = (bf16[392,768]{1,0:T(8,128)(2,1)}, bf16[392,768]{1,0:T(8,128)(2,1)}, u32[]{:S(2)}, u32[]{:S(2)}) collective-permute-start(bf16[392,768]{1,0:T(8,128)(2,1)} %get-tuple-element.26.own_ref), channel_id=1, source_target_pairs={{0,4},{4,0},{8,12},{12,8},{16,20},{20,16},{24,28},{28,24},{1,5},{5... | collective-permute-start | bytes 1806344 | tf_op jit(solution)/shard_map/ppermute | solution.py:302
  57.3 21.8 %collective-permute-start.9 = (bf16[392,768]{1,0:T(8,128)(2,1)}, bf16[392,768]{1,0:T(8,128)(2,1)S(1)}, u32[]{:S(2)}, u32[]{:S(2)}) collective-permute-start(bf16[392,768]{1,0:T(8,128)(2,1)} %collective-permute-done.8), channel_id=1, source_target_pairs={{1,0},{2,3},{5,4},{6,7},{9,8},{10,11},{13,12},{14,15},{17,16},{18,... | collective-permute-start | bytes 1806344 | tf_op jit(solution)/shard_map/ppermute | solution.py:298
  66.6 42.3 %collective-permute-start.5 = (bf16[392,768]{1,0:T(8,128)(2,1)}, bf16[392,768]{1,0:T(8,128)(2,1)}, u32[]{:S(2)}, u32[]{:S(2)}) collective-permute-start(bf16[392,768]{1,0:T(8,128)(2,1)} %add_convert_fusion.2), channel_id=1, source_target_pairs={{1,2},{2,1},{5,6},{6,5},{9,10},{10,9},{13,14},{14,13},{17,18},{18,... | collective-permute-start | bytes 1806344 | tf_op jit(solution)/shard_map/ppermute | solution.py:298
  84.1 3.7 %collective-permute-start.12 = (f32[2,1024]{1,0:T(2,128)S(1)}, f32[2,1024]{1,0:T(2,128)S(1)}, u32[]{:S(2)}, u32[]{:S(2)}) collective-permute-start(f32[2,1024]{1,0:T(2,128)S(1)} %fusion.15), channel_id=1, source_target_pairs={{0,1},{1,0},{2,3},{3,2},{4,5},{5,4},{6,7},{7,6},{8,9},{9,8},{10,11... | collective-permute-start | bytes 24584 | tf_op jit(solution)/shard_map/ppermute | solution.py:298
  85.8 5.6 %collective-permute-start.16 = (bf16[392,384]{1,0:T(8,128)(2,1)}, bf16[392,384]{1,0:T(8,128)(2,1)S(1)}, u32[]{:S(2)}, u32[]{:S(2)}) collective-permute-start(bf16[392,384]{1,0:T(8,128)(2,1)} %get-tuple-element.35), channel_id=1, source_target_pairs={{0,4},{4,0},{8,12},{12,8},{16,20},{20,16},{24,28},{28,24},{1,5},{5... | collective-permute-start | bytes 903176 | tf_op jit(solution)/shard_map/ppermute | solution.py:302
  85.9 8.8 %collective-permute-start.17 = (bf16[392,384]{1,0:T(8,128)(2,1)}, bf16[392,384]{1,0:T(8,128)(2,1)S(1)}, u32[]{:S(2)}, u32[]{:S(2)}) collective-permute-start(bf16[392,384]{1,0:T(8,128)(2,1)} %get-tuple-element.33), channel_id=1, source_target_pairs={{0,4},{4,0},{8,12},{12,8},{16,20},{20,16},{24,28},{28,24},{1,5},{5... | collective-permute-start | bytes 903176 | tf_op jit(solution)/shard_map/ppermute | solution.py:302
  87.8 7.6 %collective-permute-start.18 = (bf16[392,384]{1,0:T(8,128)(2,1)}, bf16[392,384]{1,0:T(8,128)(2,1)}, u32[]{:S(2)}, u32[]{:S(2)}) collective-permute-start(bf16[392,384]{1,0:T(8,128)(2,1)} %get-tuple-element.31), channel_id=1, source_target_pairs={{0,4},{4,0},{8,12},{12,8},{16,20},{20,16},{24,28},{28,24},{1,5},{5... | collective-permute-start | bytes 903176 | tf_op jit(solution)/shard_map/ppermute | solution.py:302
  87.9 7.5 %copy-start.18 = (bf16[392,384]{1,0:T(8,128)(2,1)S(1)}, bf16[392,384]{1,0:T(8,128)(2,1)}, u32[]{:S(2)}) copy-start(bf16[392,384]{1,0:T(8,128)(2,1)} %get-tuple-element.32.refs_3_) | copy-start | bytes 903172
  90.0 40.6 %collective-permute-start.3 = (bf16[392,768]{1,0:T(8,128)(2,1)}, bf16[392,768]{1,0:T(8,128)(2,1)}, u32[]{:S(2)}, u32[]{:S(2)}) collective-permute-start(bf16[392,768]{1,0:T(8,128)(2,1)} %add_convert_fusion.4), channel_id=1, source_target_pairs={{1,2},{2,1},{5,6},{6,5},{9,10},{10,9},{13,14},{14,13},{17,18},{18,... | collective-permute-start | bytes 1806344 | tf_op jit(solution)/shard_map/ppermute | solution.py:298
  92.2 21.1 %collective-permute-start.13 = (f32[2,1024]{1,0:T(2,128)S(1)}, f32[2,1024]{1,0:T(2,128)S(1)}, u32[]{:S(2)}, u32[]{:S(2)}) collective-permute-start(f32[2,1024]{1,0:T(2,128)S(1)} %add.99), channel_id=1, source_target_pairs={{0,3},{3,0},{1,2},{2,1},{4,7},{7,4},{5,6},{6,5},{8,11},{11,8},{9,1... | collective-permute-start | bytes 24584 | tf_op jit(solution)/shard_map/ppermute | solution.py:298
  100.3 8.6 %copy-start.10 = (bf16[392,768]{1,0:T(8,128)(2,1)S(1)}, bf16[392,768]{1,0:T(8,128)(2,1)}, u32[]{:S(2)}) copy-start(bf16[392,768]{1,0:T(8,128)(2,1)} %copy-done.9) | copy-start | bytes 1806340
  100.3 13.1 %copy-start.30 = (bf16[768,1024]{1,0:T(8,128)(2,1)S(1)}, bf16[768,1024]{1,0:T(8,128)(2,1)}, u32[]{:S(2)}) copy-start(bf16[768,1024]{1,0:T(8,128)(2,1)} %param.9) | copy-start | bytes 4718596
  107.4 7.3 %copy-start.11 = (bf16[2,384,384]{2,1,0:T(8,128)(2,1)}, bf16[2,384,384]{2,1,0:T(8,128)(2,1)S(1)}, u32[]{:S(2)}) copy-start(bf16[2,384,384]{2,1,0:T(8,128)(2,1)S(1)} %get-tuple-element.29) | copy-start | bytes 1769476
  107.4 7.3 %copy-start.13 = (bf16[2,384,384]{2,1,0:T(8,128)(2,1)}, bf16[2,384,384]{2,1,0:T(8,128)(2,1)S(1)}, u32[]{:S(2)}) copy-start(bf16[2,384,384]{2,1,0:T(8,128)(2,1)S(1)} %get-tuple-element.27) | copy-start | bytes 1769476
  107.4 15.8 %collective-permute-start.19 = (bf16[2,384,384]{2,1,0:T(8,128)(2,1)}, bf16[2,384,384]{2,1,0:T(8,128)(2,1)}, u32[]{:S(2)}, u32[]{:S(2)}) collective-permute-start(bf16[2,384,384]{2,1,0:T(8,128)(2,1)} %get-tuple-element.28), channel_id=1, source_target_pairs={{0,8},{4,12},{8,0},{12,4},{16,24},{20,28},{24,16},{28,20},{1,9},{5... | collective-permute-start | bytes 1769480 | tf_op jit(solution)/shard_map/ppermute | solution.py:302
  108.9 5.8 %copy-start.22 = (bf16[3,3,64,768]{3,2,1,0:T(8,128)(2,1)S(1)}, bf16[3,3,64,768]{3,2,1,0:T(8,128)(2,1)}, u32[]{:S(2)}) copy-start(bf16[3,3,64,768]{3,2,1,0:T(8,128)(2,1)} %w_ref.5) | copy-start | bytes 2654212
  108.9 5.8 %copy-start.28 = (f32[392,768]{1,0:T(8,128)S(1)}, f32[392,768]{1,0:T(8,128)}, u32[]{:S(2)}) copy-start(f32[392,768]{1,0:T(8,128)} %copy-done.27) | copy-start | bytes 3612676
  111.1 19.5 %collective-permute-start.6 = (bf16[392,768]{1,0:T(8,128)(2,1)}, bf16[392,768]{1,0:T(8,128)(2,1)}, u32[]{:S(2)}, u32[]{:S(2)}) collective-permute-start(bf16[392,768]{1,0:T(8,128)(2,1)} %fusion.4), channel_id=1, source_target_pairs={{0,1},{1,0},{2,3},{3,2},{4,5},{5,4},{6,7},{7,6},{8,9},{9,8},{10,11... | collective-permute-start | bytes 1806344 | tf_op jit(solution)/shard_map/ppermute | solution.py:298
  111.8 14.9 %collective-permute-start.21 = (bf16[2,384,384]{2,1,0:T(8,128)(2,1)}, bf16[2,384,384]{2,1,0:T(8,128)(2,1)}, u32[]{:S(2)}, u32[]{:S(2)}) collective-permute-start(bf16[2,384,384]{2,1,0:T(8,128)(2,1)} %get-tuple-element.30), channel_id=1, source_target_pairs={{0,16},{4,20},{8,24},{12,28},{16,0},{20,4},{24,8},{28,12},{1,17},{... | collective-permute-start | bytes 1769480 | tf_op jit(solution)/shard_map/ppermute | solution.py:302
  117.8 5.4 %copy-start.14 = (bf16[2,384,384]{2,1,0:T(8,128)(2,1)S(1)}, bf16[2,384,384]{2,1,0:T(8,128)(2,1)}, u32[]{:S(2)}) copy-start(bf16[2,384,384]{2,1,0:T(8,128)(2,1)} %copy-done.13) | copy-start | bytes 1769476
  125.2 8.6 %collective-permute-start.20 = (bf16[384,384]{1,0:T(8,128)(2,1)}, bf16[384,384]{1,0:T(8,128)(2,1)}, u32[]{:S(2)}, u32[]{:S(2)}) collective-permute-start(bf16[384,384]{1,0:T(8,128)(2,1)} %fusion.5), channel_id=1, source_target_pairs={{0,16},{4,20},{8,24},{12,28},{16,0},{20,4},{24,8},{28,12},{1,17},{... | collective-permute-start | bytes 884744 | tf_op jit(solution)/shard_map/ppermute | solution.py:302
  129.1 8.4 %collective-permute-start.22 = (bf16[384,384]{1,0:T(8,128)(2,1)}, bf16[384,384]{1,0:T(8,128)(2,1)}, u32[]{:S(2)}, u32[]{:S(2)}) collective-permute-start(bf16[384,384]{1,0:T(8,128)(2,1)} %fusion.6), channel_id=1, source_target_pairs={{0,8},{4,12},{8,0},{12,4},{16,24},{20,28},{24,16},{28,20},{1,9},{5... | collective-permute-start | bytes 884744 | tf_op jit(solution)/shard_map/ppermute | solution.py:302
  (27 other events, 56.8 us)

commit v2 on v0

v2 whole, which is shorter than its diff:
```python
import functools

import jax
import jax.numpy as jnp
from jax import lax
from jax.experimental import pallas as pl
from jax.experimental.pallas import tpu as pltpu
from jax.sharding import PartitionSpec as P

LANES = 256
VMEM = 20 * 1024 * 1024
F32 = jnp.float32
BF16 = jnp.bfloat16
HIGHEST = lax.Precision.HIGHEST


def params(**more):
    return pltpu.CompilerParams(vmem_limit_bytes=VMEM, **more)


SCALE = 0.3


def cost(micros):
    return pl.CostEstimate(
        flops=int(micros * SCALE * 1.15e9), bytes_accessed=1, transcendentals=0
    )


def exact_dot(values, weight, dims):
    high = values.astype(BF16).astype(F32)
    rest = values - high
    middle = rest.astype(BF16).astype(F32)
    count = values.shape[0]
    terms = [high, middle, rest - middle, jnp.zeros_like(values)]
    stacked = jnp.concatenate(terms, axis=0).astype(BF16)
    out = lax.dot_general(stacked, weight, (dims, ((), ())), preferred_element_type=F32)
    return out[:count] + out[count : 2 * count] + out[2 * count : 3 * count]


def silu_grad(values):
    logistic = jax.nn.sigmoid(values)
    return logistic * (1.0 + values * (1.0 - logistic))


def to_rows(images):
    return jnp.transpose(images, (1, 2, 0, 3)).reshape(-1, images.shape[3])


def from_rows(rows, shape):
    count, height, width, channels = shape
    return jnp.transpose(rows.reshape(height, width, count, channels), (1 + 1, 0, 1, 3))


def per_row(values, rows):
    tiled = jnp.concatenate([values] * (8 // values.shape[0]), axis=0)
    return jnp.broadcast_to(tiled[None], (rows // 8, 8, values.shape[1])).reshape(rows, -1)


def image_sum(values, images):
    folded = values.reshape(-1, 8, values.shape[1]).sum(axis=0)
    total = folded[:images]
    for start in range(images, 8, images):
        total = total + folded[start : start + images]
    return total


def convolve(rows_ref, pad_ref, weight_ref, height, width, images, turn):
    line, unit = width * images, 16 * images
    group = weight_ref.shape[2]
    pad_ref[...] = jnp.zeros_like(pad_ref)
    for h in range(height):
        pad_ref[pl.ds(8 + (h + 1) * unit + images, line), :] = rows_ref[pl.ds(h * line, line), :]
    row_group = lax.broadcasted_iota(jnp.int32, (LANES, LANES), 0) // group
    col_group = lax.broadcasted_iota(jnp.int32, (LANES, LANES), 1) // group
    mask = (row_group == col_group).astype(F32).astype(BF16)
    total = None
    for dw in range(3):
        shifted = pad_ref[pl.ds(8 + images * (dw - 1), (height + 2) * unit), :].astype(BF16)
        for dh in range(3):
            tap = weight_ref[2 - dh, 2 - dw] if turn else weight_ref[dh, dw]
            dense = jnp.concatenate([tap] * (LANES // group), axis=0) * mask
            part = lax.dot_general(
                shifted[dh * unit : (dh + height) * unit],
                dense,
                (((1,), (1 if turn else 0,)), ((), ())),
                preferred_element_type=F32,
            )
            total = part if total is None else total + part
    pad_ref[pl.ds(0, height * unit), :] = total
    for h in range(height):
        rows_ref[pl.ds(h * line, line), :] = pad_ref[pl.ds(h * unit + images, line), :]


HBM = pl.BlockSpec(memory_space=pltpu.HBM)
HERE = pl.BlockSpec(memory_space=pltpu.VMEM)


def lanes_of(i):
    return pl.ds(i * LANES, LANES)


def fetch(source, target, sem):
    copy = pltpu.make_async_copy(source, target, sem)
    copy.start()
    return copy


def conv_forward_body(
    x_hbm,
    w_hbm,
    down_hbm,
    conv_ref,
    act_ref,
    pre_ref,
    x_buf,
    w_buf,
    down_buf,
    rows_ref,
    pad_ref,
    sems,
    *,
    height,
    width,
    images,
):
    blocks = conv_ref.shape[1] // LANES
    copies = [fetch(x_hbm, x_buf, sems.at[0])]
    for i in range(blocks):
        part = w_hbm.at[:, :, :, lanes_of(i)]
        copies.append(fetch(part, w_buf.at[i], sems.at[2 + i]))
    down_copy = fetch(down_hbm, down_buf, sems.at[1])
    copies[0].wait()
    means = []
    for i in range(blocks):
        rows_ref[...] = x_buf[:, lanes_of(i)].astype(F32)
        copies[1 + i].wait()
        convolve(rows_ref, pad_ref, w_buf.at[i], height, width, images, False)
        conv = rows_ref[...]
        conv_ref[:, lanes_of(i)] = conv
        act = (conv * jax.nn.sigmoid(conv)).astype(BF16)
        act_ref[:, lanes_of(i)] = act
        means.append(image_sum(act.astype(F32), images) / (height * width))
    down_copy.wait()
    pre_ref[...] = exact_dot(jnp.concatenate(means, axis=1), down_buf[...], ((1,), (0,)))


def conv_forward(rows, weight, down, shape):
    images, height, width, channels = shape
    count, inner = rows.shape[0], down.shape[1]
    blocks = channels // LANES
    return pl.pallas_call(
        functools.partial(conv_forward_body, height=height, width=width, images=images),
        in_specs=[HBM, HBM, HBM],
        out_specs=[HERE, HERE, HERE],
        out_shape=[
            jax.ShapeDtypeStruct((count, channels), F32),
            jax.ShapeDtypeStruct((count, channels), BF16),
            jax.ShapeDtypeStruct((images, inner), F32),
        ],
        scratch_shapes=[
            pltpu.VMEM((count, channels), BF16),
            pltpu.VMEM((blocks, 3, 3, weight.shape[2], LANES), BF16),
            pltpu.VMEM(down.shape, BF16),
            pltpu.VMEM((count, LANES), F32),
            pltpu.VMEM((16 + (height + 2) * 16 * images, LANES), F32),
            pltpu.SemaphoreType.DMA((2 + blocks,)),
        ],
        compiler_params=params(),
        cost_estimate=cost(3),
        name="conv_forward",
    )(rows, weight, down)


def conv_backward_body(
    grad_ref,
    gate_ref,
    sum_ref,
    pre_ref,
    down_hbm,
    conv_ref,
    w_hbm,
    out_hbm,
    down_buf,
    w_buf,
    out_buf,
    rows_ref,
    pad_ref,
    sems,
    *,
    height,
    width,
    images,
):
    count, channels = grad_ref.shape
    blocks = channels // LANES
    down_copy = fetch(down_hbm, down_buf, sems.at[0])
    copies = []
    for i in range(blocks):
        part = w_hbm.at[:, :, :, lanes_of(i)]
        copies.append(fetch(part, w_buf.at[i], sems.at[1 + i]))
    excite_grad = sum_ref[...] * silu_grad(pre_ref[...])
    down_copy.wait()
    squeeze_grad = exact_dot(excite_grad, down_buf[...], ((1,), (1,))) / (height * width)
    outs = []
    for i in range(blocks):
        gate = per_row(gate_ref[:, lanes_of(i)], count)
        squeeze = per_row(squeeze_grad[:, i * LANES : (i + 1) * LANES], count)
        act_grad = grad_ref[:, lanes_of(i)] * gate + squeeze
        rows_ref[...] = act_grad * silu_grad(conv_ref[:, lanes_of(i)])
        copies[i].wait()
        convolve(rows_ref, pad_ref, w_buf.at[i], height, width, images, True)
        out_buf[:, lanes_of(i)] = rows_ref[...].astype(BF16)
        target = out_hbm.at[:, lanes_of(i)]
        outs.append(fetch(out_buf.at[:, lanes_of(i)], target, sems.at[1 + blocks + i]))
    for out in outs:
        out.wait()


def conv_backward(scaled_grad, gating, excite_sum, excite_pre, down, convolved, weight, shape):
    images, height, width, channels = shape
    count = convolved.shape[0]
    blocks = channels // LANES
    return pl.pallas_call(
        functools.partial(conv_backward_body, height=height, width=width, images=images),
        in_specs=[HERE, HERE, HERE, HERE, HBM, HERE, HBM],
        out_specs=HBM,
        out_shape=jax.ShapeDtypeStruct((count, channels), BF16),
        scratch_shapes=[
            pltpu.VMEM(down.shape, BF16),
            pltpu.VMEM((blocks, 3, 3, weight.shape[2], LANES), BF16),
            pltpu.VMEM((count, channels), BF16),
            pltpu.VMEM((count, LANES), F32),
            pltpu.VMEM((16 + (height + 2) * 16 * images, LANES), F32),
            pltpu.SemaphoreType.DMA((1 + 2 * blocks,)),
        ],
        compiler_params=params(),
        cost_estimate=cost(3),
        name="conv_backward",
    )(scaled_grad, gating, excite_sum, excite_pre, down, convolved, weight)


def block_of(weight_ref, block, width):
    return weight_ref.at[:, pl.ds(pl.multiple_of(block * width, width), width)]


def scale_body(
    order_ref,
    act_ref,
    pre_ref,
    up_hbm,
    w_hbm,
    middle_hbm,
    gate_ref,
    scaled_hbm,
    far_hbm,
    send_hbm,
    up_buf,
    w_buf,
    middle_buf,
    scaled_buf,
    far_buf,
    sems,
):
    channels = act_ref.shape[1]
    up_copy = fetch(up_hbm, up_buf, sems.at[0])
    w_copy = fetch(block_of(w_hbm, order_ref[3], channels), w_buf, sems.at[1])
    middle_copy = fetch(middle_hbm, middle_buf, sems.at[2])
    pre = pre_ref[...]
    excited = pre * jax.nn.sigmoid(pre)
    up_copy.wait()
    gate_ref[...] = jax.nn.sigmoid(exact_dot(excited, up_buf[...], ((1,), (0,))))
    gate = per_row(gate_ref[...], act_ref.shape[0])
    scaled_buf[...] = (act_ref[...].astype(F32) * gate).astype(BF16)
    sent = [fetch(scaled_buf, scaled_hbm, sems.at[3])]
    w_copy.wait()
    far = jnp.dot(scaled_buf[...], w_buf[...], preferred_element_type=F32).astype(BF16)
    far_buf[...] = far
    sent.append(fetch(far_buf, far_hbm, sems.at[4]))
    middle_copy.wait()

    @pl.when(order_ref[4] == 1)
    def _():
        middle_buf[...] = far

    sent.append(fetch(middle_buf, send_hbm, sems.at[5]))
    for copy in sent:
        copy.wait()


def scale(order, act, excite_pre, up, weight, middle):
    count, channels = act.shape
    gates = (excite_pre.shape[0], channels)
    array = jax.ShapeDtypeStruct((count, channels), BF16)
    return pl.pallas_call(
        scale_body,
        in_specs=[pl.BlockSpec(memory_space=pltpu.SMEM), HERE, HERE, HBM, HBM, HBM],
        out_specs=[HERE, HBM, HBM, HBM],
        out_shape=[jax.ShapeDtypeStruct(gates, F32)] + [array] * 3,
        scratch_shapes=[
            pltpu.VMEM(up.shape, BF16),
            pltpu.VMEM((channels, channels), BF16),
            pltpu.VMEM((count, channels), BF16),
            pltpu.VMEM((count, channels), BF16),
            pltpu.VMEM((count, channels), BF16),
            pltpu.SemaphoreType.DMA((6,)),
        ],
        compiler_params=params(),
        cost_estimate=cost(3),
        name="scale",
    )(order, act, excite_pre, up, weight, middle)


def project_body(order_ref, scaled_hbm, w_hbm, *refs, parts):
    outs, (scaled_buf, w_buf, out_buf, sems) = refs[:parts], refs[parts:]
    channels = scaled_buf.shape[1]
    scaled_copy = fetch(scaled_hbm, scaled_buf, sems.at[0])
    copies = [
        fetch(block_of(w_hbm, order_ref[k], channels), w_buf.at[k], sems.at[1 + k])
        for k in range(parts)
    ]
    scaled_copy.wait()
    sent = []
    for k in range(parts):
        copies[k].wait()
        part = jnp.dot(scaled_buf[...], w_buf[k], preferred_element_type=F32)
        out_buf[k] = part.astype(BF16)
        sent.append(fetch(out_buf.at[k], outs[k], sems.at[1 + parts + k]))
    for copy in sent:
        copy.wait()


def project(order, parts, scaled, weight):
    count, channels = scaled.shape
    array = jax.ShapeDtypeStruct((count, channels), BF16)
    return pl.pallas_call(
        functools.partial(project_body, parts=parts),
        in_specs=[pl.BlockSpec(memory_space=pltpu.SMEM), HBM, HBM],
        out_specs=[HBM] * parts,
        out_shape=[array] * parts,
        scratch_shapes=[
            pltpu.VMEM((count, channels), BF16),
            pltpu.VMEM((parts, channels, channels), BF16),
            pltpu.VMEM((parts, count, channels), BF16),
            pltpu.SemaphoreType.DMA((1 + 2 * parts,)),
        ],
        compiler_params=params(),
        cost_estimate=cost(3),
        name="project",
    )(order, scaled, weight)


def second_body(end_ref, came, middle, far, p_fourth, p_third, third, to_far, send):
    at_end = end_ref[0] == 1
    to_far[...] = (p_fourth[...].astype(F32) + came[...].astype(F32)).astype(BF16)

    @pl.when(at_end)
    def _():
        third[...] = came[...]
        send[...] = p_third[...]

    @pl.when(jnp.logical_not(at_end))
    def _():
        third[...] = middle[...]
        send[...] = far[...]


def third_body(end_ref, came, crossed, far, p_outer, p_third, fourth, to_mid, send):
    at_end = end_ref[0] == 1
    to_mid[...] = (p_third[...].astype(F32) + came[...].astype(F32)).astype(BF16)

    @pl.when(at_end)
    def _():
        fourth[...] = came[...]
        send[...] = p_outer[...]

    @pl.when(jnp.logical_not(at_end))
    def _():
        fourth[...] = far[...]
        send[...] = (p_outer[...].astype(F32) + crossed[...].astype(F32)).astype(BF16)


def between(body, at_end, *arrays):
    shape = arrays[0].shape
    block = pl.BlockSpec(shape, lambda i: (0, 0))
    return pl.pallas_call(
        body,
        grid=(1,),
        in_specs=[pl.BlockSpec(memory_space=pltpu.SMEM)] + [block] * 5,
        out_specs=[block] * 3,
        out_shape=[jax.ShapeDtypeStruct(shape, BF16)] * 3,
        compiler_params=params(),
        cost_estimate=cost(2),
        name="between",
    )(at_end, *arrays)


def input_grad_body(order_ref, *refs, pieces, started, last, images):
    piece_refs, w_hbm, refs = refs[:pieces], refs[pieces], refs[pieces + 1 :]
    if started:
        start_ref, refs = refs[0], refs[1:]
    if last:
        act_ref, gate_ref, up_hbm, out_ref, excite_ref, piece_buf, w_buf, sems, up_buf = refs
    else:
        out_ref, piece_buf, w_buf, sems = refs
    width = out_ref.shape[1]
    copies = []
    for k, piece_ref in enumerate(piece_refs):
        block = block_of(w_hbm, order_ref[k], width)
        copies.append(
            (
                fetch(piece_ref, piece_buf.at[k], sems.at[2 * k]),
                fetch(block, w_buf.at[k], sems.at[2 * k + 1]),
            )
        )
    if last:
        up_copy = fetch(up_hbm, up_buf, sems.at[2 * pieces])
    for k in range(pieces):
        for copy in copies[k]:
            copy.wait()
        part = lax.dot_general(
            piece_buf[k], w_buf[k], (((1,), (1,)), ((), ())), preferred_element_type=F32
        )
        if k > 0:
            part = out_ref[...] + part
        elif started:
            part = start_ref[...] + part
        out_ref[...] = part
    if last:
        gating = gate_ref[...]
        gate_grad = image_sum(out_ref[...] * act_ref[...].astype(F32), images)
        pre_grad = gate_grad * gating * (1.0 - gating)
        up_copy.wait()
        excite_ref[...] = exact_dot(pre_grad, up_buf[...], ((1,), (1,)))


def input_grad(order, pieces, weight, images, start=None, act=None, gating=None, up=None):
    count, channels = pieces[0].shape
    started, last = start is not None, act is not None
    operands = list(pieces) + [weight]
    in_specs = [pl.BlockSpec(memory_space=pltpu.SMEM)] + [HBM] * (len(pieces) + 1)
    out_shape = [jax.ShapeDtypeStruct((count, channels), F32)]
    scratch = [
        pltpu.VMEM((len(pieces), count, channels), BF16),
        pltpu.VMEM((len(pieces), channels, channels), BF16),
        pltpu.SemaphoreType.DMA((2 * len(pieces) + 1,)),
    ]
    if started:
        operands.append(start)
        in_specs.append(HERE)
    if last:
        operands += [act, gating, up]
        in_specs += [HERE, HERE, HBM]
        out_shape.append(jax.ShapeDtypeStruct((images, up.shape[0]), F32))
        scratch.append(pltpu.VMEM(up.shape, BF16))
    return pl.pallas_call(
        functools.partial(
            input_grad_body, pieces=len(pieces), started=started, last=last, images=images
        ),
        in_specs=in_specs,
        out_specs=[HERE] * len(out_shape),
        out_shape=out_shape,
        scratch_shapes=scratch,
        compiler_params=params(),
        cost_estimate=cost(len(pieces)),
        name="input_grad_last" if last else "input_grad",
    )(order, *operands)


def place_block(total, block, x, y, x_send, x_keep, y_send, y_keep, store):
    half = total.shape[0] // 2
    to_x, to_y = block % 2, block // 2

    @pl.when(to_x != x)
    def _():
        store(x_send, to_y, total[:half])

    @pl.when(to_x == x)
    def _():
        store(x_keep, to_y, total[:half])

    @pl.when(to_y != y)
    def _():
        store(y_send, to_x, total[half:])

    @pl.when(to_y == y)
    def _():
        store(y_keep, to_x, total[half:])


def put(ref, index, values):
    ref[index] = values


def weight_grad_body(place_ref, own_ref, other_ref, *refs, pieces):
    mine, theirs, outs = refs[:pieces], refs[pieces : 2 * pieces], refs[2 * pieces :]
    x, y = place_ref[pieces], place_ref[pieces + 1]
    own, other = own_ref[...].T, other_ref[...].T
    for k in range(pieces):
        total = jnp.dot(own, mine[k][...], preferred_element_type=F32)
        total += jnp.dot(other, theirs[k][...], preferred_element_type=F32)
        place_block(total.astype(BF16), place_ref[k], x, y, *outs, put)


def weight_grad_more_body(place_ref, own_ref, other_ref, mine, theirs, *refs):
    outs = refs[4:8]
    buffer, sem = refs[8:]
    x, y = place_ref[1], place_ref[2]
    half = own_ref.shape[1] // 2
    total = jnp.dot(own_ref[...].T, mine[...], preferred_element_type=F32)
    total += jnp.dot(other_ref[...].T, theirs[...], preferred_element_type=F32)
    buffer[0] = total[:half].astype(BF16)
    buffer[1] = total[half:].astype(BF16)
    block = place_ref[0]
    to_x, to_y = block % 2, block // 2

    def move(ref, index, part):
        copy = pltpu.make_async_copy(buffer.at[part], ref.at[index], sem)
        copy.start()
        copy.wait()

    @pl.when(to_x != x)
    def _():
        move(outs[0], to_y, 0)

    @pl.when(to_x == x)
    def _():
        move(outs[1], to_y, 0)

    @pl.when(to_y != y)
    def _():
        move(outs[2], to_x, 1)

    @pl.when(to_y == y)
    def _():
        move(outs[3], to_x, 1)


def weight_grad(place, own, other, mine, theirs, begun=None):
    count, channels = own.shape
    columns = channels // 2
    array = jax.ShapeDtypeStruct((2, channels // 2, columns), BF16)
    pieces = len(mine)
    whole = pl.BlockSpec((count, channels), lambda i, place: (0, 0))
    part = pl.BlockSpec((count, columns), lambda i, place: (0, place[pieces + 2]))
    out = pl.BlockSpec(array.shape, lambda i, place: (0, 0, 0))
    scratch = []
    if begun is not None:
        out = pl.BlockSpec(memory_space=pl.ANY)
        scratch = [pltpu.VMEM(array.shape, BF16), pltpu.SemaphoreType.DMA]
    body = functools.partial(weight_grad_body, pieces=pieces)
    return pl.pallas_call(
        body if begun is None else weight_grad_more_body,
        grid_spec=pltpu.PrefetchScalarGridSpec(
            num_scalar_prefetch=1,
            grid=(1,),
            in_specs=[whole] * 2 + [part] * (2 * pieces) + [out] * len(begun or ()),
            out_specs=[out] * 4,
            scratch_shapes=scratch,
        ),
        out_shape=[array] * 4,
        input_output_aliases={} if begun is None else {5 + k: k for k in range(4)},
        compiler_params=params(),
        cost_estimate=cost(2 * pieces),
        name="weight_grad" if begun is None else "weight_grad_more",
    )(place, own, other, *mine, *theirs, *(begun or ()))


def merge_body(place_ref, x_keep, x_came, y_keep, y_came, top, to_y, bottom, to_x):
    x, y = place_ref[0], place_ref[1]
    top[...] = x_keep[y].astype(F32) + x_came[y].astype(F32)
    to_y[...] = (x_keep[1 - y].astype(F32) + x_came[1 - y].astype(F32)).astype(BF16)
    bottom[...] = y_keep[x].astype(F32) + y_came[x].astype(F32)
    to_x[...] = (y_keep[1 - x].astype(F32) + y_came[1 - x].astype(F32)).astype(BF16)


def merge(place, x_keep, x_came, y_keep, y_came):
    rows, columns = x_keep.shape[1:]
    pair = pl.BlockSpec((2, rows, columns), lambda i, place: (0, 0, 0))
    one = pl.BlockSpec((rows, columns), lambda i, place: (0, 0))
    kept = jax.ShapeDtypeStruct((rows, columns), F32)
    sent = jax.ShapeDtypeStruct((rows, columns), BF16)
    return pl.pallas_call(
        merge_body,
        grid_spec=pltpu.PrefetchScalarGridSpec(
            num_scalar_prefetch=1, grid=(1,), in_specs=[pair] * 4, out_specs=[one] * 4
        ),
        out_shape=[kept, sent, kept, sent],
        compiler_params=params(),
        cost_estimate=cost(2),
        name="merge",
    )(place, x_keep, x_came, y_keep, y_came)


def finish_body(top, top_came, bottom, bottom_came, out):
    rows = top.shape[0]
    out[:rows] = top[...] + top_came[...].astype(F32)
    out[rows:] = bottom[...] + bottom_came[...].astype(F32)


def finish(top, top_came, bottom, bottom_came):
    rows, columns = top.shape
    one = pl.BlockSpec((rows, columns), lambda i: (0, 0))
    return pl.pallas_call(
        finish_body,
        grid=(1,),
        in_specs=[one] * 4,
        out_specs=pl.BlockSpec((2 * rows, columns), lambda i: (0, 0)),
        out_shape=jax.ShapeDtypeStruct((2 * rows, columns), F32),
        compiler_params=params(),
        cost_estimate=cost(2),
        name="finish",
    )(top, top_came, bottom, bottom_came)


def add_body(a, b, out):
    out[...] = (a[...].astype(F32) + b[...].astype(F32)).astype(BF16)


def add(a, b):
    block = pl.BlockSpec(a.shape, lambda i: (0, 0))
    return pl.pallas_call(
        add_body,
        grid=(1,),
        in_specs=[block, block],
        out_specs=block,
        out_shape=jax.ShapeDtypeStruct(a.shape, BF16),
        compiler_params=params(),
        cost_estimate=cost(1),
        name="add",
    )(a, b)


OUTER = [(0, 1), (1, 0), (2, 3), (3, 2)]
INWARD = [(0, 1), (3, 2)]
OUTWARD = [(1, 0), (2, 3)]
MIDDLE = [(1, 2), (2, 1)]
OVER = [(0, 2), (2, 0), (1, 3), (3, 1)]
CROSS = [(0, 3), (3, 0), (1, 2), (2, 1)]


def along_chan(array, pairs):
    return lax.ppermute(array, "chan", pairs)


def along_dp(array, bit):
    return lax.ppermute(array, "dp", [(i, i ^ bit) for i in range(8)])


def small_sum(values):
    near, across, over = (along_chan(values, pairs) for pairs in (OUTER, CROSS, OVER))
    return (values + near) + (across + over)


def after(array, *others):
    return lax.optimization_barrier((array, *others))[0]


def on_line(hidden, conv_weight, se_down, se_up, proj_weight, grad_out):
    shape = hidden.shape
    images = shape[0]
    z, place = lax.axis_index("chan"), lax.axis_index("dp")
    at_end = (z == 0) | (z == 3)
    core, x, y = place % 2, (place // 2) % 2, place // 4
    spot = jnp.stack([x, y, core]).astype(jnp.int32)
    order = jnp.array([[0, 1, 2, 3], [1, 0, 2, 3], [2, 3, 1, 0], [3, 2, 1, 0]], jnp.int32)[z]

    own = to_rows(grad_out)
    outer = along_chan(own, OUTER)
    middle = along_chan(own, MIDDLE)

    convolved, act, terms = conv_forward(to_rows(hidden), conv_weight, se_down, shape)
    excite_pre = small_sum(terms)

    role = jnp.concatenate([order, at_end.astype(jnp.int32)[None]])
    gating, scaled, p_fourth, send = scale(role, act, excite_pre, se_up, proj_weight, middle)
    came = along_chan(send, OUTER)
    far = along_chan(after(outer, send), MIDDLE)
    other = along_dp(scaled, 1)
    theirs = [along_dp(piece, 1) for piece in (own, outer)]
    p_own, p_outer, p_third = project(order[:3], 3, scaled, proj_weight)
    (begun,) = input_grad(order[:2], [after(own, p_own), outer], proj_weight, images)

    came, far = lax.optimization_barrier((came, far, begun))[:2]
    third, to_far, send = between(second_body, role[4:], came, middle, far, p_fourth, p_third)
    came = along_chan(send, OUTER)
    crossed = along_chan(to_far, MIDDLE)
    theirs.append(along_dp(third, 1))
    pieces = [own, outer, third]
    weights = weight_grad(jnp.concatenate([order[:3], spot]), scaled, other, pieces, theirs)
    (begun,) = input_grad(order[2:3], [third], proj_weight, images, begun)

    came, crossed = lax.optimization_barrier((came, crossed, begun, *weights))[:2]
    fourth, to_mid, send = between(third_body, role[4:], came, crossed, far, p_outer, p_third)
    came = along_chan(send, OUTER)
    crossed = along_chan(to_mid, MIDDLE)
    weights = weight_grad(
        jnp.concatenate([order[3:], spot]), scaled, other, [fourth], [along_dp(fourth, 1)], weights
    )
    x_send, x_keep, y_send, y_keep = weights
    x_came, y_came = along_dp(x_send, 2), along_dp(y_send, 4)
    scaled_grad, terms = input_grad(
        order[3:], [after(fourth, *weights)], proj_weight, images, begun, act, gating, se_up
    )

    terms, came, crossed = lax.optimization_barrier((terms, came, crossed))
    excite_sum = small_sum(terms)
    total = p_own.astype(F32) + came.astype(F32)
    total = total + jnp.where(at_end, 0.0, crossed.astype(F32))
    projected = from_rows(total.astype(BF16), shape)

    top, to_y, bottom, to_x = merge(spot, x_keep, x_came, y_keep, y_came)
    excite_sum = after(excite_sum, to_x)
    grad_hidden = conv_backward(
        scaled_grad, gating, excite_sum, excite_pre, se_down, convolved, conv_weight, shape
    )
    grad_proj = finish(top, along_dp(to_y, 4), bottom, along_dp(to_x, 2))
    return (projected, from_rows(grad_hidden, shape), grad_proj)


def on_any(hidden, conv_weight, se_down, se_up, proj_weight, grad_out):
    shape = hidden.shape
    images = shape[0]
    convolved, act, terms = conv_forward(to_rows(hidden), conv_weight, se_down, shape)
    excite_pre = lax.psum(terms, "chan")
    gating = jax.nn.sigmoid(jnp.dot(jax.nn.silu(excite_pre), se_up.astype(F32), precision=HIGHEST))
    count = act.shape[0]
    act_float = act.astype(F32)
    scaled = (act_float * per_row(gating, count)).astype(BF16)
    terms = jnp.dot(scaled, proj_weight, preferred_element_type=F32).astype(BF16)
    projected = lax.psum_scatter(terms, "chan", scatter_dimension=1, tiled=True)
    pieces = lax.all_gather(to_rows(grad_out), "chan", axis=1, tiled=True)
    scaled_grad = lax.dot_general(
        pieces, proj_weight, (((1,), (1,)), ((), ())), preferred_element_type=F32
    )
    terms = lax.dot_general(scaled, pieces, (((0,), (0,)), ((), ())), preferred_element_type=F32)
    grad_proj = lax.psum_scatter(terms, "dp", scatter_dimension=1, tiled=True)
    gate_grad = image_sum(scaled_grad * act_float, images)
    pre_grad = gate_grad * gating * (1.0 - gating)
    excite_sum = lax.psum(jnp.dot(pre_grad, se_up.astype(F32).T, precision=HIGHEST), "chan")
    grad_hidden = conv_backward(
        scaled_grad, gating, excite_sum, excite_pre, se_down, convolved, conv_weight, shape
    )
    return (from_rows(projected, shape), from_rows(grad_hidden, shape), grad_proj)


def solution(mesh):
    in_specs = (
        P("dp", None, None, "chan"),
        P(None, None, None, "chan"),
        P("chan", None),
        P(None, "chan"),
        P("chan", None),
        P("dp", None, None, "chan"),
    )
    out_specs = (P("dp", None, None, "chan"), P("dp", None, None, "chan"), P("chan", "dp"))
    on_device = on_line if (mesh.shape["dp"], mesh.shape["chan"]) == (8, 4) else on_any
    return jax.shard_map(
        on_device, mesh=mesh, in_specs=in_specs, out_specs=out_specs, check_vma=False
    )
```

time: 208 us -> 114 us (0.55)
  waiting for transfers between devices: 86.5 us -> 9.73 us
  matrix products: 52.5 us -> 0 us
  Pallas kernels: 0 us -> 43.1 us
  starting transfers between devices: 0.12 us -> 33.6 us
  blocking collectives: 25 us -> 0 us
  between operations: 13.9 us -> 1.12 us
  local copies, waits for them, and re-layouts: 28.1 us -> 23.2 us
    reduce_scatter x2 -> x0, waiting for transfers between devices: 78.5 us -> none  [the longest x1 77.8 us: on_device(): lax.psum_scatter(dw_block, 'dp', scatter_dimension=1, tiled=True)]
    pallas_call x0 -> x13, Pallas kernels: none -> 43.1 us  [the longest x2 11.1 us: weight_grad(): pl.pallas_call(body if begun is None else weight_grad_more_body, grid_spe...]
    ppermute x0 -> x23, starting transfers between devices: none -> 33.6 us  [the longest x14 28.1 us: along_chan(): return lax.ppermute(array, 'chan', pairs)]
    dot_general x7 -> x0, matrix products: 26.3 us -> none  [the longest x1 8.51 us: on_device(): lax.dot_general(act_rows, piece_rows, (((0,), (0,)), ((), ())), preferred...]
    conv_general_dilated x2 -> x0, matrix products: 26.3 us -> none  [grouped(): lax.conv_general_dilated(inputs, kernel, (1, 1), 'SAME', dimension_number...]
    psum x2 -> x0, blocking collectives: 25 us -> none  [the longest x1 14.4 us: on_device(): lax.psum(jnp.dot(squeezed, se_down.astype(jnp.float32), precision=highest...]
    unnamed x12 -> x72, local copies, waits for them, and re-layouts: 3.64 us -> 15 us
    conv_general_dilated x3 -> x0, local copies, waits for them, and re-layouts: 10.9 us -> none  [grouped(): lax.conv_general_dilated(inputs, kernel, (1, 1), 'SAME', dimension_number...]
  transfers between devices with their start and end apart: 3 -> 23, of which waited for: 3 -> 6; matrix products, arithmetic and copies ran while one was open for 39% -> 7% of each run, Pallas kernels for 0% -> 35%
where the time goes in v2:
time: 114 us; the launch traced here: 113 us
  Pallas kernels  43.1 us (38%)
  starting transfers between devices  33.6 us (29%)
  local copies, waits for them, and re-layouts  23.2 us (20%)
  waiting for transfers between devices  9.73 us (9%)
  other arithmetic  2.04 us (2%)
    ppermute x14, starting transfers between devices, along_chan(): return lax.ppermute(array, 'chan', pairs)  28.1 us
    unnamed x72, local copies, waits for them, and re-layouts  15 us
    pallas_call x2, Pallas kernels, weight_grad(): pl.pallas_call(body if begun is None else weight_grad_more_body, grid_spe...  11.1 us
    ppermute x14, waiting for transfers between devices, along_chan(): return lax.ppermute(array, 'chan', pairs)  9.09 us
    pallas_call x3, Pallas kernels, input_grad(): pl.pallas_call(functools.partial(input_grad_body, pieces=len(pieces), sta...  8.07 us
    ppermute x9, starting transfers between devices, along_dp(): return lax.ppermute(array, 'dp', [(i, i ^ bit) for i in range(8)])  5.56 us
    pallas_call x1, Pallas kernels, conv_backward(): pl.pallas_call(functools.partial(conv_backward_body, height=height, width...  4.88 us
    pallas_call x1, Pallas kernels, conv_forward(): pl.pallas_call(functools.partial(conv_forward_body, height=height, width=...  4.5 us
  transfers between devices with their start and end apart: 23, of which 6 were waited for; matrix products, arithmetic and copies ran while one was open for 7% of the time, Pallas kernels for 35%

profile of v2, /device:TPU:0, one launch (start us, length us, event | category | flops | bytes accessed | tf_op | source)
XLA Modules:
  0.0 112.8 jit_solution(7247358305532088708)
XLA Ops:
  0.6 2.1 %reshape.23.refs_0_ = bf16[392,768]{1,0:T(8,128)(2,1)S(1)} reshape(bf16[14,14,2,768]{3,2,1,0:T(2,128)(2,1)} %bitcast.18) | data formatting | bytes 1204224 | tf_op jit(solution)/shard_map/reshape | solution.py:47
  3.4 5.9 %collective-permute-start.5 = (bf16[392,768]{1,0:T(8,128)(2,1)S(1)}, bf16[392,768]{1,0:T(8,128)(2,1)}, u32[]{:S(2)}, u32[]{:S(2)}) collective-permute-start(bf16[392,768]{1,0:T(8,128)(2,1)S(1)} %reshape.23.refs_0_), channel_id=1, source_target_pairs={{0,1},{1,0},{2,3},{3,2},{4,5},{5,4},{6,7},{7,6},{8,9},{9,8},{10,11... | collective-permute-start | bytes 1806344 | tf_op jit(solution)/shard_map/ppermute | solution.py:643
  10.3 1.4 %copy-done.12 = bf16[768,1024]{1,0:T(8,128)(2,1)S(1)} copy-done((bf16[768,1024]{1,0:T(8,128)(2,1)S(1)}, bf16[768,1024]{1,0:T(8,128)(2,1)}, u32[]{:S(2)}) %copy-start.12) | copy-done | bytes 1572888
  11.7 1.2 %copy-done.16 = bf16[3,3,64,768]{3,2,1,0:T(8,128)(2,1)S(1)} copy-done((bf16[3,3,64,768]{3,2,1,0:T(8,128)(2,1)S(1)}, bf16[3,3,64,768]{3,2,1,0:T(8,128)(2,1)}, u32[]{:S(2)}) %copy-start.16) | copy-done | bytes 884760
  14.0 4.5 %conv_forward.1 = (f32[392,768]{1,0:T(8,128)S(1)}, bf16[392,768]{1,0:T(8,128)(2,1)S(1)}, f32[2,1024]{1,0:T(2,128)S(1)}) custom-call(bf16[392,768]{1,0:T(8,128)(2,1)S(1)} %copy-done.20, bf16[3,3,64,768]{3,2,1,0:T(8,128)(2,1)S(1)} %copy-done.16, bf16[768,1024]{1,0:T(8,128)(2,1)S(1)} %copy-done.12), custom_call_target="tpu_custom_call" | custom-call | flops 1035000000 | bytes 1 | tf_op jit(solution)/shard_map/conv_forward/pallas_call | solution.py:152
  19.5 2.4 %collective-permute-start.1 = (f32[2,1024]{1,0:T(2,128)S(1)}, f32[2,1024]{1,0:T(2,128)S(1)}, u32[]{:S(2)}, u32[]{:S(2)}) collective-permute-start(f32[2,1024]{1,0:T(2,128)S(1)} %get-tuple-element.45), channel_id=1, source_target_pairs={{0,3},{3,0},{1,2},{2,1},{4,7},{7,4},{5,6},{6,5},{8,11},{11,8},{9,1... | collective-permute-start | bytes 24584 | tf_op jit(solution)/shard_map/ppermute | solution.py:643
  25.6 2.5 %copy-done = bf16[768,3072]{1,0:T(8,128)(2,1)S(1)} copy-done((bf16[768,3072]{1,0:T(8,128)(2,1)S(1)}, bf16[768,3072]{1,0:T(8,128)(2,1)}, u32[]{:S(2)}) %copy-start) | copy-done | bytes 4718616
  28.2 2.5 %scale.1 = (f32[2,768]{1,0:T(2,128)S(1)}, bf16[392,768]{1,0:T(8,128)(2,1)}, bf16[392,768]{1,0:T(8,128)(2,1)S(1)}, bf16[392,768]{1,0:T(8,128)(2,1)S(1)}) custom-call(s32[5]{0:T(128)S(1)} %pad_add_fusion.order_ref, bf16[392,768]{1,0:T(8,128)(2,1)S(1)} %get-tuple-element.44.act_ref.refs_3_, f32[2,1024]{1,0:T(2,128)S(1)} %add_add_fusion.1.pre_ref, ...), custom_call_target="tpu_custom_call" | custom-call | flops 1035000000 | bytes 1 | tf_op jit(solution)/shard_map/scale/pallas_call | solution.py:295
  30.7 1.1 %collective-permute-start.4 = (bf16[392,768]{1,0:T(8,128)(2,1)S(1)}, bf16[392,768]{1,0:T(8,128)(2,1)S(1)}, u32[]{:S(2)}, u32[]{:S(2)}) collective-permute-start(bf16[392,768]{1,0:T(8,128)(2,1)S(1)} %get-tuple-element.48), channel_id=1, source_target_pairs={{0,1},{1,0},{2,3},{3,2},{4,5},{5,4},{6,7},{7,6},{8,9},{9,8},{10,11... | collective-permute-start | bytes 1806344 | tf_op jit(solution)/shard_map/ppermute | solution.py:643
  32.7 4.3 %project.1 = (bf16[392,768]{1,0:T(8,128)(2,1)S(1)}, bf16[392,768]{1,0:T(8,128)(2,1)S(1)}, bf16[392,768]{1,0:T(8,128)(2,1)S(1)}) custom-call(s32[3]{0:T(128)S(1)} %slice_bitcast_fusion.1.order_ref, bf16[392,768]{1,0:T(8,128)(2,1)} %get-tuple-element.46.scaled_hbm.own_ref, bf16[768,3072]{1,0:T(8,128)(2,1)S(1)} %copy-done.1), custom_call_target="tpu_custom_call" | custom-call | flops 1035000000 | bytes 1 | tf_op jit(solution)/shard_map/project/pallas_call | solution.py:336
  38.3 2.8 %input_grad.2.refs_2_ = f32[392,768]{1,0:T(8,128)S(1)} custom-call(s32[2]{0:T(128)S(1)} %slice_bitcast_fusion.order_ref, bf16[392,768]{1,0:T(8,128)(2,1)S(1)} %reshape.23.refs_0_, bf16[392,768]{1,0:T(8,128)(2,1)} %collective-permute-done.5.refs_1_, bf16[768,3072]{1,0:T(8,128)(2,1)S(1)} %copy-done.1), custom_call_target="tpu_custom_call" | custom-call | flops 690000000 | bytes 1 | tf_op jit(solution)/shard_map/input_grad/pallas_call | solution.py:456
  41.1 4.2 %collective-permute-done.4.came = bf16[392,768]{1,0:T(8,128)(2,1)S(1)} collective-permute-done((bf16[392,768]{1,0:T(8,128)(2,1)S(1)}, bf16[392,768]{1,0:T(8,128)(2,1)S(1)}, u32[]{:S(2)}, u32[]{:S(2)}) %collective-permute-start.4) | collective-permute-done | bytes 602144 | tf_op jit(solution)/shard_map/ppermute | solution.py:643
  45.3 1.5 %between.2 = (bf16[392,768]{1,0:T(8,128)(2,1)}, bf16[392,768]{1,0:T(8,128)(2,1)}, bf16[392,768]{1,0:T(8,128)(2,1)}) custom-call(s32[1]{0:T(128)} %bitcast.2.end_ref, bf16[392,768]{1,0:T(8,128)(2,1)S(1)} %collective-permute-done.4.came, bf16[392,768]{1,0:T(8,128)(2,1)S(1)} %copy-done.11, bf16[392,768]{1,0:T(8,128)(2,1)S(1)} %collective-permute-done.6.far, ...), custom_call_target="tpu_custom_call" | custom-call | flops 690000000 | bytes 1 | tf_op jit(solution)/shard_map/between/pallas_call | solution.py:386
  46.8 3.9 %collective-permute-start.7 = (bf16[392,768]{1,0:T(8,128)(2,1)}, bf16[392,768]{1,0:T(8,128)(2,1)}, u32[]{:S(2)}, u32[]{:S(2)}) collective-permute-start(bf16[392,768]{1,0:T(8,128)(2,1)} %get-tuple-element.55), channel_id=1, source_target_pairs={{0,1},{1,0},{2,3},{3,2},{4,5},{5,4},{6,7},{7,6},{8,9},{9,8},{10,11... | collective-permute-start | bytes 1806344 | tf_op jit(solution)/shard_map/ppermute | solution.py:643
  51.5 1.5 %collective-permute-start.8 = (bf16[392,768]{1,0:T(8,128)(2,1)}, bf16[392,768]{1,0:T(8,128)(2,1)}, u32[]{:S(2)}, u32[]{:S(2)}) collective-permute-start(bf16[392,768]{1,0:T(8,128)(2,1)} %get-tuple-element.56), channel_id=1, source_target_pairs={{1,2},{2,1},{5,6},{6,5},{9,10},{10,9},{13,14},{14,13},{17,18},{18,... | collective-permute-start | bytes 1806344 | tf_op jit(solution)/shard_map/ppermute | solution.py:643
  53.7 2.3 %copy-done.2 = bf16[768,3072]{1,0:T(8,128)(2,1)S(1)} copy-done((bf16[768,3072]{1,0:T(8,128)(2,1)S(1)}, bf16[768,3072]{1,0:T(8,128)(2,1)}, u32[]{:S(2)}) %copy-start.2) | copy-done | bytes 4718616
  56.1 2.5 %input_grad.3.refs_2_ = f32[392,768]{1,0:T(8,128)S(1)} custom-call(s32[1]{0:T(128)} %bitcast.7.order_ref, bf16[392,768]{1,0:T(8,128)(2,1)} %get-tuple-element.57.refs_0_.refs_2_, bf16[768,3072]{1,0:T(8,128)(2,1)S(1)} %copy-done.2, f32[392,768]{1,0:T(8,128)S(1)} %input_grad.2.refs_2_), custom_call_target="tpu_custom_call" | custom-call | flops 345000000 | bytes 1 | tf_op jit(solution)/shard_map/input_grad/pallas_call | solution.py:456
  58.7 6.8 %weight_grad.1 = (bf16[2,384,384]{2,1,0:T(8,128)(2,1)}, bf16[2,384,384]{2,1,0:T(8,128)(2,1)S(1)}, bf16[2,384,384]{2,1,0:T(8,128)(2,1)}, bf16[2,384,384]{2,1,0:T(8,128)(2,1)S(1)}) custom-call(s32[6]{0:T(128)S(1)} %pad_add_fusion.1.place_ref, bf16[392,768]{1,0:T(8,128)(2,1)} %get-tuple-element.46.scaled_hbm.own_ref, ...), custom_call_target="tpu_custom_call" | custom-call | flops 2070000000 | bytes 1 | tf_op jit(solution)/shard_map/weight_grad/pallas_call | solution.py:552
  65.6 1.5 %between.3 = (bf16[392,768]{1,0:T(8,128)(2,1)S(1)}, bf16[392,768]{1,0:T(8,128)(2,1)S(1)}, bf16[392,768]{1,0:T(8,128)(2,1)S(1)}) custom-call(s32[1]{0:T(128)} %bitcast.2.end_ref, bf16[392,768]{1,0:T(8,128)(2,1)} %collective-permute-done.7.came, bf16[392,768]{1,0:T(8,128)(2,1)} %collective-permute-done.8.crossed, bf16[392,768]{1,0:T(8,128)(2,1)S(1)} %copy-done.5, ...), custom_call_target="tpu_custom_call" | custom-call | flops 690000000 | bytes 1 | tf_op jit(solution)/shard_map/between/pallas_call | solution.py:386
  67.4 4.1 %collective-permute-start.14 = (bf16[392,768]{1,0:T(8,128)(2,1)S(1)}, bf16[392,768]{1,0:T(8,128)(2,1)S(1)}, u32[]{:S(2)}, u32[]{:S(2)}) collective-permute-start(bf16[392,768]{1,0:T(8,128)(2,1)S(1)} %get-tuple-element.73), channel_id=1, source_target_pairs={{0,1},{1,0},{2,3},{3,2},{4,5},{5,4},{6,7},{7,6},{8,9},{9,8},{10,11... | collective-permute-start | bytes 1806344 | tf_op jit(solution)/shard_map/ppermute | solution.py:643
  72.9 4.3 %weight_grad_more.1 = (bf16[2,384,384]{2,1,0:T(8,128)(2,1)}, bf16[2,384,384]{2,1,0:T(8,128)(2,1)S(1)}, bf16[2,384,384]{2,1,0:T(8,128)(2,1)}, bf16[2,384,384]{2,1,0:T(8,128)(2,1)S(1)}) custom-call(s32[4]{0:T(128)S(1)} %pad_add_fusion.2.place_ref, ...), custom_call_target="tpu_custom_call", output_to_operand_aliasing={{0}: (5, {}), {1}: (6, {}), {2}: (7, {}), {3}: (8, {})} | custom-call | flops 690000000 | bytes 1 | tf_op jit(solution)/shard_map/weight_grad_more/pallas_call | solution.py:552
  79.8 2.8 %input_grad_last.1 = (f32[392,768]{1,0:T(8,128)S(1)}, f32[2,1024]{1,0:T(2,128)S(1)}) custom-call(s32[1]{0:T(128)} %bitcast.5.order_ref, bf16[392,768]{1,0:T(8,128)(2,1)S(1)} %get-tuple-element.70.mine.refs_0_, bf16[768,3072]{1,0:T(8,128)(2,1)S(1)} %bitcast.17, f32[392,768]{1,0:T(8,128)S(1)} %input_grad.3.refs_2_, bf16[392,768]{1,0:T(8,128)(2,1)S(1)} %copy-done.9, ...), custom_call_target="tpu_custom_call" | custom-call | flops 345000000 | bytes 1 | tf_op jit(solution)/shard_map/input_grad_last/pallas_call | solution.py:456
  82.6 3.1 %collective-permute-done.14 = bf16[392,768]{1,0:T(8,128)(2,1)S(1)} collective-permute-done((bf16[392,768]{1,0:T(8,128)(2,1)S(1)}, bf16[392,768]{1,0:T(8,128)(2,1)S(1)}, u32[]{:S(2)}, u32[]{:S(2)}) %collective-permute-start.14) | collective-permute-done | bytes 602144 | tf_op jit(solution)/shard_map/ppermute | solution.py:643
  85.7 3.5 %collective-permute-start.18 = (f32[2,1024]{1,0:T(2,128)S(1)}, f32[2,1024]{1,0:T(2,128)S(1)}, u32[]{:S(2)}, u32[]{:S(2)}) collective-permute-start(f32[2,1024]{1,0:T(2,128)S(1)} %get-tuple-element.78), channel_id=1, source_target_pairs={{0,2},{2,0},{1,3},{3,1},{4,6},{6,4},{5,7},{7,5},{8,10},{10,8},{9,1... | collective-permute-start | bytes 24584 | tf_op jit(solution)/shard_map/ppermute | solution.py:643
  89.3 2.5 %collective-permute-start.17 = (f32[2,1024]{1,0:T(2,128)S(1)}, f32[2,1024]{1,0:T(2,128)S(1)}, u32[]{:S(2)}, u32[]{:S(2)}) collective-permute-start(f32[2,1024]{1,0:T(2,128)S(1)} %get-tuple-element.78), channel_id=1, source_target_pairs={{0,3},{3,0},{1,2},{2,1},{4,7},{7,4},{5,6},{6,5},{8,11},{11,8},{9,1... | collective-permute-start | bytes 24584 | tf_op jit(solution)/shard_map/ppermute | solution.py:643
  92.8 2.7 %reshape.24 = bf16[14,14,2,768]{3,2,1,0:T(2,128)(2,1)} reshape(bf16[392,768]{1,0:T(8,128)(2,1)} %add_convert_fusion) | data formatting | bytes 1204224 | tf_op jit(solution)/shard_map/reshape | solution.py:52
  95.6 1.2 %copy-done.26 = bf16[2,384,384]{2,1,0:T(8,128)(2,1)S(1)} copy-done((bf16[2,384,384]{2,1,0:T(8,128)(2,1)S(1)}, bf16[2,384,384]{2,1,0:T(8,128)(2,1)}, u32[]{:S(2)}) %copy-start.26) | copy-done | bytes 589848
  96.8 2.7 %merge.1 = (f32[384,384]{1,0:T(8,128)S(1)}, bf16[384,384]{1,0:T(8,128)(2,1)}, f32[384,384]{1,0:T(8,128)S(1)}, bf16[384,384]{1,0:T(8,128)(2,1)}) custom-call(s32[3]{0:T(128)S(1)} %pad_add_fusion.3.place_ref, bf16[2,384,384]{2,1,0:T(8,128)(2,1)S(1)} %copy-done.24, bf16[2,384,384]{2,1,0:T(8,128)(2,1)} %collective-permute-done.19.x_came, ...), custom_call_target="tpu_custom_call" | custom-call | flops 690000000 | bytes 1 | tf_op jit(solution)/shard_map/merge/pallas_call | solution.py:583
  101.1 1.5 %collective-permute-start.21 = (bf16[384,384]{1,0:T(8,128)(2,1)}, bf16[384,384]{1,0:T(8,128)(2,1)S(1)}, u32[]{:S(2)}, u32[]{:S(2)}) collective-permute-start(bf16[384,384]{1,0:T(8,128)(2,1)} %get-tuple-element.83), channel_id=1, source_target_pairs={{0,16},{4,20},{8,24},{12,28},{16,0},{20,4},{24,8},{28,12},{1,17},{... | collective-permute-start | bytes 884744 | tf_op jit(solution)/shard_map/ppermute | solution.py:647
  102.6 1.5 %collective-permute-start.22 = (bf16[384,384]{1,0:T(8,128)(2,1)}, bf16[384,384]{1,0:T(8,128)(2,1)}, u32[]{:S(2)}, u32[]{:S(2)}) collective-permute-start(bf16[384,384]{1,0:T(8,128)(2,1)} %get-tuple-element.79), channel_id=1, source_target_pairs={{0,8},{4,12},{8,0},{12,4},{16,24},{20,28},{24,16},{28,20},{1,9},{5... | collective-permute-start | bytes 884744 | tf_op jit(solution)/shard_map/ppermute | solution.py:647
  104.2 4.9 %conv_backward.1 = bf16[392,768]{1,0:T(8,128)(2,1)S(1)} custom-call(f32[392,768]{1,0:T(8,128)S(1)} %get-tuple-element.77.grad_ref, f32[2,768]{1,0:T(2,128)S(1)} %get-tuple-element.71.refs_4_.gate_ref, f32[2,1024]{1,0:T(2,128)S(1)} %add_add_fusion.sum_ref, f32[2,1024]{1,0:T(2,128)S(1)} %add_add_fusion.1.pre_ref, bf16[768,1024]{1,0:T(8,128)(2,1)S(1)} %copy-done.13, ...), custom_call_target="tpu_custom_call" | custom-call | flops 1035000000 | bytes 1 | tf_op jit(solution)/shard_map/conv_backward/pallas_call | solution.py:224
  110.7 2.1 %finish.1 = f32[768,384]{1,0:T(8,128)} custom-call(f32[384,384]{1,0:T(8,128)S(1)} %copy-done.28, bf16[384,384]{1,0:T(8,128)(2,1)S(1)} %collective-permute-done.21.top_came, f32[384,384]{1,0:T(8,128)S(1)} %copy-done.30, bf16[384,384]{1,0:T(8,128)(2,1)} %collective-permute-done.22.bottom_came), custom_call_target="tpu_custom_call" | custom-call | flops 690000000 | bytes 1 | tf_op jit(solution)/shard_map/finish/pallas_call | solution.py:604
  (115 shorter events, 20.0 us)
Async XLA Ops:
  0.6 8.7 %copy-start.33 = (bf16[2,14,14,768]{3,0,2,1:T(2,128)(2,1)S(1)}, bf16[2,14,14,768]{3,0,2,1:T(2,128)(2,1)}, u32[]{:S(2)}) copy-start(bf16[2,14,14,768]{3,0,2,1:T(2,128)(2,1)} %param.7) | copy-start | bytes 1806340
  2.7 22.9 %collective-permute-start.3 = (bf16[392,768]{1,0:T(8,128)(2,1)S(1)}, bf16[392,768]{1,0:T(8,128)(2,1)S(1)}, u32[]{:S(2)}, u32[]{:S(2)}) collective-permute-start(bf16[392,768]{1,0:T(8,128)(2,1)S(1)} %reshape.23.refs_0_), channel_id=1, source_target_pairs={{1,2},{2,1},{5,6},{6,5},{9,10},{10,9},{13,14},{14,13},{17,18},{18,... | collective-permute-start | bytes 1806344 | tf_op jit(solution)/shard_map/ppermute | solution.py:643
  3.4 28.4 %collective-permute-start.5 = (bf16[392,768]{1,0:T(8,128)(2,1)S(1)}, bf16[392,768]{1,0:T(8,128)(2,1)}, u32[]{:S(2)}, u32[]{:S(2)}) collective-permute-start(bf16[392,768]{1,0:T(8,128)(2,1)S(1)} %reshape.23.refs_0_), channel_id=1, source_target_pairs={{0,1},{1,0},{2,3},{3,2},{4,5},{5,4},{6,7},{7,6},{8,9},{9,8},{10,11... | collective-permute-start | bytes 1806344 | tf_op jit(solution)/shard_map/ppermute | solution.py:643
  14.0 11.6 %copy-start.3 = (bf16[1024,768]{1,0:T(8,128)(2,1)S(1)}, bf16[1024,768]{1,0:T(8,128)(2,1)}, u32[]{:S(2)}) copy-start(bf16[1024,768]{1,0:T(8,128)(2,1)} %refs_5_.1) | copy-start | bytes 4718596
  19.5 11.1 %copy-start.8 = (bf16[392,768]{1,0:T(8,128)(2,1)}, bf16[392,768]{1,0:T(8,128)(2,1)S(1)}, u32[]{:S(2)}) copy-start(bf16[392,768]{1,0:T(8,128)(2,1)S(1)} %get-tuple-element.44.act_ref.refs_3_) | copy-start | bytes 1806340
  19.5 4.6 %collective-permute-start.2 = (f32[2,1024]{1,0:T(2,128)S(1)}, f32[2,1024]{1,0:T(2,128)S(1)}, u32[]{:S(2)}, u32[]{:S(2)}) collective-permute-start(f32[2,1024]{1,0:T(2,128)S(1)} %get-tuple-element.45), channel_id=1, source_target_pairs={{0,2},{2,0},{1,3},{3,1},{4,6},{6,4},{5,7},{7,5},{8,10},{10,8},{9,1... | collective-permute-start | bytes 24584 | tf_op jit(solution)/shard_map/ppermute | solution.py:643
  19.5 5.4 %collective-permute-start.1 = (f32[2,1024]{1,0:T(2,128)S(1)}, f32[2,1024]{1,0:T(2,128)S(1)}, u32[]{:S(2)}, u32[]{:S(2)}) collective-permute-start(f32[2,1024]{1,0:T(2,128)S(1)} %get-tuple-element.45), channel_id=1, source_target_pairs={{0,3},{3,0},{1,2},{2,1},{4,7},{7,4},{5,6},{6,5},{8,11},{11,8},{9,1... | collective-permute-start | bytes 24584 | tf_op jit(solution)/shard_map/ppermute | solution.py:643
  21.9 3.7 %collective-permute-start = (f32[2,1024]{1,0:T(2,128)S(1)}, f32[2,1024]{1,0:T(2,128)S(1)}, u32[]{:S(2)}, u32[]{:S(2)}) collective-permute-start(f32[2,1024]{1,0:T(2,128)S(1)} %get-tuple-element.45), channel_id=1, source_target_pairs={{0,1},{1,0},{2,3},{3,2},{4,5},{5,4},{6,7},{7,6},{8,9},{9,8},{10,11... | collective-permute-start | bytes 24584 | tf_op jit(solution)/shard_map/ppermute | solution.py:643
  24.1 26.6 %collective-permute-start.10 = (bf16[392,768]{1,0:T(8,128)(2,1)S(1)}, bf16[392,768]{1,0:T(8,128)(2,1)S(1)}, u32[]{:S(2)}, u32[]{:S(2)}) collective-permute-start(bf16[392,768]{1,0:T(8,128)(2,1)S(1)} %reshape.23.refs_0_), channel_id=1, source_target_pairs={{0,4},{4,0},{8,12},{12,8},{16,20},{20,16},{24,28},{28,24},{1,5},{5... | collective-permute-start | bytes 1806344 | tf_op jit(solution)/shard_map/ppermute | solution.py:647
  30.7 14.6 %collective-permute-start.4 = (bf16[392,768]{1,0:T(8,128)(2,1)S(1)}, bf16[392,768]{1,0:T(8,128)(2,1)S(1)}, u32[]{:S(2)}, u32[]{:S(2)}) collective-permute-start(bf16[392,768]{1,0:T(8,128)(2,1)S(1)} %get-tuple-element.48), channel_id=1, source_target_pairs={{0,1},{1,0},{2,3},{3,2},{4,5},{5,4},{6,7},{7,6},{8,9},{9,8},{10,11... | collective-permute-start | bytes 1806344 | tf_op jit(solution)/shard_map/ppermute | solution.py:643
  31.8 9.3 %collective-permute-start.6 = (bf16[392,768]{1,0:T(8,128)(2,1)}, bf16[392,768]{1,0:T(8,128)(2,1)S(1)}, u32[]{:S(2)}, u32[]{:S(2)}) collective-permute-start(bf16[392,768]{1,0:T(8,128)(2,1)} %collective-permute-done.5.refs_1_), channel_id=1, source_target_pairs={{1,2},{2,1},{5,6},{6,5},{9,10},{10,9},{13,14},{14,13},{17,18},{18,... | collective-permute-start | bytes 1806344 | tf_op jit(solution)/shard_map/ppermute | solution.py:643
  32.6 26.1 %collective-permute-start.9 = (bf16[392,768]{1,0:T(8,128)(2,1)}, bf16[392,768]{1,0:T(8,128)(2,1)}, u32[]{:S(2)}, u32[]{:S(2)}) collective-permute-start(bf16[392,768]{1,0:T(8,128)(2,1)} %get-tuple-element.46.scaled_hbm.own_ref), channel_id=1, source_target_pairs={{0,4},{4,0},{8,12},{12,8},{16,20},{20,16},{24,28},{28,24},{1,5},{5... | collective-permute-start | bytes 1806344 | tf_op jit(solution)/shard_map/ppermute | solution.py:647
  37.8 20.8 %collective-permute-start.11 = (bf16[392,768]{1,0:T(8,128)(2,1)}, bf16[392,768]{1,0:T(8,128)(2,1)}, u32[]{:S(2)}, u32[]{:S(2)}) collective-permute-start(bf16[392,768]{1,0:T(8,128)(2,1)} %collective-permute-done.5.refs_1_), channel_id=1, source_target_pairs={{0,4},{4,0},{8,12},{12,8},{16,20},{20,16},{24,28},{28,24},{1,5},{5... | collective-permute-start | bytes 1806344 | tf_op jit(solution)/shard_map/ppermute | solution.py:647
  46.8 11.9 %collective-permute-start.12 = (bf16[392,768]{1,0:T(8,128)(2,1)}, bf16[392,768]{1,0:T(8,128)(2,1)}, u32[]{:S(2)}, u32[]{:S(2)}) collective-permute-start(bf16[392,768]{1,0:T(8,128)(2,1)} %get-tuple-element.57.refs_0_.refs_2_), channel_id=1, source_target_pairs={{0,4},{4,0},{8,12},{12,8},{16,20},{20,16},{24,28},{28,24},{1,5},{5... | collective-permute-start | bytes 1806344 | tf_op jit(solution)/shard_map/ppermute | solution.py:647
  46.8 18.7 %collective-permute-start.7 = (bf16[392,768]{1,0:T(8,128)(2,1)}, bf16[392,768]{1,0:T(8,128)(2,1)}, u32[]{:S(2)}, u32[]{:S(2)}) collective-permute-start(bf16[392,768]{1,0:T(8,128)(2,1)} %get-tuple-element.55), channel_id=1, source_target_pairs={{0,1},{1,0},{2,3},{3,2},{4,5},{5,4},{6,7},{7,6},{8,9},{9,8},{10,11... | collective-permute-start | bytes 1806344 | tf_op jit(solution)/shard_map/ppermute | solution.py:643
  51.5 14.0 %collective-permute-start.8 = (bf16[392,768]{1,0:T(8,128)(2,1)}, bf16[392,768]{1,0:T(8,128)(2,1)}, u32[]{:S(2)}, u32[]{:S(2)}) collective-permute-start(bf16[392,768]{1,0:T(8,128)(2,1)} %get-tuple-element.56), channel_id=1, source_target_pairs={{1,2},{2,1},{5,6},{6,5},{9,10},{10,9},{13,14},{14,13},{17,18},{18,... | collective-permute-start | bytes 1806344 | tf_op jit(solution)/shard_map/ppermute | solution.py:643
  58.7 21.1 %slice-start = ((s8[4718592]{0:T(1024)(128)(4,1)}), s8[4194304]{0:T(1024)(128)(4,1)S(1)}, s32[]{:S(2)}) async-start(s8[4718592]{0:T(1024)(128)(4,1)} %bitcast.16), calls=%async_computation | async-start | bytes 8388608
  65.5 14.3 %slice-start.1 = ((s8[4718592]{0:T(1024)(128)(4,1)}), s8[524288]{0:T(1024)(128)(4,1)S(1)}, s32[]{:S(2)}) async-start(s8[4718592]{0:T(1024)(128)(4,1)} %bitcast.16), calls=%async_computation.1 | async-start | bytes 1048576
  67.1 5.8 %collective-permute-start.13 = (bf16[392,768]{1,0:T(8,128)(2,1)S(1)}, bf16[392,768]{1,0:T(8,128)(2,1)S(1)}, u32[]{:S(2)}, u32[]{:S(2)}) collective-permute-start(bf16[392,768]{1,0:T(8,128)(2,1)S(1)} %get-tuple-element.70.mine.refs_0_), channel_id=1, source_target_pairs={{0,4},{4,0},{8,12},{12,8},{16,20},{20,16},{24,28},{28,24},{1,5},{5... | collective-permute-start | bytes 1806344 | tf_op jit(solution)/shard_map/ppermute | solution.py:647
  67.4 18.3 %collective-permute-start.14 = (bf16[392,768]{1,0:T(8,128)(2,1)S(1)}, bf16[392,768]{1,0:T(8,128)(2,1)S(1)}, u32[]{:S(2)}, u32[]{:S(2)}) collective-permute-start(bf16[392,768]{1,0:T(8,128)(2,1)S(1)} %get-tuple-element.73), channel_id=1, source_target_pairs={{0,1},{1,0},{2,3},{3,2},{4,5},{5,4},{6,7},{7,6},{8,9},{9,8},{10,11... | collective-permute-start | bytes 1806344 | tf_op jit(solution)/shard_map/ppermute | solution.py:643
  71.5 14.2 %collective-permute-start.15 = (bf16[392,768]{1,0:T(8,128)(2,1)S(1)}, bf16[392,768]{1,0:T(8,128)(2,1)S(1)}, u32[]{:S(2)}, u32[]{:S(2)}) collective-permute-start(bf16[392,768]{1,0:T(8,128)(2,1)S(1)} %get-tuple-element.74), channel_id=1, source_target_pairs={{1,2},{2,1},{5,6},{6,5},{9,10},{10,9},{13,14},{14,13},{17,18},{18,... | collective-permute-start | bytes 1806344 | tf_op jit(solution)/shard_map/ppermute | solution.py:643
  78.0 17.5 %collective-permute-start.19 = (bf16[2,384,384]{2,1,0:T(8,128)(2,1)}, bf16[2,384,384]{2,1,0:T(8,128)(2,1)}, u32[]{:S(2)}, u32[]{:S(2)}) collective-permute-start(bf16[2,384,384]{2,1,0:T(8,128)(2,1)} %get-tuple-element.66), channel_id=1, source_target_pairs={{0,8},{4,12},{8,0},{12,4},{16,24},{20,28},{24,16},{28,20},{1,9},{5... | collective-permute-start | bytes 1769480 | tf_op jit(solution)/shard_map/ppermute | solution.py:647
  78.9 16.7 %collective-permute-start.20 = (bf16[2,384,384]{2,1,0:T(8,128)(2,1)}, bf16[2,384,384]{2,1,0:T(8,128)(2,1)}, u32[]{:S(2)}, u32[]{:S(2)}) collective-permute-start(bf16[2,384,384]{2,1,0:T(8,128)(2,1)} %get-tuple-element.68), channel_id=1, source_target_pairs={{0,16},{4,20},{8,24},{12,28},{16,0},{20,4},{24,8},{28,12},{1,17},{... | collective-permute-start | bytes 1769480 | tf_op jit(solution)/shard_map/ppermute | solution.py:647
  79.8 11.9 %copy-start.22 = (bf16[392,768]{1,0:T(8,128)(2,1)S(1)}, bf16[392,768]{1,0:T(8,128)(2,1)}, u32[]{:S(2)}) copy-start(bf16[392,768]{1,0:T(8,128)(2,1)} %copy-done.21) | copy-start | bytes 1806340
  85.7 9.8 %copy-start.24 = (bf16[2,384,384]{2,1,0:T(8,128)(2,1)S(1)}, bf16[2,384,384]{2,1,0:T(8,128)(2,1)}, u32[]{:S(2)}) copy-start(bf16[2,384,384]{2,1,0:T(8,128)(2,1)} %copy-done.23) | copy-start | bytes 1769476
  85.7 18.4 %collective-permute-start.18 = (f32[2,1024]{1,0:T(2,128)S(1)}, f32[2,1024]{1,0:T(2,128)S(1)}, u32[]{:S(2)}, u32[]{:S(2)}) collective-permute-start(f32[2,1024]{1,0:T(2,128)S(1)} %get-tuple-element.78), channel_id=1, source_target_pairs={{0,2},{2,0},{1,3},{3,1},{4,6},{6,4},{5,7},{7,5},{8,10},{10,8},{9,1... | collective-permute-start | bytes 24584 | tf_op jit(solution)/shard_map/ppermute | solution.py:643
  89.3 14.8 %collective-permute-start.17 = (f32[2,1024]{1,0:T(2,128)S(1)}, f32[2,1024]{1,0:T(2,128)S(1)}, u32[]{:S(2)}, u32[]{:S(2)}) collective-permute-start(f32[2,1024]{1,0:T(2,128)S(1)} %get-tuple-element.78), channel_id=1, source_target_pairs={{0,3},{3,0},{1,2},{2,1},{4,7},{7,4},{5,6},{6,5},{8,11},{11,8},{9,1... | collective-permute-start | bytes 24584 | tf_op jit(solution)/shard_map/ppermute | solution.py:643
  91.7 12.4 %collective-permute-start.16 = (f32[2,1024]{1,0:T(2,128)S(1)}, f32[2,1024]{1,0:T(2,128)S(1)}, u32[]{:S(2)}, u32[]{:S(2)}) collective-permute-start(f32[2,1024]{1,0:T(2,128)S(1)} %get-tuple-element.78), channel_id=1, source_target_pairs={{0,1},{1,0},{2,3},{3,2},{4,5},{5,4},{6,7},{7,6},{8,9},{9,8},{10,11... | collective-permute-start | bytes 24584 | tf_op jit(solution)/shard_map/ppermute | solution.py:643
  92.8 11.3 %copy-start.15 = (f32[392,768]{1,0:T(8,128)S(1)}, f32[392,768]{1,0:T(8,128)}, u32[]{:S(2)}) copy-start(f32[392,768]{1,0:T(8,128)} %copy-done.14) | copy-start | bytes 3612676
  95.5 8.6 %copy-start.17 = (bf16[3,3,64,768]{3,2,1,0:T(8,128)(2,1)S(1)}, bf16[3,3,64,768]{3,2,1,0:T(8,128)(2,1)}, u32[]{:S(2)}) copy-start(bf16[3,3,64,768]{3,2,1,0:T(8,128)(2,1)} %w_hbm.7) | copy-start | bytes 2654212
  101.1 9.0 %collective-permute-start.21 = (bf16[384,384]{1,0:T(8,128)(2,1)}, bf16[384,384]{1,0:T(8,128)(2,1)S(1)}, u32[]{:S(2)}, u32[]{:S(2)}) collective-permute-start(bf16[384,384]{1,0:T(8,128)(2,1)} %get-tuple-element.83), channel_id=1, source_target_pairs={{0,16},{4,20},{8,24},{12,28},{16,0},{20,4},{24,8},{28,12},{1,17},{... | collective-permute-start | bytes 884744 | tf_op jit(solution)/shard_map/ppermute | solution.py:647
  102.6 8.1 %collective-permute-start.22 = (bf16[384,384]{1,0:T(8,128)(2,1)}, bf16[384,384]{1,0:T(8,128)(2,1)}, u32[]{:S(2)}, u32[]{:S(2)}) collective-permute-start(bf16[384,384]{1,0:T(8,128)(2,1)} %get-tuple-element.79), channel_id=1, source_target_pairs={{0,8},{4,12},{8,0},{12,4},{16,24},{20,28},{24,16},{28,20},{1,9},{5... | collective-permute-start | bytes 884744 | tf_op jit(solution)/shard_map/ppermute | solution.py:647
  (27 other events, 95.1 us)

commit v3 on v2

v3 whole, which is shorter than its diff:
```python
import functools

import jax
import jax.numpy as jnp
import numpy as np
from jax import lax
from jax.experimental import pallas as pl
from jax.experimental.pallas import tpu as pltpu
from jax.sharding import PartitionSpec as P

LANES = 256
F32 = jnp.float32
BF16 = jnp.bfloat16
HIGHEST = lax.Precision.HIGHEST


def params(mebibytes=20):
    return pltpu.CompilerParams(vmem_limit_bytes=mebibytes * 1024 * 1024)


SCALE = 0.3
CONV_MIB = 62


def cost(micros):
    return pl.CostEstimate(
        flops=int(micros * SCALE * 1.15e9), bytes_accessed=1, transcendentals=0
    )


def exact_dot(values, weight, dims):
    high = values.astype(BF16).astype(F32)
    rest = values - high
    middle = rest.astype(BF16).astype(F32)
    count = values.shape[0]
    terms = [high, middle, rest - middle, jnp.zeros_like(values)]
    stacked = jnp.concatenate(terms, axis=0).astype(BF16)
    out = lax.dot_general(stacked, weight, (dims, ((), ())), preferred_element_type=F32)
    return out[:count] + out[count : 2 * count] + out[2 * count : 3 * count]


def silu_grad(values):
    logistic = jax.nn.sigmoid(values)
    return logistic * (1.0 + values * (1.0 - logistic))


def to_cells(images):
    return jnp.transpose(images, (1, 2, 0, 3))


def from_cells(cells):
    return jnp.transpose(cells, (2, 0, 1, 3))


def as_rows(values):
    return values.reshape(-1, values.shape[-1])


def whole(shape):
    return pl.BlockSpec(shape, lambda *_: (0,) * len(shape))


def per_row(values, rows):
    tiled = jnp.concatenate([values] * (8 // values.shape[0]), axis=0)
    return jnp.broadcast_to(tiled[None], (rows // 8, 8, values.shape[1])).reshape(rows, -1)


def image_sum(values, images):
    folded = values.reshape(-1, 8, values.shape[1]).sum(axis=0)
    total = folded[:images]
    for start in range(images, 8, images):
        total = total + folded[start : start + images]
    return total


def convolve(rows_ref, pad_ref, weight_ref, height, width, images, turn):
    line, unit = width * images, 16 * images
    group = weight_ref.shape[2]
    pad_ref[...] = jnp.zeros_like(pad_ref)
    for h in range(height):
        pad_ref[pl.ds(8 + (h + 1) * unit + images, line), :] = rows_ref[pl.ds(h * line, line), :]
    row_group = lax.broadcasted_iota(jnp.int32, (LANES, LANES), 0) // group
    col_group = lax.broadcasted_iota(jnp.int32, (LANES, LANES), 1) // group
    mask = (row_group == col_group).astype(F32).astype(BF16)
    total = None
    for dw in range(3):
        shifted = pad_ref[pl.ds(8 + images * (dw - 1), (height + 2) * unit), :].astype(BF16)
        for dh in range(3):
            tap = weight_ref[2 - dh, 2 - dw] if turn else weight_ref[dh, dw]
            dense = jnp.concatenate([tap] * (LANES // group), axis=0) * mask
            part = lax.dot_general(
                shifted[dh * unit : (dh + height) * unit],
                dense,
                (((1,), (1 if turn else 0,)), ((), ())),
                preferred_element_type=F32,
            )
            total = part if total is None else total + part
    pad_ref[pl.ds(0, height * unit), :] = total
    for h in range(height):
        rows_ref[pl.ds(h * line, line), :] = pad_ref[pl.ds(h * unit + images, line), :]


HBM = pl.BlockSpec(memory_space=pltpu.HBM)
HERE = pl.BlockSpec(memory_space=pltpu.VMEM)


def lanes_of(i):
    return pl.ds(i * LANES, LANES)


def fetch(source, target, sem):
    copy = pltpu.make_async_copy(source, target, sem)
    copy.start()
    return copy


def conv_forward_body(
    x_hbm,
    w_hbm,
    down_hbm,
    *refs,
    height,
    width,
    images,
):
    conv_hbm, act_ref, pre_ref, x_buf, w_buf, down_buf, conv_buf, rows_ref, pad_ref, sems = refs
    blocks = act_ref.shape[1] // LANES
    copies = [fetch(x_hbm, x_buf, sems.at[0])]
    for i in range(blocks):
        part = w_hbm.at[:, :, :, lanes_of(i)]
        copies.append(fetch(part, w_buf.at[i], sems.at[2 + i]))
    copies[0].wait()
    means = []
    for i in range(blocks):
        rows_ref[...] = as_rows(x_buf[:, :, :, lanes_of(i)]).astype(F32)
        copies[1 + i].wait()
        if i == 0:
            last = [fetch(down_hbm, down_buf, sems.at[1])]
        convolve(rows_ref, pad_ref, w_buf.at[i], height, width, images, False)
        conv = rows_ref[...]
        conv_buf[i] = conv
        last.append(fetch(conv_buf.at[i], conv_hbm.at[:, lanes_of(i)], sems.at[2 + blocks + i]))
        act = (conv * jax.nn.sigmoid(conv)).astype(BF16)
        act_ref[:, lanes_of(i)] = act
        means.append(image_sum(act.astype(F32), images) / (height * width))
    last[0].wait()
    pre_ref[...] = exact_dot(jnp.concatenate(means, axis=1), down_buf[...], ((1,), (0,)))
    for copy in last[1:]:
        copy.wait()


def conv_forward(cells, weight, down):
    height, width, images, channels = cells.shape
    count, inner = height * width * images, down.shape[1]
    blocks = channels // LANES
    return pl.pallas_call(
        functools.partial(conv_forward_body, height=height, width=width, images=images),
        in_specs=[HBM] * 3,
        out_specs=[HBM, HERE, HERE],
        out_shape=[
            jax.ShapeDtypeStruct((count, channels), F32),
            jax.ShapeDtypeStruct((count, channels), BF16),
            jax.ShapeDtypeStruct((images, inner), F32),
        ],
        scratch_shapes=[
            pltpu.VMEM(cells.shape, BF16),
            pltpu.VMEM((blocks, 3, 3, weight.shape[2], LANES), BF16),
            pltpu.VMEM(down.shape, BF16),
            pltpu.VMEM((blocks, count, LANES), F32),
            pltpu.VMEM((count, LANES), F32),
            pltpu.VMEM((16 + (height + 2) * 16 * images, LANES), F32),
            pltpu.SemaphoreType.DMA((2 + 2 * blocks,)),
        ],
        compiler_params=params(CONV_MIB),
        cost_estimate=cost(3),
        name="conv_forward",
    )(cells, weight, down)


def conv_backward_body(
    grad_ref,
    gate_ref,
    sum_ref,
    pre_ref,
    down_hbm,
    conv_ref,
    w_hbm,
    out_hbm,
    down_buf,
    w_buf,
    out_buf,
    rows_ref,
    pad_ref,
    sems,
    *,
    height,
    width,
    images,
):
    count, channels = grad_ref.shape
    blocks = channels // LANES
    down_copy = fetch(down_hbm, down_buf, sems.at[0])
    copies = []
    for i in range(blocks):
        part = w_hbm.at[:, :, :, lanes_of(i)]
        copies.append(fetch(part, w_buf.at[i], sems.at[1 + i]))
    excite_grad = sum_ref[...] * silu_grad(pre_ref[...])
    down_copy.wait()
    squeeze_grad = exact_dot(excite_grad, down_buf[...], ((1,), (1,))) / (height * width)
    outs = []
    for i in range(blocks):
        gate = per_row(gate_ref[:, lanes_of(i)], count)
        squeeze = per_row(squeeze_grad[:, i * LANES : (i + 1) * LANES], count)
        act_grad = grad_ref[:, lanes_of(i)] * gate + squeeze
        rows_ref[...] = act_grad * silu_grad(conv_ref[:, lanes_of(i)])
        copies[i].wait()
        convolve(rows_ref, pad_ref, w_buf.at[i], height, width, images, True)
        part = rows_ref[...].astype(BF16).reshape(height, width, images, LANES)
        out_buf[:, :, :, lanes_of(i)] = part
        target = out_hbm.at[:, :, :, lanes_of(i)]
        outs.append(fetch(out_buf.at[:, :, :, lanes_of(i)], target, sems.at[1 + blocks + i]))
    for out in outs:
        out.wait()


def conv_backward(scaled_grad, gating, excite_sum, excite_pre, down, convolved, weight, shape):
    height, width, images, channels = shape
    count = convolved.shape[0]
    blocks = channels // LANES
    return pl.pallas_call(
        functools.partial(conv_backward_body, height=height, width=width, images=images),
        in_specs=[HERE, HERE, HERE, HERE, HBM, HERE, HBM],
        out_specs=HBM,
        out_shape=jax.ShapeDtypeStruct(shape, BF16),
        scratch_shapes=[
            pltpu.VMEM(down.shape, BF16),
            pltpu.VMEM((blocks, 3, 3, weight.shape[2], LANES), BF16),
            pltpu.VMEM(shape, BF16),
            pltpu.VMEM((count, LANES), F32),
            pltpu.VMEM((16 + (height + 2) * 16 * images, LANES), F32),
            pltpu.SemaphoreType.DMA((1 + 2 * blocks,)),
        ],
        compiler_params=params(),
        cost_estimate=cost(3),
        name="conv_backward",
    )(scaled_grad, gating, excite_sum, excite_pre, down, convolved, weight)


def block_of(weight_ref, block, width):
    return weight_ref.at[:, pl.ds(pl.multiple_of(block * width, width), width)]


def scale_body(
    role_ref,
    act_ref,
    pre_ref,
    up_ref,
    w_ref,
    middle_hbm,
    gate_ref,
    scaled_hbm,
    far_hbm,
    send_hbm,
    middle_buf,
    send_buf,
    scaled_buf,
    far_buf,
    sems,
):
    middle_copy = fetch(middle_hbm, middle_buf, sems.at[0])
    pre = pre_ref[...]
    excited = pre * jax.nn.sigmoid(pre)
    gate_ref[...] = jax.nn.sigmoid(exact_dot(excited, up_ref[...], ((1,), (0,))))
    gate = per_row(gate_ref[...], act_ref.shape[0])
    scaled_buf[...] = (act_ref[...].astype(F32) * gate).astype(BF16)
    far = jnp.dot(scaled_buf[...], w_ref[...], preferred_element_type=F32).astype(BF16)
    far_buf[...] = far
    middle_copy.wait()

    @pl.when(role_ref[4] == 1)
    def _():
        send_buf[...] = far

    @pl.when(role_ref[4] == 0)
    def _():
        send_buf[...] = as_rows(middle_buf[...])

    sent = [
        fetch(send_buf, send_hbm, sems.at[1]),
        fetch(scaled_buf, scaled_hbm, sems.at[2]),
        fetch(far_buf, far_hbm, sems.at[3]),
    ]
    for copy in sent:
        copy.wait()


def scale(role, act, excite_pre, up, w_far, middle):
    count, channels = act.shape
    gates = (excite_pre.shape[0], channels)
    array = jax.ShapeDtypeStruct((count, channels), BF16)
    return pl.pallas_call(
        scale_body,
        in_specs=[pl.BlockSpec(memory_space=pltpu.SMEM), HERE, HERE, HERE, HERE, HBM],
        out_specs=[HERE, HBM, HBM, HBM],
        out_shape=[jax.ShapeDtypeStruct(gates, F32)] + [array] * 3,
        scratch_shapes=[
            pltpu.VMEM(middle.shape, BF16),
            pltpu.VMEM((count, channels), BF16),
            pltpu.VMEM((count, channels), BF16),
            pltpu.VMEM((count, channels), BF16),
            pltpu.SemaphoreType.DMA((4,)),
        ],
        compiler_params=params(),
        cost_estimate=cost(3),
        name="scale",
    )(role, act, excite_pre, up, w_far, middle)


def project_body(order_ref, scaled_hbm, w_hbm, *refs, parts):
    outs, (scaled_buf, w_buf, out_buf, sems) = refs[:parts], refs[parts:]
    channels = scaled_buf.shape[1]
    scaled_copy = fetch(scaled_hbm, scaled_buf, sems.at[0])
    copies = [
        fetch(block_of(w_hbm, order_ref[k], channels), w_buf.at[k], sems.at[1 + k])
        for k in range(parts)
    ]
    scaled_copy.wait()
    sent = []
    for k in range(parts):
        copies[k].wait()
        part = jnp.dot(scaled_buf[...], w_buf[k], preferred_element_type=F32)
        out_buf[k] = part.astype(BF16)
        sent.append(fetch(out_buf.at[k], outs[k], sems.at[1 + parts + k]))
    for copy in sent:
        copy.wait()


def project(order, parts, scaled, weight):
    count, channels = scaled.shape
    array = jax.ShapeDtypeStruct((count, channels), BF16)
    return pl.pallas_call(
        functools.partial(project_body, parts=parts),
        in_specs=[pl.BlockSpec(memory_space=pltpu.SMEM), HBM, HBM],
        out_specs=[HBM] * parts,
        out_shape=[array] * parts,
        scratch_shapes=[
            pltpu.VMEM((count, channels), BF16),
            pltpu.VMEM((parts, channels, channels), BF16),
            pltpu.VMEM((parts, count, channels), BF16),
            pltpu.SemaphoreType.DMA((1 + 2 * parts,)),
        ],
        compiler_params=params(),
        cost_estimate=cost(3),
        name="project",
    )(order, scaled, weight)


def second_body(role_ref, came, held, far, p_fourth, p_third, third, to_far, send):
    at_end = role_ref[4] == 1
    to_far[...] = (p_fourth[...].astype(F32) + came[...].astype(F32)).astype(BF16)

    @pl.when(at_end)
    def _():
        third[...] = came[...]
        send[...] = p_third[...]

    @pl.when(jnp.logical_not(at_end))
    def _():
        third[...] = held[...]
        send[...] = as_rows(far[...])


def third_body(role_ref, came, crossed, held, p_outer, p_third, fourth, to_mid, send, give):
    at_end = role_ref[4] == 1
    to_mid[...] = (p_third[...].astype(F32) + came[...].astype(F32)).astype(BF16)

    @pl.when(at_end)
    def _():
        fourth[...] = came[...]
        send[...] = p_outer[...]

    @pl.when(jnp.logical_not(at_end))
    def _():
        fourth[...] = held[...]
        send[...] = (p_outer[...].astype(F32) + crossed[...].astype(F32)).astype(BF16)

    half = give.shape[1]
    give[...] = fourth[:, pl.ds(pl.multiple_of((1 - role_ref[5]) * half, half), half)]


def fourth_body(role_ref, p_own, came, crossed, total):
    at_end = role_ref[4] == 1
    near = p_own[...].astype(F32) + came[...].astype(F32)

    @pl.when(at_end)
    def _():
        total[...] = near.astype(BF16).reshape(total.shape)

    @pl.when(jnp.logical_not(at_end))
    def _():
        total[...] = (near + crossed[...].astype(F32)).astype(BF16).reshape(total.shape)


def between(body, extents, role, *arrays):
    return pl.pallas_call(
        body,
        grid=(1,),
        in_specs=[pl.BlockSpec(memory_space=pltpu.SMEM)] + [whole(a.shape) for a in arrays],
        out_specs=[whole(extent) for extent in extents],
        out_shape=[jax.ShapeDtypeStruct(extent, BF16) for extent in extents],
        compiler_params=params(),
        cost_estimate=cost(0.02),
        name="between",
    )(role, *arrays)


def input_grad_body(role_ref, *refs, first, pieces, started, last, images):
    piece_refs, w_hbm, refs = refs[:pieces], refs[pieces], refs[pieces + 1 :]
    if started:
        start_ref, refs = refs[0], refs[1:]
    if last:
        act_ref, gate_ref, up_hbm, out_ref, excite_ref, w_buf, sems, up_buf = refs[:8]
    else:
        out_ref, w_buf, sems = refs[:3]
    piece_bufs = refs[-pieces:]
    width = out_ref.shape[1]
    copies = []
    for k, piece_ref in enumerate(piece_refs):
        block = block_of(w_hbm, role_ref[first + k], width)
        copies.append(
            (
                fetch(piece_ref, piece_bufs[k], sems.at[2 * k]),
                fetch(block, w_buf.at[k], sems.at[2 * k + 1]),
            )
        )
    if last:
        up_copy = fetch(up_hbm, up_buf, sems.at[2 * pieces])
    for k in range(pieces):
        for copy in copies[k]:
            copy.wait()
        part = lax.dot_general(
            as_rows(piece_bufs[k][...]),
            w_buf[k],
            (((1,), (1,)), ((), ())),
            preferred_element_type=F32,
        )
        if k > 0:
            part = out_ref[...] + part
        elif started:
            part = start_ref[...] + part
        out_ref[...] = part
    if last:
        gating = gate_ref[...]
        gate_grad = image_sum(out_ref[...] * act_ref[...].astype(F32), images)
        pre_grad = gate_grad * gating * (1.0 - gating)
        up_copy.wait()
        excite_ref[...] = exact_dot(pre_grad, up_buf[...], ((1,), (1,)))


def input_grad(role, first, pieces, weight, start=None, act=None, gating=None, up=None):
    channels = weight.shape[0]
    count = pieces[0].size // channels
    images = 1 if gating is None else gating.shape[0]
    started, last = start is not None, act is not None
    operands = list(pieces) + [weight]
    in_specs = [pl.BlockSpec(memory_space=pltpu.SMEM)] + [HBM] * (len(pieces) + 1)
    out_shape = [jax.ShapeDtypeStruct((count, channels), F32)]
    scratch = [
        pltpu.VMEM((len(pieces), channels, channels), BF16),
        pltpu.SemaphoreType.DMA((2 * len(pieces) + 1,)),
    ]
    if started:
        operands.append(start)
        in_specs.append(HERE)
    if last:
        operands += [act, gating, up]
        in_specs += [HERE, HERE, HBM]
        out_shape.append(jax.ShapeDtypeStruct((images, up.shape[0]), F32))
        scratch.append(pltpu.VMEM(up.shape, BF16))
    scratch += [pltpu.VMEM(piece.shape, BF16) for piece in pieces]
    return pl.pallas_call(
        functools.partial(
            input_grad_body,
            first=first,
            pieces=len(pieces),
            started=started,
            last=last,
            images=images,
        ),
        in_specs=in_specs,
        out_specs=[HERE] * len(out_shape),
        out_shape=out_shape,
        scratch_shapes=scratch,
        compiler_params=params(),
        cost_estimate=cost(10 if last else 0.02),
        name="input_grad_last" if last else "input_grad",
    )(role, *operands)


def place_block(total, block, x, y, x_send, x_keep, y_send, y_keep):
    half = total.shape[0] // 2
    to_x, to_y = block % 2, block // 2

    @pl.when(to_x != x)
    def _():
        x_send[to_y] = total[:half]

    @pl.when(to_x == x)
    def _():
        x_keep[to_y] = total[:half]

    @pl.when(to_y != y)
    def _():
        y_send[to_x] = total[half:]

    @pl.when(to_y == y)
    def _():
        y_keep[to_x] = total[half:]


def weight_grad_body(place_ref, own_ref, other_ref, *refs, pieces):
    mine, theirs, outs = refs[:pieces], refs[pieces : 2 * pieces], refs[2 * pieces :]
    x, y = place_ref[6], place_ref[7]
    own, other = own_ref[...].T, other_ref[...].T
    for k in range(pieces):
        total = jnp.dot(own, as_rows(mine[k][...]), preferred_element_type=F32)
        total += jnp.dot(other, as_rows(theirs[k][...]), preferred_element_type=F32)
        total = total.astype(BF16)
        if pieces > 1:
            place_block(total, place_ref[k], x, y, *outs)
        else:
            half = total.shape[0] // 2
            outs[0][...] = total[:half]
            outs[1][...] = total[half:]
    if pieces > 1:
        place_block(jnp.zeros_like(total), place_ref[pieces], x, y, *outs)


def weight_grad(place, own, other, mine, theirs):
    count, channels = own.shape
    columns = channels // 2
    pieces = len(mine)

    def part(array):
        if array.shape[-1] == columns:
            return whole(array.shape)
        lead = array.shape[:-1]
        return pl.BlockSpec((*lead, columns), lambda i, place: (0,) * len(lead) + (place[5],))

    extent = (channels // 2, columns)
    if pieces > 1:
        extent = (2, *extent)
    outs = 4 if pieces > 1 else 2
    return pl.pallas_call(
        functools.partial(weight_grad_body, pieces=pieces),
        grid_spec=pltpu.PrefetchScalarGridSpec(
            num_scalar_prefetch=1,
            grid=(1,),
            in_specs=[whole(own.shape)] * 2 + [part(piece) for piece in (*mine, *theirs)],
            out_specs=[whole(extent)] * outs,
        ),
        out_shape=[jax.ShapeDtypeStruct(extent, BF16)] * outs,
        compiler_params=params(),
        cost_estimate=cost(2 * pieces if pieces > 1 else 0.02),
        name="weight_grad" if pieces > 1 else "weight_grad_more",
    )(place, own, other, *mine, *theirs)


def merge_body(place_ref, *refs):
    x_keep, x_came, y_keep, y_came, upper, upper_came, lower, lower_came = refs[:8]
    top, to_y, bottom, to_x = refs[8:]
    block, x, y = place_ref[3], place_ref[6], place_ref[7]
    to_bx, to_by = block % 2 == x, block // 2 == y

    def both(a, b):
        return a[...].astype(F32) + b[...].astype(F32)

    for keep, came, index, more, more_came, here, there, stay, leave in (
        (x_keep, x_came, y, upper, upper_came, to_bx, to_by, top, to_y),
        (y_keep, y_came, x, lower, lower_came, to_by, to_bx, bottom, to_x),
    ):
        extra = jnp.where(here, both(more, more_came), 0.0)
        stay[...] = both(keep.at[index], came.at[index]) + jnp.where(there, extra, 0.0)
        rest = both(keep.at[1 - index], came.at[1 - index]) + jnp.where(there, 0.0, extra)
        leave[...] = rest.astype(BF16)


def merge(place, *arrays):
    rows, columns = arrays[0].shape[1:]
    pair = pl.BlockSpec((2, rows, columns), lambda i, place: (0, 0, 0))
    one = pl.BlockSpec((rows, columns), lambda i, place: (0, 0))
    kept = jax.ShapeDtypeStruct((rows, columns), F32)
    sent = jax.ShapeDtypeStruct((rows, columns), BF16)
    return pl.pallas_call(
        merge_body,
        grid_spec=pltpu.PrefetchScalarGridSpec(
            num_scalar_prefetch=1, grid=(1,), in_specs=[pair] * 4 + [one] * 4, out_specs=[one] * 4
        ),
        out_shape=[kept, sent, kept, sent],
        compiler_params=params(),
        cost_estimate=cost(2),
        name="merge",
    )(place, *arrays)


def finish_body(top, top_came, bottom, bottom_came, out):
    rows = top.shape[0]
    out[:rows] = top[...] + top_came[...].astype(F32)
    out[rows:] = bottom[...] + bottom_came[...].astype(F32)


def finish(top, top_came, bottom, bottom_came):
    rows, columns = top.shape
    one = pl.BlockSpec((rows, columns), lambda i: (0, 0))
    return pl.pallas_call(
        finish_body,
        grid=(1,),
        in_specs=[one] * 4,
        out_specs=pl.BlockSpec((2 * rows, columns), lambda i: (0, 0)),
        out_shape=jax.ShapeDtypeStruct((2 * rows, columns), F32),
        compiler_params=params(),
        cost_estimate=cost(2),
        name="finish",
    )(top, top_came, bottom, bottom_came)


OUTER = [(0, 1), (1, 0), (2, 3), (3, 2)]
INWARD = [(0, 1), (3, 2)]
OUTWARD = [(1, 0), (2, 3)]
MIDDLE = [(1, 2), (2, 1)]
OVER = [(0, 2), (2, 0), (1, 3), (3, 1)]
CROSS = [(0, 3), (3, 0), (1, 2), (2, 1)]


def along_chan(array, pairs):
    return lax.ppermute(array, "chan", pairs)


def along_dp(array, bit):
    return lax.ppermute(array, "dp", [(i, i ^ bit) for i in range(8)])


def small_sum(values):
    near, across, over = (along_chan(values, pairs) for pairs in (OUTER, CROSS, OVER))
    return (values + near) + (across + over)


def after(array, *others):
    return lax.optimization_barrier((array, *others))[0]


def places():
    rows = []
    for place in range(8):
        for z in range(4):
            order = [[0, 1, 2, 3], [1, 0, 2, 3], [2, 3, 1, 0], [3, 2, 1, 0]][z]
            rows.append(order + [int(z in (0, 3)), place % 2, place // 2 % 2, place // 4])
    return np.array(rows, np.int32)


def on_line(hidden, conv_weight, se_down, se_up, proj_weight, grad_out):
    hidden, own = to_cells(hidden), to_cells(grad_out)
    shape = own.shape
    channels = shape[3]
    extent = (own.size // channels, channels)
    role = jnp.asarray(places())[lax.axis_index("dp") * 4 + lax.axis_index("chan")]

    outer = along_chan(own, OUTER)
    middle = along_chan(own, MIDDLE)
    w_far = lax.dynamic_slice_in_dim(proj_weight, role[3] * channels, channels, axis=1)
    convolved, act, terms = conv_forward(after(hidden, w_far), conv_weight, se_down)
    excite_pre = small_sum(terms)

    gating, scaled, p_fourth, send = scale(role, act, excite_pre, se_up, w_far, middle)
    came = along_chan(send, OUTER)
    far = along_chan(after(outer, send), MIDDLE)
    other = along_dp(scaled, 1)
    theirs = [along_dp(piece, 1) for piece in (own, outer)]
    p_own, p_outer, p_third = project(role, 3, scaled, proj_weight)
    (begun,) = input_grad(role, 0, [after(own, p_own), outer], proj_weight)

    far, came = lax.optimization_barrier((far, came, begun))[:2]
    third, to_far, send = between(
        second_body, [extent] * 3, role, came, send, far, p_fourth, p_third
    )
    crossed = along_chan(to_far, MIDDLE)
    came = along_chan(send, OUTER)
    theirs.append(along_dp(third, 1))
    pieces = [own, outer, third]
    x_send, x_keep, y_send, y_keep = weight_grad(role, scaled, other, pieces, theirs)
    x_came, y_came = along_dp(x_send, 2), along_dp(y_send, 4)
    (begun,) = input_grad(role, 2, [after(third, y_send)], proj_weight, begun)

    crossed, came = lax.optimization_barrier((crossed, came, begun))[:2]
    half = (extent[0], channels // 2)
    fourth, to_mid, send, give = between(
        third_body, [extent] * 3 + [half], role, came, crossed, send, p_outer, p_third
    )
    crossed = along_chan(to_mid, MIDDLE)
    came = along_chan(send, OUTER)
    upper, lower = weight_grad(role, scaled, other, [fourth], [along_dp(give, 1)])
    upper_came, lower_came = along_dp(upper, 2), along_dp(lower, 4)
    fourth, x_came, y_came = lax.optimization_barrier((fourth, x_came, y_came, lower))[:3]
    scaled_grad, terms = input_grad(
        role, 3, [fourth], proj_weight, begun, act, gating, se_up
    )
    terms, came, crossed = lax.optimization_barrier((terms, came, crossed))
    excite_sum = small_sum(terms)

    top, to_y, bottom, to_x = merge(
        role, x_keep, x_came, y_keep, y_came, upper, upper_came, lower, lower_came
    )
    (projected,) = between(fourth_body, [shape], role, p_own, came, crossed)
    excite_sum = after(excite_sum, to_x, projected)
    grad_hidden = conv_backward(
        scaled_grad, gating, excite_sum, excite_pre, se_down, convolved, conv_weight, shape
    )
    grad_proj = finish(top, along_dp(to_y, 4), bottom, along_dp(to_x, 2))
    return (from_cells(projected), from_cells(grad_hidden), grad_proj)


def on_any(hidden, conv_weight, se_down, se_up, proj_weight, grad_out):
    hidden, pieces = to_cells(hidden), to_cells(grad_out)
    shape = hidden.shape
    images = shape[2]
    convolved, act, terms = conv_forward(hidden, conv_weight, se_down)
    excite_pre = lax.psum(terms, "chan")
    gating = jax.nn.sigmoid(jnp.dot(jax.nn.silu(excite_pre), se_up.astype(F32), precision=HIGHEST))
    act_float = act.astype(F32)
    scaled = (act_float * per_row(gating, act.shape[0])).astype(BF16)
    terms = jnp.dot(scaled, proj_weight, preferred_element_type=F32).astype(BF16)
    projected = lax.psum_scatter(terms, "chan", scatter_dimension=1, tiled=True)
    pieces = lax.all_gather(as_rows(pieces), "chan", axis=1, tiled=True)
    scaled_grad = lax.dot_general(
        pieces, proj_weight, (((1,), (1,)), ((), ())), preferred_element_type=F32
    )
    terms = lax.dot_general(scaled, pieces, (((0,), (0,)), ((), ())), preferred_element_type=F32)
    grad_proj = lax.psum_scatter(terms, "dp", scatter_dimension=1, tiled=True)
    gate_grad = image_sum(scaled_grad * act_float, images)
    pre_grad = gate_grad * gating * (1.0 - gating)
    excite_sum = lax.psum(jnp.dot(pre_grad, se_up.astype(F32).T, precision=HIGHEST), "chan")
    grad_hidden = conv_backward(
        scaled_grad, gating, excite_sum, excite_pre, se_down, convolved, conv_weight, shape
    )
    return (from_cells(projected.reshape(shape)), from_cells(grad_hidden), grad_proj)


def solution(mesh):
    in_specs = (
        P("dp", None, None, "chan"),
        P(None, None, None, "chan"),
        P("chan", None),
        P(None, "chan"),
        P("chan", None),
        P("dp", None, None, "chan"),
    )
    out_specs = (P("dp", None, None, "chan"), P("dp", None, None, "chan"), P("chan", "dp"))
    on_device = on_line if (mesh.shape["dp"], mesh.shape["chan"]) == (8, 4) else on_any
    return jax.shard_map(
        on_device, mesh=mesh, in_specs=in_specs, out_specs=out_specs, check_vma=False
    )
```

time: 114 us -> 100 us (0.88)
  local copies, waits for them, and re-layouts: 23.2 us -> 7.47 us
  Pallas kernels: 43.1 us -> 36.7 us
  waiting for transfers between devices: 9.73 us -> 16 us
  starting transfers between devices: 33.6 us -> 37.2 us
  other arithmetic: 2.04 us -> 0.72 us
    unnamed x72 -> x22, local copies, waits for them, and re-layouts: 15 us -> 4.85 us
    ppermute x14, waiting for transfers between devices: 9.09 us -> 16 us  [along_chan(): return lax.ppermute(array, 'chan', pairs)]
    reshape x4 -> x0, local copies, waits for them, and re-layouts: 6.82 us -> none  [the longest x2 3.71 us: from_rows(): rows.reshape(height, width, count, channels)]
    pallas_call x5, Pallas kernels: 19.1 us -> 12.8 us  [the longest x3 6.91 us: input_grad(): pl.pallas_call(functools.partial(input_grad_body, first=first, pieces=len...]
    ppermute x9 -> x11, starting transfers between devices: 5.56 us -> 9.95 us  [along_dp(): return lax.ppermute(array, 'dp', [(i, i ^ bit) for i in range(8)])]
    dynamic_slice x0 -> x2, local copies, waits for them, and re-layouts: none -> 2.04 us  [the longest x1 1.35 us: on_line(): lax.dynamic_slice_in_dim(proj_weight, role[3] * channels, channels, axis=1)]
    pallas_call x1, Pallas kernels: 4.5 us -> 6.39 us  [conv_forward(): pl.pallas_call(functools.partial(conv_forward_body, height=height, width=...]
    pallas_call x1, Pallas kernels: 2.69 us -> 1.12 us  [merge(): pl.pallas_call(merge_body, grid_spec=pltpu.PrefetchScalarGridSpec(num_sca...]
  transfers between devices with their start and end apart: 23 -> 25, of which waited for: 6 -> 6; matrix products, arithmetic and copies ran while one was open for 7% -> 3% of each run, Pallas kernels for 35% -> 36%
where the time goes in v3:
time: 100 us; the launch traced here: 99.7 us
  starting transfers between devices  37.2 us (37%)
  Pallas kernels  36.7 us (37%)
  waiting for transfers between devices  16 us (16%)
  local copies, waits for them, and re-layouts  7.47 us (7%)
  between operations  1.59 us (2%)
    ppermute x14, starting transfers between devices, along_chan(): return lax.ppermute(array, 'chan', pairs)  27.3 us
    ppermute x14, waiting for transfers between devices, along_chan(): return lax.ppermute(array, 'chan', pairs)  16 us
    ppermute x11, starting transfers between devices, along_dp(): return lax.ppermute(array, 'dp', [(i, i ^ bit) for i in range(8)])  9.95 us
    pallas_call x3, Pallas kernels, input_grad(): pl.pallas_call(functools.partial(input_grad_body, first=first, pieces=len...  6.91 us
    pallas_call x1, Pallas kernels, conv_forward(): pl.pallas_call(functools.partial(conv_forward_body, height=height, width=...  6.39 us
    pallas_call x2, Pallas kernels, weight_grad(): pl.pallas_call(functools.partial(weight_grad_body, pieces=pieces), grid_s...  5.85 us
    pallas_call x1, Pallas kernels, conv_backward(): pl.pallas_call(functools.partial(conv_backward_body, height=height, width...  5.3 us
    unnamed x22, local copies, waits for them, and re-layouts  4.85 us
  transfers between devices with their start and end apart: 25, of which 6 were waited for; matrix products, arithmetic and copies ran while one was open for 3% of the time, Pallas kernels for 36%

profile of v3, /device:TPU:0, one launch (start us, length us, event | category | flops | bytes accessed | tf_op | source)
XLA Modules:
  0.0 99.7 jit_solution(6038945967989891948)
XLA Ops:
  0.6 1.5 %collective-permute-start.3 = (bf16[14,14,2,768]{3,2,1,0:T(2,128)(2,1)}, bf16[14,14,2,768]{3,2,1,0:T(2,128)(2,1)}, u32[]{:S(2)}, u32[]{:S(2)}) collective-permute-start(bf16[14,14,2,768]{3,2,1,0:T(2,128)(2,1)} %bitcast.9), channel_id=1, source_target_pairs={{1,2},{2,1},{5,6},{6,5},{9,10},{10,9},{13,14},{14,13},{17,18},{18,... | collective-permute-start | bytes 1806344 | tf_op jit(solution)/shard_map/ppermute | solution.py:636
  2.1 5.1 %collective-permute-start.4 = (bf16[14,14,2,768]{3,2,1,0:T(2,128)(2,1)}, bf16[14,14,2,768]{3,2,1,0:T(2,128)(2,1)S(1)}, u32[]{:S(2)}, u32[]{:S(2)}) collective-permute-start(bf16[14,14,2,768]{3,2,1,0:T(2,128)(2,1)} %bitcast.10), channel_id=1, source_target_pairs={{0,1},{1,0},{2,3},{3,2},{4,5},{5,4},{6,7},{7,6},{8,9},{9,8},{10,11... | collective-permute-start | bytes 1806344 | tf_op jit(solution)/shard_map/ppermute | solution.py:636
  9.1 1.4 %constant_dynamic-slice_fusion.w_ref = bf16[768,768]{1,0:T(8,128)(2,1)S(1)} fusion(bf16[768,3072]{1,0:T(8,128)(2,1)} %refs_1_.3, s32[]{:T(128)S(6)} %select_n.7), kind=kLoop, calls=%fused_computation.2 | loop fusion | bytes 2359300 | tf_op jit(solution)/shard_map/dynamic_slice | solution.py:670
  10.5 6.4 %conv_forward.1 = (f32[392,768]{1,0:T(8,128)}, bf16[392,768]{1,0:T(8,128)(2,1)}, f32[2,1024]{1,0:T(2,128)}) custom-call(bf16[14,14,2,768]{3,2,1,0:T(2,128)(2,1)} %bitcast.16, bf16[3,3,64,768]{3,2,1,0:T(8,128)(2,1)} %w_hbm.5, bf16[768,1024]{1,0:T(8,128)(2,1)} %down_hbm.3), custom_call_target="tpu_custom_call" | custom-call | flops 1035000000 | bytes 1 | tf_op jit(solution)/shard_map/conv_forward/pallas_call | solution.py:156
  17.0 1.9 %collective-permute-start.1 = (f32[2,1024]{1,0:T(2,128)}, f32[2,1024]{1,0:T(2,128)S(1)}, u32[]{:S(2)}, u32[]{:S(2)}) collective-permute-start(f32[2,1024]{1,0:T(2,128)} %get-tuple-element.49), channel_id=1, source_target_pairs={{0,3},{3,0},{1,2},{2,1},{4,7},{7,4},{5,6},{6,5},{8,11},{11,8},{9,1... | collective-permute-start | bytes 24584 | tf_op jit(solution)/shard_map/ppermute | solution.py:636
  18.9 1.5 %collective-permute-start.2 = (f32[2,1024]{1,0:T(2,128)}, f32[2,1024]{1,0:T(2,128)S(1)}, u32[]{:S(2)}, u32[]{:S(2)}) collective-permute-start(f32[2,1024]{1,0:T(2,128)} %get-tuple-element.49), channel_id=1, source_target_pairs={{0,2},{2,0},{1,3},{3,1},{4,6},{6,4},{5,7},{7,5},{8,10},{10,8},{9,1... | collective-permute-start | bytes 24584 | tf_op jit(solution)/shard_map/ppermute | solution.py:636
  20.9 1.8 %collective-permute-done.1 = f32[2,1024]{1,0:T(2,128)S(1)} collective-permute-done((f32[2,1024]{1,0:T(2,128)}, f32[2,1024]{1,0:T(2,128)S(1)}, u32[]{:S(2)}, u32[]{:S(2)}) %collective-permute-start.1) | collective-permute-done | bytes 8224 | tf_op jit(solution)/shard_map/ppermute | solution.py:636
  24.4 1.4 %copy-done.1 = bf16[1024,768]{1,0:T(8,128)(2,1)S(1)} copy-done((bf16[1024,768]{1,0:T(8,128)(2,1)S(1)}, bf16[1024,768]{1,0:T(8,128)(2,1)}, u32[]{:S(2)}) %copy-start.1) | copy-done | bytes 1572888
  26.9 2.9 %scale.1 = (f32[2,768]{1,0:T(2,128)S(1)}, bf16[392,768]{1,0:T(8,128)(2,1)S(1)}, bf16[392,768]{1,0:T(8,128)(2,1)S(1)}, bf16[392,768]{1,0:T(8,128)(2,1)S(1)}) custom-call(s32[8]{0:T(128)S(1)} %get-tuple-element.92.role_ref.order_ref.place_ref, bf16[392,768]{1,0:T(8,128)(2,1)S(1)} %copy-done.7, f32[2,1024]{1,0:T(2,128)S(1)} %add_add_fusion.1.pre_ref, ...), custom_call_target="tpu_custom_call" | custom-call | flops 1035000000 | bytes 1 | tf_op jit(solution)/shard_map/scale/pallas_call | solution.py:301
  30.5 3.4 %collective-permute-start.6 = (bf16[392,768]{1,0:T(8,128)(2,1)S(1)}, bf16[392,768]{1,0:T(8,128)(2,1)S(1)}, u32[]{:S(2)}, u32[]{:S(2)}) collective-permute-start(bf16[392,768]{1,0:T(8,128)(2,1)S(1)} %get-tuple-element.52.held), channel_id=1, source_target_pairs={{0,1},{1,0},{2,3},{3,2},{4,5},{5,4},{6,7},{7,6},{8,9},{9,8},{10,11... | collective-permute-start | bytes 1806344 | tf_op jit(solution)/shard_map/ppermute | solution.py:636
  34.4 2.3 %copy-done = bf16[768,3072]{1,0:T(8,128)(2,1)S(1)} copy-done((bf16[768,3072]{1,0:T(8,128)(2,1)S(1)}, bf16[768,3072]{1,0:T(8,128)(2,1)}, u32[]{:S(2)}) %copy-start) | copy-done | bytes 4718616
  36.8 3.9 %project.1 = (bf16[392,768]{1,0:T(8,128)(2,1)S(1)}, bf16[392,768]{1,0:T(8,128)(2,1)S(1)}, bf16[392,768]{1,0:T(8,128)(2,1)S(1)}) custom-call(s32[8]{0:T(128)S(1)} %get-tuple-element.92.role_ref.order_ref.place_ref, bf16[392,768]{1,0:T(8,128)(2,1)S(1)} %get-tuple-element.50.scaled_hbm.own_ref, bf16[768,3072]{1,0:T(8,128)(2,1)S(1)} %copy-done), custom_call_target="tpu_custom_call" | custom-call | flops 1035000000 | bytes 1 | tf_op jit(solution)/shard_map/project/pallas_call | solution.py:341
  40.7 2.7 %input_grad.2.refs_2_ = f32[392,768]{1,0:T(8,128)S(1)} custom-call(s32[8]{0:T(128)S(1)} %get-tuple-element.92.role_ref.order_ref.place_ref, bf16[14,14,2,768]{3,2,1,0:T(2,128)(2,1)S(1)} %bitcast.12, bf16[14,14,2,768]{3,2,1,0:T(2,128)(2,1)S(1)} %collective-permute-done.4.refs_1_, bf16[768,3072]{1,0:T(8,128)(2,1)S(1)} %copy-done), custom_call_target="tpu_custom_call" | custom-call | flops 6900000 | bytes 1 | tf_op jit(solution)/shard_map/input_grad/pallas_call | solution.py:481
  43.4 1.6 %collective-permute-done.6.came = bf16[392,768]{1,0:T(8,128)(2,1)S(1)} collective-permute-done((bf16[392,768]{1,0:T(8,128)(2,1)S(1)}, bf16[392,768]{1,0:T(8,128)(2,1)S(1)}, u32[]{:S(2)}, u32[]{:S(2)}) %collective-permute-start.6) | collective-permute-done | bytes 602144 | tf_op jit(solution)/shard_map/ppermute | solution.py:636
  46.8 3.5 %collective-permute-start.8 = (bf16[392,768]{1,0:T(8,128)(2,1)S(1)}, bf16[392,768]{1,0:T(8,128)(2,1)S(1)}, u32[]{:S(2)}, u32[]{:S(2)}) collective-permute-start(bf16[392,768]{1,0:T(8,128)(2,1)S(1)} %get-tuple-element.60.held), channel_id=1, source_target_pairs={{0,1},{1,0},{2,3},{3,2},{4,5},{5,4},{6,7},{7,6},{8,9},{9,8},{10,11... | collective-permute-start | bytes 1806344 | tf_op jit(solution)/shard_map/ppermute | solution.py:636
  50.3 4.3 %weight_grad.1 = (bf16[2,384,384]{2,1,0:T(8,128)(2,1)S(1)}, bf16[2,384,384]{2,1,0:T(8,128)(2,1)S(1)}, bf16[2,384,384]{2,1,0:T(8,128)(2,1)S(1)}, bf16[2,384,384]{2,1,0:T(8,128)(2,1)S(1)}) custom-call(s32[8]{0:T(128)S(1)} %get-tuple-element.92.role_ref.order_ref.place_ref, bf16[392,768]{1,0:T(8,128)(2,1)S(1)} %get-tuple-element.50.scaled_hbm.own_ref, ...), custom_call_target="tpu_custom_call" | custom-call | flops 2070000000 | bytes 1 | tf_op jit(solution)/shard_map/weight_grad/pallas_call | solution.py:554
  54.6 1.6 %collective-permute-start.13 = (bf16[2,384,384]{2,1,0:T(8,128)(2,1)S(1)}, bf16[2,384,384]{2,1,0:T(8,128)(2,1)S(1)}, u32[]{:S(2)}, u32[]{:S(2)}) collective-permute-start(bf16[2,384,384]{2,1,0:T(8,128)(2,1)S(1)} %get-tuple-element.68), channel_id=1, source_target_pairs={{0,8},{4,12},{8,0},{12,4},{16,24},{20,28},{24,16},{28,20},{1,9},{5... | collective-permute-start | bytes 1769480 | tf_op jit(solution)/shard_map/ppermute | solution.py:640
  56.2 1.5 %collective-permute-start.14 = (bf16[2,384,384]{2,1,0:T(8,128)(2,1)S(1)}, bf16[2,384,384]{2,1,0:T(8,128)(2,1)S(1)}, u32[]{:S(2)}, u32[]{:S(2)}) collective-permute-start(bf16[2,384,384]{2,1,0:T(8,128)(2,1)S(1)} %get-tuple-element.62), channel_id=1, source_target_pairs={{0,16},{4,20},{8,24},{12,28},{16,0},{20,4},{24,8},{28,12},{1,17},{... | collective-permute-start | bytes 1769480 | tf_op jit(solution)/shard_map/ppermute | solution.py:640
  57.7 1.6 %input_grad.3.refs_2_ = f32[392,768]{1,0:T(8,128)S(1)} custom-call(s32[8]{0:T(128)S(1)} %get-tuple-element.92.role_ref.order_ref.place_ref, bf16[392,768]{1,0:T(8,128)(2,1)S(1)} %get-tuple-element.63.refs_2_.refs_0_, bf16[768,3072]{1,0:T(8,128)(2,1)S(1)} %bitcast.8, f32[392,768]{1,0:T(8,128)S(1)} %input_grad.2.refs_2_), custom_call_target="tpu_custom_call" | custom-call | flops 6900000 | bytes 1 | tf_op jit(solution)/shard_map/input_grad/pallas_call | solution.py:481
  59.3 4.9 %collective-permute-done.8.came = bf16[392,768]{1,0:T(8,128)(2,1)S(1)} collective-permute-done((bf16[392,768]{1,0:T(8,128)(2,1)S(1)}, bf16[392,768]{1,0:T(8,128)(2,1)S(1)}, u32[]{:S(2)}, u32[]{:S(2)}) %collective-permute-start.8) | collective-permute-done | bytes 602144 | tf_op jit(solution)/shard_map/ppermute | solution.py:636
  65.0 1.9 %collective-permute-start.16 = (bf16[392,768]{1,0:T(8,128)(2,1)S(1)}, bf16[392,768]{1,0:T(8,128)(2,1)S(1)}, u32[]{:S(2)}, u32[]{:S(2)}) collective-permute-start(bf16[392,768]{1,0:T(8,128)(2,1)S(1)} %get-tuple-element.74), channel_id=1, source_target_pairs={{0,1},{1,0},{2,3},{3,2},{4,5},{5,4},{6,7},{7,6},{8,9},{9,8},{10,11... | collective-permute-start | bytes 1806344 | tf_op jit(solution)/shard_map/ppermute | solution.py:636
  67.7 1.6 %weight_grad_more.1 = (bf16[384,384]{1,0:T(8,128)(2,1)S(1)}, bf16[384,384]{1,0:T(8,128)(2,1)S(1)}) custom-call(s32[8]{0:T(128)S(1)} %get-tuple-element.92.role_ref.order_ref.place_ref, bf16[392,768]{1,0:T(8,128)(2,1)S(1)} %get-tuple-element.50.scaled_hbm.own_ref, bf16[392,768]{1,0:T(8,128)(2,1)S(1)} %collective-permute-done.9.other_ref, ...), custom_call_target="tpu_custom_call" | custom-call | flops 6900000 | bytes 1 | tf_op jit(solution)/shard_map/weight_grad_more/pallas_call | solution.py:554
  69.2 1.6 %collective-permute-start.21 = (bf16[384,384]{1,0:T(8,128)(2,1)S(1)}, bf16[384,384]{1,0:T(8,128)(2,1)S(1)}, u32[]{:S(2)}, u32[]{:S(2)}) collective-permute-start(bf16[384,384]{1,0:T(8,128)(2,1)S(1)} %get-tuple-element.84.refs_4_), channel_id=1, source_target_pairs={{0,8},{4,12},{8,0},{12,4},{16,24},{20,28},{24,16},{28,20},{1,9},{5... | collective-permute-start | bytes 884744 | tf_op jit(solution)/shard_map/ppermute | solution.py:640
  70.8 1.5 %collective-permute-start.22 = (bf16[384,384]{1,0:T(8,128)(2,1)S(1)}, bf16[384,384]{1,0:T(8,128)(2,1)S(1)}, u32[]{:S(2)}, u32[]{:S(2)}) collective-permute-start(bf16[384,384]{1,0:T(8,128)(2,1)S(1)} %get-tuple-element.70.refs_6_), channel_id=1, source_target_pairs={{0,16},{4,20},{8,24},{12,28},{16,0},{20,4},{24,8},{28,12},{1,17},{... | collective-permute-start | bytes 884744 | tf_op jit(solution)/shard_map/ppermute | solution.py:640
  72.3 2.6 %input_grad_last.1 = (f32[392,768]{1,0:T(8,128)S(1)}, f32[2,1024]{1,0:T(2,128)S(1)}) custom-call(s32[8]{0:T(128)S(1)} %get-tuple-element.92.role_ref.order_ref.place_ref, bf16[392,768]{1,0:T(8,128)(2,1)S(1)} %get-tuple-element.71.refs_0_, bf16[768,3072]{1,0:T(8,128)(2,1)S(1)} %bitcast.8, f32[392,768]{1,0:T(8,128)S(1)} %input_grad.3.refs_2_, ...), custom_call_target="tpu_custom_call" | custom-call | flops 3449999872 | bytes 1 | tf_op jit(solution)/shard_map/input_grad_last/pallas_call | solution.py:481
  75.0 6.2 %collective-permute-done.16.came = bf16[392,768]{1,0:T(8,128)(2,1)S(1)} collective-permute-done((bf16[392,768]{1,0:T(8,128)(2,1)S(1)}, bf16[392,768]{1,0:T(8,128)(2,1)S(1)}, u32[]{:S(2)}, u32[]{:S(2)}) %collective-permute-start.16) | collective-permute-done | bytes 602144 | tf_op jit(solution)/shard_map/ppermute | solution.py:636
  81.1 3.6 %collective-permute-start.18 = (f32[2,1024]{1,0:T(2,128)S(1)}, f32[2,1024]{1,0:T(2,128)S(1)}, u32[]{:S(2)}, u32[]{:S(2)}) collective-permute-start(f32[2,1024]{1,0:T(2,128)S(1)} %get-tuple-element.79), channel_id=1, source_target_pairs={{0,1},{1,0},{2,3},{3,2},{4,5},{5,4},{6,7},{7,6},{8,9},{9,8},{10,11... | collective-permute-start | bytes 24584 | tf_op jit(solution)/shard_map/ppermute | solution.py:636
  84.8 2.5 %collective-permute-start.19 = (f32[2,1024]{1,0:T(2,128)S(1)}, f32[2,1024]{1,0:T(2,128)S(1)}, u32[]{:S(2)}, u32[]{:S(2)}) collective-permute-start(f32[2,1024]{1,0:T(2,128)S(1)} %get-tuple-element.79), channel_id=1, source_target_pairs={{0,3},{3,0},{1,2},{2,1},{4,7},{7,4},{5,6},{6,5},{8,11},{11,8},{9,1... | collective-permute-start | bytes 24584 | tf_op jit(solution)/shard_map/ppermute | solution.py:636
  88.4 1.6 %collective-permute-start.23 = (bf16[384,384]{1,0:T(8,128)(2,1)S(1)}, bf16[384,384]{1,0:T(8,128)(2,1)S(1)}, u32[]{:S(2)}, u32[]{:S(2)}) collective-permute-start(bf16[384,384]{1,0:T(8,128)(2,1)S(1)} %get-tuple-element.89), channel_id=1, source_target_pairs={{0,16},{4,20},{8,24},{12,28},{16,0},{20,4},{24,8},{28,12},{1,17},{... | collective-permute-start | bytes 884744 | tf_op jit(solution)/shard_map/ppermute | solution.py:640
  90.0 1.5 %collective-permute-start.24 = (bf16[384,384]{1,0:T(8,128)(2,1)S(1)}, bf16[384,384]{1,0:T(8,128)(2,1)S(1)}, u32[]{:S(2)}, u32[]{:S(2)}) collective-permute-start(bf16[384,384]{1,0:T(8,128)(2,1)S(1)} %get-tuple-element.85), channel_id=1, source_target_pairs={{0,8},{4,12},{8,0},{12,4},{16,24},{20,28},{24,16},{28,20},{1,9},{5... | collective-permute-start | bytes 884744 | tf_op jit(solution)/shard_map/ppermute | solution.py:640
  91.5 1.7 %between.5 = bf16[14,14,2,768]{3,2,1,0:T(2,128)(2,1)} custom-call(s32[8]{0:T(128)S(1)} %get-tuple-element.92.role_ref.order_ref.place_ref, bf16[392,768]{1,0:T(8,128)(2,1)S(1)} %get-tuple-element.51.p_own, bf16[392,768]{1,0:T(8,128)(2,1)S(1)} %collective-permute-done.16.came, bf16[392,768]{1,0:T(8,128)(2,1)S(1)} %collective-permute-done.17.crossed), custom_call_target="tpu_custom_call" | custom-call | flops 6900000 | bytes 1 | tf_op jit(solution)/shard_map/between/pallas_call | solution.py:405
  93.3 5.3 %conv_backward.1 = bf16[14,14,2,768]{3,2,1,0:T(2,128)(2,1)} custom-call(f32[392,768]{1,0:T(8,128)S(1)} %get-tuple-element.78.grad_ref, f32[2,768]{1,0:T(2,128)S(1)} %get-tuple-element.72.refs_4_.gate_ref, f32[2,1024]{1,0:T(2,128)S(1)} %add_add_fusion.sum_ref, f32[2,1024]{1,0:T(2,128)S(1)} %add_add_fusion.1.pre_ref, bf16[768,1024]{1,0:T(8,128)(2,1)S(1)} %copy-done.3, ...), custom_call_target="tpu_custom_call" | custom-call | flops 1035000000 | bytes 1 | tf_op jit(solution)/shard_map/conv_backward/pallas_call | solution.py:230
  (60 shorter events, 11.5 us)
Async XLA Ops:
  0.6 23.8 %collective-permute-start.3 = (bf16[14,14,2,768]{3,2,1,0:T(2,128)(2,1)}, bf16[14,14,2,768]{3,2,1,0:T(2,128)(2,1)}, u32[]{:S(2)}, u32[]{:S(2)}) collective-permute-start(bf16[14,14,2,768]{3,2,1,0:T(2,128)(2,1)} %bitcast.9), channel_id=1, source_target_pairs={{1,2},{2,1},{5,6},{6,5},{9,10},{10,9},{13,14},{14,13},{17,18},{18,... | collective-permute-start | bytes 1806344 | tf_op jit(solution)/shard_map/ppermute | solution.py:636
  2.1 27.7 %collective-permute-start.4 = (bf16[14,14,2,768]{3,2,1,0:T(2,128)(2,1)}, bf16[14,14,2,768]{3,2,1,0:T(2,128)(2,1)S(1)}, u32[]{:S(2)}, u32[]{:S(2)}) collective-permute-start(bf16[14,14,2,768]{3,2,1,0:T(2,128)(2,1)} %bitcast.10), channel_id=1, source_target_pairs={{0,1},{1,0},{2,3},{3,2},{4,5},{5,4},{6,7},{7,6},{8,9},{9,8},{10,11... | collective-permute-start | bytes 1806344 | tf_op jit(solution)/shard_map/ppermute | solution.py:636
  16.9 4.0 %collective-permute-start = (f32[2,1024]{1,0:T(2,128)}, f32[2,1024]{1,0:T(2,128)S(1)}, u32[]{:S(2)}, u32[]{:S(2)}) collective-permute-start(f32[2,1024]{1,0:T(2,128)} %get-tuple-element.49), channel_id=1, source_target_pairs={{0,1},{1,0},{2,3},{3,2},{4,5},{5,4},{6,7},{7,6},{8,9},{9,8},{10,11... | collective-permute-start | bytes 24584 | tf_op jit(solution)/shard_map/ppermute | solution.py:636
  17.0 5.7 %collective-permute-start.1 = (f32[2,1024]{1,0:T(2,128)}, f32[2,1024]{1,0:T(2,128)S(1)}, u32[]{:S(2)}, u32[]{:S(2)}) collective-permute-start(f32[2,1024]{1,0:T(2,128)} %get-tuple-element.49), channel_id=1, source_target_pairs={{0,3},{3,0},{1,2},{2,1},{4,7},{7,4},{5,6},{6,5},{8,11},{11,8},{9,1... | collective-permute-start | bytes 24584 | tf_op jit(solution)/shard_map/ppermute | solution.py:636
  18.9 4.8 %collective-permute-start.2 = (f32[2,1024]{1,0:T(2,128)}, f32[2,1024]{1,0:T(2,128)S(1)}, u32[]{:S(2)}, u32[]{:S(2)}) collective-permute-start(f32[2,1024]{1,0:T(2,128)} %get-tuple-element.49), channel_id=1, source_target_pairs={{0,2},{2,0},{1,3},{3,1},{4,6},{6,4},{5,7},{7,5},{8,10},{10,8},{9,1... | collective-permute-start | bytes 24584 | tf_op jit(solution)/shard_map/ppermute | solution.py:636
  26.9 7.0 %copy-start.6 = (bf16[2,14,14,768]{3,0,2,1:T(2,128)(2,1)S(1)}, bf16[2,14,14,768]{3,0,2,1:T(2,128)(2,1)}, u32[]{:S(2)}) copy-start(bf16[2,14,14,768]{3,0,2,1:T(2,128)(2,1)} %param.12) | copy-start | bytes 1806340
  29.8 13.6 %collective-permute-start.5 = (bf16[14,14,2,768]{3,2,1,0:T(2,128)(2,1)S(1)}, bf16[14,14,2,768]{3,2,1,0:T(2,128)(2,1)S(1)}, u32[]{:S(2)}, u32[]{:S(2)}) collective-permute-start(bf16[14,14,2,768]{3,2,1,0:T(2,128)(2,1)S(1)} %collective-permute-done.4.refs_1_), channel_id=1, source_target_pairs={{1,2},{2,1},{5,6},{6,5},{9,10},{10,9},{13,14},{14,13},{17,18},{18,... | collective-permute-start | bytes 1806344 | tf_op jit(solution)/shard_map/ppermute | solution.py:636
  30.5 14.6 %collective-permute-start.6 = (bf16[392,768]{1,0:T(8,128)(2,1)S(1)}, bf16[392,768]{1,0:T(8,128)(2,1)S(1)}, u32[]{:S(2)}, u32[]{:S(2)}) collective-permute-start(bf16[392,768]{1,0:T(8,128)(2,1)S(1)} %get-tuple-element.52.held), channel_id=1, source_target_pairs={{0,1},{1,0},{2,3},{3,2},{4,5},{5,4},{6,7},{7,6},{8,9},{9,8},{10,11... | collective-permute-start | bytes 1806344 | tf_op jit(solution)/shard_map/ppermute | solution.py:636
  33.9 12.9 %collective-permute-start.10 = (bf16[14,14,2,768]{3,2,1,0:T(2,128)(2,1)S(1)}, bf16[14,14,2,768]{3,2,1,0:T(2,128)(2,1)S(1)}, u32[]{:S(2)}, u32[]{:S(2)}) collective-permute-start(bf16[14,14,2,768]{3,2,1,0:T(2,128)(2,1)S(1)} %bitcast.11), channel_id=1, source_target_pairs={{0,4},{4,0},{8,12},{12,8},{16,20},{20,16},{24,28},{28,24},{1,5},{5... | collective-permute-start | bytes 1806344 | tf_op jit(solution)/shard_map/ppermute | solution.py:640
  33.9 16.4 %collective-permute-start.9 = (bf16[392,768]{1,0:T(8,128)(2,1)S(1)}, bf16[392,768]{1,0:T(8,128)(2,1)S(1)}, u32[]{:S(2)}, u32[]{:S(2)}) collective-permute-start(bf16[392,768]{1,0:T(8,128)(2,1)S(1)} %get-tuple-element.50.scaled_hbm.own_ref), channel_id=1, source_target_pairs={{0,4},{4,0},{8,12},{12,8},{16,20},{20,16},{24,28},{28,24},{1,5},{5... | collective-permute-start | bytes 1806344 | tf_op jit(solution)/shard_map/ppermute | solution.py:640
  40.6 9.7 %collective-permute-start.11 = (bf16[14,14,2,768]{3,2,1,0:T(2,128)(2,1)S(1)}, bf16[14,14,2,768]{3,2,1,0:T(2,128)(2,1)S(1)}, u32[]{:S(2)}, u32[]{:S(2)}) collective-permute-start(bf16[14,14,2,768]{3,2,1,0:T(2,128)(2,1)S(1)} %collective-permute-done.4.refs_1_), channel_id=1, source_target_pairs={{0,4},{4,0},{8,12},{12,8},{16,20},{20,16},{24,28},{28,24},{1,5},{5... | collective-permute-start | bytes 1806344 | tf_op jit(solution)/shard_map/ppermute | solution.py:640
  45.1 12.6 %slice-start = ((s8[4718592]{0:T(1024)(128)(4,1)}), s8[4194304]{0:T(1024)(128)(4,1)S(1)}, s32[]{:S(2)}) async-start(s8[4718592]{0:T(1024)(128)(4,1)} %bitcast.7), calls=%async_computation | async-start | bytes 8388608
  45.9 4.5 %collective-permute-start.12 = (bf16[392,768]{1,0:T(8,128)(2,1)S(1)}, bf16[392,768]{1,0:T(8,128)(2,1)S(1)}, u32[]{:S(2)}, u32[]{:S(2)}) collective-permute-start(bf16[392,768]{1,0:T(8,128)(2,1)S(1)} %get-tuple-element.63.refs_2_.refs_0_), channel_id=1, source_target_pairs={{0,4},{4,0},{8,12},{12,8},{16,20},{20,16},{24,28},{28,24},{1,5},{5... | collective-permute-start | bytes 1806344 | tf_op jit(solution)/shard_map/ppermute | solution.py:640
  45.9 13.3 %collective-permute-start.7 = (bf16[392,768]{1,0:T(8,128)(2,1)S(1)}, bf16[392,768]{1,0:T(8,128)(2,1)S(1)}, u32[]{:S(2)}, u32[]{:S(2)}) collective-permute-start(bf16[392,768]{1,0:T(8,128)(2,1)S(1)} %get-tuple-element.59), channel_id=1, source_target_pairs={{1,2},{2,1},{5,6},{6,5},{9,10},{10,9},{13,14},{14,13},{17,18},{18,... | collective-permute-start | bytes 1806344 | tf_op jit(solution)/shard_map/ppermute | solution.py:636
  46.8 10.9 %slice-start.1 = ((s8[4718592]{0:T(1024)(128)(4,1)}), s8[524288]{0:T(1024)(128)(4,1)S(1)}, s32[]{:S(2)}) async-start(s8[4718592]{0:T(1024)(128)(4,1)} %bitcast.7), calls=%async_computation.1 | async-start | bytes 1048576
  46.8 17.4 %collective-permute-start.8 = (bf16[392,768]{1,0:T(8,128)(2,1)S(1)}, bf16[392,768]{1,0:T(8,128)(2,1)S(1)}, u32[]{:S(2)}, u32[]{:S(2)}) collective-permute-start(bf16[392,768]{1,0:T(8,128)(2,1)S(1)} %get-tuple-element.60.held), channel_id=1, source_target_pairs={{0,1},{1,0},{2,3},{3,2},{4,5},{5,4},{6,7},{7,6},{8,9},{9,8},{10,11... | collective-permute-start | bytes 1806344 | tf_op jit(solution)/shard_map/ppermute | solution.py:636
  54.6 16.2 %collective-permute-start.13 = (bf16[2,384,384]{2,1,0:T(8,128)(2,1)S(1)}, bf16[2,384,384]{2,1,0:T(8,128)(2,1)S(1)}, u32[]{:S(2)}, u32[]{:S(2)}) collective-permute-start(bf16[2,384,384]{2,1,0:T(8,128)(2,1)S(1)} %get-tuple-element.68), channel_id=1, source_target_pairs={{0,8},{4,12},{8,0},{12,4},{16,24},{20,28},{24,16},{28,20},{1,9},{5... | collective-permute-start | bytes 1769480 | tf_op jit(solution)/shard_map/ppermute | solution.py:640
  56.2 16.1 %collective-permute-start.14 = (bf16[2,384,384]{2,1,0:T(8,128)(2,1)S(1)}, bf16[2,384,384]{2,1,0:T(8,128)(2,1)S(1)}, u32[]{:S(2)}, u32[]{:S(2)}) collective-permute-start(bf16[2,384,384]{2,1,0:T(8,128)(2,1)S(1)} %get-tuple-element.62), channel_id=1, source_target_pairs={{0,16},{4,20},{8,24},{12,28},{16,0},{20,4},{24,8},{28,12},{1,17},{... | collective-permute-start | bytes 1769480 | tf_op jit(solution)/shard_map/ppermute | solution.py:640
  64.2 8.2 %copy-start.8 = (bf16[392,768]{1,0:T(8,128)(2,1)S(1)}, bf16[392,768]{1,0:T(8,128)(2,1)}, u32[]{:S(2)}) copy-start(bf16[392,768]{1,0:T(8,128)(2,1)} %get-tuple-element.48.act_ref.refs_3_) | copy-start | bytes 1806340
  65.0 7.4 %copy-start.2 = (bf16[1024,768]{1,0:T(8,128)(2,1)S(1)}, bf16[1024,768]{1,0:T(8,128)(2,1)}, u32[]{:S(2)}) copy-start(bf16[1024,768]{1,0:T(8,128)(2,1)} %refs_5_.1) | copy-start | bytes 4718596
  65.0 2.7 %collective-permute-start.15 = (bf16[392,384]{1,0:T(8,128)(2,1)S(1)}, bf16[392,384]{1,0:T(8,128)(2,1)S(1)}, u32[]{:S(2)}, u32[]{:S(2)}) collective-permute-start(bf16[392,384]{1,0:T(8,128)(2,1)S(1)} %get-tuple-element.69), channel_id=1, source_target_pairs={{0,4},{4,0},{8,12},{12,8},{16,20},{20,16},{24,28},{28,24},{1,5},{5... | collective-permute-start | bytes 903176 | tf_op jit(solution)/shard_map/ppermute | solution.py:640
  65.0 16.1 %collective-permute-start.16 = (bf16[392,768]{1,0:T(8,128)(2,1)S(1)}, bf16[392,768]{1,0:T(8,128)(2,1)S(1)}, u32[]{:S(2)}, u32[]{:S(2)}) collective-permute-start(bf16[392,768]{1,0:T(8,128)(2,1)S(1)} %get-tuple-element.74), channel_id=1, source_target_pairs={{0,1},{1,0},{2,3},{3,2},{4,5},{5,4},{6,7},{7,6},{8,9},{9,8},{10,11... | collective-permute-start | bytes 1806344 | tf_op jit(solution)/shard_map/ppermute | solution.py:636
  66.9 14.2 %collective-permute-start.17 = (bf16[392,768]{1,0:T(8,128)(2,1)S(1)}, bf16[392,768]{1,0:T(8,128)(2,1)S(1)}, u32[]{:S(2)}, u32[]{:S(2)}) collective-permute-start(bf16[392,768]{1,0:T(8,128)(2,1)S(1)} %get-tuple-element.75), channel_id=1, source_target_pairs={{1,2},{2,1},{5,6},{6,5},{9,10},{10,9},{13,14},{14,13},{17,18},{18,... | collective-permute-start | bytes 1806344 | tf_op jit(solution)/shard_map/ppermute | solution.py:636
  69.2 18.0 %collective-permute-start.21 = (bf16[384,384]{1,0:T(8,128)(2,1)S(1)}, bf16[384,384]{1,0:T(8,128)(2,1)S(1)}, u32[]{:S(2)}, u32[]{:S(2)}) collective-permute-start(bf16[384,384]{1,0:T(8,128)(2,1)S(1)} %get-tuple-element.84.refs_4_), channel_id=1, source_target_pairs={{0,8},{4,12},{8,0},{12,4},{16,24},{20,28},{24,16},{28,20},{1,9},{5... | collective-permute-start | bytes 884744 | tf_op jit(solution)/shard_map/ppermute | solution.py:640
  70.8 16.5 %collective-permute-start.22 = (bf16[384,384]{1,0:T(8,128)(2,1)S(1)}, bf16[384,384]{1,0:T(8,128)(2,1)S(1)}, u32[]{:S(2)}, u32[]{:S(2)}) collective-permute-start(bf16[384,384]{1,0:T(8,128)(2,1)S(1)} %get-tuple-element.70.refs_6_), channel_id=1, source_target_pairs={{0,16},{4,20},{8,24},{12,28},{16,0},{20,4},{24,8},{28,12},{1,17},{... | collective-permute-start | bytes 884744 | tf_op jit(solution)/shard_map/ppermute | solution.py:640
  81.1 12.1 %collective-permute-start.18 = (f32[2,1024]{1,0:T(2,128)S(1)}, f32[2,1024]{1,0:T(2,128)S(1)}, u32[]{:S(2)}, u32[]{:S(2)}) collective-permute-start(f32[2,1024]{1,0:T(2,128)S(1)} %get-tuple-element.79), channel_id=1, source_target_pairs={{0,1},{1,0},{2,3},{3,2},{4,5},{5,4},{6,7},{7,6},{8,9},{9,8},{10,11... | collective-permute-start | bytes 24584 | tf_op jit(solution)/shard_map/ppermute | solution.py:636
  84.8 8.5 %collective-permute-start.19 = (f32[2,1024]{1,0:T(2,128)S(1)}, f32[2,1024]{1,0:T(2,128)S(1)}, u32[]{:S(2)}, u32[]{:S(2)}) collective-permute-start(f32[2,1024]{1,0:T(2,128)S(1)} %get-tuple-element.79), channel_id=1, source_target_pairs={{0,3},{3,0},{1,2},{2,1},{4,7},{7,4},{5,6},{6,5},{8,11},{11,8},{9,1... | collective-permute-start | bytes 24584 | tf_op jit(solution)/shard_map/ppermute | solution.py:636
  87.2 6.0 %collective-permute-start.20 = (f32[2,1024]{1,0:T(2,128)S(1)}, f32[2,1024]{1,0:T(2,128)S(1)}, u32[]{:S(2)}, u32[]{:S(2)}) collective-permute-start(f32[2,1024]{1,0:T(2,128)S(1)} %get-tuple-element.79), channel_id=1, source_target_pairs={{0,2},{2,0},{1,3},{3,1},{4,6},{6,4},{5,7},{7,5},{8,10},{10,8},{9,1... | collective-permute-start | bytes 24584 | tf_op jit(solution)/shard_map/ppermute | solution.py:636
  87.3 6.0 %copy-start.4 = (f32[392,768]{1,0:T(8,128)S(1)}, f32[392,768]{1,0:T(8,128)}, u32[]{:S(2)}) copy-start(f32[392,768]{1,0:T(8,128)} %get-tuple-element.87.conv_ref) | copy-start | bytes 3612676
  87.3 6.0 %copy-start.5 = (bf16[3,3,64,768]{3,2,1,0:T(8,128)(2,1)S(1)}, bf16[3,3,64,768]{3,2,1,0:T(8,128)(2,1)}, u32[]{:S(2)}) copy-start(bf16[3,3,64,768]{3,2,1,0:T(8,128)(2,1)} %w_hbm.5) | copy-start | bytes 2654212
  88.4 10.2 %collective-permute-start.23 = (bf16[384,384]{1,0:T(8,128)(2,1)S(1)}, bf16[384,384]{1,0:T(8,128)(2,1)S(1)}, u32[]{:S(2)}, u32[]{:S(2)}) collective-permute-start(bf16[384,384]{1,0:T(8,128)(2,1)S(1)} %get-tuple-element.89), channel_id=1, source_target_pairs={{0,16},{4,20},{8,24},{12,28},{16,0},{20,4},{24,8},{28,12},{1,17},{... | collective-permute-start | bytes 884744 | tf_op jit(solution)/shard_map/ppermute | solution.py:640
  90.0 8.6 %collective-permute-start.24 = (bf16[384,384]{1,0:T(8,128)(2,1)S(1)}, bf16[384,384]{1,0:T(8,128)(2,1)S(1)}, u32[]{:S(2)}, u32[]{:S(2)}) collective-permute-start(bf16[384,384]{1,0:T(8,128)(2,1)S(1)} %get-tuple-element.85), channel_id=1, source_target_pairs={{0,8},{4,12},{8,0},{12,4},{16,24},{20,28},{24,16},{28,20},{1,9},{5... | collective-permute-start | bytes 884744 | tf_op jit(solution)/shard_map/ppermute | solution.py:640
  (4 other events, 8.1 us)

commit v4 on v3

--- a/solution.py
+++ b/solution.py
@@ -19,13 +19,19 @@
 
 
 SCALE = 0.3
-CONV_MIB = 62
+CONV_MIB = 50
+FAR_COST = 10
 
 
 def cost(micros):
     return pl.CostEstimate(
         flops=int(micros * SCALE * 1.15e9), bytes_accessed=1, transcendentals=0
     )
+
+
+def sum_of(refs):
+    own, near, across, over = (ref[...] for ref in refs)
+    return (own + near) + (across + over)
 
 
 def exact_dot(values, weight, dims):
@@ -82,19 +88,19 @@
     row_group = lax.broadcasted_iota(jnp.int32, (LANES, LANES), 0) // group
     col_group = lax.broadcasted_iota(jnp.int32, (LANES, LANES), 1) // group
     mask = (row_group == col_group).astype(F32).astype(BF16)
-    total = None
+    cells, taps = [], []
     for dw in range(3):
         shifted = pad_ref[pl.ds(8 + images * (dw - 1), (height + 2) * unit), :].astype(BF16)
         for dh in range(3):
             tap = weight_ref[2 - dh, 2 - dw] if turn else weight_ref[dh, dw]
-            dense = jnp.concatenate([tap] * (LANES // group), axis=0) * mask
-            part = lax.dot_general(
-                shifted[dh * unit : (dh + height) * unit],
-                dense,
-                (((1,), (1 if turn else 0,)), ((), ())),
-                preferred_element_type=F32,
-            )
-            total = part if total is None else total + part
+            taps.append(jnp.concatenate([tap] * (LANES // group), axis=0) * mask)
+            cells.append(shifted[dh * unit : (dh + height) * unit])
+    total = lax.dot_general(
+        jnp.concatenate(cells, axis=1),
+        jnp.concatenate(taps, axis=1 if turn else 0),
+        (((1,), (1 if turn else 0,)), ((), ())),
+        preferred_element_type=F32,
+    )
     pad_ref[pl.ds(0, height * unit), :] = total
     for h in range(height):
         rows_ref[pl.ds(h * line, line), :] = pad_ref[pl.ds(h * unit + images, line), :]
@@ -180,7 +186,10 @@
 def conv_backward_body(
     grad_ref,
     gate_ref,
-    sum_ref,
+    own_ref,
+    near_ref,
+    across_ref,
+    over_ref,
     pre_ref,
     down_hbm,
     conv_ref,
@@ -204,7 +213,8 @@
     for i in range(blocks):
         part = w_hbm.at[:, :, :, lanes_of(i)]
         copies.append(fetch(part, w_buf.at[i], sems.at[1 + i]))
-    excite_grad = sum_ref[...] * silu_grad(pre_ref[...])
+    excite_sum = sum_of((own_ref, near_ref, across_ref, over_ref))
+    excite_grad = excite_sum * silu_grad(pre_ref[...])
     down_copy.wait()
     squeeze_grad = exact_dot(excite_grad, down_buf[...], ((1,), (1,))) / (height * width)
     outs = []
@@ -223,13 +233,13 @@
         out.wait()
 
 
-def conv_backward(scaled_grad, gating, excite_sum, excite_pre, down, convolved, weight, shape):
+def conv_backward(scaled_grad, gating, terms, excite_pre, down, convolved, weight, shape):
     height, width, images, channels = shape
     count = convolved.shape[0]
     blocks = channels // LANES
     return pl.pallas_call(
         functools.partial(conv_backward_body, height=height, width=width, images=images),
-        in_specs=[HERE, HERE, HERE, HERE, HBM, HERE, HBM],
+        in_specs=[HERE] * 7 + [HBM, HERE, HBM],
         out_specs=HBM,
         out_shape=jax.ShapeDtypeStruct(shape, BF16),
         scratch_shapes=[
@@ -243,7 +253,7 @@
         compiler_params=params(),
         cost_estimate=cost(3),
         name="conv_backward",
-    )(scaled_grad, gating, excite_sum, excite_pre, down, convolved, weight)
+    )(scaled_grad, gating, *terms, excite_pre, down, convolved, weight)
 
 
 def block_of(weight_ref, block, width):
@@ -253,11 +263,15 @@
 def scale_body(
     role_ref,
     act_ref,
-    pre_ref,
+    own_ref,
+    near_ref,
+    across_ref,
+    over_ref,
     up_ref,
     w_ref,
     middle_hbm,
     gate_ref,
+    pre_ref,
     scaled_hbm,
     far_hbm,
     send_hbm,
@@ -268,7 +282,8 @@
     sems,
 ):
     middle_copy = fetch(middle_hbm, middle_buf, sems.at[0])
-    pre = pre_ref[...]
+    pre = sum_of((own_ref, near_ref, across_ref, over_ref))
+    pre_ref[...] = pre
     excited = pre * jax.nn.sigmoid(pre)
     gate_ref[...] = jax.nn.sigmoid(exact_dot(excited, up_ref[...], ((1,), (0,))))
     gate = per_row(gate_ref[...], act_ref.shape[0])
@@ -294,15 +309,19 @@
         copy.wait()
 
 
-def scale(role, act, excite_pre, up, w_far, middle):
+def scale(role, act, terms, up, w_far, middle):
     count, channels = act.shape
-    gates = (excite_pre.shape[0], channels)
+    gates = (terms[0].shape[0], channels)
     array = jax.ShapeDtypeStruct((count, channels), BF16)
     return pl.pallas_call(
         scale_body,
-        in_specs=[pl.BlockSpec(memory_space=pltpu.SMEM), HERE, HERE, HERE, HERE, HBM],
-        out_specs=[HERE, HBM, HBM, HBM],
-        out_shape=[jax.ShapeDtypeStruct(gates, F32)] + [array] * 3,
+        in_specs=[pl.BlockSpec(memory_space=pltpu.SMEM)] + [HERE] * 7 + [HBM],
+        out_specs=[HERE, HERE, HBM, HBM, HBM],
+        out_shape=[
+            jax.ShapeDtypeStruct(gates, F32),
+            jax.ShapeDtypeStruct(terms[0].shape, F32),
+        ]
+        + [array] * 3,
         scratch_shapes=[
             pltpu.VMEM(middle.shape, BF16),
             pltpu.VMEM((count, channels), BF16),
@@ -313,7 +332,7 @@
         compiler_params=params(),
         cost_estimate=cost(3),
         name="scale",
-    )(role, act, excite_pre, up, w_far, middle)
+    )(role, act, *terms, up, w_far, middle)
 
 
 def project_body(order_ref, scaled_hbm, w_hbm, *refs, parts):
@@ -355,37 +374,44 @@
     )(order, scaled, weight)
 
 
-def second_body(role_ref, came, held, far, p_fourth, p_third, third, to_far, send):
-    at_end = role_ref[4] == 1
-    to_far[...] = (p_fourth[...].astype(F32) + came[...].astype(F32)).astype(BF16)
-
-    @pl.when(at_end)
-    def _():
-        third[...] = came[...]
-        send[...] = p_third[...]
-
-    @pl.when(jnp.logical_not(at_end))
-    def _():
-        third[...] = held[...]
-        send[...] = as_rows(far[...])
-
-
-def third_body(role_ref, came, crossed, held, p_outer, p_third, fourth, to_mid, send, give):
-    at_end = role_ref[4] == 1
-    to_mid[...] = (p_third[...].astype(F32) + came[...].astype(F32)).astype(BF16)
-
-    @pl.when(at_end)
-    def _():
-        fourth[...] = came[...]
-        send[...] = p_outer[...]
-
-    @pl.when(jnp.logical_not(at_end))
-    def _():
-        fourth[...] = held[...]
-        send[...] = (p_outer[...].astype(F32) + crossed[...].astype(F32)).astype(BF16)
-
+def sum_into(ref, a, b):
+    ref[...] = (a[...].astype(F32) + b[...].astype(F32)).astype(BF16)
+
+
+def choose(role_ref, ref, at_end, else_):
+    @pl.when(role_ref[4] == 1)
+    def _():
+        ref[...] = as_rows(at_end[...])
+
+    @pl.when(role_ref[4] == 0)
+    def _():
+        ref[...] = as_rows(else_[...])
+
+
+def far_body(role_ref, p_third, far, send):
+    choose(role_ref, send, p_third, far)
+
+
+def second_body(role_ref, came, held, p_fourth, third, to_far):
+    sum_into(to_far, p_fourth, came)
+    choose(role_ref, third, came, held)
+
+
+def third_body(role_ref, came, held, p_third, fourth, to_mid, give):
+    sum_into(to_mid, p_third, came)
+    choose(role_ref, fourth, came, held)
     half = give.shape[1]
     give[...] = fourth[:, pl.ds(pl.multiple_of((1 - role_ref[5]) * half, half), half)]
+
+
+def outer_body(role_ref, crossed, p_outer, send):
+    @pl.when(role_ref[4] == 1)
+    def _():
+        send[...] = p_outer[...]
+
+    @pl.when(role_ref[4] == 0)
+    def _():
+        sum_into(send, p_outer, crossed)
 
 
 def fourth_body(role_ref, p_own, came, crossed, total):
@@ -401,7 +427,7 @@
         total[...] = (near + crossed[...].astype(F32)).astype(BF16).reshape(total.shape)
 
 
-def between(body, extents, role, *arrays):
+def between(body, extents, role, *arrays, micros=0.02):
     return pl.pallas_call(
         body,
         grid=(1,),
@@ -409,8 +435,8 @@
         out_specs=[whole(extent) for extent in extents],
         out_shape=[jax.ShapeDtypeStruct(extent, BF16) for extent in extents],
         compiler_params=params(),
-        cost_estimate=cost(0.02),
-        name="between",
+        cost_estimate=cost(micros),
+        name=body.__name__.replace("_body", "_turn"),
     )(role, *arrays)
 
 
@@ -492,7 +518,7 @@
         out_shape=out_shape,
         scratch_shapes=scratch,
         compiler_params=params(),
-        cost_estimate=cost(10 if last else 0.02),
+        cost_estimate=cost(10 if last or first == 0 else 0.02),
         name="input_grad_last" if last else "input_grad",
     )(role, *operands)
 
@@ -640,9 +666,8 @@
     return lax.ppermute(array, "dp", [(i, i ^ bit) for i in range(8)])
 
 
-def small_sum(values):
-    near, across, over = (along_chan(values, pairs) for pairs in (OUTER, CROSS, OVER))
-    return (values + near) + (across + over)
+def gather_small(values):
+    return [values] + [along_chan(values, pairs) for pairs in (OUTER, CROSS, OVER)]
 
 
 def after(array, *others):
@@ -669,51 +694,53 @@
     middle = along_chan(own, MIDDLE)
     w_far = lax.dynamic_slice_in_dim(proj_weight, role[3] * channels, channels, axis=1)
     convolved, act, terms = conv_forward(after(hidden, w_far), conv_weight, se_down)
-    excite_pre = small_sum(terms)
-
-    gating, scaled, p_fourth, send = scale(role, act, excite_pre, se_up, w_far, middle)
+    terms = gather_small(terms)
+    far = along_chan(after(outer, *terms), MIDDLE)
+    gating, excite_pre, scaled, p_fourth, send = scale(role, act, terms, se_up, w_far, middle)
     came = along_chan(send, OUTER)
-    far = along_chan(after(outer, send), MIDDLE)
     other = along_dp(scaled, 1)
     theirs = [along_dp(piece, 1) for piece in (own, outer)]
     p_own, p_outer, p_third = project(role, 3, scaled, proj_weight)
     (begun,) = input_grad(role, 0, [after(own, p_own), outer], proj_weight)
 
-    far, came = lax.optimization_barrier((far, came, begun))[:2]
-    third, to_far, send = between(
-        second_body, [extent] * 3, role, came, send, far, p_fourth, p_third
-    )
+    (send_far,) = between(
+        far_body, [extent], role, p_third, after(far, begun), micros=FAR_COST
+    )
+    came_far = along_chan(send_far, OUTER)
+    third, to_far = between(second_body, [extent] * 2, role, came, send, p_fourth)
     crossed = along_chan(to_far, MIDDLE)
-    came = along_chan(send, OUTER)
     theirs.append(along_dp(third, 1))
-    pieces = [own, outer, third]
+    pieces = [own, outer, after(third, to_far)]
     x_send, x_keep, y_send, y_keep = weight_grad(role, scaled, other, pieces, theirs)
     x_came, y_came = along_dp(x_send, 2), along_dp(y_send, 4)
     (begun,) = input_grad(role, 2, [after(third, y_send)], proj_weight, begun)
 
-    crossed, came = lax.optimization_barrier((crossed, came, begun))[:2]
+    came_far = after(came_far, begun)
     half = (extent[0], channels // 2)
-    fourth, to_mid, send, give = between(
-        third_body, [extent] * 3 + [half], role, came, crossed, send, p_outer, p_third
-    )
-    crossed = along_chan(to_mid, MIDDLE)
+    fourth, to_mid, give = between(
+        third_body, [extent] * 2 + [half], role, came_far, send_far, p_third
+    )
+    crossed_mid = along_chan(to_mid, MIDDLE)
+    (send,) = between(outer_body, [extent], role, after(crossed, to_mid), p_outer)
     came = along_chan(send, OUTER)
+    crossed = crossed_mid
+    fourth = after(fourth, send)
     upper, lower = weight_grad(role, scaled, other, [fourth], [along_dp(give, 1)])
     upper_came, lower_came = along_dp(upper, 2), along_dp(lower, 4)
     fourth, x_came, y_came = lax.optimization_barrier((fourth, x_came, y_came, lower))[:3]
     scaled_grad, terms = input_grad(
         role, 3, [fourth], proj_weight, begun, act, gating, se_up
     )
-    terms, came, crossed = lax.optimization_barrier((terms, came, crossed))
-    excite_sum = small_sum(terms)
-
+    upper_came = after(upper_came, terms)
     top, to_y, bottom, to_x = merge(
         role, x_keep, x_came, y_keep, y_came, upper, upper_came, lower, lower_came
     )
+    terms, came, crossed = lax.optimization_barrier((terms, came, crossed, to_x))[:3]
+    terms = gather_small(terms)
     (projected,) = between(fourth_body, [shape], role, p_own, came, crossed)
-    excite_sum = after(excite_sum, to_x, projected)
+    terms[0] = after(terms[0], projected)
     grad_hidden = conv_backward(
-        scaled_grad, gating, excite_sum, excite_pre, se_down, convolved, conv_weight, shape
+        scaled_grad, gating, terms, excite_pre, se_down, convolved, conv_weight, shape
     )
     grad_proj = finish(top, along_dp(to_y, 4), bottom, along_dp(to_x, 2))
     return (from_cells(projected), from_cells(grad_hidden), grad_proj)
@@ -725,6 +752,7 @@
     images = shape[2]
     convolved, act, terms = conv_forward(hidden, conv_weight, se_down)
     excite_pre = lax.psum(terms, "chan")
+    nothing = jnp.zeros_like(excite_pre)
     gating = jax.nn.sigmoid(jnp.dot(jax.nn.silu(excite_pre), se_up.astype(F32), precision=HIGHEST))
     act_float = act.astype(F32)
     scaled = (act_float * per_row(gating, act.shape[0])).astype(BF16)
@@ -739,8 +767,9 @@
     gate_grad = image_sum(scaled_grad * act_float, images)
     pre_grad = gate_grad * gating * (1.0 - gating)
     excite_sum = lax.psum(jnp.dot(pre_grad, se_up.astype(F32).T, precision=HIGHEST), "chan")
+    terms = [excite_sum] + [nothing] * 3
     grad_hidden = conv_backward(
-        scaled_grad, gating, excite_sum, excite_pre, se_down, convolved, conv_weight, shape
+        scaled_grad, gating, terms, excite_pre, se_down, convolved, conv_weight, shape
     )
     return (from_cells(projected.reshape(shape)), from_cells(grad_hidden), grad_proj)
 

time: 100 us -> 94.7 us (0.947)
  starting transfers between devices: 37.2 us -> 31.3 us
  waiting for transfers between devices: 16 us -> 20.3 us
  local copies, waits for them, and re-layouts: 7.47 us -> 5.57 us
  Pallas kernels: 36.7 us -> 35.7 us
    ppermute x14, starting transfers between devices: 27.3 us -> 22.2 us  [along_chan(): return lax.ppermute(array, 'chan', pairs)]
    ppermute x11, waiting for transfers between devices: 0.03 us -> 3.58 us  [along_dp(): return lax.ppermute(array, 'dp', [(i, i ^ bit) for i in range(8)])]
    unnamed x22 -> x16, local copies, waits for them, and re-layouts: 4.85 us -> 2.79 us
    pallas_call x1, Pallas kernels: 6.39 us -> 4.86 us  [conv_forward(): pl.pallas_call(functools.partial(conv_forward_body, height=height, width=...]
    pallas_call x3 -> x5, Pallas kernels: 3.28 us -> 4.4 us  [between(): pl.pallas_call(body, grid=(1,), in_specs=[pl.BlockSpec(memory_space=pltpu...]
  transfers between devices with their start and end apart: 25 -> 25, of which waited for: 6 -> 9; matrix products, arithmetic and copies ran while one was open for 3% -> 3% of each run, Pallas kernels for 36% -> 37%
where the time goes in v4:
time: 94.7 us; the launch traced here: 94.4 us
  Pallas kernels  35.7 us (38%)
  starting transfers between devices  31.3 us (33%)
  waiting for transfers between devices  20.3 us (21%)
  local copies, waits for them, and re-layouts  5.57 us (6%)
  between operations  1.58 us (2%)
    ppermute x14, starting transfers between devices, along_chan(): return lax.ppermute(array, 'chan', pairs)  22.2 us
    ppermute x14, waiting for transfers between devices, along_chan(): return lax.ppermute(array, 'chan', pairs)  16.7 us
    ppermute x11, starting transfers between devices, along_dp(): return lax.ppermute(array, 'dp', [(i, i ^ bit) for i in range(8)])  9.11 us
    pallas_call x3, Pallas kernels, input_grad(): pl.pallas_call(functools.partial(input_grad_body, first=first, pieces=len...  6.94 us
    pallas_call x2, Pallas kernels, weight_grad(): pl.pallas_call(functools.partial(weight_grad_body, pieces=pieces), grid_s...  5.86 us
    pallas_call x1, Pallas kernels, conv_backward(): pl.pallas_call(functools.partial(conv_backward_body, height=height, width...  5.28 us
    pallas_call x1, Pallas kernels, conv_forward(): pl.pallas_call(functools.partial(conv_forward_body, height=height, width=...  4.86 us
    pallas_call x5, Pallas kernels, between(): pl.pallas_call(body, grid=(1,), in_specs=[pl.BlockSpec(memory_space=pltpu...  4.4 us
  transfers between devices with their start and end apart: 25, of which 9 were waited for; matrix products, arithmetic and copies ran while one was open for 3% of the time, Pallas kernels for 37%

profile of v4, /device:TPU:0, one launch (start us, length us, event | category | flops | bytes accessed | tf_op | source)
XLA Modules:
  0.0 94.4 jit_solution(498302774565965068)
XLA Ops:
  1.3 5.9 %collective-permute-start.4 = (bf16[14,14,2,768]{3,2,1,0:T(2,128)(2,1)}, bf16[14,14,2,768]{3,2,1,0:T(2,128)(2,1)S(1)}, u32[]{:S(2)}, u32[]{:S(2)}) collective-permute-start(bf16[14,14,2,768]{3,2,1,0:T(2,128)(2,1)} %bitcast.11), channel_id=1, source_target_pairs={{0,1},{1,0},{2,3},{3,2},{4,5},{5,4},{6,7},{7,6},{8,9},{9,8},{10,11... | collective-permute-start | bytes 1806344 | tf_op jit(solution)/shard_map/ppermute | solution.py:662
  9.2 1.5 %constant_dynamic-slice_fusion.w_ref = bf16[768,768]{1,0:T(8,128)(2,1)S(1)} fusion(bf16[768,3072]{1,0:T(8,128)(2,1)} %refs_1_.3, s32[]{:T(128)S(6)} %select_n.7), kind=kLoop, calls=%fused_computation | loop fusion | bytes 2359300 | tf_op jit(solution)/shard_map/dynamic_slice | solution.py:695
  10.7 1.7 %copy-done.2 = bf16[3,3,64,768]{3,2,1,0:T(8,128)(2,1)S(1)} copy-done((bf16[3,3,64,768]{3,2,1,0:T(8,128)(2,1)S(1)}, bf16[3,3,64,768]{3,2,1,0:T(8,128)(2,1)}, u32[]{:S(2)}) %copy-start.2) | copy-done | bytes 884760
  12.4 1.1 %copy-done.4 = bf16[2,14,14,768]{3,0,2,1:T(2,128)(2,1)S(1)} copy-done((bf16[2,14,14,768]{3,0,2,1:T(2,128)(2,1)S(1)}, bf16[2,14,14,768]{3,0,2,1:T(2,128)(2,1)}, u32[]{:S(2)}) %copy-start.4) | copy-done | bytes 602136
  13.4 4.9 %conv_forward.1 = (f32[392,768]{1,0:T(8,128)S(1)}, bf16[392,768]{1,0:T(8,128)(2,1)S(1)}, f32[2,1024]{1,0:T(2,128)S(1)}) custom-call(bf16[14,14,2,768]{3,2,1,0:T(2,128)(2,1)S(1)} %bitcast.9, bf16[3,3,64,768]{3,2,1,0:T(8,128)(2,1)S(1)} %copy-done.2, bf16[768,1024]{1,0:T(8,128)(2,1)} %down_hbm.3), custom_call_target="tpu_custom_call" | custom-call | flops 1035000000 | bytes 1 | tf_op jit(solution)/shard_map/conv_forward/pallas_call | solution.py:162
  18.4 2.4 %collective-permute-start.1 = (f32[2,1024]{1,0:T(2,128)S(1)}, f32[2,1024]{1,0:T(2,128)S(1)}, u32[]{:S(2)}, u32[]{:S(2)}) collective-permute-start(f32[2,1024]{1,0:T(2,128)S(1)} %get-tuple-element.50.own_ref), channel_id=1, source_target_pairs={{0,3},{3,0},{1,2},{2,1},{4,7},{7,4},{5,6},{6,5},{8,11},{11,8},{9,1... | collective-permute-start | bytes 24584 | tf_op jit(solution)/shard_map/ppermute | solution.py:662
  20.8 1.1 %collective-permute-start = (f32[2,1024]{1,0:T(2,128)S(1)}, f32[2,1024]{1,0:T(2,128)S(1)}, u32[]{:S(2)}, u32[]{:S(2)}) collective-permute-start(f32[2,1024]{1,0:T(2,128)S(1)} %get-tuple-element.50.own_ref), channel_id=1, source_target_pairs={{0,1},{1,0},{2,3},{3,2},{4,5},{5,4},{6,7},{7,6},{8,9},{9,8},{10,11... | collective-permute-start | bytes 24584 | tf_op jit(solution)/shard_map/ppermute | solution.py:662
  24.4 2.2 %scale.1 = (f32[2,768]{1,0:T(2,128)S(1)}, f32[2,1024]{1,0:T(2,128)S(1)}, bf16[392,768]{1,0:T(8,128)(2,1)S(1)}, bf16[392,768]{1,0:T(8,128)(2,1)S(1)}, bf16[392,768]{1,0:T(8,128)(2,1)S(1)}) custom-call(s32[8]{0:T(128)S(1)} %get-tuple-element.93.role_ref.order_ref.place_ref, bf16[392,768]{1,0:T(8,128)(2,1)S(1)} %get-tuple-element.49.act_ref.refs_3_, ...), custom_call_target="tpu_custom_call" | custom-call | flops 1035000000 | bytes 1 | tf_op jit(solution)/shard_map/scale/pallas_call | solution.py:316
  26.6 1.2 %collective-permute-start.7 = (bf16[392,768]{1,0:T(8,128)(2,1)S(1)}, bf16[392,768]{1,0:T(8,128)(2,1)S(1)}, u32[]{:S(2)}, u32[]{:S(2)}) collective-permute-start(bf16[392,768]{1,0:T(8,128)(2,1)S(1)} %get-tuple-element.57.held), channel_id=1, source_target_pairs={{0,1},{1,0},{2,3},{3,2},{4,5},{5,4},{6,7},{7,6},{8,9},{9,8},{10,11... | collective-permute-start | bytes 1806344 | tf_op jit(solution)/shard_map/ppermute | solution.py:662
  29.1 3.9 %project.1 = (bf16[392,768]{1,0:T(8,128)(2,1)S(1)}, bf16[392,768]{1,0:T(8,128)(2,1)S(1)}, bf16[392,768]{1,0:T(8,128)(2,1)S(1)}) custom-call(s32[8]{0:T(128)S(1)} %get-tuple-element.93.role_ref.order_ref.place_ref, bf16[392,768]{1,0:T(8,128)(2,1)S(1)} %get-tuple-element.51.scaled_hbm.own_ref, bf16[768,3072]{1,0:T(8,128)(2,1)S(1)} %bitcast.8), custom_call_target="tpu_custom_call" | custom-call | flops 1035000000 | bytes 1 | tf_op jit(solution)/shard_map/project/pallas_call | solution.py:360
  33.2 6.9 %collective-permute-done.7.came = bf16[392,768]{1,0:T(8,128)(2,1)S(1)} collective-permute-done((bf16[392,768]{1,0:T(8,128)(2,1)S(1)}, bf16[392,768]{1,0:T(8,128)(2,1)S(1)}, u32[]{:S(2)}, u32[]{:S(2)}) %collective-permute-start.7) | collective-permute-done | bytes 602144 | tf_op jit(solution)/shard_map/ppermute | solution.py:662
  40.8 2.7 %input_grad.2.refs_2_ = f32[392,768]{1,0:T(8,128)S(1)} custom-call(s32[8]{0:T(128)S(1)} %get-tuple-element.93.role_ref.order_ref.place_ref, bf16[14,14,2,768]{3,2,1,0:T(2,128)(2,1)S(1)} %bitcast.13, bf16[14,14,2,768]{3,2,1,0:T(2,128)(2,1)S(1)} %collective-permute-done.4.refs_1_, bf16[768,3072]{1,0:T(8,128)(2,1)S(1)} %bitcast.8), custom_call_target="tpu_custom_call" | custom-call | flops 3449999872 | bytes 1 | tf_op jit(solution)/shard_map/input_grad/pallas_call | solution.py:507
  45.9 4.3 %weight_grad.1 = (bf16[2,384,384]{2,1,0:T(8,128)(2,1)S(1)}, bf16[2,384,384]{2,1,0:T(8,128)(2,1)S(1)}, bf16[2,384,384]{2,1,0:T(8,128)(2,1)S(1)}, bf16[2,384,384]{2,1,0:T(8,128)(2,1)S(1)}) custom-call(s32[8]{0:T(128)S(1)} %get-tuple-element.93.role_ref.order_ref.place_ref, bf16[392,768]{1,0:T(8,128)(2,1)S(1)} %get-tuple-element.51.scaled_hbm.own_ref, ...), custom_call_target="tpu_custom_call" | custom-call | flops 2070000000 | bytes 1 | tf_op jit(solution)/shard_map/weight_grad/pallas_call | solution.py:580
  50.2 1.6 %collective-permute-start.13 = (bf16[2,384,384]{2,1,0:T(8,128)(2,1)S(1)}, bf16[2,384,384]{2,1,0:T(8,128)(2,1)S(1)}, u32[]{:S(2)}, u32[]{:S(2)}) collective-permute-start(bf16[2,384,384]{2,1,0:T(8,128)(2,1)S(1)} %get-tuple-element.69), channel_id=1, source_target_pairs={{0,8},{4,12},{8,0},{12,4},{16,24},{20,28},{24,16},{28,20},{1,9},{5... | collective-permute-start | bytes 1769480 | tf_op jit(solution)/shard_map/ppermute | solution.py:666
  51.8 1.5 %collective-permute-start.14 = (bf16[2,384,384]{2,1,0:T(8,128)(2,1)S(1)}, bf16[2,384,384]{2,1,0:T(8,128)(2,1)S(1)}, u32[]{:S(2)}, u32[]{:S(2)}) collective-permute-start(bf16[2,384,384]{2,1,0:T(8,128)(2,1)S(1)} %get-tuple-element.60), channel_id=1, source_target_pairs={{0,16},{4,20},{8,24},{12,28},{16,0},{20,4},{24,8},{28,12},{1,17},{... | collective-permute-start | bytes 1769480 | tf_op jit(solution)/shard_map/ppermute | solution.py:666
  53.3 1.6 %input_grad.3.refs_2_ = f32[392,768]{1,0:T(8,128)S(1)} custom-call(s32[8]{0:T(128)S(1)} %get-tuple-element.93.role_ref.order_ref.place_ref, bf16[392,768]{1,0:T(8,128)(2,1)S(1)} %get-tuple-element.61.refs_2_.refs_0_, bf16[768,3072]{1,0:T(8,128)(2,1)S(1)} %bitcast.8, f32[392,768]{1,0:T(8,128)S(1)} %input_grad.2.refs_2_), custom_call_target="tpu_custom_call" | custom-call | flops 6900000 | bytes 1 | tf_op jit(solution)/shard_map/input_grad/pallas_call | solution.py:507
  54.8 5.4 %collective-permute-done.6.came = bf16[392,768]{1,0:T(8,128)(2,1)S(1)} collective-permute-done((bf16[392,768]{1,0:T(8,128)(2,1)S(1)}, bf16[392,768]{1,0:T(8,128)(2,1)S(1)}, u32[]{:S(2)}, u32[]{:S(2)}) %collective-permute-start.6) | collective-permute-done | bytes 602144 | tf_op jit(solution)/shard_map/ppermute | solution.py:662
  61.7 2.9 %collective-permute-start.16 = (bf16[392,768]{1,0:T(8,128)(2,1)S(1)}, bf16[392,768]{1,0:T(8,128)(2,1)S(1)}, u32[]{:S(2)}, u32[]{:S(2)}) collective-permute-start(bf16[392,768]{1,0:T(8,128)(2,1)S(1)} %outer_turn.1), channel_id=1, source_target_pairs={{0,1},{1,0},{2,3},{3,2},{4,5},{5,4},{6,7},{7,6},{8,9},{9,8},{10,11... | collective-permute-start | bytes 1806344 | tf_op jit(solution)/shard_map/ppermute | solution.py:662
  65.3 1.6 %weight_grad_more.1 = (bf16[384,384]{1,0:T(8,128)(2,1)S(1)}, bf16[384,384]{1,0:T(8,128)(2,1)S(1)}) custom-call(s32[8]{0:T(128)S(1)} %get-tuple-element.93.role_ref.order_ref.place_ref, bf16[392,768]{1,0:T(8,128)(2,1)S(1)} %get-tuple-element.51.scaled_hbm.own_ref, bf16[392,768]{1,0:T(8,128)(2,1)S(1)} %collective-permute-done.8.other_ref, ...), custom_call_target="tpu_custom_call" | custom-call | flops 6900000 | bytes 1 | tf_op jit(solution)/shard_map/weight_grad_more/pallas_call | solution.py:580
  66.9 1.6 %collective-permute-start.18 = (bf16[384,384]{1,0:T(8,128)(2,1)S(1)}, bf16[384,384]{1,0:T(8,128)(2,1)S(1)}, u32[]{:S(2)}, u32[]{:S(2)}) collective-permute-start(bf16[384,384]{1,0:T(8,128)(2,1)S(1)} %get-tuple-element.79.refs_4_), channel_id=1, source_target_pairs={{0,8},{4,12},{8,0},{12,4},{16,24},{20,28},{24,16},{28,20},{1,9},{5... | collective-permute-start | bytes 884744 | tf_op jit(solution)/shard_map/ppermute | solution.py:666
  68.5 1.5 %collective-permute-start.19 = (bf16[384,384]{1,0:T(8,128)(2,1)S(1)}, bf16[384,384]{1,0:T(8,128)(2,1)S(1)}, u32[]{:S(2)}, u32[]{:S(2)}) collective-permute-start(bf16[384,384]{1,0:T(8,128)(2,1)S(1)} %get-tuple-element.71.refs_6_), channel_id=1, source_target_pairs={{0,16},{4,20},{8,24},{12,28},{16,0},{20,4},{24,8},{28,12},{1,17},{... | collective-permute-start | bytes 884744 | tf_op jit(solution)/shard_map/ppermute | solution.py:666
  70.0 2.7 %input_grad_last.1 = (f32[392,768]{1,0:T(8,128)S(1)}, f32[2,1024]{1,0:T(2,128)S(1)}) custom-call(s32[8]{0:T(128)S(1)} %get-tuple-element.93.role_ref.order_ref.place_ref, bf16[392,768]{1,0:T(8,128)(2,1)S(1)} %get-tuple-element.72.refs_0_, bf16[768,3072]{1,0:T(8,128)(2,1)S(1)} %bitcast.8, f32[392,768]{1,0:T(8,128)S(1)} %input_grad.3.refs_2_, ...), custom_call_target="tpu_custom_call" | custom-call | flops 3449999872 | bytes 1 | tf_op jit(solution)/shard_map/input_grad_last/pallas_call | solution.py:507
  72.7 2.3 %collective-permute-done.18.refs_5_ = bf16[384,384]{1,0:T(8,128)(2,1)S(1)} collective-permute-done((bf16[384,384]{1,0:T(8,128)(2,1)S(1)}, bf16[384,384]{1,0:T(8,128)(2,1)S(1)}, u32[]{:S(2)}, u32[]{:S(2)}) %collective-permute-start.18) | collective-permute-done | bytes 294944 | tf_op jit(solution)/shard_map/ppermute | solution.py:666
  75.0 1.2 %collective-permute-done.19.refs_7_ = bf16[384,384]{1,0:T(8,128)(2,1)S(1)} collective-permute-done((bf16[384,384]{1,0:T(8,128)(2,1)S(1)}, bf16[384,384]{1,0:T(8,128)(2,1)S(1)}, u32[]{:S(2)}, u32[]{:S(2)}) %collective-permute-start.19) | collective-permute-done | bytes 294944 | tf_op jit(solution)/shard_map/ppermute | solution.py:666
  76.2 1.1 %merge.1 = (f32[384,384]{1,0:T(8,128)S(1)}, bf16[384,384]{1,0:T(8,128)(2,1)S(1)}, f32[384,384]{1,0:T(8,128)S(1)}, bf16[384,384]{1,0:T(8,128)(2,1)S(1)}) custom-call(s32[8]{0:T(128)S(1)} %get-tuple-element.93.role_ref.order_ref.place_ref, bf16[2,384,384]{2,1,0:T(8,128)(2,1)S(1)} %get-tuple-element.75.refs_0_, ...), custom_call_target="tpu_custom_call" | custom-call | flops 690000000 | bytes 1 | tf_op jit(solution)/shard_map/merge/pallas_call | solution.py:620
  77.4 1.6 %collective-permute-start.23 = (bf16[384,384]{1,0:T(8,128)(2,1)S(1)}, bf16[384,384]{1,0:T(8,128)(2,1)S(1)}, u32[]{:S(2)}, u32[]{:S(2)}) collective-permute-start(bf16[384,384]{1,0:T(8,128)(2,1)S(1)} %get-tuple-element.90), channel_id=1, source_target_pairs={{0,16},{4,20},{8,24},{12,28},{16,0},{20,4},{24,8},{28,12},{1,17},{... | collective-permute-start | bytes 884744 | tf_op jit(solution)/shard_map/ppermute | solution.py:666
  79.5 2.7 %collective-permute-start.22 = (f32[2,1024]{1,0:T(2,128)S(1)}, f32[2,1024]{1,0:T(2,128)S(1)}, u32[]{:S(2)}, u32[]{:S(2)}) collective-permute-start(f32[2,1024]{1,0:T(2,128)S(1)} %get-tuple-element.86.own_ref), channel_id=1, source_target_pairs={{0,2},{2,0},{1,3},{3,1},{4,6},{6,4},{5,7},{7,5},{8,10},{10,8},{9,1... | collective-permute-start | bytes 24584 | tf_op jit(solution)/shard_map/ppermute | solution.py:662
  82.2 2.1 %collective-permute-start.21 = (f32[2,1024]{1,0:T(2,128)S(1)}, f32[2,1024]{1,0:T(2,128)S(1)}, u32[]{:S(2)}, u32[]{:S(2)}) collective-permute-start(f32[2,1024]{1,0:T(2,128)S(1)} %get-tuple-element.86.own_ref), channel_id=1, source_target_pairs={{0,3},{3,0},{1,2},{2,1},{4,7},{7,4},{5,6},{6,5},{8,11},{11,8},{9,1... | collective-permute-start | bytes 24584 | tf_op jit(solution)/shard_map/ppermute | solution.py:662
  84.3 1.7 %fourth_turn.1 = bf16[14,14,2,768]{3,2,1,0:T(2,128)(2,1)} custom-call(s32[8]{0:T(128)S(1)} %get-tuple-element.93.role_ref.order_ref.place_ref, bf16[392,768]{1,0:T(8,128)(2,1)S(1)} %get-tuple-element.52.p_own, bf16[392,768]{1,0:T(8,128)(2,1)S(1)} %collective-permute-done.16.came, bf16[392,768]{1,0:T(8,128)(2,1)S(1)} %collective-permute-done.17.crossed), custom_call_target="tpu_custom_call" | custom-call | flops 6900000 | bytes 1 | tf_op jit(solution)/shard_map/fourth_turn/pallas_call | solution.py:431
  86.0 1.6 %collective-permute-done.21.across_ref = f32[2,1024]{1,0:T(2,128)S(1)} collective-permute-done((f32[2,1024]{1,0:T(2,128)S(1)}, f32[2,1024]{1,0:T(2,128)S(1)}, u32[]{:S(2)}, u32[]{:S(2)}) %collective-permute-start.21) | collective-permute-done | bytes 8224 | tf_op jit(solution)/shard_map/ppermute | solution.py:662
  88.0 5.3 %conv_backward.1 = bf16[14,14,2,768]{3,2,1,0:T(2,128)(2,1)} custom-call(f32[392,768]{1,0:T(8,128)S(1)} %get-tuple-element.84.grad_ref, f32[2,768]{1,0:T(2,128)S(1)} %get-tuple-element.73.refs_4_.gate_ref, f32[2,1024]{1,0:T(2,128)S(1)} %get-tuple-element.86.own_ref, f32[2,1024]{1,0:T(2,128)S(1)} %collective-permute-done.20.near_ref, ...), custom_call_target="tpu_custom_call" | custom-call | flops 1035000000 | bytes 1 | tf_op jit(solution)/shard_map/conv_backward/pallas_call | solution.py:240
  93.3 1.2 %finish.1 = f32[768,384]{1,0:T(8,128)} custom-call(f32[384,384]{1,0:T(8,128)S(1)} %get-tuple-element.89.top, bf16[384,384]{1,0:T(8,128)(2,1)S(1)} %collective-permute-done.23.top_came, f32[384,384]{1,0:T(8,128)S(1)} %get-tuple-element.91.bottom, bf16[384,384]{1,0:T(8,128)(2,1)S(1)} %collective-permute-done.24.bottom_came), custom_call_target="tpu_custom_call" | custom-call | flops 690000000 | bytes 1 | tf_op jit(solution)/shard_map/finish/pallas_call | solution.py:641
  (54 shorter events, 12.1 us)
Async XLA Ops:
  0.6 23.8 %collective-permute-start.3 = (bf16[14,14,2,768]{3,2,1,0:T(2,128)(2,1)}, bf16[14,14,2,768]{3,2,1,0:T(2,128)(2,1)S(1)}, u32[]{:S(2)}, u32[]{:S(2)}) collective-permute-start(bf16[14,14,2,768]{3,2,1,0:T(2,128)(2,1)} %bitcast.10), channel_id=1, source_target_pairs={{1,2},{2,1},{5,6},{6,5},{9,10},{10,9},{13,14},{14,13},{17,18},{18,... | collective-permute-start | bytes 1806344 | tf_op jit(solution)/shard_map/ppermute | solution.py:662
  1.3 26.5 %collective-permute-start.4 = (bf16[14,14,2,768]{3,2,1,0:T(2,128)(2,1)}, bf16[14,14,2,768]{3,2,1,0:T(2,128)(2,1)S(1)}, u32[]{:S(2)}, u32[]{:S(2)}) collective-permute-start(bf16[14,14,2,768]{3,2,1,0:T(2,128)(2,1)} %bitcast.11), channel_id=1, source_target_pairs={{0,1},{1,0},{2,3},{3,2},{4,5},{5,4},{6,7},{7,6},{8,9},{9,8},{10,11... | collective-permute-start | bytes 1806344 | tf_op jit(solution)/shard_map/ppermute | solution.py:662
  9.1 15.3 %copy-start = (bf16[1024,768]{1,0:T(8,128)(2,1)S(1)}, bf16[1024,768]{1,0:T(8,128)(2,1)}, u32[]{:S(2)}) copy-start(bf16[1024,768]{1,0:T(8,128)(2,1)} %refs_5_.1) | copy-start | bytes 4718596
  9.2 20.0 %slice-start = ((s8[4718592]{0:T(1024)(128)(4,1)}), s8[4194304]{0:T(1024)(128)(4,1)S(1)}, s32[]{:S(2)}) async-start(s8[4718592]{0:T(1024)(128)(4,1)} %bitcast.7), calls=%async_computation | async-start | bytes 8388608
  10.7 1.7 %copy-start.2 = (bf16[3,3,64,768]{3,2,1,0:T(8,128)(2,1)S(1)}, bf16[3,3,64,768]{3,2,1,0:T(8,128)(2,1)}, u32[]{:S(2)}) copy-start(bf16[3,3,64,768]{3,2,1,0:T(8,128)(2,1)} %w_hbm.5) | copy-start | bytes 2654212
  13.4 15.7 %slice-start.1 = ((s8[4718592]{0:T(1024)(128)(4,1)}), s8[524288]{0:T(1024)(128)(4,1)S(1)}, s32[]{:S(2)}) async-start(s8[4718592]{0:T(1024)(128)(4,1)} %bitcast.7), calls=%async_computation.1 | async-start | bytes 1048576
  18.3 4.6 %collective-permute-start.2 = (f32[2,1024]{1,0:T(2,128)S(1)}, f32[2,1024]{1,0:T(2,128)S(1)}, u32[]{:S(2)}, u32[]{:S(2)}) collective-permute-start(f32[2,1024]{1,0:T(2,128)S(1)} %get-tuple-element.50.own_ref), channel_id=1, source_target_pairs={{0,2},{2,0},{1,3},{3,1},{4,6},{6,4},{5,7},{7,5},{8,10},{10,8},{9,1... | collective-permute-start | bytes 24584 | tf_op jit(solution)/shard_map/ppermute | solution.py:662
  18.4 5.5 %collective-permute-start.1 = (f32[2,1024]{1,0:T(2,128)S(1)}, f32[2,1024]{1,0:T(2,128)S(1)}, u32[]{:S(2)}, u32[]{:S(2)}) collective-permute-start(f32[2,1024]{1,0:T(2,128)S(1)} %get-tuple-element.50.own_ref), channel_id=1, source_target_pairs={{0,3},{3,0},{1,2},{2,1},{4,7},{7,4},{5,6},{6,5},{8,11},{11,8},{9,1... | collective-permute-start | bytes 24584 | tf_op jit(solution)/shard_map/ppermute | solution.py:662
  20.8 3.7 %collective-permute-start = (f32[2,1024]{1,0:T(2,128)S(1)}, f32[2,1024]{1,0:T(2,128)S(1)}, u32[]{:S(2)}, u32[]{:S(2)}) collective-permute-start(f32[2,1024]{1,0:T(2,128)S(1)} %get-tuple-element.50.own_ref), channel_id=1, source_target_pairs={{0,1},{1,0},{2,3},{3,2},{4,5},{5,4},{6,7},{7,6},{8,9},{9,8},{10,11... | collective-permute-start | bytes 24584 | tf_op jit(solution)/shard_map/ppermute | solution.py:662
  24.4 4.1 %copy-start.5 = (bf16[2,14,14,768]{3,0,2,1:T(2,128)(2,1)S(1)}, bf16[2,14,14,768]{3,0,2,1:T(2,128)(2,1)}, u32[]{:S(2)}) copy-start(bf16[2,14,14,768]{3,0,2,1:T(2,128)(2,1)} %param.12) | copy-start | bytes 1806340
  26.6 13.4 %collective-permute-start.7 = (bf16[392,768]{1,0:T(8,128)(2,1)S(1)}, bf16[392,768]{1,0:T(8,128)(2,1)S(1)}, u32[]{:S(2)}, u32[]{:S(2)}) collective-permute-start(bf16[392,768]{1,0:T(8,128)(2,1)S(1)} %get-tuple-element.57.held), channel_id=1, source_target_pairs={{0,1},{1,0},{2,3},{3,2},{4,5},{5,4},{6,7},{7,6},{8,9},{9,8},{10,11... | collective-permute-start | bytes 1806344 | tf_op jit(solution)/shard_map/ppermute | solution.py:662
  27.8 15.7 %collective-permute-start.5 = (bf16[14,14,2,768]{3,2,1,0:T(2,128)(2,1)S(1)}, bf16[14,14,2,768]{3,2,1,0:T(2,128)(2,1)S(1)}, u32[]{:S(2)}, u32[]{:S(2)}) collective-permute-start(bf16[14,14,2,768]{3,2,1,0:T(2,128)(2,1)S(1)} %collective-permute-done.4.refs_1_), channel_id=1, source_target_pairs={{1,2},{2,1},{5,6},{6,5},{9,10},{10,9},{13,14},{14,13},{17,18},{18,... | collective-permute-start | bytes 1806344 | tf_op jit(solution)/shard_map/ppermute | solution.py:662
  28.6 16.6 %collective-permute-start.9 = (bf16[14,14,2,768]{3,2,1,0:T(2,128)(2,1)S(1)}, bf16[14,14,2,768]{3,2,1,0:T(2,128)(2,1)S(1)}, u32[]{:S(2)}, u32[]{:S(2)}) collective-permute-start(bf16[14,14,2,768]{3,2,1,0:T(2,128)(2,1)S(1)} %bitcast.12), channel_id=1, source_target_pairs={{0,4},{4,0},{8,12},{12,8},{16,20},{20,16},{24,28},{28,24},{1,5},{5... | collective-permute-start | bytes 1806344 | tf_op jit(solution)/shard_map/ppermute | solution.py:666
  28.6 17.3 %collective-permute-start.8 = (bf16[392,768]{1,0:T(8,128)(2,1)S(1)}, bf16[392,768]{1,0:T(8,128)(2,1)S(1)}, u32[]{:S(2)}, u32[]{:S(2)}) collective-permute-start(bf16[392,768]{1,0:T(8,128)(2,1)S(1)} %get-tuple-element.51.scaled_hbm.own_ref), channel_id=1, source_target_pairs={{0,4},{4,0},{8,12},{12,8},{16,20},{20,16},{24,28},{28,24},{1,5},{5... | collective-permute-start | bytes 1806344 | tf_op jit(solution)/shard_map/ppermute | solution.py:666
  33.0 12.9 %collective-permute-start.10 = (bf16[14,14,2,768]{3,2,1,0:T(2,128)(2,1)S(1)}, bf16[14,14,2,768]{3,2,1,0:T(2,128)(2,1)S(1)}, u32[]{:S(2)}, u32[]{:S(2)}) collective-permute-start(bf16[14,14,2,768]{3,2,1,0:T(2,128)(2,1)S(1)} %collective-permute-done.4.refs_1_), channel_id=1, source_target_pairs={{0,4},{4,0},{8,12},{12,8},{16,20},{20,16},{24,28},{28,24},{1,5},{5... | collective-permute-start | bytes 1806344 | tf_op jit(solution)/shard_map/ppermute | solution.py:666
  40.8 5.1 %collective-permute-start.11 = (bf16[392,768]{1,0:T(8,128)(2,1)S(1)}, bf16[392,768]{1,0:T(8,128)(2,1)S(1)}, u32[]{:S(2)}, u32[]{:S(2)}) collective-permute-start(bf16[392,768]{1,0:T(8,128)(2,1)S(1)} %get-tuple-element.61.refs_2_.refs_0_), channel_id=1, source_target_pairs={{0,4},{4,0},{8,12},{12,8},{16,20},{20,16},{24,28},{28,24},{1,5},{5... | collective-permute-start | bytes 1806344 | tf_op jit(solution)/shard_map/ppermute | solution.py:666
  44.2 16.1 %collective-permute-start.6 = (bf16[392,768]{1,0:T(8,128)(2,1)S(1)}, bf16[392,768]{1,0:T(8,128)(2,1)S(1)}, u32[]{:S(2)}, u32[]{:S(2)}) collective-permute-start(bf16[392,768]{1,0:T(8,128)(2,1)S(1)} %far_turn.1.held), channel_id=1, source_target_pairs={{0,1},{1,0},{2,3},{3,2},{4,5},{5,4},{6,7},{7,6},{8,9},{9,8},{10,11... | collective-permute-start | bytes 1806344 | tf_op jit(solution)/shard_map/ppermute | solution.py:662
  45.2 15.9 %collective-permute-start.12 = (bf16[392,768]{1,0:T(8,128)(2,1)S(1)}, bf16[392,768]{1,0:T(8,128)(2,1)S(1)}, u32[]{:S(2)}, u32[]{:S(2)}) collective-permute-start(bf16[392,768]{1,0:T(8,128)(2,1)S(1)} %get-tuple-element.64), channel_id=1, source_target_pairs={{1,2},{2,1},{5,6},{6,5},{9,10},{10,9},{13,14},{14,13},{17,18},{18,... | collective-permute-start | bytes 1806344 | tf_op jit(solution)/shard_map/ppermute | solution.py:662
  50.2 18.3 %collective-permute-start.13 = (bf16[2,384,384]{2,1,0:T(8,128)(2,1)S(1)}, bf16[2,384,384]{2,1,0:T(8,128)(2,1)S(1)}, u32[]{:S(2)}, u32[]{:S(2)}) collective-permute-start(bf16[2,384,384]{2,1,0:T(8,128)(2,1)S(1)} %get-tuple-element.69), channel_id=1, source_target_pairs={{0,8},{4,12},{8,0},{12,4},{16,24},{20,28},{24,16},{28,20},{1,9},{5... | collective-permute-start | bytes 1769480 | tf_op jit(solution)/shard_map/ppermute | solution.py:666
  51.8 18.2 %collective-permute-start.14 = (bf16[2,384,384]{2,1,0:T(8,128)(2,1)S(1)}, bf16[2,384,384]{2,1,0:T(8,128)(2,1)S(1)}, u32[]{:S(2)}, u32[]{:S(2)}) collective-permute-start(bf16[2,384,384]{2,1,0:T(8,128)(2,1)S(1)} %get-tuple-element.60), channel_id=1, source_target_pairs={{0,16},{4,20},{8,24},{12,28},{16,0},{20,4},{24,8},{28,12},{1,17},{... | collective-permute-start | bytes 1769480 | tf_op jit(solution)/shard_map/ppermute | solution.py:666
  61.0 4.3 %collective-permute-start.15 = (bf16[392,384]{1,0:T(8,128)(2,1)S(1)}, bf16[392,384]{1,0:T(8,128)(2,1)S(1)}, u32[]{:S(2)}, u32[]{:S(2)}) collective-permute-start(bf16[392,384]{1,0:T(8,128)(2,1)S(1)} %get-tuple-element.70), channel_id=1, source_target_pairs={{0,4},{4,0},{8,12},{12,8},{16,20},{20,16},{24,28},{28,24},{1,5},{5... | collective-permute-start | bytes 903176 | tf_op jit(solution)/shard_map/ppermute | solution.py:666
  61.7 17.8 %collective-permute-start.16 = (bf16[392,768]{1,0:T(8,128)(2,1)S(1)}, bf16[392,768]{1,0:T(8,128)(2,1)S(1)}, u32[]{:S(2)}, u32[]{:S(2)}) collective-permute-start(bf16[392,768]{1,0:T(8,128)(2,1)S(1)} %outer_turn.1), channel_id=1, source_target_pairs={{0,1},{1,0},{2,3},{3,2},{4,5},{5,4},{6,7},{7,6},{8,9},{9,8},{10,11... | collective-permute-start | bytes 1806344 | tf_op jit(solution)/shard_map/ppermute | solution.py:662
  64.6 14.9 %collective-permute-start.17 = (bf16[392,768]{1,0:T(8,128)(2,1)S(1)}, bf16[392,768]{1,0:T(8,128)(2,1)S(1)}, u32[]{:S(2)}, u32[]{:S(2)}) collective-permute-start(bf16[392,768]{1,0:T(8,128)(2,1)S(1)} %get-tuple-element.65), channel_id=1, source_target_pairs={{1,2},{2,1},{5,6},{6,5},{9,10},{10,9},{13,14},{14,13},{17,18},{18,... | collective-permute-start | bytes 1806344 | tf_op jit(solution)/shard_map/ppermute | solution.py:662
  66.9 8.1 %collective-permute-start.18 = (bf16[384,384]{1,0:T(8,128)(2,1)S(1)}, bf16[384,384]{1,0:T(8,128)(2,1)S(1)}, u32[]{:S(2)}, u32[]{:S(2)}) collective-permute-start(bf16[384,384]{1,0:T(8,128)(2,1)S(1)} %get-tuple-element.79.refs_4_), channel_id=1, source_target_pairs={{0,8},{4,12},{8,0},{12,4},{16,24},{20,28},{24,16},{28,20},{1,9},{5... | collective-permute-start | bytes 884744 | tf_op jit(solution)/shard_map/ppermute | solution.py:666
  68.5 7.7 %collective-permute-start.19 = (bf16[384,384]{1,0:T(8,128)(2,1)S(1)}, bf16[384,384]{1,0:T(8,128)(2,1)S(1)}, u32[]{:S(2)}, u32[]{:S(2)}) collective-permute-start(bf16[384,384]{1,0:T(8,128)(2,1)S(1)} %get-tuple-element.71.refs_6_), channel_id=1, source_target_pairs={{0,16},{4,20},{8,24},{12,28},{16,0},{20,4},{24,8},{28,12},{1,17},{... | collective-permute-start | bytes 884744 | tf_op jit(solution)/shard_map/ppermute | solution.py:666
  76.2 11.7 %copy-start.3 = (bf16[3,3,64,768]{3,2,1,0:T(8,128)(2,1)S(1)}, bf16[3,3,64,768]{3,2,1,0:T(8,128)(2,1)}, u32[]{:S(2)}) copy-start(bf16[3,3,64,768]{3,2,1,0:T(8,128)(2,1)} %w_hbm.5) | copy-start | bytes 2654212
  77.4 15.9 %collective-permute-start.23 = (bf16[384,384]{1,0:T(8,128)(2,1)S(1)}, bf16[384,384]{1,0:T(8,128)(2,1)S(1)}, u32[]{:S(2)}, u32[]{:S(2)}) collective-permute-start(bf16[384,384]{1,0:T(8,128)(2,1)S(1)} %get-tuple-element.90), channel_id=1, source_target_pairs={{0,16},{4,20},{8,24},{12,28},{16,0},{20,4},{24,8},{28,12},{1,17},{... | collective-permute-start | bytes 884744 | tf_op jit(solution)/shard_map/ppermute | solution.py:666
  79.0 9.0 %copy-start.1 = (bf16[768,1024]{1,0:T(8,128)(2,1)S(1)}, bf16[768,1024]{1,0:T(8,128)(2,1)}, u32[]{:S(2)}) copy-start(bf16[768,1024]{1,0:T(8,128)(2,1)} %down_hbm.3) | copy-start | bytes 4718596
  79.0 14.3 %collective-permute-start.24 = (bf16[384,384]{1,0:T(8,128)(2,1)S(1)}, bf16[384,384]{1,0:T(8,128)(2,1)S(1)}, u32[]{:S(2)}, u32[]{:S(2)}) collective-permute-start(bf16[384,384]{1,0:T(8,128)(2,1)S(1)} %get-tuple-element.81), channel_id=1, source_target_pairs={{0,8},{4,12},{8,0},{12,4},{16,24},{20,28},{24,16},{28,20},{1,9},{5... | collective-permute-start | bytes 884744 | tf_op jit(solution)/shard_map/ppermute | solution.py:666
  79.5 6.5 %collective-permute-start.22 = (f32[2,1024]{1,0:T(2,128)S(1)}, f32[2,1024]{1,0:T(2,128)S(1)}, u32[]{:S(2)}, u32[]{:S(2)}) collective-permute-start(f32[2,1024]{1,0:T(2,128)S(1)} %get-tuple-element.86.own_ref), channel_id=1, source_target_pairs={{0,2},{2,0},{1,3},{3,1},{4,6},{6,4},{5,7},{7,5},{8,10},{10,8},{9,1... | collective-permute-start | bytes 24584 | tf_op jit(solution)/shard_map/ppermute | solution.py:662
  82.2 5.4 %collective-permute-start.21 = (f32[2,1024]{1,0:T(2,128)S(1)}, f32[2,1024]{1,0:T(2,128)S(1)}, u32[]{:S(2)}, u32[]{:S(2)}) collective-permute-start(f32[2,1024]{1,0:T(2,128)S(1)} %get-tuple-element.86.own_ref), channel_id=1, source_target_pairs={{0,3},{3,0},{1,2},{2,1},{4,7},{7,4},{5,6},{6,5},{8,11},{11,8},{9,1... | collective-permute-start | bytes 24584 | tf_op jit(solution)/shard_map/ppermute | solution.py:662
  84.3 3.7 %collective-permute-start.20 = (f32[2,1024]{1,0:T(2,128)S(1)}, f32[2,1024]{1,0:T(2,128)S(1)}, u32[]{:S(2)}, u32[]{:S(2)}) collective-permute-start(f32[2,1024]{1,0:T(2,128)S(1)} %get-tuple-element.86.own_ref), channel_id=1, source_target_pairs={{0,1},{1,0},{2,3},{3,2},{4,5},{5,4},{6,7},{7,6},{8,9},{9,8},{10,11... | collective-permute-start | bytes 24584 | tf_op jit(solution)/shard_map/ppermute | solution.py:662
  (1 other events, 1.1 us)

commit v5 on v4

--- a/solution.py
+++ b/solution.py
@@ -19,8 +19,9 @@
 
 
 SCALE = 0.3
-CONV_MIB = 50
+CONV_MIB = 20
 FAR_COST = 10
+TURN_COST = 1
 
 
 def cost(micros):
@@ -41,7 +42,10 @@
     count = values.shape[0]
     terms = [high, middle, rest - middle, jnp.zeros_like(values)]
     stacked = jnp.concatenate(terms, axis=0).astype(BF16)
-    out = lax.dot_general(stacked, weight, (dims, ((), ())), preferred_element_type=F32)
+    if dims == ((1,), (1,)):
+        out = lax.dot_general(weight, stacked, (dims, ((), ())), preferred_element_type=F32).T
+    else:
+        out = lax.dot_general(stacked, weight, (dims, ((), ())), preferred_element_type=F32)
     return out[:count] + out[count : 2 * count] + out[2 * count : 3 * count]
 
 
@@ -121,38 +125,37 @@
 
 
 def conv_forward_body(
-    x_hbm,
-    w_hbm,
-    down_hbm,
-    *refs,
+    x_ref,
+    w_ref,
+    down_ref,
+    conv_hbm,
+    act_ref,
+    pre_ref,
+    conv_buf,
+    rows_ref,
+    pad_ref,
+    sems,
+    *,
     height,
     width,
     images,
 ):
-    conv_hbm, act_ref, pre_ref, x_buf, w_buf, down_buf, conv_buf, rows_ref, pad_ref, sems = refs
     blocks = act_ref.shape[1] // LANES
-    copies = [fetch(x_hbm, x_buf, sems.at[0])]
+    means, outs = [], []
     for i in range(blocks):
-        part = w_hbm.at[:, :, :, lanes_of(i)]
-        copies.append(fetch(part, w_buf.at[i], sems.at[2 + i]))
-    copies[0].wait()
-    means = []
-    for i in range(blocks):
-        rows_ref[...] = as_rows(x_buf[:, :, :, lanes_of(i)]).astype(F32)
-        copies[1 + i].wait()
-        if i == 0:
-            last = [fetch(down_hbm, down_buf, sems.at[1])]
-        convolve(rows_ref, pad_ref, w_buf.at[i], height, width, images, False)
-        conv = rows_ref[...]
+        rows = rows_ref.at[i]
+        rows[...] = as_rows(x_ref[:, :, :, lanes_of(i)]).astype(F32)
+        part = w_ref.at[:, :, :, lanes_of(i)]
+        convolve(rows, pad_ref.at[i], part, height, width, images, False)
+        conv = rows[...]
         conv_buf[i] = conv
-        last.append(fetch(conv_buf.at[i], conv_hbm.at[:, lanes_of(i)], sems.at[2 + blocks + i]))
+        outs.append(fetch(conv_buf.at[i], conv_hbm.at[:, lanes_of(i)], sems.at[i]))
         act = (conv * jax.nn.sigmoid(conv)).astype(BF16)
         act_ref[:, lanes_of(i)] = act
         means.append(image_sum(act.astype(F32), images) / (height * width))
-    last[0].wait()
-    pre_ref[...] = exact_dot(jnp.concatenate(means, axis=1), down_buf[...], ((1,), (0,)))
-    for copy in last[1:]:
-        copy.wait()
+    pre_ref[...] = exact_dot(jnp.concatenate(means, axis=1), down_ref[...], ((1,), (0,)))
+    for out in outs:
+        out.wait()
 
 
 def conv_forward(cells, weight, down):
@@ -161,7 +164,7 @@
     blocks = channels // LANES
     return pl.pallas_call(
         functools.partial(conv_forward_body, height=height, width=width, images=images),
-        in_specs=[HBM] * 3,
+        in_specs=[HERE] * 3,
         out_specs=[HBM, HERE, HERE],
         out_shape=[
             jax.ShapeDtypeStruct((count, channels), F32),
@@ -169,13 +172,10 @@
             jax.ShapeDtypeStruct((images, inner), F32),
         ],
         scratch_shapes=[
-            pltpu.VMEM(cells.shape, BF16),
-            pltpu.VMEM((blocks, 3, 3, weight.shape[2], LANES), BF16),
-            pltpu.VMEM(down.shape, BF16),
             pltpu.VMEM((blocks, count, LANES), F32),
-            pltpu.VMEM((count, LANES), F32),
-            pltpu.VMEM((16 + (height + 2) * 16 * images, LANES), F32),
-            pltpu.SemaphoreType.DMA((2 + 2 * blocks,)),
+            pltpu.VMEM((blocks, count, LANES), F32),
+            pltpu.VMEM((blocks, 16 + (height + 2) * 16 * images, LANES), F32),
+            pltpu.SemaphoreType.DMA((blocks,)),
         ],
         compiler_params=params(CONV_MIB),
         cost_estimate=cost(3),
@@ -183,20 +183,37 @@
     )(cells, weight, down)
 
 
+def conv_grad_body(grad_ref, gate_ref, conv_ref, part_ref, slope_ref, *, cells):
+    slope = silu_grad(conv_ref[...])
+    part_ref[...] = grad_ref[...] * per_row(gate_ref[...], conv_ref.shape[0]) * slope
+    slope_ref[...] = slope / cells
+
+
+def conv_grad_terms(scaled_grad, gating, convolved, cells):
+    array = jax.ShapeDtypeStruct(convolved.shape, F32)
+    return pl.pallas_call(
+        functools.partial(conv_grad_body, cells=cells),
+        grid=(1,),
+        in_specs=[whole(a.shape) for a in (scaled_grad, gating, convolved)],
+        out_specs=[whole(array.shape)] * 2,
+        out_shape=[array] * 2,
+        compiler_params=params(),
+        cost_estimate=cost(0.02),
+        name="conv_grad",
+    )(scaled_grad, gating, convolved)
+
+
 def conv_backward_body(
-    grad_ref,
-    gate_ref,
+    part_ref,
+    slope_ref,
     own_ref,
     near_ref,
     across_ref,
     over_ref,
     pre_ref,
-    down_hbm,
-    conv_ref,
-    w_hbm,
+    down_ref,
+    w_ref,
     out_hbm,
-    down_buf,
-    w_buf,
     out_buf,
     rows_ref,
     pad_ref,
@@ -206,54 +223,45 @@
     width,
     images,
 ):
-    count, channels = grad_ref.shape
+    count, channels = part_ref.shape
     blocks = channels // LANES
-    down_copy = fetch(down_hbm, down_buf, sems.at[0])
-    copies = []
-    for i in range(blocks):
-        part = w_hbm.at[:, :, :, lanes_of(i)]
-        copies.append(fetch(part, w_buf.at[i], sems.at[1 + i]))
     excite_sum = sum_of((own_ref, near_ref, across_ref, over_ref))
     excite_grad = excite_sum * silu_grad(pre_ref[...])
-    down_copy.wait()
-    squeeze_grad = exact_dot(excite_grad, down_buf[...], ((1,), (1,))) / (height * width)
+    squeeze_grad = exact_dot(excite_grad, down_ref[...], ((1,), (1,)))
     outs = []
     for i in range(blocks):
-        gate = per_row(gate_ref[:, lanes_of(i)], count)
+        rows = rows_ref.at[i]
         squeeze = per_row(squeeze_grad[:, i * LANES : (i + 1) * LANES], count)
-        act_grad = grad_ref[:, lanes_of(i)] * gate + squeeze
-        rows_ref[...] = act_grad * silu_grad(conv_ref[:, lanes_of(i)])
-        copies[i].wait()
-        convolve(rows_ref, pad_ref, w_buf.at[i], height, width, images, True)
-        part = rows_ref[...].astype(BF16).reshape(height, width, images, LANES)
+        rows[...] = part_ref[:, lanes_of(i)] + squeeze * slope_ref[:, lanes_of(i)]
+        part = w_ref.at[:, :, :, lanes_of(i)]
+        convolve(rows, pad_ref.at[i], part, height, width, images, True)
+        part = rows[...].astype(BF16).reshape(height, width, images, LANES)
         out_buf[:, :, :, lanes_of(i)] = part
         target = out_hbm.at[:, :, :, lanes_of(i)]
-        outs.append(fetch(out_buf.at[:, :, :, lanes_of(i)], target, sems.at[1 + blocks + i]))
+        outs.append(fetch(out_buf.at[:, :, :, lanes_of(i)], target, sems.at[i]))
     for out in outs:
         out.wait()
 
 
-def conv_backward(scaled_grad, gating, terms, excite_pre, down, convolved, weight, shape):
+def conv_backward(part, slope, terms, excite_pre, down, weight, shape):
     height, width, images, channels = shape
-    count = convolved.shape[0]
+    count = part.shape[0]
     blocks = channels // LANES
     return pl.pallas_call(
         functools.partial(conv_backward_body, height=height, width=width, images=images),
-        in_specs=[HERE] * 7 + [HBM, HERE, HBM],
+        in_specs=[HERE] * 9,
         out_specs=HBM,
         out_shape=jax.ShapeDtypeStruct(shape, BF16),
         scratch_shapes=[
-            pltpu.VMEM(down.shape, BF16),
-            pltpu.VMEM((blocks, 3, 3, weight.shape[2], LANES), BF16),
             pltpu.VMEM(shape, BF16),
-            pltpu.VMEM((count, LANES), F32),
-            pltpu.VMEM((16 + (height + 2) * 16 * images, LANES), F32),
-            pltpu.SemaphoreType.DMA((1 + 2 * blocks,)),
+            pltpu.VMEM((blocks, count, LANES), F32),
+            pltpu.VMEM((blocks, 16 + (height + 2) * 16 * images, LANES), F32),
+            pltpu.SemaphoreType.DMA((blocks,)),
         ],
         compiler_params=params(),
         cost_estimate=cost(3),
         name="conv_backward",
-    )(scaled_grad, gating, *terms, excite_pre, down, convolved, weight)
+    )(part, slope, *terms, excite_pre, down, weight)
 
 
 def block_of(weight_ref, block, width):
@@ -518,7 +526,7 @@
         out_shape=out_shape,
         scratch_shapes=scratch,
         compiler_params=params(),
-        cost_estimate=cost(10 if last or first == 0 else 0.02),
+        cost_estimate=cost(10 if last else 0.02),
         name="input_grad_last" if last else "input_grad",
     )(role, *operands)
 
@@ -692,7 +700,8 @@
 
     outer = along_chan(own, OUTER)
     middle = along_chan(own, MIDDLE)
-    w_far = lax.dynamic_slice_in_dim(proj_weight, role[3] * channels, channels, axis=1)
+    furthest = jnp.where(lax.axis_index("chan") < 2, 3, 0)
+    w_far = lax.dynamic_slice_in_dim(proj_weight, furthest * channels, channels, axis=1)
     convolved, act, terms = conv_forward(after(hidden, w_far), conv_weight, se_down)
     terms = gather_small(terms)
     far = along_chan(after(outer, *terms), MIDDLE)
@@ -701,37 +710,36 @@
     other = along_dp(scaled, 1)
     theirs = [along_dp(piece, 1) for piece in (own, outer)]
     p_own, p_outer, p_third = project(role, 3, scaled, proj_weight)
-    (begun,) = input_grad(role, 0, [after(own, p_own), outer], proj_weight)
-
-    (send_far,) = between(
-        far_body, [extent], role, p_third, after(far, begun), micros=FAR_COST
-    )
-    came_far = along_chan(send_far, OUTER)
+
+    came = after(came, p_own)
     third, to_far = between(second_body, [extent] * 2, role, came, send, p_fourth)
     crossed = along_chan(to_far, MIDDLE)
+    (send_far,) = between(
+        far_body, [extent], role, p_third, after(far, to_far), micros=FAR_COST
+    )
+    came_far = along_chan(send_far, OUTER)
     theirs.append(along_dp(third, 1))
-    pieces = [own, outer, after(third, to_far)]
+    pieces = [own, outer, after(third, send_far)]
     x_send, x_keep, y_send, y_keep = weight_grad(role, scaled, other, pieces, theirs)
     x_came, y_came = along_dp(x_send, 2), along_dp(y_send, 4)
-    (begun,) = input_grad(role, 2, [after(third, y_send)], proj_weight, begun)
-
-    came_far = after(came_far, begun)
+    (begun,) = input_grad(role, 0, [own, outer, after(third, y_send)], proj_weight)
+
+    crossed = after(crossed, begun)
+    (send,) = between(outer_body, [extent], role, crossed, p_outer, micros=TURN_COST)
+    came = along_chan(send, OUTER)
     half = (extent[0], channels // 2)
     fourth, to_mid, give = between(
-        third_body, [extent] * 2 + [half], role, came_far, send_far, p_third
-    )
-    crossed_mid = along_chan(to_mid, MIDDLE)
-    (send,) = between(outer_body, [extent], role, after(crossed, to_mid), p_outer)
-    came = along_chan(send, OUTER)
-    crossed = crossed_mid
-    fourth = after(fourth, send)
+        third_body, [extent] * 2 + [half], role, after(came_far, send), send_far, p_third
+    )
+    crossed = along_chan(to_mid, MIDDLE)
     upper, lower = weight_grad(role, scaled, other, [fourth], [along_dp(give, 1)])
     upper_came, lower_came = along_dp(upper, 2), along_dp(lower, 4)
     fourth, x_came, y_came = lax.optimization_barrier((fourth, x_came, y_came, lower))[:3]
     scaled_grad, terms = input_grad(
         role, 3, [fourth], proj_weight, begun, act, gating, se_up
     )
-    upper_came = after(upper_came, terms)
+    part, slope = conv_grad_terms(scaled_grad, gating, convolved, shape[0] * shape[1])
+    upper_came = after(upper_came, terms, part)
     top, to_y, bottom, to_x = merge(
         role, x_keep, x_came, y_keep, y_came, upper, upper_came, lower, lower_came
     )
@@ -739,9 +747,7 @@
     terms = gather_small(terms)
     (projected,) = between(fourth_body, [shape], role, p_own, came, crossed)
     terms[0] = after(terms[0], projected)
-    grad_hidden = conv_backward(
-        scaled_grad, gating, terms, excite_pre, se_down, convolved, conv_weight, shape
-    )
+    grad_hidden = conv_backward(part, slope, terms, excite_pre, se_down, conv_weight, shape)
     grad_proj = finish(top, along_dp(to_y, 4), bottom, along_dp(to_x, 2))
     return (from_cells(projected), from_cells(grad_hidden), grad_proj)
 
@@ -768,9 +774,8 @@
     pre_grad = gate_grad * gating * (1.0 - gating)
     excite_sum = lax.psum(jnp.dot(pre_grad, se_up.astype(F32).T, precision=HIGHEST), "chan")
     terms = [excite_sum] + [nothing] * 3
-    grad_hidden = conv_backward(
-        scaled_grad, gating, terms, excite_pre, se_down, convolved, conv_weight, shape
-    )
+    part, slope = conv_grad_terms(scaled_grad, gating, convolved, shape[0] * shape[1])
+    grad_hidden = conv_backward(part, slope, terms, excite_pre, se_down, conv_weight, shape)
     return (from_cells(projected.reshape(shape)), from_cells(grad_hidden), grad_proj)
 
 

time: 94.7 us -> 92.1 us (0.973)
  waiting for transfers between devices: 20.3 us -> 14.3 us
  starting transfers between devices: 31.3 us -> 34 us
  local copies, waits for them, and re-layouts: 5.57 us -> 7.19 us
    ppermute x14, waiting for transfers between devices: 16.7 us -> 10.3 us  [along_chan(): return lax.ppermute(array, 'chan', pairs)]
    ppermute x14, starting transfers between devices: 22.2 us -> 25 us  [along_chan(): return lax.ppermute(array, 'chan', pairs)]
    unnamed x16 -> x24, local copies, waits for them, and re-layouts: 2.79 us -> 5 us
    pallas_call x1, Pallas kernels: 5.28 us -> 4.02 us  [conv_backward(): pl.pallas_call(functools.partial(conv_backward_body, height=height, width...]
    dynamic_slice x2 -> x1, local copies, waits for them, and re-layouts: 2.19 us -> 1.5 us  [on_line(): lax.dynamic_slice_in_dim(proj_weight, furthest * channels, channels, axis=1)]
    pallas_call x3 -> x2, Pallas kernels: 6.94 us -> 6.38 us  [input_grad(): pl.pallas_call(functools.partial(input_grad_body, first=first, pieces=len...]
  transfers between devices with their start and end apart: 25 -> 25, of which waited for: 9 -> 8; matrix products, arithmetic and copies ran while one was open for 3% -> 2% of each run, Pallas kernels for 37% -> 37%
where the time goes in v5:
time: 92.1 us; the launch traced here: 91.7 us
  Pallas kernels  35.3 us (38%)
  starting transfers between devices  34 us (37%)
  waiting for transfers between devices  14.3 us (16%)
  local copies, waits for them, and re-layouts  7.19 us (8%)
    ppermute x14, starting transfers between devices, along_chan(): return lax.ppermute(array, 'chan', pairs)  25 us
    ppermute x14, waiting for transfers between devices, along_chan(): return lax.ppermute(array, 'chan', pairs)  10.3 us
    ppermute x11, starting transfers between devices, along_dp(): return lax.ppermute(array, 'dp', [(i, i ^ bit) for i in range(8)])  9.06 us
    pallas_call x2, Pallas kernels, weight_grad(): pl.pallas_call(functools.partial(weight_grad_body, pieces=pieces), grid_s...  6.58 us
    pallas_call x2, Pallas kernels, input_grad(): pl.pallas_call(functools.partial(input_grad_body, first=first, pieces=len...  6.38 us
    unnamed x24, local copies, waits for them, and re-layouts  5 us
    pallas_call x1, Pallas kernels, conv_forward(): pl.pallas_call(functools.partial(conv_forward_body, height=height, width=...  4.44 us
    pallas_call x5, Pallas kernels, between(): pl.pallas_call(body, grid=(1,), in_specs=[pl.BlockSpec(memory_space=pltpu...  4.39 us
  transfers between devices with their start and end apart: 25, of which 8 were waited for; matrix products, arithmetic and copies ran while one was open for 2% of the time, Pallas kernels for 37%

profile of v5, /device:TPU:0, one launch (start us, length us, event | category | flops | bytes accessed | tf_op | source)
XLA Modules:
  0.0 91.7 jit_solution(15196322044906540539)
XLA Ops:
  0.6 1.5 %collective-permute-start.3 = (bf16[14,14,2,768]{3,2,1,0:T(2,128)(2,1)}, bf16[14,14,2,768]{3,2,1,0:T(2,128)(2,1)}, u32[]{:S(2)}, u32[]{:S(2)}) collective-permute-start(bf16[14,14,2,768]{3,2,1,0:T(2,128)(2,1)} %bitcast.8), channel_id=1, source_target_pairs={{1,2},{2,1},{5,6},{6,5},{9,10},{10,9},{13,14},{14,13},{17,18},{18,... | collective-permute-start | bytes 1806344 | tf_op jit(solution)/shard_map/ppermute | solution.py:670
  2.1 5.1 %collective-permute-start.4 = (bf16[14,14,2,768]{3,2,1,0:T(2,128)(2,1)}, bf16[14,14,2,768]{3,2,1,0:T(2,128)(2,1)}, u32[]{:S(2)}, u32[]{:S(2)}) collective-permute-start(bf16[14,14,2,768]{3,2,1,0:T(2,128)(2,1)} %bitcast.9), channel_id=1, source_target_pairs={{0,1},{1,0},{2,3},{3,2},{4,5},{5,4},{6,7},{7,6},{8,9},{9,8},{10,11... | collective-permute-start | bytes 1806344 | tf_op jit(solution)/shard_map/ppermute | solution.py:670
  7.2 1.5 %constant_dynamic-slice_fusion.w_ref = bf16[768,768]{1,0:T(8,128)(2,1)S(1)} fusion(bf16[768,3072]{1,0:T(8,128)(2,1)} %refs_1_.1, s32[]{:T(128)S(6)} %select_n.12), kind=kLoop, calls=%fused_computation.1 | loop fusion | bytes 2359300 | tf_op jit(solution)/shard_map/dynamic_slice | solution.py:704
  9.1 1.2 %copy-done.6 = bf16[3,3,64,768]{3,2,1,0:T(8,128)(2,1)S(1)} copy-done((bf16[3,3,64,768]{3,2,1,0:T(8,128)(2,1)S(1)}, bf16[3,3,64,768]{3,2,1,0:T(8,128)(2,1)}, u32[]{:S(2)}) %copy-start.6) | copy-done | bytes 884760
  10.3 4.4 %conv_forward.1 = (f32[392,768]{1,0:T(8,128)S(1)}, bf16[392,768]{1,0:T(8,128)(2,1)S(1)}, f32[2,1024]{1,0:T(2,128)S(1)}) custom-call(bf16[14,14,2,768]{3,2,1,0:T(2,128)(2,1)S(1)} %bitcast.13, bf16[3,3,64,768]{3,2,1,0:T(8,128)(2,1)S(1)} %copy-done.6, bf16[768,1024]{1,0:T(8,128)(2,1)S(1)} %copy-done.2), custom_call_target="tpu_custom_call" | custom-call | flops 1035000000 | bytes 1 | tf_op jit(solution)/shard_map/conv_forward/pallas_call | solution.py:165
  15.8 2.0 %collective-permute-start.1 = (f32[2,1024]{1,0:T(2,128)S(1)}, f32[2,1024]{1,0:T(2,128)S(1)}, u32[]{:S(2)}, u32[]{:S(2)}) collective-permute-start(f32[2,1024]{1,0:T(2,128)S(1)} %get-tuple-element.51.own_ref), channel_id=1, source_target_pairs={{0,3},{3,0},{1,2},{2,1},{4,7},{7,4},{5,6},{6,5},{8,11},{11,8},{9,1... | collective-permute-start | bytes 24584 | tf_op jit(solution)/shard_map/ppermute | solution.py:670
  17.8 1.5 %collective-permute-start.2 = (f32[2,1024]{1,0:T(2,128)S(1)}, f32[2,1024]{1,0:T(2,128)S(1)}, u32[]{:S(2)}, u32[]{:S(2)}) collective-permute-start(f32[2,1024]{1,0:T(2,128)S(1)} %get-tuple-element.51.own_ref), channel_id=1, source_target_pairs={{0,2},{2,0},{1,3},{3,1},{4,6},{6,4},{5,7},{7,5},{8,10},{10,8},{9,1... | collective-permute-start | bytes 24584 | tf_op jit(solution)/shard_map/ppermute | solution.py:670
  20.0 1.1 %collective-permute-done.near_ref = f32[2,1024]{1,0:T(2,128)S(1)} collective-permute-done((f32[2,1024]{1,0:T(2,128)S(1)}, f32[2,1024]{1,0:T(2,128)S(1)}, u32[]{:S(2)}, u32[]{:S(2)}) %collective-permute-start) | collective-permute-done | bytes 8224 | tf_op jit(solution)/shard_map/ppermute | solution.py:670
  21.1 1.1 %collective-permute-done.1.across_ref = f32[2,1024]{1,0:T(2,128)S(1)} collective-permute-done((f32[2,1024]{1,0:T(2,128)S(1)}, f32[2,1024]{1,0:T(2,128)S(1)}, u32[]{:S(2)}, u32[]{:S(2)}) %collective-permute-start.1) | collective-permute-done | bytes 8224 | tf_op jit(solution)/shard_map/ppermute | solution.py:670
  22.4 2.9 %scale.1 = (f32[2,768]{1,0:T(2,128)S(1)}, f32[2,1024]{1,0:T(2,128)S(1)}, bf16[392,768]{1,0:T(8,128)(2,1)S(1)}, bf16[392,768]{1,0:T(8,128)(2,1)S(1)}, bf16[392,768]{1,0:T(8,128)(2,1)S(1)}) custom-call(s32[8]{0:T(128)S(1)} %dynamic-slice_bitcast_fusion.role_ref.order_ref.place_ref, bf16[392,768]{1,0:T(8,128)(2,1)S(1)} %get-tuple-element.50.act_ref.refs_3_, ...), custom_call_target="tpu_custom_call" | custom-call | flops 1035000000 | bytes 1 | tf_op jit(solution)/shard_map/scale/pallas_call | solution.py:324
  27.3 2.3 %copy-done = bf16[768,3072]{1,0:T(8,128)(2,1)S(1)} copy-done((bf16[768,3072]{1,0:T(8,128)(2,1)S(1)}, bf16[768,3072]{1,0:T(8,128)(2,1)}, u32[]{:S(2)}) %copy-start) | copy-done | bytes 4718616
  29.6 3.9 %project.1 = (bf16[392,768]{1,0:T(8,128)(2,1)S(1)}, bf16[392,768]{1,0:T(8,128)(2,1)S(1)}, bf16[392,768]{1,0:T(8,128)(2,1)S(1)}) custom-call(s32[8]{0:T(128)S(1)} %dynamic-slice_bitcast_fusion.role_ref.order_ref.place_ref, bf16[392,768]{1,0:T(8,128)(2,1)S(1)} %get-tuple-element.52.scaled_hbm.own_ref, bf16[768,3072]{1,0:T(8,128)(2,1)S(1)} %copy-done), custom_call_target="tpu_custom_call" | custom-call | flops 1035000000 | bytes 1 | tf_op jit(solution)/shard_map/project/pallas_call | solution.py:368
  33.5 5.5 %collective-permute-done.6.came = bf16[392,768]{1,0:T(8,128)(2,1)S(1)} collective-permute-done((bf16[392,768]{1,0:T(8,128)(2,1)S(1)}, bf16[392,768]{1,0:T(8,128)(2,1)S(1)}, u32[]{:S(2)}, u32[]{:S(2)}) %collective-permute-start.6) | collective-permute-done | bytes 602144 | tf_op jit(solution)/shard_map/ppermute | solution.py:670
  41.3 5.8 %collective-permute-start.7 = (bf16[392,768]{1,0:T(8,128)(2,1)S(1)}, bf16[392,768]{1,0:T(8,128)(2,1)S(1)}, u32[]{:S(2)}, u32[]{:S(2)}) collective-permute-start(bf16[392,768]{1,0:T(8,128)(2,1)S(1)} %far_turn.1.held), channel_id=1, source_target_pairs={{0,1},{1,0},{2,3},{3,2},{4,5},{5,4},{6,7},{7,6},{8,9},{9,8},{10,11... | collective-permute-start | bytes 1806344 | tf_op jit(solution)/shard_map/ppermute | solution.py:670
  47.1 5.0 %weight_grad.1 = (bf16[2,384,384]{2,1,0:T(8,128)(2,1)S(1)}, bf16[2,384,384]{2,1,0:T(8,128)(2,1)S(1)}, bf16[2,384,384]{2,1,0:T(8,128)(2,1)S(1)}, bf16[2,384,384]{2,1,0:T(8,128)(2,1)S(1)}) custom-call(s32[8]{0:T(128)S(1)} %dynamic-slice_bitcast_fusion.role_ref.order_ref.place_ref, bf16[392,768]{1,0:T(8,128)(2,1)S(1)} %get-tuple-element.52.scaled_hbm.own_ref, ...), custom_call_target="tpu_custom_call" | custom-call | flops 2070000000 | bytes 1 | tf_op jit(solution)/shard_map/weight_grad/pallas_call | solution.py:588
  52.1 1.6 %collective-permute-start.13 = (bf16[2,384,384]{2,1,0:T(8,128)(2,1)S(1)}, bf16[2,384,384]{2,1,0:T(8,128)(2,1)S(1)}, u32[]{:S(2)}, u32[]{:S(2)}) collective-permute-start(bf16[2,384,384]{2,1,0:T(8,128)(2,1)S(1)} %get-tuple-element.69), channel_id=1, source_target_pairs={{0,8},{4,12},{8,0},{12,4},{16,24},{20,28},{24,16},{28,20},{1,9},{5... | collective-permute-start | bytes 1769480 | tf_op jit(solution)/shard_map/ppermute | solution.py:674
  53.6 1.5 %collective-permute-start.14 = (bf16[2,384,384]{2,1,0:T(8,128)(2,1)S(1)}, bf16[2,384,384]{2,1,0:T(8,128)(2,1)S(1)}, u32[]{:S(2)}, u32[]{:S(2)}) collective-permute-start(bf16[2,384,384]{2,1,0:T(8,128)(2,1)S(1)} %get-tuple-element.63), channel_id=1, source_target_pairs={{0,16},{4,20},{8,24},{12,28},{16,0},{20,4},{24,8},{28,12},{1,17},{... | collective-permute-start | bytes 1769480 | tf_op jit(solution)/shard_map/ppermute | solution.py:674
  55.2 3.8 %input_grad.1.refs_2_ = f32[392,768]{1,0:T(8,128)S(1)} custom-call(s32[8]{0:T(128)S(1)} %dynamic-slice_bitcast_fusion.role_ref.order_ref.place_ref, bf16[14,14,2,768]{3,2,1,0:T(2,128)(2,1)S(1)} %bitcast.12, bf16[14,14,2,768]{3,2,1,0:T(2,128)(2,1)} %collective-permute-done.4.refs_1_, bf16[392,768]{1,0:T(8,128)(2,1)S(1)} %get-tuple-element.64.refs_2_, ...), custom_call_target="tpu_custom_call" | custom-call | flops 6900000 | bytes 1 | tf_op jit(solution)/shard_map/input_grad/pallas_call | solution.py:515
  61.1 2.8 %collective-permute-start.16 = (bf16[392,768]{1,0:T(8,128)(2,1)S(1)}, bf16[392,768]{1,0:T(8,128)(2,1)S(1)}, u32[]{:S(2)}, u32[]{:S(2)}) collective-permute-start(bf16[392,768]{1,0:T(8,128)(2,1)S(1)} %outer_turn.1), channel_id=1, source_target_pairs={{0,1},{1,0},{2,3},{3,2},{4,5},{5,4},{6,7},{7,6},{8,9},{9,8},{10,11... | collective-permute-start | bytes 1806344 | tf_op jit(solution)/shard_map/ppermute | solution.py:670
  64.0 1.6 %weight_grad_more.1 = (bf16[384,384]{1,0:T(8,128)(2,1)S(1)}, bf16[384,384]{1,0:T(8,128)(2,1)S(1)}) custom-call(s32[8]{0:T(128)S(1)} %dynamic-slice_bitcast_fusion.role_ref.order_ref.place_ref, bf16[392,768]{1,0:T(8,128)(2,1)S(1)} %get-tuple-element.52.scaled_hbm.own_ref, bf16[392,768]{1,0:T(8,128)(2,1)S(1)} %collective-permute-done.9.other_ref, ...), custom_call_target="tpu_custom_call" | custom-call | flops 6900000 | bytes 1 | tf_op jit(solution)/shard_map/weight_grad_more/pallas_call | solution.py:588
  65.5 1.6 %collective-permute-start.18 = (bf16[384,384]{1,0:T(8,128)(2,1)S(1)}, bf16[384,384]{1,0:T(8,128)(2,1)S(1)}, u32[]{:S(2)}, u32[]{:S(2)}) collective-permute-start(bf16[384,384]{1,0:T(8,128)(2,1)S(1)} %get-tuple-element.80.refs_4_), channel_id=1, source_target_pairs={{0,8},{4,12},{8,0},{12,4},{16,24},{20,28},{24,16},{28,20},{1,9},{5... | collective-permute-start | bytes 884744 | tf_op jit(solution)/shard_map/ppermute | solution.py:674
  67.1 1.5 %collective-permute-start.19 = (bf16[384,384]{1,0:T(8,128)(2,1)S(1)}, bf16[384,384]{1,0:T(8,128)(2,1)S(1)}, u32[]{:S(2)}, u32[]{:S(2)}) collective-permute-start(bf16[384,384]{1,0:T(8,128)(2,1)S(1)} %get-tuple-element.71.refs_6_), channel_id=1, source_target_pairs={{0,16},{4,20},{8,24},{12,28},{16,0},{20,4},{24,8},{28,12},{1,17},{... | collective-permute-start | bytes 884744 | tf_op jit(solution)/shard_map/ppermute | solution.py:674
  68.6 2.6 %input_grad_last.1 = (f32[392,768]{1,0:T(8,128)S(1)}, f32[2,1024]{1,0:T(2,128)S(1)}) custom-call(s32[8]{0:T(128)S(1)} %dynamic-slice_bitcast_fusion.role_ref.order_ref.place_ref, bf16[392,768]{1,0:T(8,128)(2,1)S(1)} %get-tuple-element.72.refs_0_, bf16[768,3072]{1,0:T(8,128)(2,1)S(1)} %bitcast.7, f32[392,768]{1,0:T(8,128)S(1)} %input_grad.1.refs_2_, ...), custom_call_target="tpu_custom_call" | custom-call | flops 3449999872 | bytes 1 | tf_op jit(solution)/shard_map/input_grad_last/pallas_call | solution.py:515
  71.7 2.7 %collective-permute-done.18.refs_5_ = bf16[384,384]{1,0:T(8,128)(2,1)S(1)} collective-permute-done((bf16[384,384]{1,0:T(8,128)(2,1)S(1)}, bf16[384,384]{1,0:T(8,128)(2,1)S(1)}, u32[]{:S(2)}, u32[]{:S(2)}) %collective-permute-start.18) | collective-permute-done | bytes 294944 | tf_op jit(solution)/shard_map/ppermute | solution.py:674
  74.5 1.2 %collective-permute-done.19.refs_7_ = bf16[384,384]{1,0:T(8,128)(2,1)S(1)} collective-permute-done((bf16[384,384]{1,0:T(8,128)(2,1)S(1)}, bf16[384,384]{1,0:T(8,128)(2,1)S(1)}, u32[]{:S(2)}, u32[]{:S(2)}) %collective-permute-start.19) | collective-permute-done | bytes 294944 | tf_op jit(solution)/shard_map/ppermute | solution.py:674
  75.7 1.1 %merge.1 = (f32[384,384]{1,0:T(8,128)S(1)}, bf16[384,384]{1,0:T(8,128)(2,1)S(1)}, f32[384,384]{1,0:T(8,128)S(1)}, bf16[384,384]{1,0:T(8,128)(2,1)S(1)}) custom-call(s32[8]{0:T(128)S(1)} %dynamic-slice_bitcast_fusion.role_ref.order_ref.place_ref, bf16[2,384,384]{2,1,0:T(8,128)(2,1)S(1)} %get-tuple-element.76.refs_0_, ...), custom_call_target="tpu_custom_call" | custom-call | flops 690000000 | bytes 1 | tf_op jit(solution)/shard_map/merge/pallas_call | solution.py:628
  76.8 1.6 %collective-permute-start.23 = (bf16[384,384]{1,0:T(8,128)(2,1)S(1)}, bf16[384,384]{1,0:T(8,128)(2,1)S(1)}, u32[]{:S(2)}, u32[]{:S(2)}) collective-permute-start(bf16[384,384]{1,0:T(8,128)(2,1)S(1)} %get-tuple-element.93), channel_id=1, source_target_pairs={{0,16},{4,20},{8,24},{12,28},{16,0},{20,4},{24,8},{28,12},{1,17},{... | collective-permute-start | bytes 884744 | tf_op jit(solution)/shard_map/ppermute | solution.py:674
  79.7 2.3 %collective-permute-start.21 = (f32[2,1024]{1,0:T(2,128)S(1)}, f32[2,1024]{1,0:T(2,128)S(1)}, u32[]{:S(2)}, u32[]{:S(2)}) collective-permute-start(f32[2,1024]{1,0:T(2,128)S(1)} %get-tuple-element.90.own_ref), channel_id=1, source_target_pairs={{0,3},{3,0},{1,2},{2,1},{4,7},{7,4},{5,6},{6,5},{8,11},{11,8},{9,1... | collective-permute-start | bytes 24584 | tf_op jit(solution)/shard_map/ppermute | solution.py:670
  82.4 1.7 %fourth_turn.1 = bf16[14,14,2,768]{3,2,1,0:T(2,128)(2,1)} custom-call(s32[8]{0:T(128)S(1)} %dynamic-slice_bitcast_fusion.role_ref.order_ref.place_ref, bf16[392,768]{1,0:T(8,128)(2,1)S(1)} %get-tuple-element.53.p_own, bf16[392,768]{1,0:T(8,128)(2,1)S(1)} %collective-permute-done.16.came, bf16[392,768]{1,0:T(8,128)(2,1)S(1)} %collective-permute-done.17.crossed), custom_call_target="tpu_custom_call" | custom-call | flops 6900000 | bytes 1 | tf_op jit(solution)/shard_map/fourth_turn/pallas_call | solution.py:439
  85.1 1.4 %collective-permute-done.22.over_ref = f32[2,1024]{1,0:T(2,128)S(1)} collective-permute-done((f32[2,1024]{1,0:T(2,128)S(1)}, f32[2,1024]{1,0:T(2,128)S(1)}, u32[]{:S(2)}, u32[]{:S(2)}) %collective-permute-start.22) | collective-permute-done | bytes 8224 | tf_op jit(solution)/shard_map/ppermute | solution.py:670
  86.5 4.0 %conv_backward.1 = bf16[14,14,2,768]{3,2,1,0:T(2,128)(2,1)} custom-call(f32[392,768]{1,0:T(8,128)S(1)} %get-tuple-element.83.part_ref, f32[392,768]{1,0:T(8,128)S(1)} %get-tuple-element.88.slope_ref, f32[2,1024]{1,0:T(2,128)S(1)} %get-tuple-element.90.own_ref, f32[2,1024]{1,0:T(2,128)S(1)} %collective-permute-done.20.near_ref, ...), custom_call_target="tpu_custom_call" | custom-call | flops 1035000000 | bytes 1 | tf_op jit(solution)/shard_map/conv_backward/pallas_call | solution.py:250
  90.6 1.1 %finish.1 = f32[768,384]{1,0:T(8,128)} custom-call(f32[384,384]{1,0:T(8,128)S(1)} %get-tuple-element.92.top, bf16[384,384]{1,0:T(8,128)(2,1)S(1)} %collective-permute-done.23.top_came, f32[384,384]{1,0:T(8,128)S(1)} %get-tuple-element.94.bottom, bf16[384,384]{1,0:T(8,128)(2,1)S(1)} %collective-permute-done.24.bottom_came), custom_call_target="tpu_custom_call" | custom-call | flops 690000000 | bytes 1 | tf_op jit(solution)/shard_map/finish/pallas_call | solution.py:649
  (61 shorter events, 11.9 us)
Async XLA Ops:
  0.6 21.8 %collective-permute-start.3 = (bf16[14,14,2,768]{3,2,1,0:T(2,128)(2,1)}, bf16[14,14,2,768]{3,2,1,0:T(2,128)(2,1)}, u32[]{:S(2)}, u32[]{:S(2)}) collective-permute-start(bf16[14,14,2,768]{3,2,1,0:T(2,128)(2,1)} %bitcast.8), channel_id=1, source_target_pairs={{1,2},{2,1},{5,6},{6,5},{9,10},{10,9},{13,14},{14,13},{17,18},{18,... | collective-permute-start | bytes 1806344 | tf_op jit(solution)/shard_map/ppermute | solution.py:670
  2.1 23.8 %collective-permute-start.4 = (bf16[14,14,2,768]{3,2,1,0:T(2,128)(2,1)}, bf16[14,14,2,768]{3,2,1,0:T(2,128)(2,1)}, u32[]{:S(2)}, u32[]{:S(2)}) collective-permute-start(bf16[14,14,2,768]{3,2,1,0:T(2,128)(2,1)} %bitcast.9), channel_id=1, source_target_pairs={{0,1},{1,0},{2,3},{3,2},{4,5},{5,4},{6,7},{7,6},{8,9},{9,8},{10,11... | collective-permute-start | bytes 1806344 | tf_op jit(solution)/shard_map/ppermute | solution.py:670
  10.3 12.1 %copy-start.1 = (bf16[1024,768]{1,0:T(8,128)(2,1)S(1)}, bf16[1024,768]{1,0:T(8,128)(2,1)}, u32[]{:S(2)}) copy-start(bf16[1024,768]{1,0:T(8,128)(2,1)} %refs_5_.1) | copy-start | bytes 4718596
  15.8 5.3 %collective-permute-start = (f32[2,1024]{1,0:T(2,128)S(1)}, f32[2,1024]{1,0:T(2,128)S(1)}, u32[]{:S(2)}, u32[]{:S(2)}) collective-permute-start(f32[2,1024]{1,0:T(2,128)S(1)} %get-tuple-element.51.own_ref), channel_id=1, source_target_pairs={{0,1},{1,0},{2,3},{3,2},{4,5},{5,4},{6,7},{7,6},{8,9},{9,8},{10,11... | collective-permute-start | bytes 24584 | tf_op jit(solution)/shard_map/ppermute | solution.py:670
  15.8 6.4 %collective-permute-start.1 = (f32[2,1024]{1,0:T(2,128)S(1)}, f32[2,1024]{1,0:T(2,128)S(1)}, u32[]{:S(2)}, u32[]{:S(2)}) collective-permute-start(f32[2,1024]{1,0:T(2,128)S(1)} %get-tuple-element.51.own_ref), channel_id=1, source_target_pairs={{0,3},{3,0},{1,2},{2,1},{4,7},{7,4},{5,6},{6,5},{8,11},{11,8},{9,1... | collective-permute-start | bytes 24584 | tf_op jit(solution)/shard_map/ppermute | solution.py:670
  17.8 4.6 %collective-permute-start.2 = (f32[2,1024]{1,0:T(2,128)S(1)}, f32[2,1024]{1,0:T(2,128)S(1)}, u32[]{:S(2)}, u32[]{:S(2)}) collective-permute-start(f32[2,1024]{1,0:T(2,128)S(1)} %get-tuple-element.51.own_ref), channel_id=1, source_target_pairs={{0,2},{2,0},{1,3},{3,1},{4,6},{6,4},{5,7},{7,5},{8,10},{10,8},{9,1... | collective-permute-start | bytes 24584 | tf_op jit(solution)/shard_map/ppermute | solution.py:670
  22.4 4.2 %copy-start.8 = (bf16[2,14,14,768]{3,0,2,1:T(2,128)(2,1)S(1)}, bf16[2,14,14,768]{3,0,2,1:T(2,128)(2,1)}, u32[]{:S(2)}) copy-start(bf16[2,14,14,768]{3,0,2,1:T(2,128)(2,1)} %param.12) | copy-start | bytes 1806340
  25.3 13.7 %collective-permute-start.6 = (bf16[392,768]{1,0:T(8,128)(2,1)S(1)}, bf16[392,768]{1,0:T(8,128)(2,1)S(1)}, u32[]{:S(2)}, u32[]{:S(2)}) collective-permute-start(bf16[392,768]{1,0:T(8,128)(2,1)S(1)} %get-tuple-element.56.held), channel_id=1, source_target_pairs={{0,1},{1,0},{2,3},{3,2},{4,5},{5,4},{6,7},{7,6},{8,9},{9,8},{10,11... | collective-permute-start | bytes 1806344 | tf_op jit(solution)/shard_map/ppermute | solution.py:670
  25.9 13.9 %collective-permute-start.5 = (bf16[14,14,2,768]{3,2,1,0:T(2,128)(2,1)}, bf16[14,14,2,768]{3,2,1,0:T(2,128)(2,1)S(1)}, u32[]{:S(2)}, u32[]{:S(2)}) collective-permute-start(bf16[14,14,2,768]{3,2,1,0:T(2,128)(2,1)} %collective-permute-done.4.refs_1_), channel_id=1, source_target_pairs={{1,2},{2,1},{5,6},{6,5},{9,10},{10,9},{13,14},{14,13},{17,18},{18,... | collective-permute-start | bytes 1806344 | tf_op jit(solution)/shard_map/ppermute | solution.py:670
  26.6 14.7 %collective-permute-start.10 = (bf16[14,14,2,768]{3,2,1,0:T(2,128)(2,1)S(1)}, bf16[14,14,2,768]{3,2,1,0:T(2,128)(2,1)S(1)}, u32[]{:S(2)}, u32[]{:S(2)}) collective-permute-start(bf16[14,14,2,768]{3,2,1,0:T(2,128)(2,1)S(1)} %bitcast.10), channel_id=1, source_target_pairs={{0,4},{4,0},{8,12},{12,8},{16,20},{20,16},{24,28},{28,24},{1,5},{5... | collective-permute-start | bytes 1806344 | tf_op jit(solution)/shard_map/ppermute | solution.py:674
  26.7 20.4 %collective-permute-start.9 = (bf16[392,768]{1,0:T(8,128)(2,1)S(1)}, bf16[392,768]{1,0:T(8,128)(2,1)S(1)}, u32[]{:S(2)}, u32[]{:S(2)}) collective-permute-start(bf16[392,768]{1,0:T(8,128)(2,1)S(1)} %get-tuple-element.52.scaled_hbm.own_ref), channel_id=1, source_target_pairs={{0,4},{4,0},{8,12},{12,8},{16,20},{20,16},{24,28},{28,24},{1,5},{5... | collective-permute-start | bytes 1806344 | tf_op jit(solution)/shard_map/ppermute | solution.py:674
  27.2 19.9 %collective-permute-start.11 = (bf16[14,14,2,768]{3,2,1,0:T(2,128)(2,1)}, bf16[14,14,2,768]{3,2,1,0:T(2,128)(2,1)S(1)}, u32[]{:S(2)}, u32[]{:S(2)}) collective-permute-start(bf16[14,14,2,768]{3,2,1,0:T(2,128)(2,1)} %collective-permute-done.4.refs_1_), channel_id=1, source_target_pairs={{0,4},{4,0},{8,12},{12,8},{16,20},{20,16},{24,28},{28,24},{1,5},{5... | collective-permute-start | bytes 1806344 | tf_op jit(solution)/shard_map/ppermute | solution.py:674
  39.0 16.1 %slice-start = ((s8[4718592]{0:T(1024)(128)(4,1)}), s8[4194304]{0:T(1024)(128)(4,1)S(1)}, s32[]{:S(2)}) async-start(s8[4718592]{0:T(1024)(128)(4,1)} %bitcast.6), calls=%async_computation | async-start | bytes 8388608
  39.7 7.3 %collective-permute-start.12 = (bf16[392,768]{1,0:T(8,128)(2,1)S(1)}, bf16[392,768]{1,0:T(8,128)(2,1)S(1)}, u32[]{:S(2)}, u32[]{:S(2)}) collective-permute-start(bf16[392,768]{1,0:T(8,128)(2,1)S(1)} %get-tuple-element.64.refs_2_), channel_id=1, source_target_pairs={{0,4},{4,0},{8,12},{12,8},{16,20},{20,16},{24,28},{28,24},{1,5},{5... | collective-permute-start | bytes 1806344 | tf_op jit(solution)/shard_map/ppermute | solution.py:674
  39.8 19.1 %collective-permute-start.8 = (bf16[392,768]{1,0:T(8,128)(2,1)S(1)}, bf16[392,768]{1,0:T(8,128)(2,1)S(1)}, u32[]{:S(2)}, u32[]{:S(2)}) collective-permute-start(bf16[392,768]{1,0:T(8,128)(2,1)S(1)} %get-tuple-element.59), channel_id=1, source_target_pairs={{1,2},{2,1},{5,6},{6,5},{9,10},{10,9},{13,14},{14,13},{17,18},{18,... | collective-permute-start | bytes 1806344 | tf_op jit(solution)/shard_map/ppermute | solution.py:670
  40.7 14.5 %slice-start.1 = ((s8[4718592]{0:T(1024)(128)(4,1)}), s8[524288]{0:T(1024)(128)(4,1)S(1)}, s32[]{:S(2)}) async-start(s8[4718592]{0:T(1024)(128)(4,1)} %bitcast.6), calls=%async_computation.1 | async-start | bytes 1048576
  41.3 18.3 %collective-permute-start.7 = (bf16[392,768]{1,0:T(8,128)(2,1)S(1)}, bf16[392,768]{1,0:T(8,128)(2,1)S(1)}, u32[]{:S(2)}, u32[]{:S(2)}) collective-permute-start(bf16[392,768]{1,0:T(8,128)(2,1)S(1)} %far_turn.1.held), channel_id=1, source_target_pairs={{0,1},{1,0},{2,3},{3,2},{4,5},{5,4},{6,7},{7,6},{8,9},{9,8},{10,11... | collective-permute-start | bytes 1806344 | tf_op jit(solution)/shard_map/ppermute | solution.py:670
  52.1 15.0 %collective-permute-start.13 = (bf16[2,384,384]{2,1,0:T(8,128)(2,1)S(1)}, bf16[2,384,384]{2,1,0:T(8,128)(2,1)S(1)}, u32[]{:S(2)}, u32[]{:S(2)}) collective-permute-start(bf16[2,384,384]{2,1,0:T(8,128)(2,1)S(1)} %get-tuple-element.69), channel_id=1, source_target_pairs={{0,8},{4,12},{8,0},{12,4},{16,24},{20,28},{24,16},{28,20},{1,9},{5... | collective-permute-start | bytes 1769480 | tf_op jit(solution)/shard_map/ppermute | solution.py:674
  53.6 15.0 %collective-permute-start.14 = (bf16[2,384,384]{2,1,0:T(8,128)(2,1)S(1)}, bf16[2,384,384]{2,1,0:T(8,128)(2,1)S(1)}, u32[]{:S(2)}, u32[]{:S(2)}) collective-permute-start(bf16[2,384,384]{2,1,0:T(8,128)(2,1)S(1)} %get-tuple-element.63), channel_id=1, source_target_pairs={{0,16},{4,20},{8,24},{12,28},{16,0},{20,4},{24,8},{28,12},{1,17},{... | collective-permute-start | bytes 1769480 | tf_op jit(solution)/shard_map/ppermute | solution.py:674
  60.4 3.6 %collective-permute-start.15 = (bf16[392,384]{1,0:T(8,128)(2,1)S(1)}, bf16[392,384]{1,0:T(8,128)(2,1)S(1)}, u32[]{:S(2)}, u32[]{:S(2)}) collective-permute-start(bf16[392,384]{1,0:T(8,128)(2,1)S(1)} %get-tuple-element.70), channel_id=1, source_target_pairs={{0,4},{4,0},{8,12},{12,8},{16,20},{20,16},{24,28},{28,24},{1,5},{5... | collective-permute-start | bytes 903176 | tf_op jit(solution)/shard_map/ppermute | solution.py:674
  60.4 18.5 %collective-permute-start.17 = (bf16[392,768]{1,0:T(8,128)(2,1)S(1)}, bf16[392,768]{1,0:T(8,128)(2,1)S(1)}, u32[]{:S(2)}, u32[]{:S(2)}) collective-permute-start(bf16[392,768]{1,0:T(8,128)(2,1)S(1)} %get-tuple-element.75), channel_id=1, source_target_pairs={{1,2},{2,1},{5,6},{6,5},{9,10},{10,9},{13,14},{14,13},{17,18},{18,... | collective-permute-start | bytes 1806344 | tf_op jit(solution)/shard_map/ppermute | solution.py:670
  61.1 17.8 %collective-permute-start.16 = (bf16[392,768]{1,0:T(8,128)(2,1)S(1)}, bf16[392,768]{1,0:T(8,128)(2,1)S(1)}, u32[]{:S(2)}, u32[]{:S(2)}) collective-permute-start(bf16[392,768]{1,0:T(8,128)(2,1)S(1)} %outer_turn.1), channel_id=1, source_target_pairs={{0,1},{1,0},{2,3},{3,2},{4,5},{5,4},{6,7},{7,6},{8,9},{9,8},{10,11... | collective-permute-start | bytes 1806344 | tf_op jit(solution)/shard_map/ppermute | solution.py:670
  65.5 8.9 %collective-permute-start.18 = (bf16[384,384]{1,0:T(8,128)(2,1)S(1)}, bf16[384,384]{1,0:T(8,128)(2,1)S(1)}, u32[]{:S(2)}, u32[]{:S(2)}) collective-permute-start(bf16[384,384]{1,0:T(8,128)(2,1)S(1)} %get-tuple-element.80.refs_4_), channel_id=1, source_target_pairs={{0,8},{4,12},{8,0},{12,4},{16,24},{20,28},{24,16},{28,20},{1,9},{5... | collective-permute-start | bytes 884744 | tf_op jit(solution)/shard_map/ppermute | solution.py:674
  67.1 8.5 %collective-permute-start.19 = (bf16[384,384]{1,0:T(8,128)(2,1)S(1)}, bf16[384,384]{1,0:T(8,128)(2,1)S(1)}, u32[]{:S(2)}, u32[]{:S(2)}) collective-permute-start(bf16[384,384]{1,0:T(8,128)(2,1)S(1)} %get-tuple-element.71.refs_6_), channel_id=1, source_target_pairs={{0,16},{4,20},{8,24},{12,28},{16,0},{20,4},{24,8},{28,12},{1,17},{... | collective-permute-start | bytes 884744 | tf_op jit(solution)/shard_map/ppermute | solution.py:674
  68.6 2.6 %copy-start.5 = (f32[392,768]{1,0:T(8,128)S(1)}, f32[392,768]{1,0:T(8,128)}, u32[]{:S(2)}) copy-start(f32[392,768]{1,0:T(8,128)} %copy-done.4) | copy-start | bytes 3612676
  75.7 10.9 %copy-start.7 = (bf16[3,3,64,768]{3,2,1,0:T(8,128)(2,1)S(1)}, bf16[3,3,64,768]{3,2,1,0:T(8,128)(2,1)}, u32[]{:S(2)}) copy-start(bf16[3,3,64,768]{3,2,1,0:T(8,128)(2,1)} %w_ref.3) | copy-start | bytes 2654212
  76.8 13.7 %collective-permute-start.23 = (bf16[384,384]{1,0:T(8,128)(2,1)S(1)}, bf16[384,384]{1,0:T(8,128)(2,1)S(1)}, u32[]{:S(2)}, u32[]{:S(2)}) collective-permute-start(bf16[384,384]{1,0:T(8,128)(2,1)S(1)} %get-tuple-element.93), channel_id=1, source_target_pairs={{0,16},{4,20},{8,24},{12,28},{16,0},{20,4},{24,8},{28,12},{1,17},{... | collective-permute-start | bytes 884744 | tf_op jit(solution)/shard_map/ppermute | solution.py:674
  78.4 8.1 %copy-start.3 = (bf16[768,1024]{1,0:T(8,128)(2,1)S(1)}, bf16[768,1024]{1,0:T(8,128)(2,1)}, u32[]{:S(2)}) copy-start(bf16[768,1024]{1,0:T(8,128)(2,1)} %down_ref.3) | copy-start | bytes 4718596
  78.4 12.2 %collective-permute-start.24 = (bf16[384,384]{1,0:T(8,128)(2,1)S(1)}, bf16[384,384]{1,0:T(8,128)(2,1)S(1)}, u32[]{:S(2)}, u32[]{:S(2)}) collective-permute-start(bf16[384,384]{1,0:T(8,128)(2,1)S(1)} %get-tuple-element.85), channel_id=1, source_target_pairs={{0,8},{4,12},{8,0},{12,4},{16,24},{20,28},{24,16},{28,20},{1,9},{5... | collective-permute-start | bytes 884744 | tf_op jit(solution)/shard_map/ppermute | solution.py:674
  78.9 5.2 %collective-permute-start.20 = (f32[2,1024]{1,0:T(2,128)S(1)}, f32[2,1024]{1,0:T(2,128)S(1)}, u32[]{:S(2)}, u32[]{:S(2)}) collective-permute-start(f32[2,1024]{1,0:T(2,128)S(1)} %get-tuple-element.90.own_ref), channel_id=1, source_target_pairs={{0,1},{1,0},{2,3},{3,2},{4,5},{5,4},{6,7},{7,6},{8,9},{9,8},{10,11... | collective-permute-start | bytes 24584 | tf_op jit(solution)/shard_map/ppermute | solution.py:670
  79.7 5.4 %collective-permute-start.21 = (f32[2,1024]{1,0:T(2,128)S(1)}, f32[2,1024]{1,0:T(2,128)S(1)}, u32[]{:S(2)}, u32[]{:S(2)}) collective-permute-start(f32[2,1024]{1,0:T(2,128)S(1)} %get-tuple-element.90.own_ref), channel_id=1, source_target_pairs={{0,3},{3,0},{1,2},{2,1},{4,7},{7,4},{5,6},{6,5},{8,11},{11,8},{9,1... | collective-permute-start | bytes 24584 | tf_op jit(solution)/shard_map/ppermute | solution.py:670
  82.0 4.5 %collective-permute-start.22 = (f32[2,1024]{1,0:T(2,128)S(1)}, f32[2,1024]{1,0:T(2,128)S(1)}, u32[]{:S(2)}, u32[]{:S(2)}) collective-permute-start(f32[2,1024]{1,0:T(2,128)S(1)} %get-tuple-element.90.own_ref), channel_id=1, source_target_pairs={{0,2},{2,0},{1,3},{3,1},{4,6},{6,4},{5,7},{7,5},{8,10},{10,8},{9,1... | collective-permute-start | bytes 24584 | tf_op jit(solution)/shard_map/ppermute | solution.py:670
  (5 other events, 8.2 us)

commit v6 on v5

--- a/solution.py
+++ b/solution.py
@@ -280,41 +280,30 @@
     middle_hbm,
     gate_ref,
     pre_ref,
-    scaled_hbm,
-    far_hbm,
-    send_hbm,
+    scaled_ref,
+    far_ref,
+    send_ref,
     middle_buf,
-    send_buf,
-    scaled_buf,
-    far_buf,
-    sems,
+    sem,
 ):
-    middle_copy = fetch(middle_hbm, middle_buf, sems.at[0])
+    middle_copy = fetch(middle_hbm, middle_buf, sem)
     pre = sum_of((own_ref, near_ref, across_ref, over_ref))
     pre_ref[...] = pre
     excited = pre * jax.nn.sigmoid(pre)
     gate_ref[...] = jax.nn.sigmoid(exact_dot(excited, up_ref[...], ((1,), (0,))))
     gate = per_row(gate_ref[...], act_ref.shape[0])
-    scaled_buf[...] = (act_ref[...].astype(F32) * gate).astype(BF16)
-    far = jnp.dot(scaled_buf[...], w_ref[...], preferred_element_type=F32).astype(BF16)
-    far_buf[...] = far
+    scaled_ref[...] = (act_ref[...].astype(F32) * gate).astype(BF16)
+    far = jnp.dot(scaled_ref[...], w_ref[...], preferred_element_type=F32).astype(BF16)
+    far_ref[...] = far
     middle_copy.wait()
 
     @pl.when(role_ref[4] == 1)
     def _():
-        send_buf[...] = far
+        send_ref[...] = far
 
     @pl.when(role_ref[4] == 0)
     def _():
-        send_buf[...] = as_rows(middle_buf[...])
-
-    sent = [
-        fetch(send_buf, send_hbm, sems.at[1]),
-        fetch(scaled_buf, scaled_hbm, sems.at[2]),
-        fetch(far_buf, far_hbm, sems.at[3]),
-    ]
-    for copy in sent:
-        copy.wait()
+        send_ref[...] = as_rows(middle_buf[...])
 
 
 def scale(role, act, terms, up, w_far, middle):
@@ -324,7 +313,7 @@
     return pl.pallas_call(
         scale_body,
         in_specs=[pl.BlockSpec(memory_space=pltpu.SMEM)] + [HERE] * 7 + [HBM],
-        out_specs=[HERE, HERE, HBM, HBM, HBM],
+        out_specs=[HERE] * 5,
         out_shape=[
             jax.ShapeDtypeStruct(gates, F32),
             jax.ShapeDtypeStruct(terms[0].shape, F32),
@@ -332,10 +321,7 @@
         + [array] * 3,
         scratch_shapes=[
             pltpu.VMEM(middle.shape, BF16),
-            pltpu.VMEM((count, channels), BF16),
-            pltpu.VMEM((count, channels), BF16),
-            pltpu.VMEM((count, channels), BF16),
-            pltpu.SemaphoreType.DMA((4,)),
+            pltpu.SemaphoreType.DMA,
         ],
         compiler_params=params(),
         cost_estimate=cost(3),
@@ -343,39 +329,21 @@
     )(role, act, *terms, up, w_far, middle)
 
 
-def project_body(order_ref, scaled_hbm, w_hbm, *refs, parts):
-    outs, (scaled_buf, w_buf, out_buf, sems) = refs[:parts], refs[parts:]
-    channels = scaled_buf.shape[1]
-    scaled_copy = fetch(scaled_hbm, scaled_buf, sems.at[0])
-    copies = [
-        fetch(block_of(w_hbm, order_ref[k], channels), w_buf.at[k], sems.at[1 + k])
-        for k in range(parts)
-    ]
-    scaled_copy.wait()
-    sent = []
-    for k in range(parts):
-        copies[k].wait()
-        part = jnp.dot(scaled_buf[...], w_buf[k], preferred_element_type=F32)
-        out_buf[k] = part.astype(BF16)
-        sent.append(fetch(out_buf.at[k], outs[k], sems.at[1 + parts + k]))
-    for copy in sent:
-        copy.wait()
+def project_body(order_ref, scaled_ref, w_ref, *outs):
+    for k, out in enumerate(outs):
+        block = block_of(w_ref, order_ref[k], scaled_ref.shape[1])
+        part = jnp.dot(scaled_ref[...], block[...], preferred_element_type=F32)
+        out[...] = part.astype(BF16)
 
 
 def project(order, parts, scaled, weight):
     count, channels = scaled.shape
     array = jax.ShapeDtypeStruct((count, channels), BF16)
     return pl.pallas_call(
-        functools.partial(project_body, parts=parts),
-        in_specs=[pl.BlockSpec(memory_space=pltpu.SMEM), HBM, HBM],
-        out_specs=[HBM] * parts,
+        project_body,
+        in_specs=[pl.BlockSpec(memory_space=pltpu.SMEM), HERE, HERE],
+        out_specs=[HERE] * parts,
         out_shape=[array] * parts,
-        scratch_shapes=[
-            pltpu.VMEM((count, channels), BF16),
-            pltpu.VMEM((parts, channels, channels), BF16),
-            pltpu.VMEM((parts, count, channels), BF16),
-            pltpu.SemaphoreType.DMA((1 + 2 * parts,)),
-        ],
         compiler_params=params(),
         cost_estimate=cost(3),
         name="project",

time: 92.1 us -> 91.3 us (level)
  Pallas kernels: 35.3 us -> 32.9 us
  waiting for transfers between devices: 14.3 us -> 16 us
    pallas_call x1, Pallas kernels: 3.87 us -> 2.17 us  [project(): pl.pallas_call(project_body, in_specs=[pl.BlockSpec(memory_space=pltpu.SM...]
    ppermute x14, waiting for transfers between devices: 10.3 us -> 12 us  [along_chan(): return lax.ppermute(array, 'chan', pairs)]
  transfers between devices with their start and end apart: 25 -> 25, of which waited for: 8 -> 8; matrix products, arithmetic and copies ran while one was open for 2% -> 2% of each run, Pallas kernels for 37% -> 35%
where the time goes in v6:
time: 91.3 us; the launch traced here: 91 us
  starting transfers between devices  34 us (37%)
  Pallas kernels  32.9 us (36%)
  waiting for transfers between devices  16 us (18%)
  local copies, waits for them, and re-layouts  7.19 us (8%)
    ppermute x14, starting transfers between devices, along_chan(): return lax.ppermute(array, 'chan', pairs)  25 us
    ppermute x14, waiting for transfers between devices, along_chan(): return lax.ppermute(array, 'chan', pairs)  12 us
    ppermute x11, starting transfers between devices, along_dp(): return lax.ppermute(array, 'dp', [(i, i ^ bit) for i in range(8)])  9.07 us
    pallas_call x2, Pallas kernels, weight_grad(): pl.pallas_call(functools.partial(weight_grad_body, pieces=pieces), grid_s...  6.39 us
    pallas_call x2, Pallas kernels, input_grad(): pl.pallas_call(functools.partial(input_grad_body, first=first, pieces=len...  6.38 us
    unnamed x24, local copies, waits for them, and re-layouts  5 us
    pallas_call x5, Pallas kernels, between(): pl.pallas_call(body, grid=(1,), in_specs=[pl.BlockSpec(memory_space=pltpu...  4.57 us
    pallas_call x1, Pallas kernels, conv_forward(): pl.pallas_call(functools.partial(conv_forward_body, height=height, width=...  4.44 us
  transfers between devices with their start and end apart: 25, of which 8 were waited for; matrix products, arithmetic and copies ran while one was open for 2% of the time, Pallas kernels for 35%

profile of v6, /device:TPU:0, one launch (start us, length us, event | category | flops | bytes accessed | tf_op | source)
XLA Modules:
  0.0 91.0 jit_solution(5264149847286869317)
XLA Ops:
  0.6 1.5 %collective-permute-start.3 = (bf16[14,14,2,768]{3,2,1,0:T(2,128)(2,1)}, bf16[14,14,2,768]{3,2,1,0:T(2,128)(2,1)}, u32[]{:S(2)}, u32[]{:S(2)}) collective-permute-start(bf16[14,14,2,768]{3,2,1,0:T(2,128)(2,1)} %bitcast.8), channel_id=1, source_target_pairs={{1,2},{2,1},{5,6},{6,5},{9,10},{10,9},{13,14},{14,13},{17,18},{18,... | collective-permute-start | bytes 1806344 | tf_op jit(solution)/shard_map/ppermute | solution.py:638
  2.1 5.1 %collective-permute-start.4 = (bf16[14,14,2,768]{3,2,1,0:T(2,128)(2,1)}, bf16[14,14,2,768]{3,2,1,0:T(2,128)(2,1)}, u32[]{:S(2)}, u32[]{:S(2)}) collective-permute-start(bf16[14,14,2,768]{3,2,1,0:T(2,128)(2,1)} %bitcast.9), channel_id=1, source_target_pairs={{0,1},{1,0},{2,3},{3,2},{4,5},{5,4},{6,7},{7,6},{8,9},{9,8},{10,11... | collective-permute-start | bytes 1806344 | tf_op jit(solution)/shard_map/ppermute | solution.py:638
  7.2 1.5 %constant_dynamic-slice_fusion.w_ref = bf16[768,768]{1,0:T(8,128)(2,1)S(1)} fusion(bf16[768,3072]{1,0:T(8,128)(2,1)} %refs_1_.1, s32[]{:T(128)S(6)} %select_n.12), kind=kLoop, calls=%fused_computation.1 | loop fusion | bytes 2359300 | tf_op jit(solution)/shard_map/dynamic_slice | solution.py:672
  9.1 1.2 %copy-done.6 = bf16[3,3,64,768]{3,2,1,0:T(8,128)(2,1)S(1)} copy-done((bf16[3,3,64,768]{3,2,1,0:T(8,128)(2,1)S(1)}, bf16[3,3,64,768]{3,2,1,0:T(8,128)(2,1)}, u32[]{:S(2)}) %copy-start.6) | copy-done | bytes 884760
  10.3 4.4 %conv_forward.1 = (f32[392,768]{1,0:T(8,128)S(1)}, bf16[392,768]{1,0:T(8,128)(2,1)S(1)}, f32[2,1024]{1,0:T(2,128)S(1)}) custom-call(bf16[14,14,2,768]{3,2,1,0:T(2,128)(2,1)S(1)} %bitcast.13, bf16[3,3,64,768]{3,2,1,0:T(8,128)(2,1)S(1)} %copy-done.6, bf16[768,1024]{1,0:T(8,128)(2,1)S(1)} %copy-done.2), custom_call_target="tpu_custom_call" | custom-call | flops 1035000000 | bytes 1 | tf_op jit(solution)/shard_map/conv_forward/pallas_call | solution.py:165
  15.8 2.0 %collective-permute-start.1 = (f32[2,1024]{1,0:T(2,128)S(1)}, f32[2,1024]{1,0:T(2,128)S(1)}, u32[]{:S(2)}, u32[]{:S(2)}) collective-permute-start(f32[2,1024]{1,0:T(2,128)S(1)} %get-tuple-element.51.own_ref), channel_id=1, source_target_pairs={{0,3},{3,0},{1,2},{2,1},{4,7},{7,4},{5,6},{6,5},{8,11},{11,8},{9,1... | collective-permute-start | bytes 24584 | tf_op jit(solution)/shard_map/ppermute | solution.py:638
  17.8 1.5 %collective-permute-start.2 = (f32[2,1024]{1,0:T(2,128)S(1)}, f32[2,1024]{1,0:T(2,128)S(1)}, u32[]{:S(2)}, u32[]{:S(2)}) collective-permute-start(f32[2,1024]{1,0:T(2,128)S(1)} %get-tuple-element.51.own_ref), channel_id=1, source_target_pairs={{0,2},{2,0},{1,3},{3,1},{4,6},{6,4},{5,7},{7,5},{8,10},{10,8},{9,1... | collective-permute-start | bytes 24584 | tf_op jit(solution)/shard_map/ppermute | solution.py:638
  20.0 1.1 %collective-permute-done.near_ref = f32[2,1024]{1,0:T(2,128)S(1)} collective-permute-done((f32[2,1024]{1,0:T(2,128)S(1)}, f32[2,1024]{1,0:T(2,128)S(1)}, u32[]{:S(2)}, u32[]{:S(2)}) %collective-permute-start) | collective-permute-done | bytes 8224 | tf_op jit(solution)/shard_map/ppermute | solution.py:638
  21.1 1.1 %collective-permute-done.1.across_ref = f32[2,1024]{1,0:T(2,128)S(1)} collective-permute-done((f32[2,1024]{1,0:T(2,128)S(1)}, f32[2,1024]{1,0:T(2,128)S(1)}, u32[]{:S(2)}, u32[]{:S(2)}) %collective-permute-start.1) | collective-permute-done | bytes 8224 | tf_op jit(solution)/shard_map/ppermute | solution.py:638
  22.4 2.1 %scale.1 = (f32[2,768]{1,0:T(2,128)S(1)}, f32[2,1024]{1,0:T(2,128)S(1)}, bf16[392,768]{1,0:T(8,128)(2,1)S(1)}, bf16[392,768]{1,0:T(8,128)(2,1)S(1)}, bf16[392,768]{1,0:T(8,128)(2,1)S(1)}) custom-call(s32[8]{0:T(128)S(1)} %dynamic-slice_bitcast_fusion.role_ref.order_ref.place_ref, bf16[392,768]{1,0:T(8,128)(2,1)S(1)} %get-tuple-element.50.act_ref.refs_3_, ...), custom_call_target="tpu_custom_call" | custom-call | flops 1035000000 | bytes 1 | tf_op jit(solution)/shard_map/scale/pallas_call | solution.py:313
  26.5 2.3 %copy-done = bf16[768,3072]{1,0:T(8,128)(2,1)S(1)} copy-done((bf16[768,3072]{1,0:T(8,128)(2,1)S(1)}, bf16[768,3072]{1,0:T(8,128)(2,1)}, u32[]{:S(2)}) %copy-start) | copy-done | bytes 4718616
  28.9 2.2 %project.1 = (bf16[392,768]{1,0:T(8,128)(2,1)S(1)}, bf16[392,768]{1,0:T(8,128)(2,1)S(1)}, bf16[392,768]{1,0:T(8,128)(2,1)S(1)}) custom-call(s32[8]{0:T(128)S(1)} %dynamic-slice_bitcast_fusion.role_ref.order_ref.place_ref, bf16[392,768]{1,0:T(8,128)(2,1)S(1)} %get-tuple-element.52.scaled_ref.own_ref, bf16[768,3072]{1,0:T(8,128)(2,1)S(1)} %copy-done), custom_call_target="tpu_custom_call" | custom-call | flops 1035000000 | bytes 1 | tf_op jit(solution)/shard_map/project/pallas_call | solution.py:342
  31.1 7.2 %collective-permute-done.6.came = bf16[392,768]{1,0:T(8,128)(2,1)S(1)} collective-permute-done((bf16[392,768]{1,0:T(8,128)(2,1)S(1)}, bf16[392,768]{1,0:T(8,128)(2,1)S(1)}, u32[]{:S(2)}, u32[]{:S(2)}) %collective-permute-start.6) | collective-permute-done | bytes 602144 | tf_op jit(solution)/shard_map/ppermute | solution.py:638
  40.6 5.8 %collective-permute-start.7 = (bf16[392,768]{1,0:T(8,128)(2,1)S(1)}, bf16[392,768]{1,0:T(8,128)(2,1)S(1)}, u32[]{:S(2)}, u32[]{:S(2)}) collective-permute-start(bf16[392,768]{1,0:T(8,128)(2,1)S(1)} %far_turn.1.held), channel_id=1, source_target_pairs={{0,1},{1,0},{2,3},{3,2},{4,5},{5,4},{6,7},{7,6},{8,9},{9,8},{10,11... | collective-permute-start | bytes 1806344 | tf_op jit(solution)/shard_map/ppermute | solution.py:638
  46.3 4.8 %weight_grad.1 = (bf16[2,384,384]{2,1,0:T(8,128)(2,1)S(1)}, bf16[2,384,384]{2,1,0:T(8,128)(2,1)S(1)}, bf16[2,384,384]{2,1,0:T(8,128)(2,1)S(1)}, bf16[2,384,384]{2,1,0:T(8,128)(2,1)S(1)}) custom-call(s32[8]{0:T(128)S(1)} %dynamic-slice_bitcast_fusion.role_ref.order_ref.place_ref, bf16[392,768]{1,0:T(8,128)(2,1)S(1)} %get-tuple-element.52.scaled_ref.own_ref, ...), custom_call_target="tpu_custom_call" | custom-call | flops 2070000000 | bytes 1 | tf_op jit(solution)/shard_map/weight_grad/pallas_call | solution.py:556
  51.2 1.6 %collective-permute-start.13 = (bf16[2,384,384]{2,1,0:T(8,128)(2,1)S(1)}, bf16[2,384,384]{2,1,0:T(8,128)(2,1)S(1)}, u32[]{:S(2)}, u32[]{:S(2)}) collective-permute-start(bf16[2,384,384]{2,1,0:T(8,128)(2,1)S(1)} %get-tuple-element.69), channel_id=1, source_target_pairs={{0,8},{4,12},{8,0},{12,4},{16,24},{20,28},{24,16},{28,20},{1,9},{5... | collective-permute-start | bytes 1769480 | tf_op jit(solution)/shard_map/ppermute | solution.py:642
  52.7 1.5 %collective-permute-start.14 = (bf16[2,384,384]{2,1,0:T(8,128)(2,1)S(1)}, bf16[2,384,384]{2,1,0:T(8,128)(2,1)S(1)}, u32[]{:S(2)}, u32[]{:S(2)}) collective-permute-start(bf16[2,384,384]{2,1,0:T(8,128)(2,1)S(1)} %get-tuple-element.63), channel_id=1, source_target_pairs={{0,16},{4,20},{8,24},{12,28},{16,0},{20,4},{24,8},{28,12},{1,17},{... | collective-permute-start | bytes 1769480 | tf_op jit(solution)/shard_map/ppermute | solution.py:642
  54.2 3.8 %input_grad.1.refs_2_ = f32[392,768]{1,0:T(8,128)S(1)} custom-call(s32[8]{0:T(128)S(1)} %dynamic-slice_bitcast_fusion.role_ref.order_ref.place_ref, bf16[14,14,2,768]{3,2,1,0:T(2,128)(2,1)S(1)} %bitcast.12, bf16[14,14,2,768]{3,2,1,0:T(2,128)(2,1)} %collective-permute-done.4.refs_1_, bf16[392,768]{1,0:T(8,128)(2,1)S(1)} %get-tuple-element.64.refs_2_, ...), custom_call_target="tpu_custom_call" | custom-call | flops 6900000 | bytes 1 | tf_op jit(solution)/shard_map/input_grad/pallas_call | solution.py:483
  60.4 2.8 %collective-permute-start.16 = (bf16[392,768]{1,0:T(8,128)(2,1)S(1)}, bf16[392,768]{1,0:T(8,128)(2,1)S(1)}, u32[]{:S(2)}, u32[]{:S(2)}) collective-permute-start(bf16[392,768]{1,0:T(8,128)(2,1)S(1)} %outer_turn.1), channel_id=1, source_target_pairs={{0,1},{1,0},{2,3},{3,2},{4,5},{5,4},{6,7},{7,6},{8,9},{9,8},{10,11... | collective-permute-start | bytes 1806344 | tf_op jit(solution)/shard_map/ppermute | solution.py:638
  63.2 1.6 %weight_grad_more.1 = (bf16[384,384]{1,0:T(8,128)(2,1)S(1)}, bf16[384,384]{1,0:T(8,128)(2,1)S(1)}) custom-call(s32[8]{0:T(128)S(1)} %dynamic-slice_bitcast_fusion.role_ref.order_ref.place_ref, bf16[392,768]{1,0:T(8,128)(2,1)S(1)} %get-tuple-element.52.scaled_ref.own_ref, bf16[392,768]{1,0:T(8,128)(2,1)S(1)} %collective-permute-done.9.other_ref, ...), custom_call_target="tpu_custom_call" | custom-call | flops 6900000 | bytes 1 | tf_op jit(solution)/shard_map/weight_grad_more/pallas_call | solution.py:556
  64.8 1.6 %collective-permute-start.18 = (bf16[384,384]{1,0:T(8,128)(2,1)S(1)}, bf16[384,384]{1,0:T(8,128)(2,1)S(1)}, u32[]{:S(2)}, u32[]{:S(2)}) collective-permute-start(bf16[384,384]{1,0:T(8,128)(2,1)S(1)} %get-tuple-element.80.refs_4_), channel_id=1, source_target_pairs={{0,8},{4,12},{8,0},{12,4},{16,24},{20,28},{24,16},{28,20},{1,9},{5... | collective-permute-start | bytes 884744 | tf_op jit(solution)/shard_map/ppermute | solution.py:642
  66.4 1.5 %collective-permute-start.19 = (bf16[384,384]{1,0:T(8,128)(2,1)S(1)}, bf16[384,384]{1,0:T(8,128)(2,1)S(1)}, u32[]{:S(2)}, u32[]{:S(2)}) collective-permute-start(bf16[384,384]{1,0:T(8,128)(2,1)S(1)} %get-tuple-element.71.refs_6_), channel_id=1, source_target_pairs={{0,16},{4,20},{8,24},{12,28},{16,0},{20,4},{24,8},{28,12},{1,17},{... | collective-permute-start | bytes 884744 | tf_op jit(solution)/shard_map/ppermute | solution.py:642
  67.9 2.6 %input_grad_last.1 = (f32[392,768]{1,0:T(8,128)S(1)}, f32[2,1024]{1,0:T(2,128)S(1)}) custom-call(s32[8]{0:T(128)S(1)} %dynamic-slice_bitcast_fusion.role_ref.order_ref.place_ref, bf16[392,768]{1,0:T(8,128)(2,1)S(1)} %get-tuple-element.72.refs_0_, bf16[768,3072]{1,0:T(8,128)(2,1)S(1)} %bitcast.7, f32[392,768]{1,0:T(8,128)S(1)} %input_grad.1.refs_2_, ...), custom_call_target="tpu_custom_call" | custom-call | flops 3449999872 | bytes 1 | tf_op jit(solution)/shard_map/input_grad_last/pallas_call | solution.py:483
  71.0 2.7 %collective-permute-done.18.refs_5_ = bf16[384,384]{1,0:T(8,128)(2,1)S(1)} collective-permute-done((bf16[384,384]{1,0:T(8,128)(2,1)S(1)}, bf16[384,384]{1,0:T(8,128)(2,1)S(1)}, u32[]{:S(2)}, u32[]{:S(2)}) %collective-permute-start.18) | collective-permute-done | bytes 294944 | tf_op jit(solution)/shard_map/ppermute | solution.py:642
  73.7 1.2 %collective-permute-done.19.refs_7_ = bf16[384,384]{1,0:T(8,128)(2,1)S(1)} collective-permute-done((bf16[384,384]{1,0:T(8,128)(2,1)S(1)}, bf16[384,384]{1,0:T(8,128)(2,1)S(1)}, u32[]{:S(2)}, u32[]{:S(2)}) %collective-permute-start.19) | collective-permute-done | bytes 294944 | tf_op jit(solution)/shard_map/ppermute | solution.py:642
  74.9 1.1 %merge.1 = (f32[384,384]{1,0:T(8,128)S(1)}, bf16[384,384]{1,0:T(8,128)(2,1)S(1)}, f32[384,384]{1,0:T(8,128)S(1)}, bf16[384,384]{1,0:T(8,128)(2,1)S(1)}) custom-call(s32[8]{0:T(128)S(1)} %dynamic-slice_bitcast_fusion.role_ref.order_ref.place_ref, bf16[2,384,384]{2,1,0:T(8,128)(2,1)S(1)} %get-tuple-element.76.refs_0_, ...), custom_call_target="tpu_custom_call" | custom-call | flops 690000000 | bytes 1 | tf_op jit(solution)/shard_map/merge/pallas_call | solution.py:596
  76.1 1.6 %collective-permute-start.23 = (bf16[384,384]{1,0:T(8,128)(2,1)S(1)}, bf16[384,384]{1,0:T(8,128)(2,1)S(1)}, u32[]{:S(2)}, u32[]{:S(2)}) collective-permute-start(bf16[384,384]{1,0:T(8,128)(2,1)S(1)} %get-tuple-element.93), channel_id=1, source_target_pairs={{0,16},{4,20},{8,24},{12,28},{16,0},{20,4},{24,8},{28,12},{1,17},{... | collective-permute-start | bytes 884744 | tf_op jit(solution)/shard_map/ppermute | solution.py:642
  78.9 2.3 %collective-permute-start.21 = (f32[2,1024]{1,0:T(2,128)S(1)}, f32[2,1024]{1,0:T(2,128)S(1)}, u32[]{:S(2)}, u32[]{:S(2)}) collective-permute-start(f32[2,1024]{1,0:T(2,128)S(1)} %get-tuple-element.90.own_ref), channel_id=1, source_target_pairs={{0,3},{3,0},{1,2},{2,1},{4,7},{7,4},{5,6},{6,5},{8,11},{11,8},{9,1... | collective-permute-start | bytes 24584 | tf_op jit(solution)/shard_map/ppermute | solution.py:638
  81.7 1.7 %fourth_turn.1 = bf16[14,14,2,768]{3,2,1,0:T(2,128)(2,1)} custom-call(s32[8]{0:T(128)S(1)} %dynamic-slice_bitcast_fusion.role_ref.order_ref.place_ref, bf16[392,768]{1,0:T(8,128)(2,1)S(1)} %get-tuple-element.53.p_own, bf16[392,768]{1,0:T(8,128)(2,1)S(1)} %collective-permute-done.16.came, bf16[392,768]{1,0:T(8,128)(2,1)S(1)} %collective-permute-done.17.crossed), custom_call_target="tpu_custom_call" | custom-call | flops 6900000 | bytes 1 | tf_op jit(solution)/shard_map/fourth_turn/pallas_call | solution.py:407
  84.4 1.4 %collective-permute-done.22.over_ref = f32[2,1024]{1,0:T(2,128)S(1)} collective-permute-done((f32[2,1024]{1,0:T(2,128)S(1)}, f32[2,1024]{1,0:T(2,128)S(1)}, u32[]{:S(2)}, u32[]{:S(2)}) %collective-permute-start.22) | collective-permute-done | bytes 8224 | tf_op jit(solution)/shard_map/ppermute | solution.py:638
  85.8 4.0 %conv_backward.1 = bf16[14,14,2,768]{3,2,1,0:T(2,128)(2,1)} custom-call(f32[392,768]{1,0:T(8,128)S(1)} %get-tuple-element.83.part_ref, f32[392,768]{1,0:T(8,128)S(1)} %get-tuple-element.88.slope_ref, f32[2,1024]{1,0:T(2,128)S(1)} %get-tuple-element.90.own_ref, f32[2,1024]{1,0:T(2,128)S(1)} %collective-permute-done.20.near_ref, ...), custom_call_target="tpu_custom_call" | custom-call | flops 1035000000 | bytes 1 | tf_op jit(solution)/shard_map/conv_backward/pallas_call | solution.py:250
  89.8 1.1 %finish.1 = f32[768,384]{1,0:T(8,128)} custom-call(f32[384,384]{1,0:T(8,128)S(1)} %get-tuple-element.92.top, bf16[384,384]{1,0:T(8,128)(2,1)S(1)} %collective-permute-done.23.top_came, f32[384,384]{1,0:T(8,128)S(1)} %get-tuple-element.94.bottom, bf16[384,384]{1,0:T(8,128)(2,1)S(1)} %collective-permute-done.24.bottom_came), custom_call_target="tpu_custom_call" | custom-call | flops 690000000 | bytes 1 | tf_op jit(solution)/shard_map/finish/pallas_call | solution.py:617
  (61 shorter events, 12.1 us)
Async XLA Ops:
  0.6 21.8 %collective-permute-start.3 = (bf16[14,14,2,768]{3,2,1,0:T(2,128)(2,1)}, bf16[14,14,2,768]{3,2,1,0:T(2,128)(2,1)}, u32[]{:S(2)}, u32[]{:S(2)}) collective-permute-start(bf16[14,14,2,768]{3,2,1,0:T(2,128)(2,1)} %bitcast.8), channel_id=1, source_target_pairs={{1,2},{2,1},{5,6},{6,5},{9,10},{10,9},{13,14},{14,13},{17,18},{18,... | collective-permute-start | bytes 1806344 | tf_op jit(solution)/shard_map/ppermute | solution.py:638
  2.1 23.0 %collective-permute-start.4 = (bf16[14,14,2,768]{3,2,1,0:T(2,128)(2,1)}, bf16[14,14,2,768]{3,2,1,0:T(2,128)(2,1)}, u32[]{:S(2)}, u32[]{:S(2)}) collective-permute-start(bf16[14,14,2,768]{3,2,1,0:T(2,128)(2,1)} %bitcast.9), channel_id=1, source_target_pairs={{0,1},{1,0},{2,3},{3,2},{4,5},{5,4},{6,7},{7,6},{8,9},{9,8},{10,11... | collective-permute-start | bytes 1806344 | tf_op jit(solution)/shard_map/ppermute | solution.py:638
  10.3 12.1 %copy-start.1 = (bf16[1024,768]{1,0:T(8,128)(2,1)S(1)}, bf16[1024,768]{1,0:T(8,128)(2,1)}, u32[]{:S(2)}) copy-start(bf16[1024,768]{1,0:T(8,128)(2,1)} %refs_5_.1) | copy-start | bytes 4718596
  15.8 5.3 %collective-permute-start = (f32[2,1024]{1,0:T(2,128)S(1)}, f32[2,1024]{1,0:T(2,128)S(1)}, u32[]{:S(2)}, u32[]{:S(2)}) collective-permute-start(f32[2,1024]{1,0:T(2,128)S(1)} %get-tuple-element.51.own_ref), channel_id=1, source_target_pairs={{0,1},{1,0},{2,3},{3,2},{4,5},{5,4},{6,7},{7,6},{8,9},{9,8},{10,11... | collective-permute-start | bytes 24584 | tf_op jit(solution)/shard_map/ppermute | solution.py:638
  15.8 6.4 %collective-permute-start.1 = (f32[2,1024]{1,0:T(2,128)S(1)}, f32[2,1024]{1,0:T(2,128)S(1)}, u32[]{:S(2)}, u32[]{:S(2)}) collective-permute-start(f32[2,1024]{1,0:T(2,128)S(1)} %get-tuple-element.51.own_ref), channel_id=1, source_target_pairs={{0,3},{3,0},{1,2},{2,1},{4,7},{7,4},{5,6},{6,5},{8,11},{11,8},{9,1... | collective-permute-start | bytes 24584 | tf_op jit(solution)/shard_map/ppermute | solution.py:638
  17.8 4.6 %collective-permute-start.2 = (f32[2,1024]{1,0:T(2,128)S(1)}, f32[2,1024]{1,0:T(2,128)S(1)}, u32[]{:S(2)}, u32[]{:S(2)}) collective-permute-start(f32[2,1024]{1,0:T(2,128)S(1)} %get-tuple-element.51.own_ref), channel_id=1, source_target_pairs={{0,2},{2,0},{1,3},{3,1},{4,6},{6,4},{5,7},{7,5},{8,10},{10,8},{9,1... | collective-permute-start | bytes 24584 | tf_op jit(solution)/shard_map/ppermute | solution.py:638
  22.4 3.5 %copy-start.8 = (bf16[2,14,14,768]{3,0,2,1:T(2,128)(2,1)S(1)}, bf16[2,14,14,768]{3,0,2,1:T(2,128)(2,1)}, u32[]{:S(2)}) copy-start(bf16[2,14,14,768]{3,0,2,1:T(2,128)(2,1)} %param.12) | copy-start | bytes 1806340
  24.6 13.7 %collective-permute-start.6 = (bf16[392,768]{1,0:T(8,128)(2,1)S(1)}, bf16[392,768]{1,0:T(8,128)(2,1)S(1)}, u32[]{:S(2)}, u32[]{:S(2)}) collective-permute-start(bf16[392,768]{1,0:T(8,128)(2,1)S(1)} %get-tuple-element.56.held), channel_id=1, source_target_pairs={{0,1},{1,0},{2,3},{3,2},{4,5},{5,4},{6,7},{7,6},{8,9},{9,8},{10,11... | collective-permute-start | bytes 1806344 | tf_op jit(solution)/shard_map/ppermute | solution.py:638
  25.2 13.9 %collective-permute-start.5 = (bf16[14,14,2,768]{3,2,1,0:T(2,128)(2,1)}, bf16[14,14,2,768]{3,2,1,0:T(2,128)(2,1)S(1)}, u32[]{:S(2)}, u32[]{:S(2)}) collective-permute-start(bf16[14,14,2,768]{3,2,1,0:T(2,128)(2,1)} %collective-permute-done.4.refs_1_), channel_id=1, source_target_pairs={{1,2},{2,1},{5,6},{6,5},{9,10},{10,9},{13,14},{14,13},{17,18},{18,... | collective-permute-start | bytes 1806344 | tf_op jit(solution)/shard_map/ppermute | solution.py:638
  25.9 14.7 %collective-permute-start.10 = (bf16[14,14,2,768]{3,2,1,0:T(2,128)(2,1)S(1)}, bf16[14,14,2,768]{3,2,1,0:T(2,128)(2,1)S(1)}, u32[]{:S(2)}, u32[]{:S(2)}) collective-permute-start(bf16[14,14,2,768]{3,2,1,0:T(2,128)(2,1)S(1)} %bitcast.10), channel_id=1, source_target_pairs={{0,4},{4,0},{8,12},{12,8},{16,20},{20,16},{24,28},{28,24},{1,5},{5... | collective-permute-start | bytes 1806344 | tf_op jit(solution)/shard_map/ppermute | solution.py:642
  26.0 20.4 %collective-permute-start.9 = (bf16[392,768]{1,0:T(8,128)(2,1)S(1)}, bf16[392,768]{1,0:T(8,128)(2,1)S(1)}, u32[]{:S(2)}, u32[]{:S(2)}) collective-permute-start(bf16[392,768]{1,0:T(8,128)(2,1)S(1)} %get-tuple-element.52.scaled_ref.own_ref), channel_id=1, source_target_pairs={{0,4},{4,0},{8,12},{12,8},{16,20},{20,16},{24,28},{28,24},{1,5},{5... | collective-permute-start | bytes 1806344 | tf_op jit(solution)/shard_map/ppermute | solution.py:642
  26.5 19.9 %collective-permute-start.11 = (bf16[14,14,2,768]{3,2,1,0:T(2,128)(2,1)}, bf16[14,14,2,768]{3,2,1,0:T(2,128)(2,1)S(1)}, u32[]{:S(2)}, u32[]{:S(2)}) collective-permute-start(bf16[14,14,2,768]{3,2,1,0:T(2,128)(2,1)} %collective-permute-done.4.refs_1_), channel_id=1, source_target_pairs={{0,4},{4,0},{8,12},{12,8},{16,20},{20,16},{24,28},{28,24},{1,5},{5... | collective-permute-start | bytes 1806344 | tf_op jit(solution)/shard_map/ppermute | solution.py:642
  38.3 16.0 %slice-start = ((s8[4718592]{0:T(1024)(128)(4,1)}), s8[4194304]{0:T(1024)(128)(4,1)S(1)}, s32[]{:S(2)}) async-start(s8[4718592]{0:T(1024)(128)(4,1)} %bitcast.6), calls=%async_computation | async-start | bytes 8388608
  39.0 7.3 %collective-permute-start.12 = (bf16[392,768]{1,0:T(8,128)(2,1)S(1)}, bf16[392,768]{1,0:T(8,128)(2,1)S(1)}, u32[]{:S(2)}, u32[]{:S(2)}) collective-permute-start(bf16[392,768]{1,0:T(8,128)(2,1)S(1)} %get-tuple-element.64.refs_2_), channel_id=1, source_target_pairs={{0,4},{4,0},{8,12},{12,8},{16,20},{20,16},{24,28},{28,24},{1,5},{5... | collective-permute-start | bytes 1806344 | tf_op jit(solution)/shard_map/ppermute | solution.py:642
  39.1 19.0 %collective-permute-start.8 = (bf16[392,768]{1,0:T(8,128)(2,1)S(1)}, bf16[392,768]{1,0:T(8,128)(2,1)S(1)}, u32[]{:S(2)}, u32[]{:S(2)}) collective-permute-start(bf16[392,768]{1,0:T(8,128)(2,1)S(1)} %get-tuple-element.59), channel_id=1, source_target_pairs={{1,2},{2,1},{5,6},{6,5},{9,10},{10,9},{13,14},{14,13},{17,18},{18,... | collective-permute-start | bytes 1806344 | tf_op jit(solution)/shard_map/ppermute | solution.py:638
  39.9 14.3 %slice-start.1 = ((s8[4718592]{0:T(1024)(128)(4,1)}), s8[524288]{0:T(1024)(128)(4,1)S(1)}, s32[]{:S(2)}) async-start(s8[4718592]{0:T(1024)(128)(4,1)} %bitcast.6), calls=%async_computation.1 | async-start | bytes 1048576
  40.6 18.3 %collective-permute-start.7 = (bf16[392,768]{1,0:T(8,128)(2,1)S(1)}, bf16[392,768]{1,0:T(8,128)(2,1)S(1)}, u32[]{:S(2)}, u32[]{:S(2)}) collective-permute-start(bf16[392,768]{1,0:T(8,128)(2,1)S(1)} %far_turn.1.held), channel_id=1, source_target_pairs={{0,1},{1,0},{2,3},{3,2},{4,5},{5,4},{6,7},{7,6},{8,9},{9,8},{10,11... | collective-permute-start | bytes 1806344 | tf_op jit(solution)/shard_map/ppermute | solution.py:638
  51.2 15.2 %collective-permute-start.13 = (bf16[2,384,384]{2,1,0:T(8,128)(2,1)S(1)}, bf16[2,384,384]{2,1,0:T(8,128)(2,1)S(1)}, u32[]{:S(2)}, u32[]{:S(2)}) collective-permute-start(bf16[2,384,384]{2,1,0:T(8,128)(2,1)S(1)} %get-tuple-element.69), channel_id=1, source_target_pairs={{0,8},{4,12},{8,0},{12,4},{16,24},{20,28},{24,16},{28,20},{1,9},{5... | collective-permute-start | bytes 1769480 | tf_op jit(solution)/shard_map/ppermute | solution.py:642
  52.7 15.2 %collective-permute-start.14 = (bf16[2,384,384]{2,1,0:T(8,128)(2,1)S(1)}, bf16[2,384,384]{2,1,0:T(8,128)(2,1)S(1)}, u32[]{:S(2)}, u32[]{:S(2)}) collective-permute-start(bf16[2,384,384]{2,1,0:T(8,128)(2,1)S(1)} %get-tuple-element.63), channel_id=1, source_target_pairs={{0,16},{4,20},{8,24},{12,28},{16,0},{20,4},{24,8},{28,12},{1,17},{... | collective-permute-start | bytes 1769480 | tf_op jit(solution)/shard_map/ppermute | solution.py:642
  59.6 3.6 %collective-permute-start.15 = (bf16[392,384]{1,0:T(8,128)(2,1)S(1)}, bf16[392,384]{1,0:T(8,128)(2,1)S(1)}, u32[]{:S(2)}, u32[]{:S(2)}) collective-permute-start(bf16[392,384]{1,0:T(8,128)(2,1)S(1)} %get-tuple-element.70), channel_id=1, source_target_pairs={{0,4},{4,0},{8,12},{12,8},{16,20},{20,16},{24,28},{28,24},{1,5},{5... | collective-permute-start | bytes 903176 | tf_op jit(solution)/shard_map/ppermute | solution.py:642
  59.7 18.5 %collective-permute-start.17 = (bf16[392,768]{1,0:T(8,128)(2,1)S(1)}, bf16[392,768]{1,0:T(8,128)(2,1)S(1)}, u32[]{:S(2)}, u32[]{:S(2)}) collective-permute-start(bf16[392,768]{1,0:T(8,128)(2,1)S(1)} %get-tuple-element.75), channel_id=1, source_target_pairs={{1,2},{2,1},{5,6},{6,5},{9,10},{10,9},{13,14},{14,13},{17,18},{18,... | collective-permute-start | bytes 1806344 | tf_op jit(solution)/shard_map/ppermute | solution.py:638
  60.4 17.8 %collective-permute-start.16 = (bf16[392,768]{1,0:T(8,128)(2,1)S(1)}, bf16[392,768]{1,0:T(8,128)(2,1)S(1)}, u32[]{:S(2)}, u32[]{:S(2)}) collective-permute-start(bf16[392,768]{1,0:T(8,128)(2,1)S(1)} %outer_turn.1), channel_id=1, source_target_pairs={{0,1},{1,0},{2,3},{3,2},{4,5},{5,4},{6,7},{7,6},{8,9},{9,8},{10,11... | collective-permute-start | bytes 1806344 | tf_op jit(solution)/shard_map/ppermute | solution.py:638
  64.8 8.9 %collective-permute-start.18 = (bf16[384,384]{1,0:T(8,128)(2,1)S(1)}, bf16[384,384]{1,0:T(8,128)(2,1)S(1)}, u32[]{:S(2)}, u32[]{:S(2)}) collective-permute-start(bf16[384,384]{1,0:T(8,128)(2,1)S(1)} %get-tuple-element.80.refs_4_), channel_id=1, source_target_pairs={{0,8},{4,12},{8,0},{12,4},{16,24},{20,28},{24,16},{28,20},{1,9},{5... | collective-permute-start | bytes 884744 | tf_op jit(solution)/shard_map/ppermute | solution.py:642
  66.4 8.6 %collective-permute-start.19 = (bf16[384,384]{1,0:T(8,128)(2,1)S(1)}, bf16[384,384]{1,0:T(8,128)(2,1)S(1)}, u32[]{:S(2)}, u32[]{:S(2)}) collective-permute-start(bf16[384,384]{1,0:T(8,128)(2,1)S(1)} %get-tuple-element.71.refs_6_), channel_id=1, source_target_pairs={{0,16},{4,20},{8,24},{12,28},{16,0},{20,4},{24,8},{28,12},{1,17},{... | collective-permute-start | bytes 884744 | tf_op jit(solution)/shard_map/ppermute | solution.py:642
  67.9 2.6 %copy-start.5 = (f32[392,768]{1,0:T(8,128)S(1)}, f32[392,768]{1,0:T(8,128)}, u32[]{:S(2)}) copy-start(f32[392,768]{1,0:T(8,128)} %copy-done.4) | copy-start | bytes 3612676
  74.9 10.9 %copy-start.7 = (bf16[3,3,64,768]{3,2,1,0:T(8,128)(2,1)S(1)}, bf16[3,3,64,768]{3,2,1,0:T(8,128)(2,1)}, u32[]{:S(2)}) copy-start(bf16[3,3,64,768]{3,2,1,0:T(8,128)(2,1)} %w_ref.5) | copy-start | bytes 2654212
  76.1 13.7 %collective-permute-start.23 = (bf16[384,384]{1,0:T(8,128)(2,1)S(1)}, bf16[384,384]{1,0:T(8,128)(2,1)S(1)}, u32[]{:S(2)}, u32[]{:S(2)}) collective-permute-start(bf16[384,384]{1,0:T(8,128)(2,1)S(1)} %get-tuple-element.93), channel_id=1, source_target_pairs={{0,16},{4,20},{8,24},{12,28},{16,0},{20,4},{24,8},{28,12},{1,17},{... | collective-permute-start | bytes 884744 | tf_op jit(solution)/shard_map/ppermute | solution.py:642
  77.6 8.1 %copy-start.3 = (bf16[768,1024]{1,0:T(8,128)(2,1)S(1)}, bf16[768,1024]{1,0:T(8,128)(2,1)}, u32[]{:S(2)}) copy-start(bf16[768,1024]{1,0:T(8,128)(2,1)} %down_ref.3) | copy-start | bytes 4718596
  77.7 12.2 %collective-permute-start.24 = (bf16[384,384]{1,0:T(8,128)(2,1)S(1)}, bf16[384,384]{1,0:T(8,128)(2,1)S(1)}, u32[]{:S(2)}, u32[]{:S(2)}) collective-permute-start(bf16[384,384]{1,0:T(8,128)(2,1)S(1)} %get-tuple-element.85), channel_id=1, source_target_pairs={{0,8},{4,12},{8,0},{12,4},{16,24},{20,28},{24,16},{28,20},{1,9},{5... | collective-permute-start | bytes 884744 | tf_op jit(solution)/shard_map/ppermute | solution.py:642
  78.2 5.2 %collective-permute-start.20 = (f32[2,1024]{1,0:T(2,128)S(1)}, f32[2,1024]{1,0:T(2,128)S(1)}, u32[]{:S(2)}, u32[]{:S(2)}) collective-permute-start(f32[2,1024]{1,0:T(2,128)S(1)} %get-tuple-element.90.own_ref), channel_id=1, source_target_pairs={{0,1},{1,0},{2,3},{3,2},{4,5},{5,4},{6,7},{7,6},{8,9},{9,8},{10,11... | collective-permute-start | bytes 24584 | tf_op jit(solution)/shard_map/ppermute | solution.py:638
  78.9 5.4 %collective-permute-start.21 = (f32[2,1024]{1,0:T(2,128)S(1)}, f32[2,1024]{1,0:T(2,128)S(1)}, u32[]{:S(2)}, u32[]{:S(2)}) collective-permute-start(f32[2,1024]{1,0:T(2,128)S(1)} %get-tuple-element.90.own_ref), channel_id=1, source_target_pairs={{0,3},{3,0},{1,2},{2,1},{4,7},{7,4},{5,6},{6,5},{8,11},{11,8},{9,1... | collective-permute-start | bytes 24584 | tf_op jit(solution)/shard_map/ppermute | solution.py:638
  81.2 4.5 %collective-permute-start.22 = (f32[2,1024]{1,0:T(2,128)S(1)}, f32[2,1024]{1,0:T(2,128)S(1)}, u32[]{:S(2)}, u32[]{:S(2)}) collective-permute-start(f32[2,1024]{1,0:T(2,128)S(1)} %get-tuple-element.90.own_ref), channel_id=1, source_target_pairs={{0,2},{2,0},{1,3},{3,1},{4,6},{6,4},{5,7},{7,5},{8,10},{10,8},{9,1... | collective-permute-start | bytes 24584 | tf_op jit(solution)/shard_map/ppermute | solution.py:638
  (5 other events, 8.2 us)

commit v7 on v6

--- a/solution.py
+++ b/solution.py
@@ -582,7 +582,8 @@
         (y_keep, y_came, x, lower, lower_came, to_by, to_bx, bottom, to_x),
     ):
         extra = jnp.where(here, both(more, more_came), 0.0)
-        stay[...] = both(keep.at[index], came.at[index]) + jnp.where(there, extra, 0.0)
+        held = both(keep.at[index], came.at[index]) + jnp.where(there, extra, 0.0)
+        stay[...] = held.astype(BF16)
         rest = both(keep.at[1 - index], came.at[1 - index]) + jnp.where(there, 0.0, extra)
         leave[...] = rest.astype(BF16)
 
@@ -591,7 +592,7 @@
     rows, columns = arrays[0].shape[1:]
     pair = pl.BlockSpec((2, rows, columns), lambda i, place: (0, 0, 0))
     one = pl.BlockSpec((rows, columns), lambda i, place: (0, 0))
-    kept = jax.ShapeDtypeStruct((rows, columns), F32)
+    kept = jax.ShapeDtypeStruct((rows, columns), BF16)
     sent = jax.ShapeDtypeStruct((rows, columns), BF16)
     return pl.pallas_call(
         merge_body,
@@ -607,8 +608,8 @@
 
 def finish_body(top, top_came, bottom, bottom_came, out):
     rows = top.shape[0]
-    out[:rows] = top[...] + top_came[...].astype(F32)
-    out[rows:] = bottom[...] + bottom_came[...].astype(F32)
+    out[:rows] = top[...].astype(F32) + top_came[...].astype(F32)
+    out[rows:] = bottom[...].astype(F32) + bottom_came[...].astype(F32)
 
 
 def finish(top, top_came, bottom, bottom_came):

time: 91.3 us -> 91.3 us (level)
  no operation moved by 1% of the time
where the time goes in v7:
time: 91.3 us; the launch traced here: 91 us
  starting transfers between devices  34 us (37%)
  Pallas kernels  32.9 us (36%)
  waiting for transfers between devices  16 us (18%)
  local copies, waits for them, and re-layouts  7.19 us (8%)
    ppermute x14, starting transfers between devices, along_chan(): return lax.ppermute(array, 'chan', pairs)  25 us
    ppermute x14, waiting for transfers between devices, along_chan(): return lax.ppermute(array, 'chan', pairs)  12 us
    ppermute x11, starting transfers between devices, along_dp(): return lax.ppermute(array, 'dp', [(i, i ^ bit) for i in range(8)])  9.07 us
    pallas_call x2, Pallas kernels, weight_grad(): pl.pallas_call(functools.partial(weight_grad_body, pieces=pieces), grid_s...  6.39 us
    pallas_call x2, Pallas kernels, input_grad(): pl.pallas_call(functools.partial(input_grad_body, first=first, pieces=len...  6.38 us
    unnamed x24, local copies, waits for them, and re-layouts  5 us
    pallas_call x5, Pallas kernels, between(): pl.pallas_call(body, grid=(1,), in_specs=[pl.BlockSpec(memory_space=pltpu...  4.57 us
    pallas_call x1, Pallas kernels, conv_forward(): pl.pallas_call(functools.partial(conv_forward_body, height=height, width=...  4.44 us
  transfers between devices with their start and end apart: 25, of which 8 were waited for; matrix products, arithmetic and copies ran while one was open for 2% of the time, Pallas kernels for 35%

profile of v7, /device:TPU:0, one launch (start us, length us, event | category | flops | bytes accessed | tf_op | source)
XLA Modules:
  0.0 91.0 jit_solution(2226717129411058873)
XLA Ops:
  0.6 1.5 %collective-permute-start.3 = (bf16[14,14,2,768]{3,2,1,0:T(2,128)(2,1)}, bf16[14,14,2,768]{3,2,1,0:T(2,128)(2,1)}, u32[]{:S(2)}, u32[]{:S(2)}) collective-permute-start(bf16[14,14,2,768]{3,2,1,0:T(2,128)(2,1)} %bitcast.8), channel_id=1, source_target_pairs={{1,2},{2,1},{5,6},{6,5},{9,10},{10,9},{13,14},{14,13},{17,18},{18,... | collective-permute-start | bytes 1806344 | tf_op jit(solution)/shard_map/ppermute | solution.py:639
  2.1 5.1 %collective-permute-start.4 = (bf16[14,14,2,768]{3,2,1,0:T(2,128)(2,1)}, bf16[14,14,2,768]{3,2,1,0:T(2,128)(2,1)}, u32[]{:S(2)}, u32[]{:S(2)}) collective-permute-start(bf16[14,14,2,768]{3,2,1,0:T(2,128)(2,1)} %bitcast.9), channel_id=1, source_target_pairs={{0,1},{1,0},{2,3},{3,2},{4,5},{5,4},{6,7},{7,6},{8,9},{9,8},{10,11... | collective-permute-start | bytes 1806344 | tf_op jit(solution)/shard_map/ppermute | solution.py:639
  7.2 1.5 %constant_dynamic-slice_fusion.w_ref = bf16[768,768]{1,0:T(8,128)(2,1)S(1)} fusion(bf16[768,3072]{1,0:T(8,128)(2,1)} %refs_1_.1, s32[]{:T(128)S(6)} %select_n.12), kind=kLoop, calls=%fused_computation.1 | loop fusion | bytes 2359300 | tf_op jit(solution)/shard_map/dynamic_slice | solution.py:673
  9.1 1.2 %copy-done.6 = bf16[3,3,64,768]{3,2,1,0:T(8,128)(2,1)S(1)} copy-done((bf16[3,3,64,768]{3,2,1,0:T(8,128)(2,1)S(1)}, bf16[3,3,64,768]{3,2,1,0:T(8,128)(2,1)}, u32[]{:S(2)}) %copy-start.6) | copy-done | bytes 884760
  10.3 4.4 %conv_forward.1 = (f32[392,768]{1,0:T(8,128)S(1)}, bf16[392,768]{1,0:T(8,128)(2,1)S(1)}, f32[2,1024]{1,0:T(2,128)S(1)}) custom-call(bf16[14,14,2,768]{3,2,1,0:T(2,128)(2,1)S(1)} %bitcast.13, bf16[3,3,64,768]{3,2,1,0:T(8,128)(2,1)S(1)} %copy-done.6, bf16[768,1024]{1,0:T(8,128)(2,1)S(1)} %copy-done.2), custom_call_target="tpu_custom_call" | custom-call | flops 1035000000 | bytes 1 | tf_op jit(solution)/shard_map/conv_forward/pallas_call | solution.py:165
  15.8 2.0 %collective-permute-start.1 = (f32[2,1024]{1,0:T(2,128)S(1)}, f32[2,1024]{1,0:T(2,128)S(1)}, u32[]{:S(2)}, u32[]{:S(2)}) collective-permute-start(f32[2,1024]{1,0:T(2,128)S(1)} %get-tuple-element.51.own_ref), channel_id=1, source_target_pairs={{0,3},{3,0},{1,2},{2,1},{4,7},{7,4},{5,6},{6,5},{8,11},{11,8},{9,1... | collective-permute-start | bytes 24584 | tf_op jit(solution)/shard_map/ppermute | solution.py:639
  17.8 1.5 %collective-permute-start.2 = (f32[2,1024]{1,0:T(2,128)S(1)}, f32[2,1024]{1,0:T(2,128)S(1)}, u32[]{:S(2)}, u32[]{:S(2)}) collective-permute-start(f32[2,1024]{1,0:T(2,128)S(1)} %get-tuple-element.51.own_ref), channel_id=1, source_target_pairs={{0,2},{2,0},{1,3},{3,1},{4,6},{6,4},{5,7},{7,5},{8,10},{10,8},{9,1... | collective-permute-start | bytes 24584 | tf_op jit(solution)/shard_map/ppermute | solution.py:639
  20.0 1.1 %collective-permute-done.near_ref = f32[2,1024]{1,0:T(2,128)S(1)} collective-permute-done((f32[2,1024]{1,0:T(2,128)S(1)}, f32[2,1024]{1,0:T(2,128)S(1)}, u32[]{:S(2)}, u32[]{:S(2)}) %collective-permute-start) | collective-permute-done | bytes 8224 | tf_op jit(solution)/shard_map/ppermute | solution.py:639
  21.1 1.1 %collective-permute-done.1.across_ref = f32[2,1024]{1,0:T(2,128)S(1)} collective-permute-done((f32[2,1024]{1,0:T(2,128)S(1)}, f32[2,1024]{1,0:T(2,128)S(1)}, u32[]{:S(2)}, u32[]{:S(2)}) %collective-permute-start.1) | collective-permute-done | bytes 8224 | tf_op jit(solution)/shard_map/ppermute | solution.py:639
  22.4 2.1 %scale.1 = (f32[2,768]{1,0:T(2,128)S(1)}, f32[2,1024]{1,0:T(2,128)S(1)}, bf16[392,768]{1,0:T(8,128)(2,1)S(1)}, bf16[392,768]{1,0:T(8,128)(2,1)S(1)}, bf16[392,768]{1,0:T(8,128)(2,1)S(1)}) custom-call(s32[8]{0:T(128)S(1)} %dynamic-slice_bitcast_fusion.role_ref.order_ref.place_ref, bf16[392,768]{1,0:T(8,128)(2,1)S(1)} %get-tuple-element.50.act_ref.refs_3_, ...), custom_call_target="tpu_custom_call" | custom-call | flops 1035000000 | bytes 1 | tf_op jit(solution)/shard_map/scale/pallas_call | solution.py:313
  26.5 2.3 %copy-done = bf16[768,3072]{1,0:T(8,128)(2,1)S(1)} copy-done((bf16[768,3072]{1,0:T(8,128)(2,1)S(1)}, bf16[768,3072]{1,0:T(8,128)(2,1)}, u32[]{:S(2)}) %copy-start) | copy-done | bytes 4718616
  28.9 2.2 %project.1 = (bf16[392,768]{1,0:T(8,128)(2,1)S(1)}, bf16[392,768]{1,0:T(8,128)(2,1)S(1)}, bf16[392,768]{1,0:T(8,128)(2,1)S(1)}) custom-call(s32[8]{0:T(128)S(1)} %dynamic-slice_bitcast_fusion.role_ref.order_ref.place_ref, bf16[392,768]{1,0:T(8,128)(2,1)S(1)} %get-tuple-element.52.scaled_ref.own_ref, bf16[768,3072]{1,0:T(8,128)(2,1)S(1)} %copy-done), custom_call_target="tpu_custom_call" | custom-call | flops 1035000000 | bytes 1 | tf_op jit(solution)/shard_map/project/pallas_call | solution.py:342
  31.1 7.2 %collective-permute-done.6.came = bf16[392,768]{1,0:T(8,128)(2,1)S(1)} collective-permute-done((bf16[392,768]{1,0:T(8,128)(2,1)S(1)}, bf16[392,768]{1,0:T(8,128)(2,1)S(1)}, u32[]{:S(2)}, u32[]{:S(2)}) %collective-permute-start.6) | collective-permute-done | bytes 602144 | tf_op jit(solution)/shard_map/ppermute | solution.py:639
  40.6 5.8 %collective-permute-start.7 = (bf16[392,768]{1,0:T(8,128)(2,1)S(1)}, bf16[392,768]{1,0:T(8,128)(2,1)S(1)}, u32[]{:S(2)}, u32[]{:S(2)}) collective-permute-start(bf16[392,768]{1,0:T(8,128)(2,1)S(1)} %far_turn.1.held), channel_id=1, source_target_pairs={{0,1},{1,0},{2,3},{3,2},{4,5},{5,4},{6,7},{7,6},{8,9},{9,8},{10,11... | collective-permute-start | bytes 1806344 | tf_op jit(solution)/shard_map/ppermute | solution.py:639
  46.3 4.8 %weight_grad.1 = (bf16[2,384,384]{2,1,0:T(8,128)(2,1)S(1)}, bf16[2,384,384]{2,1,0:T(8,128)(2,1)S(1)}, bf16[2,384,384]{2,1,0:T(8,128)(2,1)S(1)}, bf16[2,384,384]{2,1,0:T(8,128)(2,1)S(1)}) custom-call(s32[8]{0:T(128)S(1)} %dynamic-slice_bitcast_fusion.role_ref.order_ref.place_ref, bf16[392,768]{1,0:T(8,128)(2,1)S(1)} %get-tuple-element.52.scaled_ref.own_ref, ...), custom_call_target="tpu_custom_call" | custom-call | flops 2070000000 | bytes 1 | tf_op jit(solution)/shard_map/weight_grad/pallas_call | solution.py:556
  51.2 1.6 %collective-permute-start.13 = (bf16[2,384,384]{2,1,0:T(8,128)(2,1)S(1)}, bf16[2,384,384]{2,1,0:T(8,128)(2,1)S(1)}, u32[]{:S(2)}, u32[]{:S(2)}) collective-permute-start(bf16[2,384,384]{2,1,0:T(8,128)(2,1)S(1)} %get-tuple-element.69), channel_id=1, source_target_pairs={{0,8},{4,12},{8,0},{12,4},{16,24},{20,28},{24,16},{28,20},{1,9},{5... | collective-permute-start | bytes 1769480 | tf_op jit(solution)/shard_map/ppermute | solution.py:643
  52.7 1.5 %collective-permute-start.14 = (bf16[2,384,384]{2,1,0:T(8,128)(2,1)S(1)}, bf16[2,384,384]{2,1,0:T(8,128)(2,1)S(1)}, u32[]{:S(2)}, u32[]{:S(2)}) collective-permute-start(bf16[2,384,384]{2,1,0:T(8,128)(2,1)S(1)} %get-tuple-element.63), channel_id=1, source_target_pairs={{0,16},{4,20},{8,24},{12,28},{16,0},{20,4},{24,8},{28,12},{1,17},{... | collective-permute-start | bytes 1769480 | tf_op jit(solution)/shard_map/ppermute | solution.py:643
  54.2 3.8 %input_grad.1.refs_2_ = f32[392,768]{1,0:T(8,128)S(1)} custom-call(s32[8]{0:T(128)S(1)} %dynamic-slice_bitcast_fusion.role_ref.order_ref.place_ref, bf16[14,14,2,768]{3,2,1,0:T(2,128)(2,1)S(1)} %bitcast.12, bf16[14,14,2,768]{3,2,1,0:T(2,128)(2,1)} %collective-permute-done.4.refs_1_, bf16[392,768]{1,0:T(8,128)(2,1)S(1)} %get-tuple-element.64.refs_2_, ...), custom_call_target="tpu_custom_call" | custom-call | flops 6900000 | bytes 1 | tf_op jit(solution)/shard_map/input_grad/pallas_call | solution.py:483
  60.4 2.8 %collective-permute-start.16 = (bf16[392,768]{1,0:T(8,128)(2,1)S(1)}, bf16[392,768]{1,0:T(8,128)(2,1)S(1)}, u32[]{:S(2)}, u32[]{:S(2)}) collective-permute-start(bf16[392,768]{1,0:T(8,128)(2,1)S(1)} %outer_turn.1), channel_id=1, source_target_pairs={{0,1},{1,0},{2,3},{3,2},{4,5},{5,4},{6,7},{7,6},{8,9},{9,8},{10,11... | collective-permute-start | bytes 1806344 | tf_op jit(solution)/shard_map/ppermute | solution.py:639
  63.2 1.6 %weight_grad_more.1 = (bf16[384,384]{1,0:T(8,128)(2,1)S(1)}, bf16[384,384]{1,0:T(8,128)(2,1)S(1)}) custom-call(s32[8]{0:T(128)S(1)} %dynamic-slice_bitcast_fusion.role_ref.order_ref.place_ref, bf16[392,768]{1,0:T(8,128)(2,1)S(1)} %get-tuple-element.52.scaled_ref.own_ref, bf16[392,768]{1,0:T(8,128)(2,1)S(1)} %collective-permute-done.9.other_ref, ...), custom_call_target="tpu_custom_call" | custom-call | flops 6900000 | bytes 1 | tf_op jit(solution)/shard_map/weight_grad_more/pallas_call | solution.py:556
  64.8 1.6 %collective-permute-start.18 = (bf16[384,384]{1,0:T(8,128)(2,1)S(1)}, bf16[384,384]{1,0:T(8,128)(2,1)S(1)}, u32[]{:S(2)}, u32[]{:S(2)}) collective-permute-start(bf16[384,384]{1,0:T(8,128)(2,1)S(1)} %get-tuple-element.80.refs_4_), channel_id=1, source_target_pairs={{0,8},{4,12},{8,0},{12,4},{16,24},{20,28},{24,16},{28,20},{1,9},{5... | collective-permute-start | bytes 884744 | tf_op jit(solution)/shard_map/ppermute | solution.py:643
  66.4 1.5 %collective-permute-start.19 = (bf16[384,384]{1,0:T(8,128)(2,1)S(1)}, bf16[384,384]{1,0:T(8,128)(2,1)S(1)}, u32[]{:S(2)}, u32[]{:S(2)}) collective-permute-start(bf16[384,384]{1,0:T(8,128)(2,1)S(1)} %get-tuple-element.71.refs_6_), channel_id=1, source_target_pairs={{0,16},{4,20},{8,24},{12,28},{16,0},{20,4},{24,8},{28,12},{1,17},{... | collective-permute-start | bytes 884744 | tf_op jit(solution)/shard_map/ppermute | solution.py:643
  67.9 2.6 %input_grad_last.1 = (f32[392,768]{1,0:T(8,128)S(1)}, f32[2,1024]{1,0:T(2,128)S(1)}) custom-call(s32[8]{0:T(128)S(1)} %dynamic-slice_bitcast_fusion.role_ref.order_ref.place_ref, bf16[392,768]{1,0:T(8,128)(2,1)S(1)} %get-tuple-element.72.refs_0_, bf16[768,3072]{1,0:T(8,128)(2,1)S(1)} %bitcast.7, f32[392,768]{1,0:T(8,128)S(1)} %input_grad.1.refs_2_, ...), custom_call_target="tpu_custom_call" | custom-call | flops 3449999872 | bytes 1 | tf_op jit(solution)/shard_map/input_grad_last/pallas_call | solution.py:483
  71.0 2.7 %collective-permute-done.18.refs_5_ = bf16[384,384]{1,0:T(8,128)(2,1)S(1)} collective-permute-done((bf16[384,384]{1,0:T(8,128)(2,1)S(1)}, bf16[384,384]{1,0:T(8,128)(2,1)S(1)}, u32[]{:S(2)}, u32[]{:S(2)}) %collective-permute-start.18) | collective-permute-done | bytes 294944 | tf_op jit(solution)/shard_map/ppermute | solution.py:643
  73.7 1.2 %collective-permute-done.19.refs_7_ = bf16[384,384]{1,0:T(8,128)(2,1)S(1)} collective-permute-done((bf16[384,384]{1,0:T(8,128)(2,1)S(1)}, bf16[384,384]{1,0:T(8,128)(2,1)S(1)}, u32[]{:S(2)}, u32[]{:S(2)}) %collective-permute-start.19) | collective-permute-done | bytes 294944 | tf_op jit(solution)/shard_map/ppermute | solution.py:643
  74.9 1.2 %merge.1 = (bf16[384,384]{1,0:T(8,128)(2,1)S(1)}, bf16[384,384]{1,0:T(8,128)(2,1)S(1)}, bf16[384,384]{1,0:T(8,128)(2,1)S(1)}, bf16[384,384]{1,0:T(8,128)(2,1)S(1)}) custom-call(s32[8]{0:T(128)S(1)} %dynamic-slice_bitcast_fusion.role_ref.order_ref.place_ref, bf16[2,384,384]{2,1,0:T(8,128)(2,1)S(1)} %get-tuple-element.76.refs_0_, ...), custom_call_target="tpu_custom_call" | custom-call | flops 690000000 | bytes 1 | tf_op jit(solution)/shard_map/merge/pallas_call | solution.py:597
  76.1 1.6 %collective-permute-start.23 = (bf16[384,384]{1,0:T(8,128)(2,1)S(1)}, bf16[384,384]{1,0:T(8,128)(2,1)S(1)}, u32[]{:S(2)}, u32[]{:S(2)}) collective-permute-start(bf16[384,384]{1,0:T(8,128)(2,1)S(1)} %get-tuple-element.93), channel_id=1, source_target_pairs={{0,16},{4,20},{8,24},{12,28},{16,0},{20,4},{24,8},{28,12},{1,17},{... | collective-permute-start | bytes 884744 | tf_op jit(solution)/shard_map/ppermute | solution.py:643
  78.9 2.3 %collective-permute-start.21 = (f32[2,1024]{1,0:T(2,128)S(1)}, f32[2,1024]{1,0:T(2,128)S(1)}, u32[]{:S(2)}, u32[]{:S(2)}) collective-permute-start(f32[2,1024]{1,0:T(2,128)S(1)} %get-tuple-element.90.own_ref), channel_id=1, source_target_pairs={{0,3},{3,0},{1,2},{2,1},{4,7},{7,4},{5,6},{6,5},{8,11},{11,8},{9,1... | collective-permute-start | bytes 24584 | tf_op jit(solution)/shard_map/ppermute | solution.py:639
  81.7 1.7 %fourth_turn.1 = bf16[14,14,2,768]{3,2,1,0:T(2,128)(2,1)} custom-call(s32[8]{0:T(128)S(1)} %dynamic-slice_bitcast_fusion.role_ref.order_ref.place_ref, bf16[392,768]{1,0:T(8,128)(2,1)S(1)} %get-tuple-element.53.p_own, bf16[392,768]{1,0:T(8,128)(2,1)S(1)} %collective-permute-done.16.came, bf16[392,768]{1,0:T(8,128)(2,1)S(1)} %collective-permute-done.17.crossed), custom_call_target="tpu_custom_call" | custom-call | flops 6900000 | bytes 1 | tf_op jit(solution)/shard_map/fourth_turn/pallas_call | solution.py:407
  84.4 1.4 %collective-permute-done.22.over_ref = f32[2,1024]{1,0:T(2,128)S(1)} collective-permute-done((f32[2,1024]{1,0:T(2,128)S(1)}, f32[2,1024]{1,0:T(2,128)S(1)}, u32[]{:S(2)}, u32[]{:S(2)}) %collective-permute-start.22) | collective-permute-done | bytes 8224 | tf_op jit(solution)/shard_map/ppermute | solution.py:639
  85.8 4.0 %conv_backward.1 = bf16[14,14,2,768]{3,2,1,0:T(2,128)(2,1)} custom-call(f32[392,768]{1,0:T(8,128)S(1)} %get-tuple-element.83.part_ref, f32[392,768]{1,0:T(8,128)S(1)} %get-tuple-element.88.slope_ref, f32[2,1024]{1,0:T(2,128)S(1)} %get-tuple-element.90.own_ref, f32[2,1024]{1,0:T(2,128)S(1)} %collective-permute-done.20.near_ref, ...), custom_call_target="tpu_custom_call" | custom-call | flops 1035000000 | bytes 1 | tf_op jit(solution)/shard_map/conv_backward/pallas_call | solution.py:250
  89.8 1.1 %finish.1 = f32[768,384]{1,0:T(8,128)} custom-call(bf16[384,384]{1,0:T(8,128)(2,1)S(1)} %get-tuple-element.92.top, bf16[384,384]{1,0:T(8,128)(2,1)S(1)} %collective-permute-done.23.top_came, bf16[384,384]{1,0:T(8,128)(2,1)S(1)} %get-tuple-element.94.bottom, bf16[384,384]{1,0:T(8,128)(2,1)S(1)} %collective-permute-done.24.bottom_came), custom_call_target="tpu_custom_call" | custom-call | flops 690000000 | bytes 1 | tf_op jit(solution)/shard_map/finish/pallas_call | solution.py:618
  (61 shorter events, 12.0 us)
Async XLA Ops:
  0.6 21.8 %collective-permute-start.3 = (bf16[14,14,2,768]{3,2,1,0:T(2,128)(2,1)}, bf16[14,14,2,768]{3,2,1,0:T(2,128)(2,1)}, u32[]{:S(2)}, u32[]{:S(2)}) collective-permute-start(bf16[14,14,2,768]{3,2,1,0:T(2,128)(2,1)} %bitcast.8), channel_id=1, source_target_pairs={{1,2},{2,1},{5,6},{6,5},{9,10},{10,9},{13,14},{14,13},{17,18},{18,... | collective-permute-start | bytes 1806344 | tf_op jit(solution)/shard_map/ppermute | solution.py:639
  2.1 23.0 %collective-permute-start.4 = (bf16[14,14,2,768]{3,2,1,0:T(2,128)(2,1)}, bf16[14,14,2,768]{3,2,1,0:T(2,128)(2,1)}, u32[]{:S(2)}, u32[]{:S(2)}) collective-permute-start(bf16[14,14,2,768]{3,2,1,0:T(2,128)(2,1)} %bitcast.9), channel_id=1, source_target_pairs={{0,1},{1,0},{2,3},{3,2},{4,5},{5,4},{6,7},{7,6},{8,9},{9,8},{10,11... | collective-permute-start | bytes 1806344 | tf_op jit(solution)/shard_map/ppermute | solution.py:639
  10.3 12.1 %copy-start.1 = (bf16[1024,768]{1,0:T(8,128)(2,1)S(1)}, bf16[1024,768]{1,0:T(8,128)(2,1)}, u32[]{:S(2)}) copy-start(bf16[1024,768]{1,0:T(8,128)(2,1)} %refs_5_.1) | copy-start | bytes 4718596
  15.8 5.3 %collective-permute-start = (f32[2,1024]{1,0:T(2,128)S(1)}, f32[2,1024]{1,0:T(2,128)S(1)}, u32[]{:S(2)}, u32[]{:S(2)}) collective-permute-start(f32[2,1024]{1,0:T(2,128)S(1)} %get-tuple-element.51.own_ref), channel_id=1, source_target_pairs={{0,1},{1,0},{2,3},{3,2},{4,5},{5,4},{6,7},{7,6},{8,9},{9,8},{10,11... | collective-permute-start | bytes 24584 | tf_op jit(solution)/shard_map/ppermute | solution.py:639
  15.8 6.4 %collective-permute-start.1 = (f32[2,1024]{1,0:T(2,128)S(1)}, f32[2,1024]{1,0:T(2,128)S(1)}, u32[]{:S(2)}, u32[]{:S(2)}) collective-permute-start(f32[2,1024]{1,0:T(2,128)S(1)} %get-tuple-element.51.own_ref), channel_id=1, source_target_pairs={{0,3},{3,0},{1,2},{2,1},{4,7},{7,4},{5,6},{6,5},{8,11},{11,8},{9,1... | collective-permute-start | bytes 24584 | tf_op jit(solution)/shard_map/ppermute | solution.py:639
  17.8 4.6 %collective-permute-start.2 = (f32[2,1024]{1,0:T(2,128)S(1)}, f32[2,1024]{1,0:T(2,128)S(1)}, u32[]{:S(2)}, u32[]{:S(2)}) collective-permute-start(f32[2,1024]{1,0:T(2,128)S(1)} %get-tuple-element.51.own_ref), channel_id=1, source_target_pairs={{0,2},{2,0},{1,3},{3,1},{4,6},{6,4},{5,7},{7,5},{8,10},{10,8},{9,1... | collective-permute-start | bytes 24584 | tf_op jit(solution)/shard_map/ppermute | solution.py:639
  22.4 3.5 %copy-start.8 = (bf16[2,14,14,768]{3,0,2,1:T(2,128)(2,1)S(1)}, bf16[2,14,14,768]{3,0,2,1:T(2,128)(2,1)}, u32[]{:S(2)}) copy-start(bf16[2,14,14,768]{3,0,2,1:T(2,128)(2,1)} %param.12) | copy-start | bytes 1806340
  24.6 13.7 %collective-permute-start.6 = (bf16[392,768]{1,0:T(8,128)(2,1)S(1)}, bf16[392,768]{1,0:T(8,128)(2,1)S(1)}, u32[]{:S(2)}, u32[]{:S(2)}) collective-permute-start(bf16[392,768]{1,0:T(8,128)(2,1)S(1)} %get-tuple-element.56.held), channel_id=1, source_target_pairs={{0,1},{1,0},{2,3},{3,2},{4,5},{5,4},{6,7},{7,6},{8,9},{9,8},{10,11... | collective-permute-start | bytes 1806344 | tf_op jit(solution)/shard_map/ppermute | solution.py:639
  25.2 13.9 %collective-permute-start.5 = (bf16[14,14,2,768]{3,2,1,0:T(2,128)(2,1)}, bf16[14,14,2,768]{3,2,1,0:T(2,128)(2,1)S(1)}, u32[]{:S(2)}, u32[]{:S(2)}) collective-permute-start(bf16[14,14,2,768]{3,2,1,0:T(2,128)(2,1)} %collective-permute-done.4.refs_1_), channel_id=1, source_target_pairs={{1,2},{2,1},{5,6},{6,5},{9,10},{10,9},{13,14},{14,13},{17,18},{18,... | collective-permute-start | bytes 1806344 | tf_op jit(solution)/shard_map/ppermute | solution.py:639
  25.9 14.7 %collective-permute-start.10 = (bf16[14,14,2,768]{3,2,1,0:T(2,128)(2,1)S(1)}, bf16[14,14,2,768]{3,2,1,0:T(2,128)(2,1)S(1)}, u32[]{:S(2)}, u32[]{:S(2)}) collective-permute-start(bf16[14,14,2,768]{3,2,1,0:T(2,128)(2,1)S(1)} %bitcast.10), channel_id=1, source_target_pairs={{0,4},{4,0},{8,12},{12,8},{16,20},{20,16},{24,28},{28,24},{1,5},{5... | collective-permute-start | bytes 1806344 | tf_op jit(solution)/shard_map/ppermute | solution.py:643
  26.0 20.4 %collective-permute-start.9 = (bf16[392,768]{1,0:T(8,128)(2,1)S(1)}, bf16[392,768]{1,0:T(8,128)(2,1)S(1)}, u32[]{:S(2)}, u32[]{:S(2)}) collective-permute-start(bf16[392,768]{1,0:T(8,128)(2,1)S(1)} %get-tuple-element.52.scaled_ref.own_ref), channel_id=1, source_target_pairs={{0,4},{4,0},{8,12},{12,8},{16,20},{20,16},{24,28},{28,24},{1,5},{5... | collective-permute-start | bytes 1806344 | tf_op jit(solution)/shard_map/ppermute | solution.py:643
  26.5 19.9 %collective-permute-start.11 = (bf16[14,14,2,768]{3,2,1,0:T(2,128)(2,1)}, bf16[14,14,2,768]{3,2,1,0:T(2,128)(2,1)S(1)}, u32[]{:S(2)}, u32[]{:S(2)}) collective-permute-start(bf16[14,14,2,768]{3,2,1,0:T(2,128)(2,1)} %collective-permute-done.4.refs_1_), channel_id=1, source_target_pairs={{0,4},{4,0},{8,12},{12,8},{16,20},{20,16},{24,28},{28,24},{1,5},{5... | collective-permute-start | bytes 1806344 | tf_op jit(solution)/shard_map/ppermute | solution.py:643
  38.3 16.0 %slice-start = ((s8[4718592]{0:T(1024)(128)(4,1)}), s8[4194304]{0:T(1024)(128)(4,1)S(1)}, s32[]{:S(2)}) async-start(s8[4718592]{0:T(1024)(128)(4,1)} %bitcast.6), calls=%async_computation | async-start | bytes 8388608
  39.0 7.3 %collective-permute-start.12 = (bf16[392,768]{1,0:T(8,128)(2,1)S(1)}, bf16[392,768]{1,0:T(8,128)(2,1)S(1)}, u32[]{:S(2)}, u32[]{:S(2)}) collective-permute-start(bf16[392,768]{1,0:T(8,128)(2,1)S(1)} %get-tuple-element.64.refs_2_), channel_id=1, source_target_pairs={{0,4},{4,0},{8,12},{12,8},{16,20},{20,16},{24,28},{28,24},{1,5},{5... | collective-permute-start | bytes 1806344 | tf_op jit(solution)/shard_map/ppermute | solution.py:643
  39.1 19.0 %collective-permute-start.8 = (bf16[392,768]{1,0:T(8,128)(2,1)S(1)}, bf16[392,768]{1,0:T(8,128)(2,1)S(1)}, u32[]{:S(2)}, u32[]{:S(2)}) collective-permute-start(bf16[392,768]{1,0:T(8,128)(2,1)S(1)} %get-tuple-element.59), channel_id=1, source_target_pairs={{1,2},{2,1},{5,6},{6,5},{9,10},{10,9},{13,14},{14,13},{17,18},{18,... | collective-permute-start | bytes 1806344 | tf_op jit(solution)/shard_map/ppermute | solution.py:639
  39.9 14.3 %slice-start.1 = ((s8[4718592]{0:T(1024)(128)(4,1)}), s8[524288]{0:T(1024)(128)(4,1)S(1)}, s32[]{:S(2)}) async-start(s8[4718592]{0:T(1024)(128)(4,1)} %bitcast.6), calls=%async_computation.1 | async-start | bytes 1048576
  40.6 18.3 %collective-permute-start.7 = (bf16[392,768]{1,0:T(8,128)(2,1)S(1)}, bf16[392,768]{1,0:T(8,128)(2,1)S(1)}, u32[]{:S(2)}, u32[]{:S(2)}) collective-permute-start(bf16[392,768]{1,0:T(8,128)(2,1)S(1)} %far_turn.1.held), channel_id=1, source_target_pairs={{0,1},{1,0},{2,3},{3,2},{4,5},{5,4},{6,7},{7,6},{8,9},{9,8},{10,11... | collective-permute-start | bytes 1806344 | tf_op jit(solution)/shard_map/ppermute | solution.py:639
  51.2 15.2 %collective-permute-start.13 = (bf16[2,384,384]{2,1,0:T(8,128)(2,1)S(1)}, bf16[2,384,384]{2,1,0:T(8,128)(2,1)S(1)}, u32[]{:S(2)}, u32[]{:S(2)}) collective-permute-start(bf16[2,384,384]{2,1,0:T(8,128)(2,1)S(1)} %get-tuple-element.69), channel_id=1, source_target_pairs={{0,8},{4,12},{8,0},{12,4},{16,24},{20,28},{24,16},{28,20},{1,9},{5... | collective-permute-start | bytes 1769480 | tf_op jit(solution)/shard_map/ppermute | solution.py:643
  52.7 15.2 %collective-permute-start.14 = (bf16[2,384,384]{2,1,0:T(8,128)(2,1)S(1)}, bf16[2,384,384]{2,1,0:T(8,128)(2,1)S(1)}, u32[]{:S(2)}, u32[]{:S(2)}) collective-permute-start(bf16[2,384,384]{2,1,0:T(8,128)(2,1)S(1)} %get-tuple-element.63), channel_id=1, source_target_pairs={{0,16},{4,20},{8,24},{12,28},{16,0},{20,4},{24,8},{28,12},{1,17},{... | collective-permute-start | bytes 1769480 | tf_op jit(solution)/shard_map/ppermute | solution.py:643
  59.6 3.6 %collective-permute-start.15 = (bf16[392,384]{1,0:T(8,128)(2,1)S(1)}, bf16[392,384]{1,0:T(8,128)(2,1)S(1)}, u32[]{:S(2)}, u32[]{:S(2)}) collective-permute-start(bf16[392,384]{1,0:T(8,128)(2,1)S(1)} %get-tuple-element.70), channel_id=1, source_target_pairs={{0,4},{4,0},{8,12},{12,8},{16,20},{20,16},{24,28},{28,24},{1,5},{5... | collective-permute-start | bytes 903176 | tf_op jit(solution)/shard_map/ppermute | solution.py:643
  59.7 18.5 %collective-permute-start.17 = (bf16[392,768]{1,0:T(8,128)(2,1)S(1)}, bf16[392,768]{1,0:T(8,128)(2,1)S(1)}, u32[]{:S(2)}, u32[]{:S(2)}) collective-permute-start(bf16[392,768]{1,0:T(8,128)(2,1)S(1)} %get-tuple-element.75), channel_id=1, source_target_pairs={{1,2},{2,1},{5,6},{6,5},{9,10},{10,9},{13,14},{14,13},{17,18},{18,... | collective-permute-start | bytes 1806344 | tf_op jit(solution)/shard_map/ppermute | solution.py:639
  60.4 17.8 %collective-permute-start.16 = (bf16[392,768]{1,0:T(8,128)(2,1)S(1)}, bf16[392,768]{1,0:T(8,128)(2,1)S(1)}, u32[]{:S(2)}, u32[]{:S(2)}) collective-permute-start(bf16[392,768]{1,0:T(8,128)(2,1)S(1)} %outer_turn.1), channel_id=1, source_target_pairs={{0,1},{1,0},{2,3},{3,2},{4,5},{5,4},{6,7},{7,6},{8,9},{9,8},{10,11... | collective-permute-start | bytes 1806344 | tf_op jit(solution)/shard_map/ppermute | solution.py:639
  64.8 8.9 %collective-permute-start.18 = (bf16[384,384]{1,0:T(8,128)(2,1)S(1)}, bf16[384,384]{1,0:T(8,128)(2,1)S(1)}, u32[]{:S(2)}, u32[]{:S(2)}) collective-permute-start(bf16[384,384]{1,0:T(8,128)(2,1)S(1)} %get-tuple-element.80.refs_4_), channel_id=1, source_target_pairs={{0,8},{4,12},{8,0},{12,4},{16,24},{20,28},{24,16},{28,20},{1,9},{5... | collective-permute-start | bytes 884744 | tf_op jit(solution)/shard_map/ppermute | solution.py:643
  66.4 8.6 %collective-permute-start.19 = (bf16[384,384]{1,0:T(8,128)(2,1)S(1)}, bf16[384,384]{1,0:T(8,128)(2,1)S(1)}, u32[]{:S(2)}, u32[]{:S(2)}) collective-permute-start(bf16[384,384]{1,0:T(8,128)(2,1)S(1)} %get-tuple-element.71.refs_6_), channel_id=1, source_target_pairs={{0,16},{4,20},{8,24},{12,28},{16,0},{20,4},{24,8},{28,12},{1,17},{... | collective-permute-start | bytes 884744 | tf_op jit(solution)/shard_map/ppermute | solution.py:643
  67.9 2.6 %copy-start.5 = (f32[392,768]{1,0:T(8,128)S(1)}, f32[392,768]{1,0:T(8,128)}, u32[]{:S(2)}) copy-start(f32[392,768]{1,0:T(8,128)} %copy-done.4) | copy-start | bytes 3612676
  74.9 10.9 %copy-start.7 = (bf16[3,3,64,768]{3,2,1,0:T(8,128)(2,1)S(1)}, bf16[3,3,64,768]{3,2,1,0:T(8,128)(2,1)}, u32[]{:S(2)}) copy-start(bf16[3,3,64,768]{3,2,1,0:T(8,128)(2,1)} %w_ref.5) | copy-start | bytes 2654212
  76.1 13.7 %collective-permute-start.23 = (bf16[384,384]{1,0:T(8,128)(2,1)S(1)}, bf16[384,384]{1,0:T(8,128)(2,1)S(1)}, u32[]{:S(2)}, u32[]{:S(2)}) collective-permute-start(bf16[384,384]{1,0:T(8,128)(2,1)S(1)} %get-tuple-element.93), channel_id=1, source_target_pairs={{0,16},{4,20},{8,24},{12,28},{16,0},{20,4},{24,8},{28,12},{1,17},{... | collective-permute-start | bytes 884744 | tf_op jit(solution)/shard_map/ppermute | solution.py:643
  77.7 8.1 %copy-start.3 = (bf16[768,1024]{1,0:T(8,128)(2,1)S(1)}, bf16[768,1024]{1,0:T(8,128)(2,1)}, u32[]{:S(2)}) copy-start(bf16[768,1024]{1,0:T(8,128)(2,1)} %down_ref.3) | copy-start | bytes 4718596
  77.7 12.1 %collective-permute-start.24 = (bf16[384,384]{1,0:T(8,128)(2,1)S(1)}, bf16[384,384]{1,0:T(8,128)(2,1)S(1)}, u32[]{:S(2)}, u32[]{:S(2)}) collective-permute-start(bf16[384,384]{1,0:T(8,128)(2,1)S(1)} %get-tuple-element.85), channel_id=1, source_target_pairs={{0,8},{4,12},{8,0},{12,4},{16,24},{20,28},{24,16},{28,20},{1,9},{5... | collective-permute-start | bytes 884744 | tf_op jit(solution)/shard_map/ppermute | solution.py:643
  78.2 5.2 %collective-permute-start.20 = (f32[2,1024]{1,0:T(2,128)S(1)}, f32[2,1024]{1,0:T(2,128)S(1)}, u32[]{:S(2)}, u32[]{:S(2)}) collective-permute-start(f32[2,1024]{1,0:T(2,128)S(1)} %get-tuple-element.90.own_ref), channel_id=1, source_target_pairs={{0,1},{1,0},{2,3},{3,2},{4,5},{5,4},{6,7},{7,6},{8,9},{9,8},{10,11... | collective-permute-start | bytes 24584 | tf_op jit(solution)/shard_map/ppermute | solution.py:639
  78.9 5.4 %collective-permute-start.21 = (f32[2,1024]{1,0:T(2,128)S(1)}, f32[2,1024]{1,0:T(2,128)S(1)}, u32[]{:S(2)}, u32[]{:S(2)}) collective-permute-start(f32[2,1024]{1,0:T(2,128)S(1)} %get-tuple-element.90.own_ref), channel_id=1, source_target_pairs={{0,3},{3,0},{1,2},{2,1},{4,7},{7,4},{5,6},{6,5},{8,11},{11,8},{9,1... | collective-permute-start | bytes 24584 | tf_op jit(solution)/shard_map/ppermute | solution.py:639
  81.2 4.5 %collective-permute-start.22 = (f32[2,1024]{1,0:T(2,128)S(1)}, f32[2,1024]{1,0:T(2,128)S(1)}, u32[]{:S(2)}, u32[]{:S(2)}) collective-permute-start(f32[2,1024]{1,0:T(2,128)S(1)} %get-tuple-element.90.own_ref), channel_id=1, source_target_pairs={{0,2},{2,0},{1,3},{3,1},{4,6},{6,4},{5,7},{7,5},{8,10},{10,8},{9,1... | collective-permute-start | bytes 24584 | tf_op jit(solution)/shard_map/ppermute | solution.py:639
  (5 other events, 8.2 us)
